TPU v7x, 128 devices: a whole 4x4x4 slice. The times are simulated.
128 devices in a mesh: ctx: 8 (over y_lo, x), mdl: 16 (over z, y_hi, core).
Axes of the slice: x: 4, y: 4 (y_hi: 2, y_lo: 2; y = y_hi * 2 + y_lo), z: 4, core: 2. Of those that a mesh axis runs over, the one named last changes fastest.
Arguments:
- latents: bfloat16 [2048, 5120], P('ctx', 'mdl')
- mod_shift: float32 [5120], replicated, may hold values from -3 to 3
- mod_scale: float32 [5120], replicated, may hold values from -0.5 to 0.5
- gate: float32 [5120], replicated, may hold values from 0.3 to 3
- w_query: bfloat16 [5120, 4096], P(None, 'mdl'), may hold values from -0.15625 to 0.15625
- w_key: bfloat16 [5120, 4096], P(None, 'mdl'), may hold values from -0.078125 to 0.078125
- w_value: bfloat16 [5120, 4096], P(None, 'mdl'), may hold values from -0.078125 to 0.078125
- w_out: bfloat16 [4096, 5120], P('mdl'), may hold values from -0.75 to 0.75
- cache_keys: bfloat16 [4096, 4096], P('ctx', 'mdl'), may hold values from -610 to 610
- cache_values: bfloat16 [4096, 4096], P('ctx', 'mdl'), may hold values from -6 to 6
- final_scale: float32 [5120], replicated, may hold values from -0.5 to 0.5
- w_final: bfloat16 [5120, 64], replicated, may hold values from -0.078125 to 0.078125
- state: float32 [512, 256], P(('ctx', 'mdl')), may hold values from -6 to 6
- noise: float32 [512, 256], P(('ctx', 'mdl')), may hold values from -6 to 6
- owners: int32 [512, 1], P(('ctx', 'mdl')), may hold values from 0 to 15; in each aligned block of 4 rows (0 to 3, 4 to 7, ...) at most 2 rows name the same one
- w_up: bfloat16 [256, 1024], replicated, may hold values from -0.375 to 0.375
Outputs:
- hidden_out: bfloat16 [2048, 5120], P(('ctx', 'mdl'))
- next_state: float32 [512, 256], P(('ctx', 'mdl'))
- upsampled: bfloat16 [4096, 1024], P(('ctx', 'mdl'))
Inputs may be any that keep to these rules, and one draw needn't show every extreme that they name: `owners`: among the 4 tiles of one device no owner is named more than 2 times, a bound that some block reaches.
All inputs are finite; a program needn't handle non-finite values.
Results may differ from a plain program's by a relative error of at most 0.039.
The roundings to bfloat16 on the way count: a program that leaves them out, or rounds other values in their place, can miss the bound.
Values may be sent and summed in bfloat16 or wider, within the bound.
No kernel may reach another device: no remote copies, remote signals or barrier semaphores. Data moves between devices by JAX's collectives and lax.ppermute only.
A program may use at most 128 MiB of HBM per device.

v0:
```python
import math

import jax
import jax.numpy as jnp
from jax import lax
from jax.sharding import PartitionSpec as P

HD = 128
CAP = 2


def block_stats(queries, keys, values, heads):
    count = queries.shape[0]
    width = keys.shape[0]
    query_heads = queries.reshape(count, heads, HD)
    key_heads = keys.reshape(width, heads, HD)
    value_heads = values.reshape(width, heads, HD)
    scores = jnp.einsum(
        "nhd,khd->hnk", query_heads, key_heads, preferred_element_type=jnp.float32
    ) / math.sqrt(HD)
    row_peak = jnp.max(scores, -1)
    probs = jnp.exp(scores - row_peak[:, :, None])
    row_total = jnp.sum(probs, -1)
    summed = jnp.einsum(
        "hnk,khd->nhd", probs.astype(jnp.bfloat16), value_heads, preferred_element_type=jnp.float32
    )
    return (row_peak, row_total, summed)


def merge_stats(first, second):
    peak_one, total_one, summed_one = first
    peak_two, total_two, summed_two = second
    new_peak = jnp.maximum(peak_one, peak_two)
    factor_one = jnp.exp(peak_one - new_peak)
    factor_two = jnp.exp(peak_two - new_peak)
    new_total = total_one * factor_one + total_two * factor_two
    new_summed = summed_one * factor_one.T[:, :, None] + summed_two * factor_two.T[:, :, None]
    return (new_peak, new_total, new_summed)


def head_stats(queries, keys, values, heads):
    width = keys.shape[0]
    block = width
    while block > 2048 and block % 2 == 0:
        block = block // 2
    blocks = width // block
    key_blocks = keys.reshape(blocks, block, keys.shape[1])
    value_blocks = values.reshape(blocks, block, values.shape[1])
    first = block_stats(queries, key_blocks[0], value_blocks[0], heads)

    def step(carry, pieces):
        return (merge_stats(carry, block_stats(queries, pieces[0], pieces[1], heads)), None)

    result, unused = lax.scan(step, first, (key_blocks[1:], value_blocks[1:]))
    return result


def shards(
    latents,
    mod_shift,
    mod_scale,
    gate,
    w_query,
    w_key,
    w_value,
    w_out,
    cache_keys,
    cache_values,
    final_scale,
    w_final,
    state,
    noise,
    owners,
    w_up,
):
    whole = lax.all_gather(latents, "mdl", axis=1, tiled=True)
    x_float = whole.astype(jnp.float32)
    row_mean = jnp.mean(x_float, -1, keepdims=True)
    centred = x_float - row_mean
    row_var = jnp.mean(centred * centred, -1, keepdims=True)
    normed_in = (centred * lax.rsqrt(row_var + 1e-06) * (1.0 + mod_scale) + mod_shift).astype(
        jnp.bfloat16
    )
    queries = jnp.dot(normed_in, w_query, preferred_element_type=jnp.float32).astype(jnp.bfloat16)
    count = queries.shape[0]
    heads = queries.shape[1] // HD
    empty = (
        jnp.full((heads, count), -jnp.inf, jnp.float32),
        jnp.zeros((heads, count), jnp.float32),
        jnp.zeros((count, heads, HD), jnp.float32),
    )
    keys_new = jnp.dot(normed_in, w_key, preferred_element_type=jnp.float32).astype(jnp.bfloat16)
    values_new = jnp.dot(normed_in, w_value, preferred_element_type=jnp.float32).astype(
        jnp.bfloat16
    )
    keys_new, values_new = (keys_new, values_new)
    joined_keys = jnp.concatenate([cache_keys, keys_new], 0)
    joined_values = jnp.concatenate([cache_values, values_new], 0)
    stats = merge_stats(
        empty,
        head_stats(
            queries,
            lax.all_gather(joined_keys, "ctx", axis=0, tiled=True),
            lax.all_gather(joined_values, "ctx", axis=0, tiled=True),
            heads,
        ),
    )
    final_total = stats[1]
    final_summed = stats[2]
    attended = (
        (final_summed / final_total.T[:, :, None]).reshape(count, heads * HD).astype(jnp.bfloat16)
    )
    n_mdl = lax.axis_size("mdl")
    rows = count // n_mdl
    projected = lax.psum_scatter(
        jnp.dot(attended, w_out, preferred_element_type=jnp.float32).astype(jnp.bfloat16),
        "mdl",
        scatter_dimension=0,
        tiled=True,
    ).astype(jnp.float32)
    own_rows = lax.dynamic_slice_in_dim(x_float, lax.axis_index("mdl") * rows, rows, 0)
    mixed = own_rows + gate * projected
    hidden_out = mixed.astype(jnp.bfloat16)
    inverse = lax.rsqrt(jnp.mean(mixed * mixed, -1, keepdims=True) + 1e-06)
    normed_out = (mixed * inverse * (1.0 + final_scale)).astype(jnp.bfloat16)
    tiles_here = state.shape[0]
    panel_width = state.shape[1]
    velocity = jnp.dot(normed_out, w_final, preferred_element_type=jnp.float32).reshape(
        tiles_here, panel_width
    )
    next_state = (
        state
        + 0.2 * (velocity + 0.5 * (0.5 * velocity - state) / (1.0 - 0.5))
        + math.sqrt(0.2) * noise
    )
    panels = next_state.astype(jnp.bfloat16)
    owner_ids = owners[:, 0]
    same = owner_ids[:, None] == owner_ids[None, :]
    earlier = jnp.arange(tiles_here)[None, :] < jnp.arange(tiles_here)[:, None]
    slots = jnp.sum(jnp.logical_and(same, earlier).astype(jnp.int32), -1)
    target = owner_ids * CAP + slots
    columns = jnp.arange(n_mdl * CAP, dtype=jnp.int32)
    one_hot = (target[:, None] == columns[None, :]).astype(jnp.bfloat16)
    slot_rows = jnp.einsum("ts,tp->sp", one_hot, panels, preferred_element_type=jnp.float32).astype(
        jnp.bfloat16
    )
    slot_rows = slot_rows.reshape(n_mdl, CAP, panel_width)
    result = jax.nn.gelu(
        jnp.einsum(
            "scp,pu->scu",
            lax.all_to_all(slot_rows, "mdl", split_axis=0, concat_axis=0, tiled=True),
            w_up,
            preferred_element_type=jnp.float32,
        )
    ).astype(jnp.bfloat16)
    upsampled = result.reshape(n_mdl * CAP, w_up.shape[1])
    return (hidden_out, next_state, upsampled)


def solution(mesh):
    return jax.shard_map(
        shards,
        mesh=mesh,
        in_specs=(
            P("ctx", "mdl"),
            P(),
            P(),
            P(),
            P(None, "mdl"),
            P(None, "mdl"),
            P(None, "mdl"),
            P("mdl", None),
            P("ctx", "mdl"),
            P("ctx", "mdl"),
            P(),
            P(),
            P(("ctx", "mdl"), None),
            P(("ctx", "mdl"), None),
            P(("ctx", "mdl"), None),
            P(),
        ),
        out_specs=(P(("ctx", "mdl"), None), P(("ctx", "mdl"), None), P(("ctx", "mdl"), None)),
        check_vma=False,
    )
```

profile of v0, /device:TPU:1, one launch (start us, length us, event | category | flops | bytes accessed | tf_op | source)
XLA Modules:
  0.0 304.5 jit_solution(11315691816668188927)
XLA Ops:
  7.2 0.7 all-gather.4.cloned.1.call-update
  8.0 0.7 broadcast_add_fusion.1
  8.7 54.7 %all-gather.4.cloned.1.call-done = bf16[256,5120]{0,1:T(8,128)(2,1)} async-done(((bf16[256,320]{0,1:T(8,128)(2,1)}), bf16[256,5120]{0,1:T(8,128)(2,1)}) %all-gather.4.cloned.1.call-update) | async-done | bytes 2621456 | tf_op jit(solution)/shard_map/all_gather | solution.py:76
  63.4 4.5 %copy.73 = bf16[256,5120]{1,0:T(8,128)(2,1)} copy(bf16[256,5120]{0,1:T(8,128)(2,1)} %all-gather.4.cloned.1.call-done) | data formatting | bytes 5242880 | tf_op jit(solution)/shard_map/all_gather | solution.py:76
  68.0 2.3 convert_reduce_fusion
  70.3 0.2 copy-done.1
  70.5 0.8 multiply_reduce_fusion
  71.4 1.3 add_convert_fusion
  72.6 1.5 copy-done.4
  74.1 0.9 convolution_convert_fusion.1
  75.0 0.1 copy-done.9
  75.1 0.8 pad_maximum_fusion.1
  75.9 0.1 copy.74
  76.1 3.4 %convolution_convert_fusion.2 = bf16[256,256]{1,0:T(8,128)(2,1)S(1)} fusion(bf16[256,5120]{1,0:T(8,128)(2,1)} %copy-done.4, bf16[5120,256]{1,0:T(8,128)(2,1)} %param.23), kind=kOutput, calls=%fused_computation.31 | convolution fusion | flops 671154176 | bytes 5373952 | tf_op jit(solution)/shard_map/dot_general | solution.py:92
  79.5 0.1 copy.75
  79.6 0.8 pad_maximum_fusion
  80.4 0.2 reduce-scatter.2.cloned.1.call-start
  80.6 3.7 %convolution_convert_fusion.3 = bf16[256,256]{0,1:T(8,128)(2,1)S(1)} fusion(bf16[256,5120]{1,0:T(8,128)(2,1)} %copy-done.4, bf16[5120,256]{1,0:T(8,128)(2,1)} %param.22), kind=kOutput, calls=%fused_computation.32 | convolution fusion | flops 671154176 | bytes 5373952 | tf_op jit(solution)/shard_map/dot_general | solution.py:84
  84.3 0.1 copy.81
  84.4 0.5 copy-done.7
  84.9 30.9 %all-gather.8.cloned.1.call-done = bf16[6144,256]{1,0:T(8,128)(2,1)} async-done(((bf16[768,256]{1,0:T(8,128)(2,1)}), bf16[6144,256]{1,0:T(8,128)(2,1)}) %all-gather.8.cloned.1.call-update) | async-done | bytes 3145744 | tf_op jit(solution)/shard_map/all_gather | solution.py:104
  115.8 1.2 slice.27
  117.0 1.2 copy.78
  118.2 43.2 %all-gather.6.cloned.1.call-done = bf16[6144,256]{0,1:T(8,128)(2,1)} async-done(((bf16[768,256]{0,1:T(8,128)(2,1)}), bf16[6144,256]{0,1:T(8,128)(2,1)}) %all-gather.6.cloned.1.call-update) | async-done | bytes 3145744 | tf_op jit(solution)/shard_map/all_gather | solution.py:103
  161.4 3.4 %slice.28 = bf16[4608,256]{0,1:T(8,128)(2,1)} slice(bf16[6144,256]{0,1:T(8,128)(2,1)} %all-gather.6.cloned.1.call-done), slice={[1536:6144], [0:256]} | slice | bytes 4718592 | tf_op jit(solution)/shard_map/slice | solution.py:54
  164.8 4.4 %copy.79 = bf16[4608,256]{1,0:T(8,128)(2,1)} copy(bf16[4608,256]{0,1:T(8,128)(2,1)} %slice.28) | data formatting | bytes 4718592 | tf_op jit(solution)/shard_map/slice | solution.py:54
  169.1 1.7 fusion.54
  170.8 0.6 fusion.20
  171.4 1.5 fusion.24
  172.9 1.6 slice.29
  174.4 26.1 %while.14 = (s32[]{:T(128)}, f32[2,256]{1,0:T(2,128)S(1)}, f32[2,256]{1,0:T(2,128)S(1)}, f32[256,2,128]{0,2,1:T(8,128)}, bf16[3,1536,256]{2,1,0:T(8,128)(2,1)}, ...) while((s32[]{:T(128)}, f32[2,256]{1,0:T(2,128)S(1)}, f32[2,256]{1,0:T(2,128)S(1)}, ...), condition=%wide.region_7.8_spmd, body=%wide.region_4.7_spmd.sunk | while | flops 407570944 | bytes 20093080 | solution.py:54
  174.4 2.4 constant_dynamic-slice_fusion.3
  176.8 1.2 copy.104
  178.0 1.4 copy.105
  179.4 1.8 fusion.83
  181.2 0.4 fusion.85
  181.7 0.8 fusion.87
  182.5 0.7 copy-done.3
  183.1 2.4 constant_dynamic-slice_fusion.3
  185.5 1.2 copy.104
  186.7 1.4 copy.105
  188.1 1.8 fusion.83
  189.9 0.4 fusion.85
  190.4 0.8 fusion.87
  191.2 0.7 copy-done.3
  191.9 2.4 constant_dynamic-slice_fusion.3
  194.2 1.2 copy.104
  195.4 1.4 copy.105
  196.8 1.8 fusion.83
  198.6 0.4 fusion.85
  199.1 0.8 fusion.87
  199.9 0.7 copy-done.3
  200.6 1.0 divide_convert_fusion
  201.6 2.4 convolution_convert_fusion
  204.0 0.2 convert_reduce_fusion.1
  204.3 4.7 %convert_element_type.52 = f32[256,5120]{1,0:T(8,128)} convert(bf16[256,5120]{1,0:T(8,128)(2,1)} %copy.73) | non-fusion elementwise | flops 1310720 | bytes 7864320 | tf_op jit(solution)/shard_map/convert_element_type | solution.py:77
  209.0 69.5 %reduce-scatter.2.cloned.1.call-done = bf16[16,5120]{1,0:T(8,128)(2,1)} async-done(((bf16[256,5120]{1,0:T(8,128)(2,1)}), bf16[16,5120]{1,0:T(8,128)(2,1)}) %reduce-scatter.2.cloned.1.call-update) | async-done | bytes 163856 | tf_op jit(solution)/shard_map/reduce_scatter | solution.py:115
  278.5 1.9 multiply_reduce_fusion.1
  280.4 1.4 fusion.29
  281.8 0.1 reshape.73
  281.9 0.3 convolution_convert_fusion.4
  282.2 13.7 %all_to_all.5 = bf16[16,2,256]{2,1,0:T(2,128)(2,1)S(1)} all-to-all(bf16[16,2,256]{2,1,0:T(2,128)(2,1)S(1)} %reshape.74), channel_id=1, replica_groups=mesh['ctx'=8,'mdl'=16] {'mdl'}, dimensions={0} | all-to-all | bytes 32768 | tf_op jit(solution)/shard_map/all_to_all | solution.py:151
  295.9 1.3 fusion.41
  297.3 0.7 reshape.75
  (65 shorter events, 0.5 us)
Async XLA Ops:
  7.2 194.4 %copy-start = (bf16[256,5120]{1,0:T(8,128)(2,1)S(1)}, bf16[256,5120]{1,0:T(8,128)(2,1)}, u32[]{:S(2)}) copy-start(bf16[256,5120]{1,0:T(8,128)(2,1)} %param.25) | copy-start | bytes 7864324
  7.2 56.2 %all-gather.4.cloned.1.call-start = ((), (), s32[]{:S(2)}) async-start(), calls=%async_computation.2 | async-start | bytes 2785280 | tf_op jit(solution)/shard_map/all_gather | solution.py:76
  7.9 107.9 %all-gather.8.cloned.1.call-start = ((), (), s32[]{:S(2)}) async-start(), calls=%async_computation.4 | async-start | bytes 3538944 | tf_op jit(solution)/shard_map/all_gather | solution.py:104
  68.0 2.5 copy-start.1
  68.0 3.4 %copy-start.12 = (f32[5120]{0:T(1024)S(1)}, f32[5120]{0:T(1024)}, u32[]{:S(2)}) copy-start(f32[5120]{0:T(1024)} %param.19) | copy-start | bytes 61444
  71.3 2.8 copy-start.17
  72.6 1.5 copy-start.4
  74.1 1.0 copy-start.9
  74.1 1.8 copy-start.10
  75.9 85.5 %all-gather.6.cloned.1.call-start = ((), (), s32[]{:S(2)}) async-start(), calls=%async_computation.3 | async-start | bytes 3538944 | tf_op jit(solution)/shard_map/all_gather | solution.py:103
  80.4 198.1 %reduce-scatter.2.cloned.1.call-start = ((), (), s32[]{:S(2)}) async-start(), calls=%async_computation.5 | async-start | bytes 2785280 | tf_op jit(solution)/shard_map/reduce_scatter | solution.py:115
  84.3 0.7 copy-start.7
  164.8 4.4 %slice-start = ((bf16[6144,256]{0,1:T(8,128)(2,1)}), bf16[1536,256]{0,1:T(8,128)(2,1)S(1)}, s32[]{:S(2)}) async-start(bf16[6144,256]{0,1:T(8,128)(2,1)} %all-gather.6.cloned.1.call-done), calls=%async_computation.6 | async-start | bytes 1572864 | tf_op jit(solution)/shard_map/slice | solution.py:49
  169.1 2.2 copy-start.6
  170.8 2.1 copy-start.5
  179.4 2.3 copy-start.2
  182.5 0.7 copy-start.3
  188.1 2.3 copy-start.2
  191.2 0.7 copy-start.3
  196.8 2.3 copy-start.2
  199.9 0.7 copy-start.3
  201.6 2.4 copy-start.18
  201.6 2.6 copy-start.13
  204.2 74.3 %copy-start.11 = (f32[5120]{0:T(1024)S(1)}, f32[5120]{0:T(1024)}, u32[]{:S(2)}) copy-start(f32[5120]{0:T(1024)} %param.21) | copy-start | bytes 61444
  204.2 76.2 %copy-start.8 = (bf16[5120,64]{0,1:T(8,128)(2,1)S(1)}, bf16[5120,64]{0,1:T(8,128)(2,1)}, u32[]{:S(2)}) copy-start(bf16[5120,64]{0,1:T(8,128)(2,1)} %param.29) | copy-start | bytes 1966084
  204.2 77.7 %copy-start.14 = (f32[4,256]{1,0:T(4,128)S(1)}, f32[4,256]{1,0:T(4,128)}, u32[]{:S(2)}) copy-start(f32[4,256]{1,0:T(4,128)} %param.31) | copy-start | bytes 12292
  204.2 77.6 %copy-start.15 = (f32[4,256]{1,0:T(4,128)S(1)}, f32[4,256]{1,0:T(4,128)}, u32[]{:S(2)}) copy-start(f32[4,256]{1,0:T(4,128)} %param.30) | copy-start | bytes 12292
  281.9 16.0 %copy-start.16 = (f32[4,256]{1,0:T(4,128)}, f32[4,256]{1,0:T(4,128)S(1)}, u32[]{:S(2)}) copy-start(f32[4,256]{1,0:T(4,128)S(1)} %multiply_add_fusion.3) | copy-start | bytes 12292
Sparse Core Ops, SparseCore 0:
  10.5 52.8 all-gather.3
  76.0 39.7 all-gather.7
  117.5 43.8 all-gather.5
  204.1 74.3 reduce-scatter.1
where the time goes:
time: 305 us; the launch traced here: 304 us
  waiting for transfers between devices  199 us (65%)
  local copies, waits for them, and re-layouts  36.6 us (12%)
  matrix products  24 us (8%)
  other arithmetic  16.5 us (5%)
  between operations  14 us (5%)
  blocking collectives  13.7 us (4%)
    reduce_scatter x1, waiting for transfers between devices, shards(): lax.psum_scatter(jnp.dot(attended, w_out, preferred_element_type=jnp.floa...  69.5 us
    all_gather x1, waiting for transfers between devices, shards(): whole = lax.all_gather(latents, 'mdl', axis=1, tiled=True)  54.7 us
    all_gather x1, waiting for transfers between devices, shards(): lax.all_gather(joined_keys, 'ctx', axis=0, tiled=True)  43.2 us
    all_gather x1, waiting for transfers between devices, shards(): lax.all_gather(joined_values, 'ctx', axis=0, tiled=True)  30.9 us
    dynamic_slice x9, local copies, waits for them, and re-layouts, head_stats(): result, unused = lax.scan(step, first, (key_blocks[1:], value_blocks[1:]))  14.8 us
    all_to_all x1, blocking collectives, shards(): lax.all_to_all(slot_rows, 'mdl', split_axis=0, concat_axis=0, tiled=True)  13.7 us
    slice x3, local copies, waits for them, and re-layouts, head_stats(): result, unused = lax.scan(step, first, (key_blocks[1:], value_blocks[1:]))  9.29 us
    dot_general x4, matrix products, block_stats(): jnp.einsum('nhd,khd->hnk', query_heads, key_heads, preferred_element_type...  7.09 us
  transfers between devices with their start and end apart: 4, of which 4 were waited for; matrix products, arithmetic and copies ran while one was open for 5% of the time, Pallas kernels for 0%

commit v1 on v0

v1 whole, which is shorter than its diff:
```python
import functools
import math

import jax
import jax.numpy as jnp
from jax import lax
from jax.experimental import pallas as pl
from jax.experimental.pallas import tpu as pltpu
from jax.sharding import PartitionSpec as P

HD = 128
CAP = 2
BF = jnp.bfloat16
F32 = jnp.float32
MIB = 1 << 20
VM = pl.BlockSpec(memory_space=pltpu.VMEM)
SM = pl.BlockSpec(memory_space=pltpu.SMEM)

CHIPS = [[2 * j + k for j in range(8)] for k in range(2)]
CORE_SWAP = [(m, m ^ 1) for m in range(16)]
Y_SWAP = [(c, c ^ 4) for c in range(8)]


def x_step(by):
    return [(c, (c // 4) * 4 + (c + by) % 4) for c in range(8)]


def core_swap(a):
    return lax.ppermute(a, "mdl", CORE_SWAP)


def chips_exchange(a):
    return lax.all_to_all(a, "mdl", 0, 0, axis_index_groups=CHIPS, tiled=True)


def call(body, outs, args, flops=0, nbytes=0, trans=0, smem=(), scratch=(), limit=32):
    return pl.pallas_call(
        body,
        out_shape=outs,
        in_specs=[SM if i in smem else VM for i in range(len(args))],
        out_specs=jax.tree.map(lambda o: VM, outs),
        scratch_shapes=list(scratch),
        compiler_params=pltpu.CompilerParams(vmem_limit_bytes=limit * MIB),
        cost_estimate=pl.CostEstimate(flops=flops, bytes_accessed=nbytes, transcendentals=trans),
    )(*args)


def shape(dims, dtype):
    return jax.ShapeDtypeStruct(dims, dtype)


def norm_body(x_ref, scale_ref, shift_ref, out_ref):
    blocks, rows, width = x_ref.shape
    total = jnp.zeros((rows, width), F32)
    for b in range(blocks):
        total = total + x_ref[b].astype(F32)
    mean = jnp.sum(total, -1, keepdims=True) / (blocks * width)
    square = jnp.zeros((rows, width), F32)
    for b in range(blocks):
        centred = x_ref[b].astype(F32) - mean
        square = square + centred * centred
    var = jnp.sum(square, -1, keepdims=True) / (blocks * width)
    inverse = lax.rsqrt(var + 1e-06)
    for b in range(blocks):
        centred = x_ref[b].astype(F32) - mean
        out_ref[b] = (
            centred * inverse * (1.0 + scale_ref[b : b + 1]) + shift_ref[b : b + 1]
        ).astype(BF)


def qkv_body(core_ref, own_ref, other_ref, wq_ref, wk_ref, wv_ref, q_ref, kv_ref, qa, kva):
    step = pl.program_id(0)
    k = core_ref[0]

    @pl.when(step == 0)
    def _():
        qa[...] = jnp.zeros_like(qa)
        kva[...] = jnp.zeros_like(kva)

    rows = own_ref.shape[1]
    own = own_ref[0]
    other = other_ref[0]
    first = jnp.where(k == 0, own, other)
    second = jnp.where(k == 0, other, own)
    x = jnp.concatenate([first, second], 0)
    qa[...] += jnp.dot(x, wq_ref[...], preferred_element_type=F32)
    kva[:, :256] += jnp.dot(x, wk_ref[...], preferred_element_type=F32)
    kva[:, 256:] += jnp.dot(x, wv_ref[...], preferred_element_type=F32)

    @pl.when(step == pl.num_programs(0) - 1)
    def _():
        q_ref[...] = qa[...].astype(BF)
        kv_ref[...] = kva[...].astype(BF)


def qkv_call(core, own, other, wq, wk, wv):
    blocks, rows, width = own.shape
    cols = wq.shape[1]
    w_spec = pl.BlockSpec((width, cols), lambda i: (i, 0))
    x_spec = pl.BlockSpec((1, rows, width), lambda i: (i, 0, 0))
    return pl.pallas_call(
        qkv_body,
        grid=(blocks,),
        out_shape=(shape((2 * rows, cols), BF), shape((2 * rows, 2 * cols), BF)),
        in_specs=[SM, x_spec, x_spec, w_spec, w_spec, w_spec],
        out_specs=(
            pl.BlockSpec((2 * rows, cols), lambda i: (0, 0)),
            pl.BlockSpec((2 * rows, 2 * cols), lambda i: (0, 0)),
        ),
        scratch_shapes=[pltpu.VMEM((2 * rows, cols), F32), pltpu.VMEM((2 * rows, 2 * cols), F32)],
        compiler_params=pltpu.CompilerParams(vmem_limit_bytes=24 * MIB),
        cost_estimate=pl.CostEstimate(
            flops=2 * 256 * 5120 * 768, bytes_accessed=10 * MIB, transcendentals=0
        ),
    )(core, own, other, wq, wk, wv)


C2 = math.log2(math.e) / math.sqrt(HD)


def attend(q_ref, kv_refs, start, h):
    q = q_ref[:, h * HD : (h + 1) * HD]
    peak, total, summed = start
    for kv in kv_refs:
        keys = kv[:, h * HD : (h + 1) * HD]
        values = kv[:, 256 + h * HD : 256 + (h + 1) * HD]
        s = lax.dot_general(q, keys, (((1,), (1,)), ((), ())), preferred_element_type=F32)
        here = jnp.max(s, -1, keepdims=True)
        new = here if peak is None else jnp.maximum(peak, here)
        p = jnp.exp2((s - new) * C2)
        t = jnp.sum(p, -1, keepdims=True)
        o = jnp.dot(p.astype(BF), values, preferred_element_type=F32)
        if peak is None:
            total, summed = t, o
        else:
            f = jnp.exp2((peak - new) * C2)
            total, summed = total * f + t, summed * f + o
        peak = new
    return peak, total, summed


def past_body(q_ref, a_ref, b_ref, c_ref, d_ref, o_ref, peak_ref, total_ref):
    for h in range(2):
        peak, total, summed = attend(
            q_ref, (a_ref, b_ref, c_ref, d_ref), (None, None, None), h
        )
        o_ref[:, h * HD : (h + 1) * HD] = summed
        peak_ref[h] = jnp.broadcast_to(peak, peak_ref.shape[1:])
        total_ref[h] = jnp.broadcast_to(total, total_ref.shape[1:])


def finish(q_ref, refs, o_ref, peak_ref, total_ref, h):
    start = (peak_ref[h][:, :1], total_ref[h][:, :1], o_ref[:, h * HD : (h + 1) * HD])
    peak, total, summed = attend(q_ref, refs, start, h)
    return summed / total, peak / math.sqrt(HD) + jnp.log(total)


def sent_body(q_ref, a_ref, b_ref, c_ref, d_ref, o_ref, peak_ref, total_ref, out_ref):
    rows = q_ref.shape[0]
    at = lax.broadcasted_iota(jnp.int32, (16, rows), 0)
    tail = jnp.zeros((16, rows), F32)
    for h in range(2):
        o, lse = finish(q_ref, (a_ref, b_ref, c_ref, d_ref), o_ref, peak_ref, total_ref, h)
        out_ref[:rows, h * HD : (h + 1) * HD] = o.astype(BF)
        rest = jnp.transpose(jnp.broadcast_to(lse, (rows, HD)))[:16]
        for i in range(3):
            piece = rest.astype(BF).astype(F32)
            tail = jnp.where(at == 3 * h + i, piece, tail)
            rest = rest - piece
    out_ref[rows:, :] = tail.astype(BF)


def kept_body(q_ref, a_ref, b_ref, c_ref, d_ref, o_ref, peak_ref, total_ref, out_ref, lse_ref):
    for h in range(2):
        o, lse = finish(q_ref, (a_ref, b_ref, c_ref, d_ref), o_ref, peak_ref, total_ref, h)
        out_ref[:, h * HD : (h + 1) * HD] = o
        lse_ref[h] = jnp.broadcast_to(lse, lse_ref.shape[1:])


def merge_body(own_ref, lse_ref, got_ref, out_ref):
    rows = own_ref.shape[0]
    tail = got_ref[rows:, :].astype(F32)
    for h in range(2):
        row = tail[3 * h : 3 * h + 1] + tail[3 * h + 1 : 3 * h + 2] + tail[3 * h + 2 : 3 * h + 3]
        theirs = jnp.transpose(jnp.broadcast_to(row, (HD, rows)))
        ours = lse_ref[h]
        top = jnp.maximum(ours, theirs)
        a, b = jnp.exp(ours - top), jnp.exp(theirs - top)
        cols = slice(h * HD, (h + 1) * HD)
        merged = (a * own_ref[:, cols] + b * got_ref[:rows, cols].astype(F32)) / (a + b)
        out_ref[:, cols] = merged.astype(BF)


def out_body(core_ref, own_ref, other_ref, wa_ref, wb_ref, out_ref):
    chips = out_ref.shape[0]
    width = out_ref.shape[2]
    for at in range(0, width, 512):
        cols = slice(at, at + 512)
        r = jnp.dot(own_ref[...], wa_ref[:, cols], preferred_element_type=F32) + jnp.dot(
            other_ref[...], wb_ref[:, cols], preferred_element_type=F32
        )
        r = r.astype(BF)
        for j in range(chips):
            out_ref[j, 0:16, cols] = r[16 * j : 16 * j + 16]
            out_ref[j, 16:32, cols] = r[128 + 16 * j : 128 + 16 * j + 16]


def sum_body(core_ref, got_ref, keep_ref, give_ref):
    k = core_ref[0]
    total = got_ref[0].astype(F32)
    for j in range(1, got_ref.shape[0]):
        total = total + got_ref[j].astype(F32)
    keep_ref[...] = jnp.where(k == 0, total[:16], total[16:])
    give_ref[...] = jnp.where(k == 0, total[16:], total[:16])


def tail_body(
    core_ref, own_ref, other_ref, x_ref, gate_ref, scale_ref, wf_ref, state_ref, noise_ref,
    owner_ref, hidden_ref, next_ref, slot_ref, vel,
):
    k = core_ref[0]
    own, other = own_ref[...], other_ref[...]
    left = jnp.where(k == 0, own, other)
    right = jnp.where(k == 0, other, own)
    blocks, rows, width = x_ref.shape
    half = blocks // 2
    mixed = []
    square = jnp.zeros((rows, width), F32)
    for b in range(blocks):
        at = (b % half) * width
        part = (left if b < half else right)[:, at : at + width]
        mix = x_ref[b].astype(F32) + gate_ref[b : b + 1] * part
        hidden_ref[:, b * width : (b + 1) * width] = mix.astype(BF)
        square = square + mix * mix
        mixed.append(mix)
    inverse = lax.rsqrt(jnp.sum(square, -1, keepdims=True) / (blocks * width) + 1e-06)
    acc = jnp.zeros(vel.shape, F32)
    for b in range(blocks):
        normed = (mixed[b] * inverse * (1.0 + scale_ref[b : b + 1])).astype(BF)
        acc = acc + jnp.dot(normed, wf_ref[b * width : (b + 1) * width], preferred_element_type=F32)
    vel[...] = acc
    tiles = state_ref.shape[0]
    lat = acc.shape[1]
    velocity = jnp.concatenate(
        [vel[pl.ds(j, tiles, stride=rows // tiles), :] for j in range(rows // tiles)], -1
    )
    state = state_ref[...]
    new = (
        state
        + 0.2 * (velocity + 0.5 * (0.5 * velocity - state) / (1.0 - 0.5))
        + math.sqrt(0.2) * noise_ref[...]
    )
    next_ref[...] = new
    panels = new.astype(BF).astype(F32)
    at = lax.broadcasted_iota(jnp.int32, slot_ref.shape, 0)
    slots = jnp.zeros(slot_ref.shape, F32)
    for t in range(tiles):
        owner = owner_ref[t]
        before = jnp.int32(0)
        for e in range(t):
            before = before + jnp.where(owner_ref[e] == owner, 1, 0)
        slots = jnp.where(at == owner * CAP + before, panels[t : t + 1], slots)
    slot_ref[...] = slots.astype(BF)


def up_body(x_ref, w_ref, out_ref):
    y = jnp.dot(x_ref[...], w_ref[...], preferred_element_type=F32)
    out_ref[...] = jax.nn.gelu(y).astype(BF)


def shards(
    latents, mod_shift, mod_scale, gate, w_query, w_key, w_value, w_out, cache_keys,
    cache_values, final_scale, w_final, state, noise, owners, w_up,
):
    count, part = latents.shape
    mdl = lax.axis_index("mdl")
    core = mdl % 2
    chip = mdl // 2
    core_1 = jnp.reshape(core, (1,)).astype(jnp.int32)
    chips = 8
    block = count // 16
    rows = count // 2

    split = latents.reshape(chips, 2, block, part)
    keep = lax.dynamic_index_in_dim(split, core, 1, keepdims=False).reshape(rows, part)
    give = lax.dynamic_index_in_dim(split, 1 - core, 1, keepdims=False).reshape(rows, part)
    got = core_swap(give)
    is_first = core == 0
    wide = jnp.concatenate(
        [jnp.where(is_first, keep, got), jnp.where(is_first, got, keep)], 1
    )
    x = chips_exchange(jnp.broadcast_to(wide[None], (chips, rows, 2 * part)))

    cached = jnp.concatenate([cache_keys, cache_values], 1)
    past = [cached] + [lax.ppermute(cached, "ctx", x_step(by)) for by in (1, 3, 2)]

    half = w_out.shape[1] // 2
    w_mine = lax.dynamic_slice_in_dim(w_out, core * half, half, 1)
    w_theirs = core_swap(lax.dynamic_slice_in_dim(w_out, (1 - core) * half, half, 1))

    normed = call(
        norm_body,
        shape(x.shape, BF),
        (x, mod_scale.reshape(chips, 2 * part), mod_shift.reshape(chips, 2 * part)),
        flops=10 * x.size,
        nbytes=4 * x.size,
    )
    query, kv = qkv_call(core_1, normed, core_swap(normed), w_query, w_key, w_value)
    fresh = [kv] + [lax.ppermute(kv, "ctx", x_step(by)) for by in (1, 3, 2)]
    query_in = lax.ppermute(query, "ctx", Y_SWAP)

    cols = query.shape[1]

    def past_call(q):
        return call(
            past_body,
            (
                shape((count, cols), F32),
                shape((2, count, HD), F32),
                shape((2, count, HD), F32),
            ),
            (q, *past),
            flops=4 * count * 2048 * 256,
            nbytes=4 * MIB,
            trans=count * 4096,
        )

    stats_own = past_call(query)
    stats_in = past_call(query_in)
    sent = call(
        sent_body,
        shape((count + 16, cols), BF),
        (query_in, *fresh, *stats_in),
        flops=4 * count * 1024 * 256,
        nbytes=2 * MIB,
        trans=count * 2048,
    )
    back = lax.ppermute(sent, "ctx", Y_SWAP)
    kept = call(
        kept_body,
        (shape((count, cols), F32), shape((2, count, HD), F32)),
        (query, *fresh, *stats_own),
        flops=4 * count * 1024 * 256,
        nbytes=2 * MIB,
        trans=count * 2048,
    )
    attended = call(merge_body, shape((count, cols), BF), (*kept, back), nbytes=MIB)

    projected = call(
        out_body,
        shape((chips, 2 * block, half), BF),
        (core_1, attended, core_swap(attended), w_mine, w_theirs),
        smem=(0,),
        flops=2 * count * 512 * half,
        nbytes=4 * MIB,
    )
    arrived = chips_exchange(projected)
    ours, theirs = call(
        sum_body,
        (shape((block, half), F32), shape((block, half), F32)),
        (core_1, arrived),
        smem=(0,),
        nbytes=2 * MIB,
    )
    own_x = lax.dynamic_slice_in_dim(x, chip * block, block, 1)
    hidden_out, next_state, slot_rows = call(
        tail_body,
        (
            shape((block, w_out.shape[1]), BF),
            shape(state.shape, F32),
            shape((16 * CAP, state.shape[1]), BF),
        ),
        (
            core_1, ours, core_swap(theirs), own_x, gate.reshape(chips, 2 * part),
            final_scale.reshape(chips, 2 * part), w_final, state, noise, owners[:, 0],
        ),
        smem=(0, 9),
        nbytes=2 * MIB,
        scratch=[pltpu.VMEM((block, w_final.shape[1]), F32)],
    )
    routed = lax.all_to_all(
        slot_rows.reshape(16, CAP, state.shape[1]), "mdl", split_axis=0, concat_axis=0, tiled=True
    ).reshape(16 * CAP, state.shape[1])
    upsampled = call(
        up_body, shape((16 * CAP, w_up.shape[1]), BF), (routed, w_up), nbytes=MIB
    )
    return (hidden_out, next_state, upsampled)


def solution(mesh):
    return jax.shard_map(
        shards,
        mesh=mesh,
        in_specs=(
            P("ctx", "mdl"),
            P(),
            P(),
            P(),
            P(None, "mdl"),
            P(None, "mdl"),
            P(None, "mdl"),
            P("mdl", None),
            P("ctx", "mdl"),
            P("ctx", "mdl"),
            P(),
            P(),
            P(("ctx", "mdl"), None),
            P(("ctx", "mdl"), None),
            P(("ctx", "mdl"), None),
            P(),
        ),
        out_specs=(P(("ctx", "mdl"), None), P(("ctx", "mdl"), None), P(("ctx", "mdl"), None)),
        check_vma=False,
    )
```

time: 305 us -> 130 us (0.43)
  waiting for transfers between devices: 199 us -> 41.3 us
  local copies, waits for them, and re-layouts: 36.6 us -> 7.87 us
  Pallas kernels: 0 us -> 24.7 us
  matrix products: 24 us -> 0 us
  starting transfers between devices: 0.34 us -> 22.5 us
  blocking collectives: 13.7 us -> 31.9 us
  other arithmetic: 16.5 us -> 0.13 us
  between operations: 14 us -> 0.94 us
    all_gather x3 -> x0, waiting for transfers between devices: 129 us -> none  [the longest x1 54.7 us: shards(): whole = lax.all_gather(latents, 'mdl', axis=1, tiled=True)]
    reduce_scatter x1 -> x0, waiting for transfers between devices: 69.5 us -> none  [shards(): lax.psum_scatter(jnp.dot(attended, w_out, preferred_element_type=jnp.floa...]
    pallas_call x0 -> x11, Pallas kernels: none -> 24.7 us  [the longest x10 18.4 us: call(): pl.pallas_call(body, out_shape=outs, in_specs=[SM if i in smem else VM fo...]
    dot_general x15 -> x0, matrix products: 24 us -> none  [the longest x4 7.09 us: block_stats(): jnp.einsum('nhd,khd->hnk', query_heads, key_heads, preferred_element_type...]
    ppermute x0 -> x13, waiting for transfers between devices: none -> 21.9 us  [the longest x3 11.8 us: shards(): lax.ppermute(cached, 'ctx', x_step(by))]
    all_to_all x0 -> x1, waiting for transfers between devices: none -> 19.4 us  [chips_exchange(): return lax.all_to_all(a, 'mdl', 0, 0, axis_index_groups=CHIPS, tiled=True)]
    all_to_all x1 -> x2, blocking collectives: 13.7 us -> 31.9 us  [the longest x1 22 us: chips_exchange(): return lax.all_to_all(a, 'mdl', 0, 0, axis_index_groups=CHIPS, tiled=True)]
    ppermute x0 -> x13, starting transfers between devices: none -> 14.7 us  [the longest x5 6.8 us: core_swap(): return lax.ppermute(a, 'mdl', CORE_SWAP)]
  transfers between devices with their start and end apart: 4 -> 14, of which waited for: 4 -> 7; matrix products, arithmetic and copies ran while one was open for 5% -> 3% of each run, Pallas kernels for 0% -> 15%
where the time goes in v1:
time: 130 us; the launch traced here: 129 us
  waiting for transfers between devices  41.3 us (32%)
  blocking collectives  31.9 us (25%)
  Pallas kernels  24.7 us (19%)
  starting transfers between devices  22.5 us (17%)
  local copies, waits for them, and re-layouts  7.87 us (6%)
    all_to_all x1, blocking collectives, chips_exchange(): return lax.all_to_all(a, 'mdl', 0, 0, axis_index_groups=CHIPS, tiled=True)  22 us
    all_to_all x1, waiting for transfers between devices, chips_exchange(): return lax.all_to_all(a, 'mdl', 0, 0, axis_index_groups=CHIPS, tiled=True)  19.4 us
    pallas_call x10, Pallas kernels, call(): pl.pallas_call(body, out_shape=outs, in_specs=[SM if i in smem else VM fo...  18.4 us
    ppermute x3, waiting for transfers between devices, shards(): lax.ppermute(cached, 'ctx', x_step(by))  11.8 us
    all_to_all x1, blocking collectives, shards(): lax.all_to_all(slot_rows.reshape(16, CAP, state.shape[1]), 'mdl', split_a...  9.95 us
    all_to_all x1, starting transfers between devices, chips_exchange(): return lax.all_to_all(a, 'mdl', 0, 0, axis_index_groups=CHIPS, tiled=True)  7.88 us
    ppermute x5, starting transfers between devices, core_swap(): return lax.ppermute(a, 'mdl', CORE_SWAP)  6.8 us
    pallas_call x1, Pallas kernels, qkv_call(): pl.pallas_call(qkv_body, grid=(blocks,), out_shape=(shape((2 * rows, cols...  6.25 us
  transfers between devices with their start and end apart: 14, of which 7 were waited for; matrix products, arithmetic and copies ran while one was open for 3% of the time, Pallas kernels for 15%

profile of v1, /device:TPU:1, one launch (start us, length us, event | category | flops | bytes accessed | tf_op | source)
XLA Modules:
  0.0 129.4 jit_solution(8726079520987452307)
XLA Ops:
  0.6 1.1 copy.22
  1.8 1.5 %collective-permute-start = (bf16[128,320]{1,0:T(8,128)(2,1)S(1)}, bf16[128,320]{1,0:T(8,128)(2,1)S(1)}, u32[]{:S(2)}, u32[]{:S(2)}) collective-permute-start(bf16[128,320]{1,0:T(8,128)(2,1)S(1)} %bitcast.9), channel_id=1, source_target_pairs={{0,1},{1,0},{2,3},{3,2},{4,5},{5,4},{6,7},{7,6},{8,9},{9,8},{10,11... | collective-permute-start | bytes 245768 | tf_op jit(solution)/shard_map/ppermute | solution.py:29
  3.3 0.9 collective-permute-done
  4.3 0.1 pad_maximum_fusion
  4.4 1.2 broadcast_in_dim.2
  5.5 0.0 copy-start.9
  5.5 0.0 copy-start.10
  5.6 7.9 %all-to-all-start = ((bf16[8,128,640]{2,1,0:T(8,128)(2,1)}), bf16[8,128,640]{2,1,0:T(8,128)(2,1)S(1)}, u32[]{:S(2)}, u32[]{:S(2)}) async-start(bf16[8,128,640]{2,1,0:T(8,128)(2,1)} %broadcast_in_dim.2), calls=%async_computation | async-start | bytes 2621440 | tf_op jit(solution)/shard_map/all_to_all | solution.py:33
  13.4 0.0 copy-done.9
  13.4 0.0 copy-done.10
  13.5 19.4 %all-to-all-done.x_ref = bf16[8,128,640]{2,1,0:T(8,128)(2,1)S(1)} async-done(((bf16[8,128,640]{2,1,0:T(8,128)(2,1)}), bf16[8,128,640]{2,1,0:T(8,128)(2,1)S(1)}, u32[]{:S(2)}, u32[]{:S(2)}) %all-to-all-start) | async-done | bytes 1310752 | tf_op jit(solution)/shard_map/all_to_all | solution.py:33
  32.9 1.3 shard_map.175.own_ref
  34.2 1.6 %collective-permute-start.1 = (bf16[8,128,640]{2,1,0:T(8,128)(2,1)S(1)}, bf16[8,128,640]{2,1,0:T(8,128)(2,1)}, u32[]{:S(2)}, u32[]{:S(2)}) collective-permute-start(bf16[8,128,640]{2,1,0:T(8,128)(2,1)S(1)} %shard_map.175.own_ref), channel_id=1, source_target_pairs={{0,1},{1,0},{2,3},{3,2},{4,5},{5,4},{6,7},{7,6},{8,9},{9,8},{10,11... | collective-permute-start | bytes 3932168 | tf_op jit(solution)/shard_map/ppermute | solution.py:29
  35.8 2.0 %constant_dynamic-slice_fusion.1 = (bf16[256,2560]{1,0:T(8,128)(2,1)S(1)}, bf16[256,2560]{1,0:T(8,128)(2,1)S(1)}) fusion(bf16[256,5120]{1,0:T(8,128)(2,1)} %param.23, s32[]{:T(128)S(6)} %select_n.46, s32[]{:T(128)S(6)} %select_n.45), kind=kLoop, calls=%fused_computation.6 | loop fusion | bytes 5242888 | tf_op jit(solution)/shard_map/dynamic_slice | solution.py:299
  37.9 0.1 collective-permute-start.11
  38.0 0.0 copy-done.7
  38.0 0.0 copy-done.8
  38.1 1.3 collective-permute-start.5
  39.3 1.5 %collective-permute-start.6 = (bf16[512,512]{1,0:T(8,128)(2,1)S(1)}, bf16[512,512]{1,0:T(8,128)(2,1)S(1)}, u32[]{:S(2)}, u32[]{:S(2)}) collective-permute-start(bf16[512,512]{1,0:T(8,128)(2,1)S(1)} %constant_dynamic-update-slice_fusion.a_ref), channel_id=1, source_target_pairs={{0,48},{16,0},{32,16},{48,32},{64,112},{80,64},{96,80},{112,96},{1... | collective-permute-start | bytes 1572872 | tf_op jit(solution)/shard_map/ppermute | solution.py:295
  40.8 1.5 %collective-permute-start.7 = (bf16[512,512]{1,0:T(8,128)(2,1)S(1)}, bf16[512,512]{1,0:T(8,128)(2,1)S(1)}, u32[]{:S(2)}, u32[]{:S(2)}) collective-permute-start(bf16[512,512]{1,0:T(8,128)(2,1)S(1)} %constant_dynamic-update-slice_fusion.a_ref), channel_id=1, source_target_pairs={{0,32},{16,48},{32,0},{48,16},{64,96},{80,112},{96,64},{112,80},{1... | collective-permute-start | bytes 1572872 | tf_op jit(solution)/shard_map/ppermute | solution.py:295
  42.3 0.0 collective-permute-done.1.other_ref
  42.3 0.0 copy-done
  42.4 0.0 copy-done.1
  42.4 0.0 copy-start.2
  42.4 1.7 %copy-done.2 = bf16[5120,256]{1,0:T(8,128)(2,1)S(1)} copy-done((bf16[5120,256]{1,0:T(8,128)(2,1)S(1)}, bf16[5120,256]{1,0:T(8,128)(2,1)}, u32[]{:S(2)}) %copy-start.2) | copy-done | bytes 2621464
  44.1 6.3 %shard_map.176 = (bf16[256,256]{1,0:T(8,128)(2,1)S(1)}, bf16[256,512]{1,0:T(8,128)(2,1)S(1)}) custom-call(s32[1]{0:T(128)} %bitcast.core_ref, bf16[8,128,640]{2,1,0:T(8,128)(2,1)S(1)} %shard_map.175.own_ref, bf16[8,128,640]{2,1,0:T(8,128)(2,1)} %collective-permute-done.1.other_ref, bf16[5120,256]{1,0:T(8,128)(2,1)S(1)} %copy-done, ...), custom_call_target="tpu_custom_call" | custom-call | flops 2013265920 | bytes 10485760 | tf_op jit(solution)/shard_map/pallas_call | solution.py:101
  50.4 0.4 collective-permute-start.2
  50.8 1.6 %collective-permute-done.5.b_ref = bf16[512,512]{1,0:T(8,128)(2,1)S(1)} collective-permute-done((bf16[512,512]{1,0:T(8,128)(2,1)S(1)}, bf16[512,512]{1,0:T(8,128)(2,1)S(1)}, u32[]{:S(2)}, u32[]{:S(2)}) %collective-permute-start.5) | collective-permute-done | bytes 524320 | tf_op jit(solution)/shard_map/ppermute | solution.py:295
  52.4 1.3 collective-permute-start.3
  53.7 0.0 collective-permute-done.6.c_ref
  53.7 0.9 collective-permute-start.4
  54.5 10.1 %collective-permute-done.7.d_ref = bf16[512,512]{1,0:T(8,128)(2,1)S(1)} collective-permute-done((bf16[512,512]{1,0:T(8,128)(2,1)S(1)}, bf16[512,512]{1,0:T(8,128)(2,1)S(1)}, u32[]{:S(2)}, u32[]{:S(2)}) %collective-permute-start.7) | collective-permute-done | bytes 524320 | tf_op jit(solution)/shard_map/ppermute | solution.py:295
  64.7 0.4 collective-permute-start.8
  65.1 3.7 %collective-permute-done.8.q_ref = bf16[256,256]{1,0:T(8,128)(2,1)S(1)} collective-permute-done((bf16[256,256]{1,0:T(8,128)(2,1)S(1)}, bf16[256,256]{1,0:T(8,128)(2,1)S(1)}, u32[]{:S(2)}, u32[]{:S(2)}) %collective-permute-start.8) | collective-permute-done | bytes 131104 | tf_op jit(solution)/shard_map/ppermute | solution.py:310
  68.8 2.6 %shard_map.179 = (f32[256,256]{1,0:T(8,128)S(1)}, f32[2,256,128]{2,1,0:T(8,128)S(1)}, f32[2,256,128]{2,1,0:T(8,128)S(1)}) custom-call(bf16[256,256]{1,0:T(8,128)(2,1)S(1)} %collective-permute-done.8.q_ref, bf16[512,512]{1,0:T(8,128)(2,1)S(1)} %constant_dynamic-update-slice_fusion.a_ref, bf16[512,512]{1,0:T(8,128)(2,1)S(1)} %collective-permute-done.5.b_ref, ...), custom_call_target="tpu_custom_call" | custom-call | flops 536870912 | bytes 4194304 | tf_op jit(solution)/shard_map/pallas_call | solution.py:37
  71.4 0.0 collective-permute-done.2.b_ref
  71.4 0.0 collective-permute-done.3.c_ref
  71.4 4.5 %collective-permute-done.4.d_ref = bf16[256,512]{1,0:T(8,128)(2,1)S(1)} collective-permute-done((bf16[256,512]{1,0:T(8,128)(2,1)S(1)}, bf16[256,512]{1,0:T(8,128)(2,1)S(1)}, u32[]{:S(2)}, u32[]{:S(2)}) %collective-permute-start.4) | collective-permute-done | bytes 262176 | tf_op jit(solution)/shard_map/ppermute | solution.py:309
  75.9 3.7 %shard_map.180 = bf16[272,256]{1,0:T(8,128)(2,1)S(1)} custom-call(bf16[256,256]{1,0:T(8,128)(2,1)S(1)} %collective-permute-done.8.q_ref, bf16[256,512]{1,0:T(8,128)(2,1)S(1)} %get-tuple-element.19.a_ref, bf16[256,512]{1,0:T(8,128)(2,1)S(1)} %collective-permute-done.2.b_ref, bf16[256,512]{1,0:T(8,128)(2,1)S(1)} %collective-permute-done.3.c_ref, ...), custom_call_target="tpu_custom_call" | custom-call | flops 268435456 | bytes 2097152 | tf_op jit(solution)/shard_map/pallas_call | solution.py:37
  79.6 0.7 collective-permute-start.9
  80.3 2.6 %shard_map.177 = (f32[256,256]{1,0:T(8,128)S(1)}, f32[2,256,128]{2,1,0:T(8,128)S(1)}, f32[2,256,128]{2,1,0:T(8,128)S(1)}) custom-call(bf16[256,256]{1,0:T(8,128)(2,1)S(1)} %get-tuple-element.18.q_ref, bf16[512,512]{1,0:T(8,128)(2,1)S(1)} %constant_dynamic-update-slice_fusion.a_ref, bf16[512,512]{1,0:T(8,128)(2,1)S(1)} %collective-permute-done.5.b_ref, ...), custom_call_target="tpu_custom_call" | custom-call | flops 536870912 | bytes 4194304 | tf_op jit(solution)/shard_map/pallas_call | solution.py:37
  82.9 3.8 %shard_map.178 = (f32[256,256]{1,0:T(8,128)S(1)}, f32[2,256,128]{2,1,0:T(8,128)S(1)}) custom-call(bf16[256,256]{1,0:T(8,128)(2,1)S(1)} %get-tuple-element.18.q_ref, bf16[256,512]{1,0:T(8,128)(2,1)S(1)} %get-tuple-element.19.a_ref, bf16[256,512]{1,0:T(8,128)(2,1)S(1)} %collective-permute-done.2.b_ref, bf16[256,512]{1,0:T(8,128)(2,1)S(1)} %collective-permute-done.3.c_ref, ...), custom_call_target="tpu_custom_call" | custom-call | flops 268435456 | bytes 2097152 | tf_op jit(solution)/shard_map/pallas_call | solution.py:37
  86.6 0.0 collective-permute-done.9.got_ref
  86.7 0.2 shard_map.181.own_ref
  86.9 1.6 %collective-permute-start.10 = (bf16[256,256]{1,0:T(8,128)(2,1)S(1)}, bf16[256,256]{1,0:T(8,128)(2,1)S(1)}, u32[]{:S(2)}, u32[]{:S(2)}) collective-permute-start(bf16[256,256]{1,0:T(8,128)(2,1)S(1)} %shard_map.181.own_ref), channel_id=1, source_target_pairs={{0,1},{1,0},{2,3},{3,2},{4,5},{5,4},{6,7},{7,6},{8,9},{9,8},{10,11... | collective-permute-start | bytes 393224 | tf_op jit(solution)/shard_map/ppermute | solution.py:29
  88.5 0.0 collective-permute-done.11.wb_ref
  88.5 1.0 collective-permute-done.10.other_ref
  89.5 0.8 shard_map.182
  90.3 22.0 %all_to_all.15.got_ref = bf16[8,32,2560]{2,1,0:T(8,128)(2,1)S(1)} all-to-all(bf16[8,32,2560]{2,1,0:T(8,128)(2,1)S(1)} %shard_map.182), channel_id=1, replica_groups={{0,2,4,6,8,10,12,14},{1,3,5,7,9,11,13,15},{16,18,20,22,24,26,28,30},{17..., dimensions={0} | all-to-all | bytes 2621440 | tf_op jit(solution)/shard_map/all_to_all | solution.py:33
  112.3 0.8 shard_map.183
  113.2 0.0 copy-start.6
  113.2 1.9 %collective-permute-start.12 = (f32[16,2560]{1,0:T(8,128)}, f32[16,2560]{1,0:T(8,128)S(1)}, u32[]{:S(2)}, u32[]{:S(2)}) collective-permute-start(f32[16,2560]{1,0:T(8,128)} %get-tuple-element.29), channel_id=1, source_target_pairs={{0,1},{1,0},{2,3},{3,2},{4,5},{5,4},{6,7},{7,6},{8,9},{9,8},{10,11... | collective-permute-start | bytes 491528 | tf_op jit(solution)/shard_map/ppermute | solution.py:29
  115.1 1.7 %copy.23.wf_ref = bf16[5120,64]{1,0:T(8,128)(2,1)S(1)} copy(bf16[5120,64]{0,1:T(8,128)(2,1)} %param.27) | data formatting | bytes 1310720 | tf_op args[11]
  116.7 0.0 copy-done.11
  116.7 0.0 copy-start.3
  116.8 0.0 copy-done.12
  116.8 0.0 collective-permute-done.12.other_ref
  116.8 0.0 copy-done.4
  116.9 0.0 copy-done.5
  116.9 0.0 copy-done.6
  116.9 1.7 %shard_map.184 = (bf16[16,5120]{1,0:T(8,128)(2,1)}, f32[4,256]{1,0:T(4,128)}, bf16[32,256]{1,0:T(8,128)(2,1)S(1)}) custom-call(s32[1]{0:T(128)} %bitcast.core_ref, f32[16,2560]{1,0:T(8,128)S(1)} %get-tuple-element.28.own_ref, f32[16,2560]{1,0:T(8,128)S(1)} %collective-permute-done.12.other_ref, bf16[8,16,640]{2,1,0:T(8,128)(2,1)S(1)} %constant_dynamic-slice_fusion.x_ref, ...), custom_call_target="tpu_custom_call" | custom-call | bytes 2097152 | tf_op jit(solution)/shard_map/pallas_call | solution.py:37
  118.6 9.9 %all_to_all.16 = bf16[16,2,256]{2,1,0:T(2,128)(2,1)S(1)} all-to-all(bf16[16,2,256]{2,1,0:T(2,128)(2,1)S(1)} %reshape.47), channel_id=1, replica_groups=mesh['ctx'=8,'mdl'=16] {'mdl'}, dimensions={0} | all-to-all | bytes 32768 | tf_op jit(solution)/shard_map/all_to_all | solution.py:381
  128.6 0.0 copy-done.3
  128.6 0.9 shard_map.185
  (19 shorter events, 0.2 us)
Async XLA Ops:
  1.8 2.4 %collective-permute-start = (bf16[128,320]{1,0:T(8,128)(2,1)S(1)}, bf16[128,320]{1,0:T(8,128)(2,1)S(1)}, u32[]{:S(2)}, u32[]{:S(2)}) collective-permute-start(bf16[128,320]{1,0:T(8,128)(2,1)S(1)} %bitcast.9), channel_id=1, source_target_pairs={{0,1},{1,0},{2,3},{3,2},{4,5},{5,4},{6,7},{7,6},{8,9},{9,8},{10,11... | collective-permute-start | bytes 245768 | tf_op jit(solution)/shard_map/ppermute | solution.py:29
  5.5 7.9 %copy-start.9 = (f32[5120]{0:T(1024)S(1)}, f32[5120]{0:T(1024)}, u32[]{:S(2)}) copy-start(f32[5120]{0:T(1024)} %param.18) | copy-start | bytes 61444
  5.5 7.9 %copy-start.10 = (f32[5120]{0:T(1024)S(1)}, f32[5120]{0:T(1024)}, u32[]{:S(2)}) copy-start(f32[5120]{0:T(1024)} %param.17) | copy-start | bytes 61444
  5.6 27.3 %all-to-all-start = ((bf16[8,128,640]{2,1,0:T(8,128)(2,1)}), bf16[8,128,640]{2,1,0:T(8,128)(2,1)S(1)}, u32[]{:S(2)}, u32[]{:S(2)}) async-start(bf16[8,128,640]{2,1,0:T(8,128)(2,1)} %broadcast_in_dim.2), calls=%async_computation | async-start | bytes 2621440 | tf_op jit(solution)/shard_map/all_to_all | solution.py:33
  32.9 5.1 %copy-start.7 = (bf16[512,256]{1,0:T(8,128)(2,1)S(1)}, bf16[512,256]{1,0:T(8,128)(2,1)}, u32[]{:S(2)}) copy-start(bf16[512,256]{1,0:T(8,128)(2,1)} %param.24) | copy-start | bytes 786436
  34.2 8.2 %collective-permute-start.1 = (bf16[8,128,640]{2,1,0:T(8,128)(2,1)S(1)}, bf16[8,128,640]{2,1,0:T(8,128)(2,1)}, u32[]{:S(2)}, u32[]{:S(2)}) collective-permute-start(bf16[8,128,640]{2,1,0:T(8,128)(2,1)S(1)} %shard_map.175.own_ref), channel_id=1, source_target_pairs={{0,1},{1,0},{2,3},{3,2},{4,5},{5,4},{6,7},{7,6},{8,9},{9,8},{10,11... | collective-permute-start | bytes 3932168 | tf_op jit(solution)/shard_map/ppermute | solution.py:29
  35.8 2.2 %copy-start.8 = (bf16[512,256]{1,0:T(8,128)(2,1)S(1)}, bf16[512,256]{1,0:T(8,128)(2,1)}, u32[]{:S(2)}) copy-start(bf16[512,256]{1,0:T(8,128)(2,1)} %param.25) | copy-start | bytes 786436
  35.8 6.5 %copy-start = (bf16[5120,256]{1,0:T(8,128)(2,1)S(1)}, bf16[5120,256]{1,0:T(8,128)(2,1)}, u32[]{:S(2)}) copy-start(bf16[5120,256]{1,0:T(8,128)(2,1)} %wq_ref.1) | copy-start | bytes 7864324
  35.8 6.5 %copy-start.1 = (bf16[5120,256]{1,0:T(8,128)(2,1)S(1)}, bf16[5120,256]{1,0:T(8,128)(2,1)}, u32[]{:S(2)}) copy-start(bf16[5120,256]{1,0:T(8,128)(2,1)} %wk_ref.1) | copy-start | bytes 7864324
  37.9 50.7 %collective-permute-start.11 = (bf16[256,2560]{1,0:T(8,128)(2,1)S(1)}, bf16[256,2560]{1,0:T(8,128)(2,1)S(1)}, u32[]{:S(2)}, u32[]{:S(2)}) collective-permute-start(bf16[256,2560]{1,0:T(8,128)(2,1)S(1)} %get-tuple-element.33), channel_id=1, source_target_pairs={{0,1},{1,0},{2,3},{3,2},{4,5},{5,4},{6,7},{7,6},{8,9},{9,8},{10,11... | collective-permute-start | bytes 3932168 | tf_op jit(solution)/shard_map/ppermute | solution.py:29
  38.1 14.3 %collective-permute-start.5 = (bf16[512,512]{1,0:T(8,128)(2,1)S(1)}, bf16[512,512]{1,0:T(8,128)(2,1)S(1)}, u32[]{:S(2)}, u32[]{:S(2)}) collective-permute-start(bf16[512,512]{1,0:T(8,128)(2,1)S(1)} %constant_dynamic-update-slice_fusion.a_ref), channel_id=1, source_target_pairs={{0,16},{16,32},{32,48},{48,0},{64,80},{80,96},{96,112},{112,64},{1... | collective-permute-start | bytes 1572872 | tf_op jit(solution)/shard_map/ppermute | solution.py:295
  39.3 14.3 %collective-permute-start.6 = (bf16[512,512]{1,0:T(8,128)(2,1)S(1)}, bf16[512,512]{1,0:T(8,128)(2,1)S(1)}, u32[]{:S(2)}, u32[]{:S(2)}) collective-permute-start(bf16[512,512]{1,0:T(8,128)(2,1)S(1)} %constant_dynamic-update-slice_fusion.a_ref), channel_id=1, source_target_pairs={{0,48},{16,0},{32,16},{48,32},{64,112},{80,64},{96,80},{112,96},{1... | collective-permute-start | bytes 1572872 | tf_op jit(solution)/shard_map/ppermute | solution.py:295
  40.8 23.9 %collective-permute-start.7 = (bf16[512,512]{1,0:T(8,128)(2,1)S(1)}, bf16[512,512]{1,0:T(8,128)(2,1)S(1)}, u32[]{:S(2)}, u32[]{:S(2)}) collective-permute-start(bf16[512,512]{1,0:T(8,128)(2,1)S(1)} %constant_dynamic-update-slice_fusion.a_ref), channel_id=1, source_target_pairs={{0,32},{16,48},{32,0},{48,16},{64,96},{80,112},{96,64},{112,80},{1... | collective-permute-start | bytes 1572872 | tf_op jit(solution)/shard_map/ppermute | solution.py:295
  42.4 1.7 %copy-start.2 = (bf16[5120,256]{1,0:T(8,128)(2,1)S(1)}, bf16[5120,256]{1,0:T(8,128)(2,1)}, u32[]{:S(2)}) copy-start(bf16[5120,256]{1,0:T(8,128)(2,1)} %wv_ref.1) | copy-start | bytes 7864324
  50.4 21.0 %collective-permute-start.2 = (bf16[256,512]{1,0:T(8,128)(2,1)S(1)}, bf16[256,512]{1,0:T(8,128)(2,1)S(1)}, u32[]{:S(2)}, u32[]{:S(2)}) collective-permute-start(bf16[256,512]{1,0:T(8,128)(2,1)S(1)} %get-tuple-element.19.a_ref), channel_id=1, source_target_pairs={{0,16},{16,32},{32,48},{48,0},{64,80},{80,96},{96,112},{112,64},{1... | collective-permute-start | bytes 786440 | tf_op jit(solution)/shard_map/ppermute | solution.py:309
  52.4 19.0 %collective-permute-start.3 = (bf16[256,512]{1,0:T(8,128)(2,1)S(1)}, bf16[256,512]{1,0:T(8,128)(2,1)S(1)}, u32[]{:S(2)}, u32[]{:S(2)}) collective-permute-start(bf16[256,512]{1,0:T(8,128)(2,1)S(1)} %get-tuple-element.19.a_ref), channel_id=1, source_target_pairs={{0,48},{16,0},{32,16},{48,32},{64,112},{80,64},{96,80},{112,96},{1... | collective-permute-start | bytes 786440 | tf_op jit(solution)/shard_map/ppermute | solution.py:309
  53.7 22.2 %collective-permute-start.4 = (bf16[256,512]{1,0:T(8,128)(2,1)S(1)}, bf16[256,512]{1,0:T(8,128)(2,1)S(1)}, u32[]{:S(2)}, u32[]{:S(2)}) collective-permute-start(bf16[256,512]{1,0:T(8,128)(2,1)S(1)} %get-tuple-element.19.a_ref), channel_id=1, source_target_pairs={{0,32},{16,48},{32,0},{48,16},{64,96},{80,112},{96,64},{112,80},{1... | collective-permute-start | bytes 786440 | tf_op jit(solution)/shard_map/ppermute | solution.py:309
  64.7 4.1 %collective-permute-start.8 = (bf16[256,256]{1,0:T(8,128)(2,1)S(1)}, bf16[256,256]{1,0:T(8,128)(2,1)S(1)}, u32[]{:S(2)}, u32[]{:S(2)}) collective-permute-start(bf16[256,256]{1,0:T(8,128)(2,1)S(1)} %get-tuple-element.18.q_ref), channel_id=1, source_target_pairs={{0,64},{16,80},{32,96},{48,112},{64,0},{80,16},{96,32},{112,48},{1... | collective-permute-start | bytes 393224 | tf_op jit(solution)/shard_map/ppermute | solution.py:310
  79.6 7.0 %collective-permute-start.9 = (bf16[272,256]{1,0:T(8,128)(2,1)S(1)}, bf16[272,256]{1,0:T(8,128)(2,1)S(1)}, u32[]{:S(2)}, u32[]{:S(2)}) collective-permute-start(bf16[272,256]{1,0:T(8,128)(2,1)S(1)} %shard_map.180), channel_id=1, source_target_pairs={{0,64},{16,80},{32,96},{48,112},{64,0},{80,16},{96,32},{112,48},{1... | collective-permute-start | bytes 417800 | tf_op jit(solution)/shard_map/ppermute | solution.py:338
  86.9 2.6 %collective-permute-start.10 = (bf16[256,256]{1,0:T(8,128)(2,1)S(1)}, bf16[256,256]{1,0:T(8,128)(2,1)S(1)}, u32[]{:S(2)}, u32[]{:S(2)}) collective-permute-start(bf16[256,256]{1,0:T(8,128)(2,1)S(1)} %shard_map.181.own_ref), channel_id=1, source_target_pairs={{0,1},{1,0},{2,3},{3,2},{4,5},{5,4},{6,7},{7,6},{8,9},{9,8},{10,11... | collective-permute-start | bytes 393224 | tf_op jit(solution)/shard_map/ppermute | solution.py:29
  113.2 3.6 %copy-start.11 = (f32[5120]{0:T(1024)S(1)}, f32[5120]{0:T(1024)}, u32[]{:S(2)}) copy-start(f32[5120]{0:T(1024)} %param.19) | copy-start | bytes 61444
  113.2 3.6 %copy-start.12 = (f32[5120]{0:T(1024)S(1)}, f32[5120]{0:T(1024)}, u32[]{:S(2)}) copy-start(f32[5120]{0:T(1024)} %param.26) | copy-start | bytes 61444
  113.2 3.7 %copy-start.4 = (f32[4,256]{1,0:T(4,128)S(1)}, f32[4,256]{1,0:T(4,128)}, u32[]{:S(2)}) copy-start(f32[4,256]{1,0:T(4,128)} %state_ref.1) | copy-start | bytes 12292
  113.2 3.7 %copy-start.5 = (f32[4,256]{1,0:T(4,128)S(1)}, f32[4,256]{1,0:T(4,128)}, u32[]{:S(2)}) copy-start(f32[4,256]{1,0:T(4,128)} %noise_ref.1) | copy-start | bytes 12292
  113.2 3.7 %copy-start.6 = (s32[4,1]{0,1:T(1,128)S(1)}, s32[4,1]{0,1:T(1,128)}, u32[]{:S(2)}) copy-start(s32[4,1]{0,1:T(1,128)} %param.30) | copy-start | bytes 52
  113.2 3.6 %collective-permute-start.12 = (f32[16,2560]{1,0:T(8,128)}, f32[16,2560]{1,0:T(8,128)S(1)}, u32[]{:S(2)}, u32[]{:S(2)}) collective-permute-start(f32[16,2560]{1,0:T(8,128)} %get-tuple-element.29), channel_id=1, source_target_pairs={{0,1},{1,0},{2,3},{3,2},{4,5},{5,4},{6,7},{7,6},{8,9},{9,8},{10,11... | collective-permute-start | bytes 491528 | tf_op jit(solution)/shard_map/ppermute | solution.py:29
  116.7 11.8 %copy-start.3 = (bf16[256,1024]{1,0:T(8,128)(2,1)S(1)}, bf16[256,1024]{1,0:T(8,128)(2,1)}, u32[]{:S(2)}) copy-start(bf16[256,1024]{1,0:T(8,128)(2,1)} %w_ref.1) | copy-start | bytes 1572868

commit v2 on v1

v2 whole, which is shorter than its diff:
```python
import functools
import math

import jax
import jax.numpy as jnp
from jax import lax
from jax.experimental import pallas as pl
from jax.experimental.pallas import tpu as pltpu
from jax.sharding import PartitionSpec as P

HD = 128
CAP = 2
BF = jnp.bfloat16
F32 = jnp.float32
MIB = 1 << 20
VM = pl.BlockSpec(memory_space=pltpu.VMEM)
SM = pl.BlockSpec(memory_space=pltpu.SMEM)
HB = pl.BlockSpec(memory_space=pltpu.HBM)

CORE_SWAP = [(m, m ^ 1) for m in range(16)]
Y_SWAP = [(c, c ^ 4) for c in range(8)]
PAIR_SWAP = [(m, m ^ 2) for m in range(16)]
STEPS = (1, 3, 2)


def x_step(by):
    return [(c, (c // 4) * 4 + (c + by) % 4) for c in range(8)]


def core_swap(a):
    return lax.ppermute(a, "mdl", CORE_SWAP)


def z_send(a, by):
    return lax.ppermute(a, "mdl", [(m, (m + 4 * by) % 16) for m in range(16)])


def slot_chips(mdl, back):
    z, h = mdl >> 2, (mdl >> 1) & 1
    around = [(z + (-by if back else by)) & 3 for by in STEPS]
    return [z * 2 + h, z * 2 + 1 - h] + [a * 2 + h for a in around] + [a * 2 + 1 - h for a in around]


def call(
    body, outs, args, flops=0, nbytes=0, trans=0, smem=(), hbm=(), scratch=(), limit=24, after=()
):
    count = len(args)
    place = [SM if i in smem else HB if i in hbm else VM for i in range(count)]

    def run(*refs):
        body(*refs[:count], *refs[count + len(after) :])

    return pl.pallas_call(
        run,
        out_shape=outs,
        in_specs=place
        + [pl.BlockSpec(memory_space=pl.ANY)] * len(after),
        out_specs=jax.tree.map(lambda o: VM, outs),
        scratch_shapes=list(scratch),
        compiler_params=pltpu.CompilerParams(vmem_limit_bytes=limit * MIB),
        cost_estimate=pl.CostEstimate(flops=flops, bytes_accessed=nbytes, transcendentals=trans),
    )(*args, *after)


def shape(dims, dtype):
    return jax.ShapeDtypeStruct(dims, dtype)


def turn_body(core_ref, x_ref, keep_ref, give_ref):
    k = core_ref[0]
    block = 16
    x = jnp.transpose(x_ref[...])
    for j in range(x.shape[0] // (2 * block)):
        first = x[2 * j * block : (2 * j + 1) * block]
        second = x[(2 * j + 1) * block : (2 * j + 2) * block]
        keep_ref[j * block : (j + 1) * block] = jnp.where(k == 0, first, second)
        give_ref[j * block : (j + 1) * block] = jnp.where(k == 0, second, first)


def join_body(a_ref, b_ref, *out_refs):
    width = a_ref.shape[1]
    for i, out_ref in enumerate(out_refs):
        some = out_ref.shape[0]
        out_ref[:, :width] = a_ref[i * some : (i + 1) * some]
        out_ref[:, width:] = b_ref[i * some : (i + 1) * some]


def load_body(*refs):
    *refs, sems = refs
    half = len(refs) // 2
    pieces = sems.shape[1]
    copies = []
    for i, (src, dst) in enumerate(zip(refs[:half], refs[half:])):
        some = src.shape[0] // pieces
        for j in range(pieces):
            rows = pl.ds(j * some, some)
            copies.append(pltpu.make_async_copy(src.at[rows], dst.at[rows], sems.at[i, j]))
    for copy in copies:
        copy.start()
    for copy in copies:
        copy.wait()


def halves_body(core_ref, w_ref, mine_ref, theirs_ref):
    k = core_ref[0]
    width = mine_ref.shape[1]
    mine_ref[...] = w_ref[:, pl.ds(pl.multiple_of(k * width, width), width)]
    theirs_ref[...] = w_ref[:, pl.ds(pl.multiple_of((1 - k) * width, width), width)]


def norm_body(mdl_ref, *refs):
    *x_refs, scale_ref, shift_ref, out_ref, own_ref = refs
    blocks = len(x_refs)
    rows, width = x_refs[0].shape
    total = sum(x_ref[...].astype(F32) for x_ref in x_refs)
    mean = jnp.sum(total, -1, keepdims=True) / (blocks * width)
    square = jnp.zeros((rows, width), F32)
    for x_ref in x_refs:
        centred = x_ref[...].astype(F32) - mean
        square = square + centred * centred
    var = jnp.sum(square, -1, keepdims=True) / (blocks * width)
    inverse = lax.rsqrt(var + 1e-06)
    chips = slot_chips(mdl_ref[0], True)
    block = own_ref.shape[1]
    here = pl.ds(pl.multiple_of(chips[0] * block, block), block)
    for chip, x_ref in zip(chips, x_refs):
        own_ref[chip] = x_ref[here, :]
        centred = x_ref[...].astype(F32) - mean
        scale, shift = scale_ref[pl.ds(chip, 1)], shift_ref[pl.ds(chip, 1)]
        cols = pl.ds(pl.multiple_of(chip * width, width), width)
        out_ref[:, cols] = (centred * inverse * (1.0 + scale) + shift).astype(BF)


def kv_body(core_ref, own_ref, other_ref, wk_ref, wv_ref, kv_ref, x):
    k = core_ref[0]
    rows = own_ref.shape[0]
    x[pl.ds(pl.multiple_of(k * rows, rows), rows), :] = own_ref[...]
    x[pl.ds(pl.multiple_of((1 - k) * rows, rows), rows), :] = other_ref[...]
    kv_ref[:, :256] = jnp.dot(x[...], wk_ref[...], preferred_element_type=F32).astype(BF)
    kv_ref[:, 256:] = jnp.dot(x[...], wv_ref[...], preferred_element_type=F32).astype(BF)


def query_body(x_ref, wq_ref, q_ref):
    q_ref[...] = jnp.dot(x_ref[...], wq_ref[...], preferred_element_type=F32).astype(BF)


C2 = math.log2(math.e) / math.sqrt(HD)


def fold(op, parts):
    return functools.reduce(
        op, [p[:, at : at + HD] for p in parts for at in range(0, p.shape[1], HD)]
    )


def attend(q_ref, kv_refs, start, h):
    q = q_ref[:, h * HD : (h + 1) * HD]
    scores = [
        lax.dot_general(
            q, kv[:, h * HD : (h + 1) * HD], (((1,), (1,)), ((), ())), preferred_element_type=F32
        )
        for kv in kv_refs
    ]
    peak = jnp.max(fold(jnp.maximum, scores), -1, keepdims=True)
    if start is not None:
        peak = jnp.maximum(peak, start[0])
    probs = [jnp.exp2((s - peak) * C2) for s in scores]
    total = jnp.sum(fold(jnp.add, probs), -1, keepdims=True)
    summed = sum(
        jnp.dot(
            p.astype(BF), kv[:, 256 + h * HD : 256 + (h + 1) * HD], preferred_element_type=F32
        )
        for p, kv in zip(probs, kv_refs)
    )
    if start is not None:
        factor = jnp.exp2((start[0] - peak) * C2)
        total, summed = start[1] * factor + total, start[2] * factor + summed
    return peak, total, summed


def past_body(q_ref, *refs):
    *kv_refs, o_ref, peak_ref, total_ref = refs
    for h in range(2):
        peak, total, summed = attend(q_ref, kv_refs, None, h)
        o_ref[:, h * HD : (h + 1) * HD] = summed
        peak_ref[h] = jnp.broadcast_to(peak, peak_ref.shape[1:])
        total_ref[h] = jnp.broadcast_to(total, total_ref.shape[1:])


def finish(q_ref, refs, o_ref, peak_ref, total_ref, h):
    start = (peak_ref[h][:, :1], total_ref[h][:, :1], o_ref[:, h * HD : (h + 1) * HD])
    peak, total, summed = attend(q_ref, refs, start, h)
    return summed * (1.0 / total), peak / math.sqrt(HD) + jnp.log(total)


def sent_body(q_ref, a_ref, b_ref, c_ref, d_ref, o_ref, peak_ref, total_ref, out_ref):
    rows = q_ref.shape[0]
    both = []
    for h in range(2):
        o, lse = finish(q_ref, (a_ref, b_ref, c_ref, d_ref), o_ref, peak_ref, total_ref, h)
        out_ref[:rows, h * HD : (h + 1) * HD] = o.astype(BF)
        both.append(lse)
    lane = lax.broadcasted_iota(jnp.int32, (rows, HD), 1)
    rest = jnp.transpose(jnp.where(lane == 0, both[0], both[1]))[:16]
    at = lax.broadcasted_iota(jnp.int32, (16, rows), 0)
    tail = jnp.zeros((16, rows), F32)
    for i in range(3):
        piece = rest.astype(BF).astype(F32)
        for h in range(2):
            tail = jnp.where(at == 3 * h + i, piece[h : h + 1], tail)
        rest = rest - piece
    out_ref[rows:, :] = tail.astype(BF)


def kept_body(q_ref, a_ref, b_ref, c_ref, d_ref, o_ref, peak_ref, total_ref, out_ref, lse_ref):
    for h in range(2):
        o, lse = finish(q_ref, (a_ref, b_ref, c_ref, d_ref), o_ref, peak_ref, total_ref, h)
        out_ref[:, h * HD : (h + 1) * HD] = o
        lse_ref[h] = jnp.broadcast_to(lse, lse_ref.shape[1:])


def merge_body(own_ref, lse_ref, got_ref, out_ref):
    rows = own_ref.shape[0]
    tail = got_ref[rows:, :].astype(F32)
    at = lax.broadcasted_iota(jnp.int32, (HD, rows), 0)
    row = [
        tail[3 * h : 3 * h + 1] + tail[3 * h + 1 : 3 * h + 2] + tail[3 * h + 2 : 3 * h + 3]
        for h in range(2)
    ]
    turned = jnp.transpose(jnp.where(at == 0, row[0], row[1]))
    for h in range(2):
        theirs = turned[:, h : h + 1]
        ours = lse_ref[h][:, :1]
        top = jnp.maximum(ours, theirs)
        a, b = jnp.exp(ours - top), jnp.exp(theirs - top)
        inverse = 1.0 / (a + b)
        cols = slice(h * HD, (h + 1) * HD)
        merged = (a * inverse) * own_ref[:, cols] + (b * inverse) * got_ref[:rows, cols].astype(F32)
        out_ref[:, cols] = merged.astype(BF)


def out_body(mdl_ref, own_ref, other_ref, wa_ref, wb_ref, *refs):
    *out_refs, x = refs
    for s, chip in enumerate(slot_chips(mdl_ref[0], False)):
        for k in range(2):
            rows = pl.ds(pl.multiple_of(128 * k + 16 * chip, 16), 16)
            x[s * 32 + 16 * k : s * 32 + 16 * k + 16, :256] = own_ref[rows, :]
            x[s * 32 + 16 * k : s * 32 + 16 * k + 16, 256:] = other_ref[rows, :]
    for at in range(0, wa_ref.shape[1], 512):
        cols = slice(at, at + 512)
        r = jnp.dot(x[:, :256], wa_ref[:, cols], preferred_element_type=F32) + jnp.dot(
            x[:, 256:], wb_ref[:, cols], preferred_element_type=F32
        )
        for s, out_ref in enumerate(out_refs):
            out_ref[:, cols] = r[32 * s : 32 * s + 32].astype(BF)


def add_body(*refs):
    *in_refs, out_ref = refs
    out_ref[...] = sum(r[...].astype(F32) for r in in_refs).astype(BF)


def sum_body(core_ref, *refs):
    *in_refs, keep_ref, give_ref = refs
    k = core_ref[0]
    total = sum(r[...].astype(F32) for r in in_refs)
    keep_ref[...] = jnp.where(k == 0, total[:16], total[16:])
    give_ref[...] = jnp.where(k == 0, total[16:], total[:16])


def tail_body(
    core_ref, own_ref, other_ref, x_ref, gate_ref, scale_ref, wf_ref, state_ref, noise_ref,
    owner_ref, hidden_ref, next_ref, slot_ref, vel,
):
    k = core_ref[0]
    own, other = own_ref[...], other_ref[...]
    left = jnp.where(k == 0, own, other)
    right = jnp.where(k == 0, other, own)
    blocks, rows, width = x_ref.shape
    half = blocks // 2
    mixed = []
    square = jnp.zeros((rows, width), F32)
    for b in range(blocks):
        at = (b % half) * width
        part = (left if b < half else right)[:, at : at + width]
        mix = x_ref[b].astype(F32) + gate_ref[b : b + 1] * part
        hidden_ref[:, b * width : (b + 1) * width] = mix.astype(BF)
        square = square + mix * mix
        mixed.append(mix)
    inverse = lax.rsqrt(jnp.sum(square, -1, keepdims=True) / (blocks * width) + 1e-06)
    acc = jnp.zeros(vel.shape, F32)
    for b in range(blocks):
        normed = (mixed[b] * inverse * (1.0 + scale_ref[b : b + 1])).astype(BF)
        acc = acc + lax.dot_general(
            normed,
            wf_ref[:, b * width : (b + 1) * width],
            (((1,), (1,)), ((), ())),
            preferred_element_type=F32,
        )
    vel[...] = acc
    tiles = state_ref.shape[0]
    lat = acc.shape[1]
    velocity = jnp.concatenate(
        [vel[pl.ds(j, tiles, stride=rows // tiles), :] for j in range(rows // tiles)], -1
    )
    state = state_ref[...]
    new = (
        state
        + 0.2 * (velocity + 0.5 * (0.5 * velocity - state) / (1.0 - 0.5))
        + math.sqrt(0.2) * noise_ref[...]
    )
    next_ref[...] = new
    panels = new.astype(BF).astype(F32)
    at = lax.broadcasted_iota(jnp.int32, slot_ref.shape, 0)
    slots = jnp.zeros(slot_ref.shape, F32)
    for t in range(tiles):
        owner = owner_ref[t]
        before = jnp.int32(0)
        for e in range(t):
            before = before + jnp.where(owner_ref[e] == owner, 1, 0)
        slots = jnp.where(at == owner * CAP + before, panels[t : t + 1], slots)
    slot_ref[...] = slots.astype(BF)


def up_body(x_ref, w_ref, out_ref):
    y = jnp.dot(x_ref[...], w_ref[...], preferred_element_type=F32)
    out_ref[...] = jax.nn.gelu(y).astype(BF)


def shards(
    latents, mod_shift, mod_scale, gate, w_query, w_key, w_value, w_out, cache_keys,
    cache_values, final_scale, w_final, state, noise, owners, w_up,
):
    count, part = latents.shape
    mdl = lax.axis_index("mdl")
    core = mdl % 2
    core_1 = jnp.reshape(core, (1,)).astype(jnp.int32)
    mdl_1 = jnp.reshape(mdl, (1,)).astype(jnp.int32)
    chips = 8
    block = count // 16
    rows = count // 2

    cached = call(
        join_body,
        (shape((cache_keys.shape[0], 2 * cache_keys.shape[1]), BF),),
        (cache_keys, cache_values),
    )[0]
    far = lax.ppermute(cached, "ctx", x_step(2))
    keep, give = call(
        turn_body,
        (shape((rows, part), BF), shape((rows, part), BF)),
        (core_1, latents.T),
        smem=(0,),
    )
    got = core_swap(give)
    is_first = core == 0
    wide = jnp.concatenate(
        [jnp.where(is_first, keep, got), jnp.where(is_first, got, keep)], 1
    )
    beside = lax.ppermute(wide, "mdl", PAIR_SWAP)
    x = [wide, beside] + [z_send(a, by) for a in (wide, beside) for by in STEPS]

    near = [lax.ppermute(cached, "ctx", x_step(by)) for by in (1, 3)]

    half = w_out.shape[1] // 2
    w_mine, w_give = call(
        halves_body,
        (shape((w_out.shape[0], half), BF), shape((w_out.shape[0], half), BF)),
        (core_1, w_out),
        smem=(0,),
        after=(beside,),
    )
    w_theirs = core_swap(w_give)

    normed, own_x = call(
        norm_body,
        (shape((rows, chips * 2 * part), BF), shape((chips, block, 2 * part), BF)),
        (mdl_1, *x, mod_scale.reshape(chips, 2 * part), mod_shift.reshape(chips, 2 * part)),
        smem=(0,),
        flops=MIB,
        nbytes=MIB,
        after=(far, *near, w_mine),
    )
    cols = w_query.shape[1]
    weights = call(
        load_body,
        tuple(shape(w.shape, BF) for w in (w_query, w_key, w_value)),
        (w_query, w_key, w_value),
        hbm=(0, 1, 2),
        nbytes=8 * MIB,
        scratch=[pltpu.SemaphoreType.DMA((3, 4))],
        after=(normed,),
    )
    kv, whole = call(
        kv_body,
        (shape((count, 2 * cols), BF), shape((count, w_query.shape[0]), BF)),
        (core_1, normed, core_swap(normed), *weights[1:]),
        smem=(0,),
        flops=2 * count * w_query.shape[0] * 2 * cols,
        nbytes=8 * MIB,
    )
    query = call(
        query_body,
        shape((count, cols), BF),
        (whole, weights[0]),
        flops=2 * count * w_query.shape[0] * cols,
        nbytes=5 * MIB,
    )
    fresh = [kv] + [lax.ppermute(kv, "ctx", x_step(by)) for by in (1, 3, 2)]
    query_in = lax.ppermute(query, "ctx", Y_SWAP)

    def past_call(q, after=()):
        return call(
            past_body,
            (
                shape((count, cols), F32),
                shape((2, count, HD), F32),
                shape((2, count, HD), F32),
            ),
            (q, cached, far, *near),
            flops=4 * count * 2048 * 256,
            nbytes=4 * MIB,
            trans=count * 4096,
            after=after,
        )

    stats_own = past_call(query)
    stats_in = past_call(query_in, stats_own[:1])
    sent = call(
        sent_body,
        shape((count + 16, cols), BF),
        (query_in, *fresh, *stats_in),
        flops=4 * count * 1024 * 256,
        nbytes=2 * MIB,
        trans=count * 2048,
    )
    back = lax.ppermute(sent, "ctx", Y_SWAP)
    kept = call(
        kept_body,
        (shape((count, cols), F32), shape((2, count, HD), F32)),
        (query, *fresh, *stats_own),
        flops=4 * count * 1024 * 256,
        nbytes=2 * MIB,
        trans=count * 2048,
    )
    attended = call(merge_body, shape((count, cols), BF), (*kept, back), nbytes=MIB)

    projected = call(
        out_body,
        tuple(shape((2 * block, half), BF) for _ in range(chips)),
        (mdl_1, attended, core_swap(attended), w_mine, w_theirs),
        smem=(0,),
        flops=2 * count * 512 * half,
        nbytes=4 * MIB,
        scratch=[pltpu.VMEM((count, 2 * cols), BF)],
    )
    here, passing = projected[0], projected[1]
    relayed = [z_send(a, by) for a, by in zip(projected[5:], STEPS)]
    direct = [z_send(a, by) for a, by in zip(projected[2:5], STEPS)]
    passed = lax.ppermute(
        call(add_body, shape(passing.shape, BF), (passing, *relayed)), "mdl", PAIR_SWAP
    )
    ours, theirs = call(
        sum_body,
        (shape((block, half), F32), shape((block, half), F32)),
        (core_1, here, *direct, passed),
        smem=(0,),
        nbytes=2 * MIB,
    )
    hidden_out, next_state, slot_rows = call(
        tail_body,
        (
            shape((block, w_out.shape[1]), BF),
            shape(state.shape, F32),
            shape((16 * CAP, state.shape[1]), BF),
        ),
        (
            core_1, ours, core_swap(theirs), own_x, gate.reshape(chips, 2 * part),
            final_scale.reshape(chips, 2 * part), w_final.T, state, noise, owners[:, 0],
        ),
        smem=(0, 9),
        nbytes=2 * MIB,
        scratch=[pltpu.VMEM((block, w_final.shape[1]), F32)],
    )
    routed = lax.all_to_all(
        slot_rows.reshape(16, CAP, state.shape[1]), "mdl", split_axis=0, concat_axis=0, tiled=True
    ).reshape(16 * CAP, state.shape[1])
    upsampled = call(
        up_body, shape((16 * CAP, w_up.shape[1]), BF), (routed, w_up), nbytes=MIB
    )
    return (hidden_out, next_state, upsampled)


def solution(mesh):
    return jax.shard_map(
        shards,
        mesh=mesh,
        in_specs=(
            P("ctx", "mdl"),
            P(),
            P(),
            P(),
            P(None, "mdl"),
            P(None, "mdl"),
            P(None, "mdl"),
            P("mdl", None),
            P("ctx", "mdl"),
            P("ctx", "mdl"),
            P(),
            P(),
            P(("ctx", "mdl"), None),
            P(("ctx", "mdl"), None),
            P(("ctx", "mdl"), None),
            P(),
        ),
        out_specs=(P(("ctx", "mdl"), None), P(("ctx", "mdl"), None), P(("ctx", "mdl"), None)),
        check_vma=False,
    )
```

time: 130 us -> 108 us (0.83)
  blocking collectives: 31.9 us -> 10.4 us
  starting transfers between devices: 22.5 us -> 35.3 us
  Pallas kernels: 24.7 us -> 17.3 us
  waiting for transfers between devices: 41.3 us -> 34.9 us
    all_to_all x1 -> x0, blocking collectives: 22 us -> none  [chips_exchange(): return lax.all_to_all(a, 'mdl', 0, 0, axis_index_groups=CHIPS, tiled=True)]
    ppermute x3 -> x17, starting transfers between devices: 4.28 us -> 24.5 us  [the longest x12 17.4 us: z_send(): return lax.ppermute(a, 'mdl', [(m, (m + 4 * by) % 16) for m in range(16)])]
    all_to_all x1 -> x0, waiting for transfers between devices: 19.4 us -> none  [chips_exchange(): return lax.all_to_all(a, 'mdl', 0, 0, axis_index_groups=CHIPS, tiled=True)]
    ppermute x3 -> x17, waiting for transfers between devices: 11.8 us -> 23.8 us  [the longest x12 20.4 us: z_send(): return lax.ppermute(a, 'mdl', [(m, (m + 4 * by) % 16) for m in range(16)])]
    all_to_all x1 -> x0, starting transfers between devices: 7.88 us -> none  [chips_exchange(): return lax.all_to_all(a, 'mdl', 0, 0, axis_index_groups=CHIPS, tiled=True)]
    pallas_call x11 -> x17, Pallas kernels: 24.7 us -> 17.3 us  [call(): pl.pallas_call(run, out_shape=outs, in_specs=place + [pl.BlockSpec(memory...]
    unnamed x29 -> x32, local copies, waits for them, and re-layouts: 4.53 us -> 7 us
    ppermute x1, waiting for transfers between devices: 0.01 us -> 2.16 us  [shards(): back = lax.ppermute(sent, 'ctx', Y_SWAP)]
  transfers between devices with their start and end apart: 14 -> 27, of which waited for: 7 -> 15; matrix products, arithmetic and copies ran while one was open for 3% -> 1% of each run, Pallas kernels for 15% -> 12%
where the time goes in v2:
time: 108 us; the launch traced here: 107 us
  starting transfers between devices  35.3 us (33%)
  waiting for transfers between devices  34.9 us (32%)
  Pallas kernels  17.3 us (16%)
  blocking collectives  10.4 us (10%)
  local copies, waits for them, and re-layouts  8.5 us (8%)
    ppermute x12, waiting for transfers between devices, z_send(): return lax.ppermute(a, 'mdl', [(m, (m + 4 * by) % 16) for m in range(16)])  20.4 us
    ppermute x12, starting transfers between devices, z_send(): return lax.ppermute(a, 'mdl', [(m, (m + 4 * by) % 16) for m in range(16)])  17.4 us
    pallas_call x17, Pallas kernels, call(): pl.pallas_call(run, out_shape=outs, in_specs=place + [pl.BlockSpec(memory...  17.3 us
    all_to_all x1, blocking collectives, shards(): lax.all_to_all(slot_rows.reshape(16, CAP, state.shape[1]), 'mdl', split_a...  10.4 us
    unnamed x32, local copies, waits for them, and re-layouts  7 us
    ppermute x5, starting transfers between devices, core_swap(): return lax.ppermute(a, 'mdl', CORE_SWAP)  6.7 us
    ppermute x3, waiting for transfers between devices, shards(): fresh = [kv] + [lax.ppermute(kv, 'ctx', x_step(by)) for by in (1, 3, 2)]  4.11 us
    ppermute x2, waiting for transfers between devices, shards(): near = [lax.ppermute(cached, 'ctx', x_step(by)) for by in (1, 3)]  3.42 us
  transfers between devices with their start and end apart: 27, of which 15 were waited for; matrix products, arithmetic and copies ran while one was open for 1% of the time, Pallas kernels for 12%

profile of v2, /device:TPU:1, one launch (start us, length us, event | category | flops | bytes accessed | tf_op | source)
XLA Modules:
  0.0 107.4 jit_solution(9747220754556313383)
XLA Ops:
  0.7 0.9 copy-done.8
  1.7 1.5 %collective-permute-start = (bf16[128,320]{1,0:T(8,128)(2,1)S(1)}, bf16[128,320]{1,0:T(8,128)(2,1)S(1)}, u32[]{:S(2)}, u32[]{:S(2)}) collective-permute-start(bf16[128,320]{1,0:T(8,128)(2,1)S(1)} %get-tuple-element.36), channel_id=1, source_target_pairs={{0,1},{1,0},{2,3},{3,2},{4,5},{5,4},{6,7},{7,6},{8,9},{9,8},{10,11... | collective-permute-start | bytes 245768 | tf_op jit(solution)/shard_map/ppermute | solution.py:31
  3.2 0.9 collective-permute-done
  4.2 3.1 %collective-permute-start.1 = (bf16[128,640]{1,0:T(8,128)(2,1)S(1)}, bf16[128,640]{1,0:T(8,128)(2,1)S(1)}, u32[]{:S(2)}, u32[]{:S(2)}) collective-permute-start(bf16[128,640]{1,0:T(8,128)(2,1)S(1)} %pad_maximum_fusion.refs_1_), channel_id=1, source_target_pairs={{0,2},{1,3},{2,0},{3,1},{4,6},{5,7},{6,4},{7,5},{8,10},{9,11},{10,... | collective-permute-start | bytes 491528 | tf_op jit(solution)/shard_map/ppermute | solution.py:360
  7.3 0.9 copy-done.6
  8.3 0.9 copy-done.7
  9.3 2.5 %collective-permute-start.10 = (bf16[512,512]{1,0:T(8,128)(2,1)S(1)}, bf16[512,512]{1,0:T(8,128)(2,1)S(1)}, u32[]{:S(2)}, u32[]{:S(2)}) collective-permute-start(bf16[512,512]{1,0:T(8,128)(2,1)S(1)} %shard_map.176.refs_1_), channel_id=1, source_target_pairs={{0,48},{16,0},{32,16},{48,32},{64,112},{80,64},{96,80},{112,96},{1... | collective-permute-start | bytes 1572872 | tf_op jit(solution)/shard_map/ppermute | solution.py:363
  11.8 0.5 collective-permute-start.8
  12.3 0.6 collective-permute-start.9
  12.9 1.6 %collective-permute-start.2 = (bf16[128,640]{1,0:T(8,128)(2,1)S(1)}, bf16[128,640]{1,0:T(8,128)(2,1)S(1)}, u32[]{:S(2)}, u32[]{:S(2)}) collective-permute-start(bf16[128,640]{1,0:T(8,128)(2,1)S(1)} %pad_maximum_fusion.refs_1_), channel_id=1, source_target_pairs={{0,4},{1,5},{2,6},{3,7},{4,8},{5,9},{6,10},{7,11},{8,12},{9,13},{1... | collective-permute-start | bytes 491528 | tf_op jit(solution)/shard_map/ppermute | solution.py:35
  14.6 2.1 %collective-permute-start.3 = (bf16[128,640]{1,0:T(8,128)(2,1)S(1)}, bf16[128,640]{1,0:T(8,128)(2,1)S(1)}, u32[]{:S(2)}, u32[]{:S(2)}) collective-permute-start(bf16[128,640]{1,0:T(8,128)(2,1)S(1)} %pad_maximum_fusion.refs_1_), channel_id=1, source_target_pairs={{0,12},{1,13},{2,14},{3,15},{4,0},{5,1},{6,2},{7,3},{8,4},{9,5},{1... | collective-permute-start | bytes 491528 | tf_op jit(solution)/shard_map/ppermute | solution.py:35
  16.7 3.0 %collective-permute-done.2.refs_3_ = bf16[128,640]{1,0:T(8,128)(2,1)S(1)} collective-permute-done((bf16[128,640]{1,0:T(8,128)(2,1)S(1)}, bf16[128,640]{1,0:T(8,128)(2,1)S(1)}, u32[]{:S(2)}, u32[]{:S(2)}) %collective-permute-start.2) | collective-permute-done | bytes 163872 | tf_op jit(solution)/shard_map/ppermute | solution.py:35
  19.7 1.3 %collective-permute-start.4 = (bf16[128,640]{1,0:T(8,128)(2,1)S(1)}, bf16[128,640]{1,0:T(8,128)(2,1)S(1)}, u32[]{:S(2)}, u32[]{:S(2)}) collective-permute-start(bf16[128,640]{1,0:T(8,128)(2,1)S(1)} %pad_maximum_fusion.refs_1_), channel_id=1, source_target_pairs={{0,8},{1,9},{2,10},{3,11},{4,12},{5,13},{6,14},{7,15},{8,0},{9,1},... | collective-permute-start | bytes 491528 | tf_op jit(solution)/shard_map/ppermute | solution.py:35
  21.0 0.7 collective-permute-start.5
  21.7 4.0 %collective-permute-done.4.refs_5_ = bf16[128,640]{1,0:T(8,128)(2,1)S(1)} collective-permute-done((bf16[128,640]{1,0:T(8,128)(2,1)S(1)}, bf16[128,640]{1,0:T(8,128)(2,1)S(1)}, u32[]{:S(2)}, u32[]{:S(2)}) %collective-permute-start.4) | collective-permute-done | bytes 163872 | tf_op jit(solution)/shard_map/ppermute | solution.py:35
  25.7 1.4 %collective-permute-start.6 = (bf16[128,640]{1,0:T(8,128)(2,1)S(1)}, bf16[128,640]{1,0:T(8,128)(2,1)S(1)}, u32[]{:S(2)}, u32[]{:S(2)}) collective-permute-start(bf16[128,640]{1,0:T(8,128)(2,1)S(1)} %collective-permute-done.1.refs_2_), channel_id=1, source_target_pairs={{0,12},{1,13},{2,14},{3,15},{4,0},{5,1},{6,2},{7,3},{8,4},{9,5},{1... | collective-permute-start | bytes 491528 | tf_op jit(solution)/shard_map/ppermute | solution.py:35
  27.1 2.2 %collective-permute-done.5.refs_6_ = bf16[128,640]{1,0:T(8,128)(2,1)S(1)} collective-permute-done((bf16[128,640]{1,0:T(8,128)(2,1)S(1)}, bf16[128,640]{1,0:T(8,128)(2,1)S(1)}, u32[]{:S(2)}, u32[]{:S(2)}) %collective-permute-start.5) | collective-permute-done | bytes 163872 | tf_op jit(solution)/shard_map/ppermute | solution.py:35
  29.3 1.4 %collective-permute-start.7 = (bf16[128,640]{1,0:T(8,128)(2,1)S(1)}, bf16[128,640]{1,0:T(8,128)(2,1)S(1)}, u32[]{:S(2)}, u32[]{:S(2)}) collective-permute-start(bf16[128,640]{1,0:T(8,128)(2,1)S(1)} %collective-permute-done.1.refs_2_), channel_id=1, source_target_pairs={{0,8},{1,9},{2,10},{3,11},{4,12},{5,13},{6,14},{7,15},{8,0},{9,1},... | collective-permute-start | bytes 491528 | tf_op jit(solution)/shard_map/ppermute | solution.py:35
  30.7 0.7 reshape.32.refs_9_
  31.4 0.7 reshape.33.refs_10_
  32.2 1.7 %copy-done = bf16[256,5120]{1,0:T(8,128)(2,1)S(1)} copy-done((bf16[256,5120]{1,0:T(8,128)(2,1)S(1)}, bf16[256,5120]{1,0:T(8,128)(2,1)}, u32[]{:S(2)}) %copy-start) | copy-done | bytes 2621464
  33.9 0.2 shard_map.177
  34.1 0.9 collective-permute-done.7.refs_8_
  35.0 3.4 %collective-permute-done.9.refs_12_.refs_3_ = bf16[512,512]{1,0:T(8,128)(2,1)S(1)} collective-permute-done((bf16[512,512]{1,0:T(8,128)(2,1)S(1)}, bf16[512,512]{1,0:T(8,128)(2,1)S(1)}, u32[]{:S(2)}, u32[]{:S(2)}) %collective-permute-start.9) | collective-permute-done | bytes 524320 | tf_op jit(solution)/shard_map/ppermute | solution.py:363
  38.4 1.3 %shard_map.178 = (bf16[128,5120]{1,0:T(8,128)(2,1)S(1)}, bf16[8,16,640]{2,1,0:T(8,128)(2,1)S(1)}) custom-call(s32[1]{0:T(128)} %bitcast.1.refs_0_, bf16[128,640]{1,0:T(8,128)(2,1)S(1)} %pad_maximum_fusion.refs_1_, bf16[128,640]{1,0:T(8,128)(2,1)S(1)} %collective-permute-done.1.refs_2_, bf16[128,640]{1,0:T(8,128)(2,1)S(1)} %collective-permute-done.2.refs_3_, ...), custom_call_target="tpu_custom_call" | custom-call | flops 1048576 | bytes 1048576 | tf_op jit(solution)/shard_map/pallas_call | solution.py:53
  39.7 0.7 copy-done.9
  40.4 0.5 collective-permute-start.11
  40.9 1.7 %copy-done.3 = bf16[5120,256]{1,0:T(8,128)(2,1)S(1)} copy-done((bf16[5120,256]{1,0:T(8,128)(2,1)S(1)}, bf16[5120,256]{1,0:T(8,128)(2,1)}, u32[]{:S(2)}) %copy-start.3) | copy-done | bytes 2621464
  42.6 2.6 %shard_map.179 = (bf16[5120,256]{1,0:T(8,128)(2,1)S(1)}, bf16[5120,256]{1,0:T(8,128)(2,1)S(1)}, bf16[5120,256]{1,0:T(8,128)(2,1)S(1)}) custom-call(bf16[5120,256]{1,0:T(8,128)(2,1)S(1)} %copy-done.1, bf16[5120,256]{1,0:T(8,128)(2,1)S(1)} %copy-done.2, bf16[5120,256]{1,0:T(8,128)(2,1)S(1)} %copy-done.3, bf16[128,5120]{1,0:T(8,128)(2,1)S(1)} %get-tuple-element.38.refs_3_.refs_1_), custom_call_target="tpu_custom_call" | custom-call | bytes 8388608 | tf_op jit(solution)/shard_map/pallas_call | solution.py:53
  45.2 1.7 %shard_map.180 = (bf16[256,512]{1,0:T(8,128)(2,1)S(1)}, bf16[256,5120]{1,0:T(8,128)(2,1)S(1)}) custom-call(s32[1]{0:T(128)} %bitcast.refs_0_, bf16[128,5120]{1,0:T(8,128)(2,1)S(1)} %get-tuple-element.38.refs_3_.refs_1_, bf16[128,5120]{1,0:T(8,128)(2,1)S(1)} %collective-permute-done.11.refs_2_, bf16[5120,256]{1,0:T(8,128)(2,1)S(1)} %get-tuple-element.39.refs_3_, ...), custom_call_target="tpu_custom_call" | custom-call | flops 1342177280 | bytes 8388608 | tf_op jit(solution)/shard_map/pallas_call | solution.py:53
  46.9 0.9 collective-permute-start.12
  47.8 1.9 %collective-permute-start.13 = (bf16[256,512]{1,0:T(8,128)(2,1)S(1)}, bf16[256,512]{1,0:T(8,128)(2,1)S(1)}, u32[]{:S(2)}, u32[]{:S(2)}) collective-permute-start(bf16[256,512]{1,0:T(8,128)(2,1)S(1)} %get-tuple-element.43.refs_1_), channel_id=1, source_target_pairs={{0,48},{16,0},{32,16},{48,32},{64,112},{80,64},{96,80},{112,96},{1... | collective-permute-start | bytes 786440 | tf_op jit(solution)/shard_map/ppermute | solution.py:409
  49.6 0.2 collective-permute-start.14
  49.9 0.9 shard_map.181.refs_0_
  50.8 0.7 collective-permute-start.15
  51.4 1.8 %shard_map.182 = (f32[256,256]{1,0:T(8,128)S(1)}, f32[2,256,128]{2,1,0:T(8,128)S(1)}, f32[2,256,128]{2,1,0:T(8,128)S(1)}) custom-call(bf16[256,256]{1,0:T(8,128)(2,1)S(1)} %shard_map.181.refs_0_, bf16[512,512]{1,0:T(8,128)(2,1)S(1)} %shard_map.176.refs_1_, bf16[512,512]{1,0:T(8,128)(2,1)S(1)} %collective-permute-done.8.refs_11_.refs_2_, ...), custom_call_target="tpu_custom_call" | custom-call | flops 536870912 | bytes 4194304 | tf_op jit(solution)/shard_map/pallas_call | solution.py:53
  53.2 1.9 %collective-permute-done.15.refs_0_ = bf16[256,256]{1,0:T(8,128)(2,1)S(1)} collective-permute-done((bf16[256,256]{1,0:T(8,128)(2,1)S(1)}, bf16[256,256]{1,0:T(8,128)(2,1)S(1)}, u32[]{:S(2)}, u32[]{:S(2)}) %collective-permute-start.15) | collective-permute-done | bytes 131104 | tf_op jit(solution)/shard_map/ppermute | solution.py:410
  55.1 1.8 %shard_map.184 = (f32[256,256]{1,0:T(8,128)S(1)}, f32[2,256,128]{2,1,0:T(8,128)S(1)}, f32[2,256,128]{2,1,0:T(8,128)S(1)}) custom-call(bf16[256,256]{1,0:T(8,128)(2,1)S(1)} %collective-permute-done.15.refs_0_, bf16[512,512]{1,0:T(8,128)(2,1)S(1)} %shard_map.176.refs_1_, bf16[512,512]{1,0:T(8,128)(2,1)S(1)} %collective-permute-done.8.refs_11_.refs_2_, ...), custom_call_target="tpu_custom_call" | custom-call | flops 536870912 | bytes 4194304 | tf_op jit(solution)/shard_map/pallas_call | solution.py:53
  57.0 4.1 %collective-permute-done.14.refs_4_ = bf16[256,512]{1,0:T(8,128)(2,1)S(1)} collective-permute-done((bf16[256,512]{1,0:T(8,128)(2,1)S(1)}, bf16[256,512]{1,0:T(8,128)(2,1)S(1)}, u32[]{:S(2)}, u32[]{:S(2)}) %collective-permute-start.14) | collective-permute-done | bytes 262176 | tf_op jit(solution)/shard_map/ppermute | solution.py:409
  61.1 1.4 %shard_map.185 = bf16[272,256]{1,0:T(8,128)(2,1)S(1)} custom-call(bf16[256,256]{1,0:T(8,128)(2,1)S(1)} %collective-permute-done.15.refs_0_, bf16[256,512]{1,0:T(8,128)(2,1)S(1)} %get-tuple-element.43.refs_1_, bf16[256,512]{1,0:T(8,128)(2,1)S(1)} %collective-permute-done.12.refs_2_, bf16[256,512]{1,0:T(8,128)(2,1)S(1)} %collective-permute-done.13.refs_3_, ...), custom_call_target="tpu_custom_call" | custom-call | flops 268435456 | bytes 2097152 | tf_op jit(solution)/shard_map/pallas_call | solution.py:53
  62.5 0.5 collective-permute-start.16
  62.9 1.3 %shard_map.183 = (f32[256,256]{1,0:T(8,128)S(1)}, f32[2,256,128]{2,1,0:T(8,128)S(1)}) custom-call(bf16[256,256]{1,0:T(8,128)(2,1)S(1)} %shard_map.181.refs_0_, bf16[256,512]{1,0:T(8,128)(2,1)S(1)} %get-tuple-element.43.refs_1_, bf16[256,512]{1,0:T(8,128)(2,1)S(1)} %collective-permute-done.12.refs_2_, bf16[256,512]{1,0:T(8,128)(2,1)S(1)} %collective-permute-done.13.refs_3_, ...), custom_call_target="tpu_custom_call" | custom-call | flops 268435456 | bytes 2097152 | tf_op jit(solution)/shard_map/pallas_call | solution.py:53
  64.3 2.2 %collective-permute-done.16.refs_2_ = bf16[272,256]{1,0:T(8,128)(2,1)S(1)} collective-permute-done((bf16[272,256]{1,0:T(8,128)(2,1)S(1)}, bf16[272,256]{1,0:T(8,128)(2,1)S(1)}, u32[]{:S(2)}, u32[]{:S(2)}) %collective-permute-start.16) | collective-permute-done | bytes 139296 | tf_op jit(solution)/shard_map/ppermute | solution.py:437
  66.5 0.6 shard_map.186.refs_1_
  67.1 2.7 %collective-permute-start.17 = (bf16[256,256]{1,0:T(8,128)(2,1)S(1)}, bf16[256,256]{1,0:T(8,128)(2,1)S(1)}, u32[]{:S(2)}, u32[]{:S(2)}) collective-permute-start(bf16[256,256]{1,0:T(8,128)(2,1)S(1)} %shard_map.186.refs_1_), channel_id=1, source_target_pairs={{0,1},{1,0},{2,3},{3,2},{4,5},{5,4},{6,7},{7,6},{8,9},{9,8},{10,11... | collective-permute-start | bytes 393224 | tf_op jit(solution)/shard_map/ppermute | solution.py:31
  69.8 1.0 collective-permute-done.17.refs_2_
  70.8 0.8 shard_map.187
  71.6 1.7 %collective-permute-start.22 = (bf16[32,2560]{1,0:T(8,128)(2,1)S(1)}, bf16[32,2560]{1,0:T(8,128)(2,1)S(1)}, u32[]{:S(2)}, u32[]{:S(2)}) collective-permute-start(bf16[32,2560]{1,0:T(8,128)(2,1)S(1)} %get-tuple-element.58), channel_id=1, source_target_pairs={{0,4},{1,5},{2,6},{3,7},{4,8},{5,9},{6,10},{7,11},{8,12},{9,13},{1... | collective-permute-start | bytes 491528 | tf_op jit(solution)/shard_map/ppermute | solution.py:35
  73.3 2.2 %collective-permute-start.23 = (bf16[32,2560]{1,0:T(8,128)(2,1)S(1)}, bf16[32,2560]{1,0:T(8,128)(2,1)S(1)}, u32[]{:S(2)}, u32[]{:S(2)}) collective-permute-start(bf16[32,2560]{1,0:T(8,128)(2,1)S(1)} %get-tuple-element.59), channel_id=1, source_target_pairs={{0,12},{1,13},{2,14},{3,15},{4,0},{5,1},{6,2},{7,3},{8,4},{9,5},{1... | collective-permute-start | bytes 491528 | tf_op jit(solution)/shard_map/ppermute | solution.py:35
  75.5 1.2 %collective-permute-start.24 = (bf16[32,2560]{1,0:T(8,128)(2,1)S(1)}, bf16[32,2560]{1,0:T(8,128)(2,1)S(1)}, u32[]{:S(2)}, u32[]{:S(2)}) collective-permute-start(bf16[32,2560]{1,0:T(8,128)(2,1)S(1)} %get-tuple-element.60), channel_id=1, source_target_pairs={{0,8},{1,9},{2,10},{3,11},{4,12},{5,13},{6,14},{7,15},{8,0},{9,1},... | collective-permute-start | bytes 491528 | tf_op jit(solution)/shard_map/ppermute | solution.py:35
  76.7 0.7 collective-permute-start.19
  77.5 1.9 %collective-permute-start.20 = (bf16[32,2560]{1,0:T(8,128)(2,1)S(1)}, bf16[32,2560]{1,0:T(8,128)(2,1)S(1)}, u32[]{:S(2)}, u32[]{:S(2)}) collective-permute-start(bf16[32,2560]{1,0:T(8,128)(2,1)S(1)} %get-tuple-element.55), channel_id=1, source_target_pairs={{0,12},{1,13},{2,14},{3,15},{4,0},{5,1},{6,2},{7,3},{8,4},{9,5},{1... | collective-permute-start | bytes 491528 | tf_op jit(solution)/shard_map/ppermute | solution.py:35
  79.4 0.3 collective-permute-done.22.refs_1_
  79.7 1.0 collective-permute-start.21
  80.7 3.4 %collective-permute-done.24.refs_3_ = bf16[32,2560]{1,0:T(8,128)(2,1)S(1)} collective-permute-done((bf16[32,2560]{1,0:T(8,128)(2,1)S(1)}, bf16[32,2560]{1,0:T(8,128)(2,1)S(1)}, u32[]{:S(2)}, u32[]{:S(2)}) %collective-permute-start.24) | collective-permute-done | bytes 163872 | tf_op jit(solution)/shard_map/ppermute | solution.py:35
  84.2 0.3 collective-permute-start.25
  84.5 2.2 %collective-permute-done.19.refs_2_ = bf16[32,2560]{1,0:T(8,128)(2,1)S(1)} collective-permute-done((bf16[32,2560]{1,0:T(8,128)(2,1)S(1)}, bf16[32,2560]{1,0:T(8,128)(2,1)S(1)}, u32[]{:S(2)}, u32[]{:S(2)}) %collective-permute-start.19) | collective-permute-done | bytes 163872 | tf_op jit(solution)/shard_map/ppermute | solution.py:35
  86.7 4.4 %collective-permute-done.21.refs_4_ = bf16[32,2560]{1,0:T(8,128)(2,1)S(1)} collective-permute-done((bf16[32,2560]{1,0:T(8,128)(2,1)S(1)}, bf16[32,2560]{1,0:T(8,128)(2,1)S(1)}, u32[]{:S(2)}, u32[]{:S(2)}) %collective-permute-start.21) | collective-permute-done | bytes 163872 | tf_op jit(solution)/shard_map/ppermute | solution.py:35
  91.2 0.1 shard_map.189
  91.3 2.0 %collective-permute-start.26 = (f32[16,2560]{1,0:T(8,128)S(1)}, f32[16,2560]{1,0:T(8,128)S(1)}, u32[]{:S(2)}, u32[]{:S(2)}) collective-permute-start(f32[16,2560]{1,0:T(8,128)S(1)} %get-tuple-element.62), channel_id=1, source_target_pairs={{0,1},{1,0},{2,3},{3,2},{4,5},{5,4},{6,7},{7,6},{8,9},{9,8},{10,11... | collective-permute-start | bytes 491528 | tf_op jit(solution)/shard_map/ppermute | solution.py:31
  93.3 1.0 collective-permute-done.26.refs_2_
  94.4 1.7 %shard_map.190 = (bf16[16,5120]{1,0:T(8,128)(2,1)}, f32[4,256]{1,0:T(4,128)}, bf16[32,256]{1,0:T(8,128)(2,1)S(1)}) custom-call(s32[1]{0:T(128)} %bitcast.refs_0_, f32[16,2560]{1,0:T(8,128)S(1)} %get-tuple-element.61.refs_1_, f32[16,2560]{1,0:T(8,128)S(1)} %collective-permute-done.26.refs_2_, bf16[8,16,640]{2,1,0:T(8,128)(2,1)S(1)} %copy-done.10, ...), custom_call_target="tpu_custom_call" | custom-call | bytes 2097152 | tf_op jit(solution)/shard_map/pallas_call | solution.py:53
  96.1 10.4 %all_to_all.5 = bf16[16,2,256]{2,1,0:T(2,128)(2,1)S(1)} all-to-all(bf16[16,2,256]{2,1,0:T(2,128)(2,1)S(1)} %reshape.36), channel_id=1, replica_groups=mesh['ctx'=8,'mdl'=16] {'mdl'}, dimensions={0} | all-to-all | bytes 32768 | tf_op jit(solution)/shard_map/all_to_all | solution.py:485
  106.6 0.9 shard_map.191
  (48 shorter events, 0.5 us)
Async XLA Ops:
  0.6 0.9 copy-start.8
  1.7 2.4 %collective-permute-start = (bf16[128,320]{1,0:T(8,128)(2,1)S(1)}, bf16[128,320]{1,0:T(8,128)(2,1)S(1)}, u32[]{:S(2)}, u32[]{:S(2)}) collective-permute-start(bf16[128,320]{1,0:T(8,128)(2,1)S(1)} %get-tuple-element.36), channel_id=1, source_target_pairs={{0,1},{1,0},{2,3},{3,2},{4,5},{5,4},{6,7},{7,6},{8,9},{9,8},{10,11... | collective-permute-start | bytes 245768 | tf_op jit(solution)/shard_map/ppermute | solution.py:31
  4.2 10.3 %collective-permute-start.1 = (bf16[128,640]{1,0:T(8,128)(2,1)S(1)}, bf16[128,640]{1,0:T(8,128)(2,1)S(1)}, u32[]{:S(2)}, u32[]{:S(2)}) collective-permute-start(bf16[128,640]{1,0:T(8,128)(2,1)S(1)} %pad_maximum_fusion.refs_1_), channel_id=1, source_target_pairs={{0,2},{1,3},{2,0},{3,1},{4,6},{5,7},{6,4},{7,5},{8,10},{9,11},{10,... | collective-permute-start | bytes 491528 | tf_op jit(solution)/shard_map/ppermute | solution.py:360
  7.3 0.9 copy-start.6
  8.3 0.9 copy-start.7
  9.3 25.7 %collective-permute-start.10 = (bf16[512,512]{1,0:T(8,128)(2,1)S(1)}, bf16[512,512]{1,0:T(8,128)(2,1)S(1)}, u32[]{:S(2)}, u32[]{:S(2)}) collective-permute-start(bf16[512,512]{1,0:T(8,128)(2,1)S(1)} %shard_map.176.refs_1_), channel_id=1, source_target_pairs={{0,48},{16,0},{32,16},{48,32},{64,112},{80,64},{96,80},{112,96},{1... | collective-permute-start | bytes 1572872 | tf_op jit(solution)/shard_map/ppermute | solution.py:363
  11.8 23.2 %collective-permute-start.8 = (bf16[512,512]{1,0:T(8,128)(2,1)S(1)}, bf16[512,512]{1,0:T(8,128)(2,1)S(1)}, u32[]{:S(2)}, u32[]{:S(2)}) collective-permute-start(bf16[512,512]{1,0:T(8,128)(2,1)S(1)} %shard_map.176.refs_1_), channel_id=1, source_target_pairs={{0,32},{16,48},{32,0},{48,16},{64,96},{80,112},{96,64},{112,80},{1... | collective-permute-start | bytes 1572872 | tf_op jit(solution)/shard_map/ppermute | solution.py:348
  12.3 26.1 %collective-permute-start.9 = (bf16[512,512]{1,0:T(8,128)(2,1)S(1)}, bf16[512,512]{1,0:T(8,128)(2,1)S(1)}, u32[]{:S(2)}, u32[]{:S(2)}) collective-permute-start(bf16[512,512]{1,0:T(8,128)(2,1)S(1)} %shard_map.176.refs_1_), channel_id=1, source_target_pairs={{0,16},{16,32},{32,48},{48,0},{64,80},{80,96},{96,112},{112,64},{1... | collective-permute-start | bytes 1572872 | tf_op jit(solution)/shard_map/ppermute | solution.py:363
  12.9 6.8 %collective-permute-start.2 = (bf16[128,640]{1,0:T(8,128)(2,1)S(1)}, bf16[128,640]{1,0:T(8,128)(2,1)S(1)}, u32[]{:S(2)}, u32[]{:S(2)}) collective-permute-start(bf16[128,640]{1,0:T(8,128)(2,1)S(1)} %pad_maximum_fusion.refs_1_), channel_id=1, source_target_pairs={{0,4},{1,5},{2,6},{3,7},{4,8},{5,9},{6,10},{7,11},{8,12},{9,13},{1... | collective-permute-start | bytes 491528 | tf_op jit(solution)/shard_map/ppermute | solution.py:35
  14.6 6.4 %collective-permute-start.3 = (bf16[128,640]{1,0:T(8,128)(2,1)S(1)}, bf16[128,640]{1,0:T(8,128)(2,1)S(1)}, u32[]{:S(2)}, u32[]{:S(2)}) collective-permute-start(bf16[128,640]{1,0:T(8,128)(2,1)S(1)} %pad_maximum_fusion.refs_1_), channel_id=1, source_target_pairs={{0,12},{1,13},{2,14},{3,15},{4,0},{5,1},{6,2},{7,3},{8,4},{9,5},{1... | collective-permute-start | bytes 491528 | tf_op jit(solution)/shard_map/ppermute | solution.py:35
  19.7 6.0 %collective-permute-start.4 = (bf16[128,640]{1,0:T(8,128)(2,1)S(1)}, bf16[128,640]{1,0:T(8,128)(2,1)S(1)}, u32[]{:S(2)}, u32[]{:S(2)}) collective-permute-start(bf16[128,640]{1,0:T(8,128)(2,1)S(1)} %pad_maximum_fusion.refs_1_), channel_id=1, source_target_pairs={{0,8},{1,9},{2,10},{3,11},{4,12},{5,13},{6,14},{7,15},{8,0},{9,1},... | collective-permute-start | bytes 491528 | tf_op jit(solution)/shard_map/ppermute | solution.py:35
  21.0 8.3 %collective-permute-start.5 = (bf16[128,640]{1,0:T(8,128)(2,1)S(1)}, bf16[128,640]{1,0:T(8,128)(2,1)S(1)}, u32[]{:S(2)}, u32[]{:S(2)}) collective-permute-start(bf16[128,640]{1,0:T(8,128)(2,1)S(1)} %collective-permute-done.1.refs_2_), channel_id=1, source_target_pairs={{0,4},{1,5},{2,6},{3,7},{4,8},{5,9},{6,10},{7,11},{8,12},{9,13},{1... | collective-permute-start | bytes 491528 | tf_op jit(solution)/shard_map/ppermute | solution.py:35
  25.7 8.4 %collective-permute-start.6 = (bf16[128,640]{1,0:T(8,128)(2,1)S(1)}, bf16[128,640]{1,0:T(8,128)(2,1)S(1)}, u32[]{:S(2)}, u32[]{:S(2)}) collective-permute-start(bf16[128,640]{1,0:T(8,128)(2,1)S(1)} %collective-permute-done.1.refs_2_), channel_id=1, source_target_pairs={{0,12},{1,13},{2,14},{3,15},{4,0},{5,1},{6,2},{7,3},{8,4},{9,5},{1... | collective-permute-start | bytes 491528 | tf_op jit(solution)/shard_map/ppermute | solution.py:35
  29.3 5.7 %collective-permute-start.7 = (bf16[128,640]{1,0:T(8,128)(2,1)S(1)}, bf16[128,640]{1,0:T(8,128)(2,1)S(1)}, u32[]{:S(2)}, u32[]{:S(2)}) collective-permute-start(bf16[128,640]{1,0:T(8,128)(2,1)S(1)} %collective-permute-done.1.refs_2_), channel_id=1, source_target_pairs={{0,8},{1,9},{2,10},{3,11},{4,12},{5,13},{6,14},{7,15},{8,0},{9,1},... | collective-permute-start | bytes 491528 | tf_op jit(solution)/shard_map/ppermute | solution.py:35
  32.2 1.7 %copy-start = (bf16[256,5120]{1,0:T(8,128)(2,1)S(1)}, bf16[256,5120]{1,0:T(8,128)(2,1)}, u32[]{:S(2)}) copy-start(bf16[256,5120]{1,0:T(8,128)(2,1)} %refs_1_.5) | copy-start | bytes 7864324
  33.9 7.0 %copy-start.2 = (bf16[5120,256]{1,0:T(8,128)(2,1)S(1)}, bf16[5120,256]{1,0:T(8,128)(2,1)}, u32[]{:S(2)}) copy-start(bf16[5120,256]{1,0:T(8,128)(2,1)} %refs_1_.6) | copy-start | bytes 7864324
  34.1 6.8 %copy-start.1 = (bf16[5120,256]{1,0:T(8,128)(2,1)S(1)}, bf16[5120,256]{1,0:T(8,128)(2,1)}, u32[]{:S(2)}) copy-start(bf16[5120,256]{1,0:T(8,128)(2,1)} %refs_0_.3) | copy-start | bytes 7864324
  39.7 0.7 copy-start.9
  40.4 4.8 %collective-permute-start.11 = (bf16[128,5120]{1,0:T(8,128)(2,1)S(1)}, bf16[128,5120]{1,0:T(8,128)(2,1)S(1)}, u32[]{:S(2)}, u32[]{:S(2)}) collective-permute-start(bf16[128,5120]{1,0:T(8,128)(2,1)S(1)} %get-tuple-element.38.refs_3_.refs_1_), channel_id=1, source_target_pairs={{0,1},{1,0},{2,3},{3,2},{4,5},{5,4},{6,7},{7,6},{8,9},{9,8},{10,11... | collective-permute-start | bytes 3932168 | tf_op jit(solution)/shard_map/ppermute | solution.py:31
  40.9 28.9 %collective-permute-start.18 = (bf16[256,2560]{1,0:T(8,128)(2,1)S(1)}, bf16[256,2560]{1,0:T(8,128)(2,1)S(1)}, u32[]{:S(2)}, u32[]{:S(2)}) collective-permute-start(bf16[256,2560]{1,0:T(8,128)(2,1)S(1)} %get-tuple-element.52), channel_id=1, source_target_pairs={{0,1},{1,0},{2,3},{3,2},{4,5},{5,4},{6,7},{7,6},{8,9},{9,8},{10,11... | collective-permute-start | bytes 3932168 | tf_op jit(solution)/shard_map/ppermute | solution.py:31
  40.9 1.7 %copy-start.3 = (bf16[5120,256]{1,0:T(8,128)(2,1)S(1)}, bf16[5120,256]{1,0:T(8,128)(2,1)}, u32[]{:S(2)}) copy-start(bf16[5120,256]{1,0:T(8,128)(2,1)} %refs_2_.1) | copy-start | bytes 7864324
  46.9 10.1 %collective-permute-start.12 = (bf16[256,512]{1,0:T(8,128)(2,1)S(1)}, bf16[256,512]{1,0:T(8,128)(2,1)S(1)}, u32[]{:S(2)}, u32[]{:S(2)}) collective-permute-start(bf16[256,512]{1,0:T(8,128)(2,1)S(1)} %get-tuple-element.43.refs_1_), channel_id=1, source_target_pairs={{0,16},{16,32},{32,48},{48,0},{64,80},{80,96},{96,112},{112,64},{1... | collective-permute-start | bytes 786440 | tf_op jit(solution)/shard_map/ppermute | solution.py:409
  47.8 9.2 %collective-permute-start.13 = (bf16[256,512]{1,0:T(8,128)(2,1)S(1)}, bf16[256,512]{1,0:T(8,128)(2,1)S(1)}, u32[]{:S(2)}, u32[]{:S(2)}) collective-permute-start(bf16[256,512]{1,0:T(8,128)(2,1)S(1)} %get-tuple-element.43.refs_1_), channel_id=1, source_target_pairs={{0,48},{16,0},{32,16},{48,32},{64,112},{80,64},{96,80},{112,96},{1... | collective-permute-start | bytes 786440 | tf_op jit(solution)/shard_map/ppermute | solution.py:409
  49.6 11.4 %collective-permute-start.14 = (bf16[256,512]{1,0:T(8,128)(2,1)S(1)}, bf16[256,512]{1,0:T(8,128)(2,1)S(1)}, u32[]{:S(2)}, u32[]{:S(2)}) collective-permute-start(bf16[256,512]{1,0:T(8,128)(2,1)S(1)} %get-tuple-element.43.refs_1_), channel_id=1, source_target_pairs={{0,32},{16,48},{32,0},{48,16},{64,96},{80,112},{96,64},{112,80},{1... | collective-permute-start | bytes 786440 | tf_op jit(solution)/shard_map/ppermute | solution.py:409
  50.8 4.4 %collective-permute-start.15 = (bf16[256,256]{1,0:T(8,128)(2,1)S(1)}, bf16[256,256]{1,0:T(8,128)(2,1)S(1)}, u32[]{:S(2)}, u32[]{:S(2)}) collective-permute-start(bf16[256,256]{1,0:T(8,128)(2,1)S(1)} %shard_map.181.refs_0_), channel_id=1, source_target_pairs={{0,64},{16,80},{32,96},{48,112},{64,0},{80,16},{96,32},{112,48},{1... | collective-permute-start | bytes 393224 | tf_op jit(solution)/shard_map/ppermute | solution.py:410
  62.5 4.0 %collective-permute-start.16 = (bf16[272,256]{1,0:T(8,128)(2,1)S(1)}, bf16[272,256]{1,0:T(8,128)(2,1)S(1)}, u32[]{:S(2)}, u32[]{:S(2)}) collective-permute-start(bf16[272,256]{1,0:T(8,128)(2,1)S(1)} %shard_map.185), channel_id=1, source_target_pairs={{0,64},{16,80},{32,96},{48,112},{64,0},{80,16},{96,32},{112,48},{1... | collective-permute-start | bytes 417800 | tf_op jit(solution)/shard_map/ppermute | solution.py:437
  66.5 26.9 %copy-start.14 = (f32[5120]{0:T(1024)S(1)}, f32[5120]{0:T(1024)}, u32[]{:S(2)}) copy-start(f32[5120]{0:T(1024)} %param.19) | copy-start | bytes 61444
  66.5 26.9 %copy-start.15 = (f32[5120]{0:T(1024)S(1)}, f32[5120]{0:T(1024)}, u32[]{:S(2)}) copy-start(f32[5120]{0:T(1024)} %param.26) | copy-start | bytes 61444
  66.5 27.9 %copy-start.4 = (bf16[5120,64]{0,1:T(8,128)(2,1)S(1)}, bf16[5120,64]{0,1:T(8,128)(2,1)}, u32[]{:S(2)}) copy-start(bf16[5120,64]{0,1:T(8,128)(2,1)} %param.27) | copy-start | bytes 1966084
  66.5 27.9 %copy-start.10 = (bf16[8,16,640]{2,1,0:T(8,128)(2,1)S(1)}, bf16[8,16,640]{2,1,0:T(8,128)(2,1)}, u32[]{:S(2)}) copy-start(bf16[8,16,640]{2,1,0:T(8,128)(2,1)} %copy-done.9) | copy-start | bytes 491524
  66.5 27.9 %copy-start.11 = (f32[4,256]{1,0:T(4,128)S(1)}, f32[4,256]{1,0:T(4,128)}, u32[]{:S(2)}) copy-start(f32[4,256]{1,0:T(4,128)} %refs_7_.1) | copy-start | bytes 12292
  66.5 27.9 %copy-start.12 = (f32[4,256]{1,0:T(4,128)S(1)}, f32[4,256]{1,0:T(4,128)}, u32[]{:S(2)}) copy-start(f32[4,256]{1,0:T(4,128)} %refs_8_.1) | copy-start | bytes 12292
  66.5 27.9 %copy-start.13 = (s32[4,1]{0,1:T(1,128)S(1)}, s32[4,1]{0,1:T(1,128)}, u32[]{:S(2)}) copy-start(s32[4,1]{0,1:T(1,128)} %param.30) | copy-start | bytes 52
  67.1 39.5 %copy-start.5 = (bf16[256,1024]{1,0:T(8,128)(2,1)S(1)}, bf16[256,1024]{1,0:T(8,128)(2,1)}, u32[]{:S(2)}) copy-start(bf16[256,1024]{1,0:T(8,128)(2,1)} %refs_1_.7) | copy-start | bytes 1572868
  67.1 3.7 %collective-permute-start.17 = (bf16[256,256]{1,0:T(8,128)(2,1)S(1)}, bf16[256,256]{1,0:T(8,128)(2,1)S(1)}, u32[]{:S(2)}, u32[]{:S(2)}) collective-permute-start(bf16[256,256]{1,0:T(8,128)(2,1)S(1)} %shard_map.186.refs_1_), channel_id=1, source_target_pairs={{0,1},{1,0},{2,3},{3,2},{4,5},{5,4},{6,7},{7,6},{8,9},{9,8},{10,11... | collective-permute-start | bytes 393224 | tf_op jit(solution)/shard_map/ppermute | solution.py:31
  71.6 8.1 %collective-permute-start.22 = (bf16[32,2560]{1,0:T(8,128)(2,1)S(1)}, bf16[32,2560]{1,0:T(8,128)(2,1)S(1)}, u32[]{:S(2)}, u32[]{:S(2)}) collective-permute-start(bf16[32,2560]{1,0:T(8,128)(2,1)S(1)} %get-tuple-element.58), channel_id=1, source_target_pairs={{0,4},{1,5},{2,6},{3,7},{4,8},{5,9},{6,10},{7,11},{8,12},{9,13},{1... | collective-permute-start | bytes 491528 | tf_op jit(solution)/shard_map/ppermute | solution.py:35
  73.3 7.4 %collective-permute-start.23 = (bf16[32,2560]{1,0:T(8,128)(2,1)S(1)}, bf16[32,2560]{1,0:T(8,128)(2,1)S(1)}, u32[]{:S(2)}, u32[]{:S(2)}) collective-permute-start(bf16[32,2560]{1,0:T(8,128)(2,1)S(1)} %get-tuple-element.59), channel_id=1, source_target_pairs={{0,12},{1,13},{2,14},{3,15},{4,0},{5,1},{6,2},{7,3},{8,4},{9,5},{1... | collective-permute-start | bytes 491528 | tf_op jit(solution)/shard_map/ppermute | solution.py:35
  75.5 8.6 %collective-permute-start.24 = (bf16[32,2560]{1,0:T(8,128)(2,1)S(1)}, bf16[32,2560]{1,0:T(8,128)(2,1)S(1)}, u32[]{:S(2)}, u32[]{:S(2)}) collective-permute-start(bf16[32,2560]{1,0:T(8,128)(2,1)S(1)} %get-tuple-element.60), channel_id=1, source_target_pairs={{0,8},{1,9},{2,10},{3,11},{4,12},{5,13},{6,14},{7,15},{8,0},{9,1},... | collective-permute-start | bytes 491528 | tf_op jit(solution)/shard_map/ppermute | solution.py:35
  76.7 10.0 %collective-permute-start.19 = (bf16[32,2560]{1,0:T(8,128)(2,1)S(1)}, bf16[32,2560]{1,0:T(8,128)(2,1)S(1)}, u32[]{:S(2)}, u32[]{:S(2)}) collective-permute-start(bf16[32,2560]{1,0:T(8,128)(2,1)S(1)} %get-tuple-element.54), channel_id=1, source_target_pairs={{0,4},{1,5},{2,6},{3,7},{4,8},{5,9},{6,10},{7,11},{8,12},{9,13},{1... | collective-permute-start | bytes 491528 | tf_op jit(solution)/shard_map/ppermute | solution.py:35
  77.5 9.2 %collective-permute-start.20 = (bf16[32,2560]{1,0:T(8,128)(2,1)S(1)}, bf16[32,2560]{1,0:T(8,128)(2,1)S(1)}, u32[]{:S(2)}, u32[]{:S(2)}) collective-permute-start(bf16[32,2560]{1,0:T(8,128)(2,1)S(1)} %get-tuple-element.55), channel_id=1, source_target_pairs={{0,12},{1,13},{2,14},{3,15},{4,0},{5,1},{6,2},{7,3},{8,4},{9,5},{1... | collective-permute-start | bytes 491528 | tf_op jit(solution)/shard_map/ppermute | solution.py:35
  79.7 11.4 %collective-permute-start.21 = (bf16[32,2560]{1,0:T(8,128)(2,1)S(1)}, bf16[32,2560]{1,0:T(8,128)(2,1)S(1)}, u32[]{:S(2)}, u32[]{:S(2)}) collective-permute-start(bf16[32,2560]{1,0:T(8,128)(2,1)S(1)} %get-tuple-element.56), channel_id=1, source_target_pairs={{0,8},{1,9},{2,10},{3,11},{4,12},{5,13},{6,14},{7,15},{8,0},{9,1},... | collective-permute-start | bytes 491528 | tf_op jit(solution)/shard_map/ppermute | solution.py:35
  84.2 6.9 %collective-permute-start.25 = (bf16[32,2560]{1,0:T(8,128)(2,1)S(1)}, bf16[32,2560]{1,0:T(8,128)(2,1)S(1)}, u32[]{:S(2)}, u32[]{:S(2)}) collective-permute-start(bf16[32,2560]{1,0:T(8,128)(2,1)S(1)} %shard_map.188), channel_id=1, source_target_pairs={{0,2},{1,3},{2,0},{3,1},{4,6},{5,7},{6,4},{7,5},{8,10},{9,11},{10,... | collective-permute-start | bytes 491528 | tf_op jit(solution)/shard_map/ppermute | solution.py:460
  91.3 3.1 %collective-permute-start.26 = (f32[16,2560]{1,0:T(8,128)S(1)}, f32[16,2560]{1,0:T(8,128)S(1)}, u32[]{:S(2)}, u32[]{:S(2)}) collective-permute-start(f32[16,2560]{1,0:T(8,128)S(1)} %get-tuple-element.62), channel_id=1, source_target_pairs={{0,1},{1,0},{2,3},{3,2},{4,5},{5,4},{6,7},{7,6},{8,9},{9,8},{10,11... | collective-permute-start | bytes 491528 | tf_op jit(solution)/shard_map/ppermute | solution.py:31

commit v3 on v2

--- a/solution.py
+++ b/solution.py
@@ -18,17 +18,24 @@
 HB = pl.BlockSpec(memory_space=pltpu.HBM)
 
 CORE_SWAP = [(m, m ^ 1) for m in range(16)]
-Y_SWAP = [(c, c ^ 4) for c in range(8)]
 PAIR_SWAP = [(m, m ^ 2) for m in range(16)]
 STEPS = (1, 3, 2)
 
 
-def x_step(by):
-    return [(c, (c // 4) * 4 + (c + by) % 4) for c in range(8)]
+def y_swap(a):
+    return lax.ppermute(a, "ctx", [(c, c ^ 4) for c in range(8)])
+
+
+def x_send(a, by):
+    return lax.ppermute(a, "ctx", [(c, (c // 4) * 4 + (c + by) % 4) for c in range(8)])
 
 
 def core_swap(a):
     return lax.ppermute(a, "mdl", CORE_SWAP)
+
+
+def pair_swap(a):
+    return lax.ppermute(a, "mdl", PAIR_SWAP)
 
 
 def z_send(a, by):
@@ -77,12 +84,20 @@
         give_ref[j * block : (j + 1) * block] = jnp.where(k == 0, second, first)
 
 
-def join_body(a_ref, b_ref, *out_refs):
+def copy_body(x_ref, out_ref):
+    out_ref[...] = x_ref[...]
+
+
+def join_body(a_ref, b_ref, out_ref, sems):
     width = a_ref.shape[1]
-    for i, out_ref in enumerate(out_refs):
-        some = out_ref.shape[0]
-        out_ref[:, :width] = a_ref[i * some : (i + 1) * some]
-        out_ref[:, width:] = b_ref[i * some : (i + 1) * some]
+    copies = [
+        pltpu.make_async_copy(ref, out_ref.at[:, pl.ds(i * width, width)], sems.at[i])
+        for i, ref in enumerate((a_ref, b_ref))
+    ]
+    for copy in copies:
+        copy.start()
+    for copy in copies:
+        copy.wait()
 
 
 def load_body(*refs):
@@ -187,19 +202,18 @@
         total_ref[h] = jnp.broadcast_to(total, total_ref.shape[1:])
 
 
-def finish(q_ref, refs, o_ref, peak_ref, total_ref, h):
-    start = (peak_ref[h][:, :1], total_ref[h][:, :1], o_ref[:, h * HD : (h + 1) * HD])
-    peak, total, summed = attend(q_ref, refs, start, h)
-    return summed * (1.0 / total), peak / math.sqrt(HD) + jnp.log(total)
-
-
-def sent_body(q_ref, a_ref, b_ref, c_ref, d_ref, o_ref, peak_ref, total_ref, out_ref):
+def log_total(peak, total):
+    return peak / math.sqrt(HD) + jnp.log(total)
+
+
+def sent_body(q_ref, *refs):
+    *kv_refs, out_ref = refs
     rows = q_ref.shape[0]
     both = []
     for h in range(2):
-        o, lse = finish(q_ref, (a_ref, b_ref, c_ref, d_ref), o_ref, peak_ref, total_ref, h)
-        out_ref[:rows, h * HD : (h + 1) * HD] = o.astype(BF)
-        both.append(lse)
+        peak, total, summed = attend(q_ref, kv_refs, None, h)
+        out_ref[:rows, h * HD : (h + 1) * HD] = (summed * (1.0 / total)).astype(BF)
+        both.append(log_total(peak, total))
     lane = lax.broadcasted_iota(jnp.int32, (rows, HD), 1)
     rest = jnp.transpose(jnp.where(lane == 0, both[0], both[1]))[:16]
     at = lax.broadcasted_iota(jnp.int32, (16, rows), 0)
@@ -212,30 +226,37 @@
     out_ref[rows:, :] = tail.astype(BF)
 
 
-def kept_body(q_ref, a_ref, b_ref, c_ref, d_ref, o_ref, peak_ref, total_ref, out_ref, lse_ref):
+def kept_body(q_ref, a_ref, b_ref, o_ref, peak_ref, total_ref, out_ref, lse_ref):
     for h in range(2):
-        o, lse = finish(q_ref, (a_ref, b_ref, c_ref, d_ref), o_ref, peak_ref, total_ref, h)
-        out_ref[:, h * HD : (h + 1) * HD] = o
-        lse_ref[h] = jnp.broadcast_to(lse, lse_ref.shape[1:])
-
-
-def merge_body(own_ref, lse_ref, got_ref, out_ref):
+        cols = slice(h * HD, (h + 1) * HD)
+        start = (peak_ref[h][:, :1], total_ref[h][:, :1], o_ref[:, cols])
+        peak, total, summed = attend(q_ref, (a_ref, b_ref), start, h)
+        out_ref[:, cols] = summed * (1.0 / total)
+        lse_ref[h] = jnp.broadcast_to(log_total(peak, total), lse_ref.shape[1:])
+
+
+def merge_body(own_ref, lse_ref, *refs):
+    *got_refs, out_ref = refs
     rows = own_ref.shape[0]
-    tail = got_ref[rows:, :].astype(F32)
     at = lax.broadcasted_iota(jnp.int32, (HD, rows), 0)
-    row = [
-        tail[3 * h : 3 * h + 1] + tail[3 * h + 1 : 3 * h + 2] + tail[3 * h + 2 : 3 * h + 3]
-        for h in range(2)
-    ]
-    turned = jnp.transpose(jnp.where(at == 0, row[0], row[1]))
+    lanes = jnp.zeros((HD, rows), F32)
+    for g, got_ref in enumerate(got_refs):
+        tail = got_ref[rows:, :].astype(F32)
+        for h in range(2):
+            row = sum(tail[3 * h + i : 3 * h + i + 1] for i in range(3))
+            lanes = jnp.where(at == 2 * g + h, row, lanes)
+    turned = jnp.transpose(lanes)
     for h in range(2):
-        theirs = turned[:, h : h + 1]
-        ours = lse_ref[h][:, :1]
-        top = jnp.maximum(ours, theirs)
-        a, b = jnp.exp(ours - top), jnp.exp(theirs - top)
-        inverse = 1.0 / (a + b)
         cols = slice(h * HD, (h + 1) * HD)
-        merged = (a * inverse) * own_ref[:, cols] + (b * inverse) * got_ref[:rows, cols].astype(F32)
+        lse = [lse_ref[h][:, :1]] + [
+            turned[:, 2 * g + h : 2 * g + h + 1] for g in range(len(got_refs))
+        ]
+        top = functools.reduce(jnp.maximum, lse)
+        part = [jnp.exp(e - top) for e in lse]
+        inverse = 1.0 / sum(part)
+        merged = (part[0] * inverse) * own_ref[:, cols]
+        for p, got_ref in zip(part[1:], got_refs):
+            merged = merged + (p * inverse) * got_ref[:rows, cols].astype(F32)
         out_ref[:, cols] = merged.astype(BF)
 
 
@@ -342,10 +363,11 @@
 
     cached = call(
         join_body,
-        (shape((cache_keys.shape[0], 2 * cache_keys.shape[1]), BF),),
+        shape((cache_keys.shape[0], 2 * cache_keys.shape[1]), BF),
         (cache_keys, cache_values),
-    )[0]
-    far = lax.ppermute(cached, "ctx", x_step(2))
+        hbm=(0, 1),
+        scratch=[pltpu.SemaphoreType.DMA((2,))],
+    )
     keep, give = call(
         turn_body,
         (shape((rows, part), BF), shape((rows, part), BF)),
@@ -357,10 +379,11 @@
     wide = jnp.concatenate(
         [jnp.where(is_first, keep, got), jnp.where(is_first, got, keep)], 1
     )
-    beside = lax.ppermute(wide, "mdl", PAIR_SWAP)
-    x = [wide, beside] + [z_send(a, by) for a in (wide, beside) for by in STEPS]
-
-    near = [lax.ppermute(cached, "ctx", x_step(by)) for by in (1, 3)]
+    beside = pair_swap(wide)
+    mine = [z_send(wide, by) for by in STEPS]
+    x = [wide, beside] + mine + [z_send(beside, by) for by in STEPS]
+
+    cached_in = y_swap(call(copy_body, shape(cached.shape, BF), (cached,), after=(beside,)))
 
     half = w_out.shape[1] // 2
     w_mine, w_give = call(
@@ -372,16 +395,6 @@
     )
     w_theirs = core_swap(w_give)
 
-    normed, own_x = call(
-        norm_body,
-        (shape((rows, chips * 2 * part), BF), shape((chips, block, 2 * part), BF)),
-        (mdl_1, *x, mod_scale.reshape(chips, 2 * part), mod_shift.reshape(chips, 2 * part)),
-        smem=(0,),
-        flops=MIB,
-        nbytes=MIB,
-        after=(far, *near, w_mine),
-    )
-    cols = w_query.shape[1]
     weights = call(
         load_body,
         tuple(shape(w.shape, BF) for w in (w_query, w_key, w_value)),
@@ -389,8 +402,22 @@
         hbm=(0, 1, 2),
         nbytes=8 * MIB,
         scratch=[pltpu.SemaphoreType.DMA((3, 4))],
-        after=(normed,),
-    )
+        limit=42,
+        flops=5000000000,
+        after=tuple(mine),
+    )
+    normed, own_x = call(
+        norm_body,
+        (shape((rows, chips * 2 * part), BF), shape((chips, block, 2 * part), BF)),
+        (
+            mdl_1, *x, mod_scale.reshape(chips, 2 * part), mod_shift.reshape(chips, 2 * part),
+        ),
+        smem=(0,),
+        flops=MIB,
+        nbytes=MIB,
+        after=(cached_in, w_mine, *weights),
+    )
+    cols = w_query.shape[1]
     kv, whole = call(
         kv_body,
         (shape((count, 2 * cols), BF), shape((count, w_query.shape[0]), BF)),
@@ -406,44 +433,40 @@
         flops=2 * count * w_query.shape[0] * cols,
         nbytes=5 * MIB,
     )
-    fresh = [kv] + [lax.ppermute(kv, "ctx", x_step(by)) for by in (1, 3, 2)]
-    query_in = lax.ppermute(query, "ctx", Y_SWAP)
-
-    def past_call(q, after=()):
-        return call(
-            past_body,
-            (
-                shape((count, cols), F32),
-                shape((2, count, HD), F32),
-                shape((2, count, HD), F32),
-            ),
-            (q, cached, far, *near),
-            flops=4 * count * 2048 * 256,
-            nbytes=4 * MIB,
-            trans=count * 4096,
-            after=after,
+    kv_in = y_swap(kv)
+    query_in = [x_send(query, by) for by in STEPS]
+
+    stats = call(
+        past_body,
+        (
+            shape((count, cols), F32),
+            shape((2, count, HD), F32),
+            shape((2, count, HD), F32),
+        ),
+        (query, cached, cached_in),
+        flops=MIB,
+        nbytes=MIB,
+    )
+    back, before = [], stats[0]
+    for by, q in zip(STEPS, query_in):
+        before = call(
+            sent_body,
+            shape((count + 16, cols), BF),
+            (q, cached, cached_in, kv, kv_in),
+            flops=MIB,
+            nbytes=MIB,
+            after=(before,),
         )
-
-    stats_own = past_call(query)
-    stats_in = past_call(query_in, stats_own[:1])
-    sent = call(
-        sent_body,
-        shape((count + 16, cols), BF),
-        (query_in, *fresh, *stats_in),
-        flops=4 * count * 1024 * 256,
-        nbytes=2 * MIB,
-        trans=count * 2048,
-    )
-    back = lax.ppermute(sent, "ctx", Y_SWAP)
+        back.append(x_send(before, -by))
     kept = call(
         kept_body,
         (shape((count, cols), F32), shape((2, count, HD), F32)),
-        (query, *fresh, *stats_own),
-        flops=4 * count * 1024 * 256,
-        nbytes=2 * MIB,
-        trans=count * 2048,
-    )
-    attended = call(merge_body, shape((count, cols), BF), (*kept, back), nbytes=MIB)
+        (query, kv, kv_in, *stats),
+        flops=MIB,
+        nbytes=MIB,
+        after=(before,),
+    )
+    attended = call(merge_body, shape((count, cols), BF), (*kept, *back), nbytes=MIB)
 
     projected = call(
         out_body,
@@ -454,16 +477,18 @@
         nbytes=4 * MIB,
         scratch=[pltpu.VMEM((count, 2 * cols), BF)],
     )
-    here, passing = projected[0], projected[1]
-    relayed = [z_send(a, by) for a, by in zip(projected[5:], STEPS)]
-    direct = [z_send(a, by) for a, by in zip(projected[2:5], STEPS)]
-    passed = lax.ppermute(
-        call(add_body, shape(passing.shape, BF), (passing, *relayed)), "mdl", PAIR_SWAP
-    )
+    def added(*parts):
+        return call(add_body, shape(parts[0].shape, BF), parts)
+
+    across = pair_swap(projected[7])
+    relayed = [z_send(projected[5], 1), z_send(projected[6], 3)]
+    direct = [z_send(projected[2], 1), z_send(projected[3], 3)]
+    direct.append(z_send(added(projected[4], across), 2))
+    passed = pair_swap(added(projected[1], *relayed))
     ours, theirs = call(
         sum_body,
         (shape((block, half), F32), shape((block, half), F32)),
-        (core_1, here, *direct, passed),
+        (core_1, projected[0], *direct, passed),
         smem=(0,),
         nbytes=2 * MIB,
     )

time: 108 us -> 95.6 us (0.89)
  waiting for transfers between devices: 34.9 us -> 18.3 us
  starting transfers between devices: 35.3 us -> 40.1 us
  local copies, waits for them, and re-layouts: 8.5 us -> 4.66 us
  Pallas kernels: 17.3 us -> 19.3 us
  blocking collectives: 10.4 us -> 11.8 us
    ppermute x12 -> x11, waiting for transfers between devices: 20.4 us -> 5.38 us  [z_send(): return lax.ppermute(a, 'mdl', [(m, (m + 4 * by) % 16) for m in range(16)])]
    ppermute x10 -> x11, starting transfers between devices: 11.2 us -> 16.5 us  [the longest x6 9.38 us: x_send(): lax.ppermute(a, 'ctx', [(c, c // 4 * 4 + (c + by) % 4) for c in range(8)])]
    ppermute x10 -> x11, waiting for transfers between devices: 11.6 us -> 7.42 us  [the longest x6 4.3 us: x_send(): lax.ppermute(a, 'ctx', [(c, c // 4 * 4 + (c + by) % 4) for c in range(8)])]
    ppermute x5, waiting for transfers between devices: 2.93 us -> 5.49 us  [core_swap(): return lax.ppermute(a, 'mdl', CORE_SWAP)]
    unnamed x32 -> x28, local copies, waits for them, and re-layouts: 7 us -> 4.61 us
    ppermute x12 -> x11, starting transfers between devices: 17.4 us -> 15.1 us  [z_send(): return lax.ppermute(a, 'mdl', [(m, (m + 4 * by) % 16) for m in range(16)])]
    pallas_call x17 -> x20, Pallas kernels: 17.3 us -> 19.3 us  [call(): pl.pallas_call(run, out_shape=outs, in_specs=place + [pl.BlockSpec(memory...]
    ppermute x5, starting transfers between devices: 6.7 us -> 8.48 us  [core_swap(): return lax.ppermute(a, 'mdl', CORE_SWAP)]
  transfers between devices with their start and end apart: 27 -> 27, of which waited for: 15 -> 13; matrix products, arithmetic and copies ran while one was open for 1% -> 0% of each run, Pallas kernels for 12% -> 15%
where the time goes in v3:
time: 95.6 us; the launch traced here: 95.3 us
  starting transfers between devices  40.1 us (42%)
  Pallas kernels  19.3 us (20%)
  waiting for transfers between devices  18.3 us (19%)
  blocking collectives  11.8 us (12%)
  local copies, waits for them, and re-layouts  4.66 us (5%)
  between operations  0.98 us (1%)
    pallas_call x20, Pallas kernels, call(): pl.pallas_call(run, out_shape=outs, in_specs=place + [pl.BlockSpec(memory...  19.3 us
    ppermute x11, starting transfers between devices, z_send(): return lax.ppermute(a, 'mdl', [(m, (m + 4 * by) % 16) for m in range(16)])  15.1 us
    all_to_all x1, blocking collectives, shards(): lax.all_to_all(slot_rows.reshape(16, CAP, state.shape[1]), 'mdl', split_a...  11.8 us
    ppermute x6, starting transfers between devices, x_send(): lax.ppermute(a, 'ctx', [(c, c // 4 * 4 + (c + by) % 4) for c in range(8)])  9.38 us
    ppermute x5, starting transfers between devices, core_swap(): return lax.ppermute(a, 'mdl', CORE_SWAP)  8.48 us
    ppermute x3, starting transfers between devices, pair_swap(): return lax.ppermute(a, 'mdl', PAIR_SWAP)  6.13 us
    ppermute x5, waiting for transfers between devices, core_swap(): return lax.ppermute(a, 'mdl', CORE_SWAP)  5.49 us
    ppermute x11, waiting for transfers between devices, z_send(): return lax.ppermute(a, 'mdl', [(m, (m + 4 * by) % 16) for m in range(16)])  5.38 us
  transfers between devices with their start and end apart: 27, of which 13 were waited for; matrix products, arithmetic and copies ran while one was open for 0% of the time, Pallas kernels for 15%

profile of v3, /device:TPU:1, one launch (start us, length us, event | category | flops | bytes accessed | tf_op | source)
XLA Modules:
  0.0 95.3 jit_solution(10723120813901729306)
XLA Ops:
  0.7 0.9 copy-done.5
  1.6 0.1 shard_map.175
  1.7 1.5 %collective-permute-start = (bf16[128,320]{1,0:T(8,128)(2,1)S(1)}, bf16[128,320]{1,0:T(8,128)(2,1)S(1)}, u32[]{:S(2)}, u32[]{:S(2)}) collective-permute-start(bf16[128,320]{1,0:T(8,128)(2,1)S(1)} %get-tuple-element.33), channel_id=1, source_target_pairs={{0,1},{1,0},{2,3},{3,2},{4,5},{5,4},{6,7},{7,6},{8,9},{9,8},{10,11... | collective-permute-start | bytes 245768 | tf_op jit(solution)/shard_map/ppermute | solution.py:34
  3.2 0.9 collective-permute-done
  4.2 0.1 pad_maximum_fusion.refs_1_
  4.3 3.1 %collective-permute-start.1 = (bf16[128,640]{1,0:T(8,128)(2,1)S(1)}, bf16[128,640]{1,0:T(8,128)(2,1)S(1)}, u32[]{:S(2)}, u32[]{:S(2)}) collective-permute-start(bf16[128,640]{1,0:T(8,128)(2,1)S(1)} %pad_maximum_fusion.refs_1_), channel_id=1, source_target_pairs={{0,2},{1,3},{2,0},{3,1},{4,6},{5,7},{6,4},{7,5},{8,10},{9,11},{10,... | collective-permute-start | bytes 491528 | tf_op jit(solution)/shard_map/ppermute | solution.py:38
  7.3 1.6 %collective-permute-start.2 = (bf16[128,640]{1,0:T(8,128)(2,1)S(1)}, bf16[128,640]{1,0:T(8,128)(2,1)S(1)}, u32[]{:S(2)}, u32[]{:S(2)}) collective-permute-start(bf16[128,640]{1,0:T(8,128)(2,1)S(1)} %pad_maximum_fusion.refs_1_), channel_id=1, source_target_pairs={{0,4},{1,5},{2,6},{3,7},{4,8},{5,9},{6,10},{7,11},{8,12},{9,13},{1... | collective-permute-start | bytes 491528 | tf_op jit(solution)/shard_map/ppermute | solution.py:42
  9.0 2.1 %collective-permute-start.3 = (bf16[128,640]{1,0:T(8,128)(2,1)S(1)}, bf16[128,640]{1,0:T(8,128)(2,1)S(1)}, u32[]{:S(2)}, u32[]{:S(2)}) collective-permute-start(bf16[128,640]{1,0:T(8,128)(2,1)S(1)} %pad_maximum_fusion.refs_1_), channel_id=1, source_target_pairs={{0,12},{1,13},{2,14},{3,15},{4,0},{5,1},{6,2},{7,3},{8,4},{9,5},{1... | collective-permute-start | bytes 491528 | tf_op jit(solution)/shard_map/ppermute | solution.py:42
  11.1 1.3 %collective-permute-start.4 = (bf16[128,640]{1,0:T(8,128)(2,1)S(1)}, bf16[128,640]{1,0:T(8,128)(2,1)S(1)}, u32[]{:S(2)}, u32[]{:S(2)}) collective-permute-start(bf16[128,640]{1,0:T(8,128)(2,1)S(1)} %pad_maximum_fusion.refs_1_), channel_id=1, source_target_pairs={{0,8},{1,9},{2,10},{3,11},{4,12},{5,13},{6,14},{7,15},{8,0},{9,1},... | collective-permute-start | bytes 491528 | tf_op jit(solution)/shard_map/ppermute | solution.py:42
  12.4 0.9 copy-done.3
  13.4 0.9 copy-done.4
  14.3 0.1 shard_map.176.refs_0_.refs_1_
  14.4 0.5 collective-permute-start.8
  14.9 0.0 copy-start
  15.0 0.8 collective-permute-start.5
  15.8 1.9 %collective-permute-start.6 = (bf16[128,640]{1,0:T(8,128)(2,1)S(1)}, bf16[128,640]{1,0:T(8,128)(2,1)S(1)}, u32[]{:S(2)}, u32[]{:S(2)}) collective-permute-start(bf16[128,640]{1,0:T(8,128)(2,1)S(1)} %collective-permute-done.1.refs_1_.refs_2_), channel_id=1, source_target_pairs={{0,12},{1,13},{2,14},{3,15},{4,0},{5,1},{6,2},{7,3},{8,4},{9,5},{1... | collective-permute-start | bytes 491528 | tf_op jit(solution)/shard_map/ppermute | solution.py:42
  17.7 0.5 collective-permute-start.7
  18.2 1.3 %collective-permute-done.4.refs_5_ = bf16[128,640]{1,0:T(8,128)(2,1)S(1)} collective-permute-done((bf16[128,640]{1,0:T(8,128)(2,1)S(1)}, bf16[128,640]{1,0:T(8,128)(2,1)S(1)}, u32[]{:S(2)}, u32[]{:S(2)}) %collective-permute-start.4) | collective-permute-done | bytes 163872 | tf_op jit(solution)/shard_map/ppermute | solution.py:42
  19.4 1.7 %copy-done.9 = bf16[5120,256]{1,0:T(8,128)(2,1)S(1)} copy-done((bf16[5120,256]{1,0:T(8,128)(2,1)S(1)}, bf16[5120,256]{1,0:T(8,128)(2,1)}, u32[]{:S(2)}) %copy-start.9) | copy-done | bytes 2621464
  21.2 3.4 %shard_map.179 = (bf16[5120,256]{1,0:T(8,128)(2,1)S(1)}, bf16[5120,256]{1,0:T(8,128)(2,1)S(1)}, bf16[5120,256]{1,0:T(8,128)(2,1)S(1)}) custom-call(bf16[5120,256]{1,0:T(8,128)(2,1)S(1)} %copy-done.9, bf16[5120,256]{1,0:T(8,128)(2,1)} %refs_1_.6, bf16[5120,256]{1,0:T(8,128)(2,1)} %refs_2_.1, bf16[128,640]{1,0:T(8,128)(2,1)S(1)} %collective-permute-done.2.refs_3_, ...), custom_call_target="tpu_custom_call" | custom-call | flops 5000000000 | bytes 8388608 | tf_op jit(solution)/shard_map/pallas_call | solution.py:60
  24.6 0.2 shard_map.178
  24.8 1.7 %collective-permute-done.7.refs_8_ = bf16[128,640]{1,0:T(8,128)(2,1)S(1)} collective-permute-done((bf16[128,640]{1,0:T(8,128)(2,1)S(1)}, bf16[128,640]{1,0:T(8,128)(2,1)S(1)}, u32[]{:S(2)}, u32[]{:S(2)}) %collective-permute-start.7) | collective-permute-done | bytes 163872 | tf_op jit(solution)/shard_map/ppermute | solution.py:42
  26.5 1.3 %shard_map.180 = (bf16[128,5120]{1,0:T(8,128)(2,1)S(1)}, bf16[8,16,640]{2,1,0:T(8,128)(2,1)S(1)}) custom-call(s32[1]{0:T(128)} %bitcast.1.refs_0_, bf16[128,640]{1,0:T(8,128)(2,1)S(1)} %pad_maximum_fusion.refs_1_, bf16[128,640]{1,0:T(8,128)(2,1)S(1)} %collective-permute-done.1.refs_1_.refs_2_, bf16[128,640]{1,0:T(8,128)(2,1)S(1)} %collective-permute-done.2.refs_3_, ...), custom_call_target="tpu_custom_call" | custom-call | flops 1048576 | bytes 1048576 | tf_op jit(solution)/shard_map/pallas_call | solution.py:60
  27.8 2.5 %collective-permute-start.9 = (bf16[128,5120]{1,0:T(8,128)(2,1)S(1)}, bf16[128,5120]{1,0:T(8,128)(2,1)S(1)}, u32[]{:S(2)}, u32[]{:S(2)}) collective-permute-start(bf16[128,5120]{1,0:T(8,128)(2,1)S(1)} %get-tuple-element.38.refs_1_), channel_id=1, source_target_pairs={{0,1},{1,0},{2,3},{3,2},{4,5},{5,4},{6,7},{7,6},{8,9},{9,8},{10,11... | collective-permute-start | bytes 3932168 | tf_op jit(solution)/shard_map/ppermute | solution.py:34
  30.2 0.1 collective-permute-start.18
  30.3 2.6 %collective-permute-done.9.refs_2_ = bf16[128,5120]{1,0:T(8,128)(2,1)S(1)} collective-permute-done((bf16[128,5120]{1,0:T(8,128)(2,1)S(1)}, bf16[128,5120]{1,0:T(8,128)(2,1)S(1)}, u32[]{:S(2)}, u32[]{:S(2)}) %collective-permute-start.9) | collective-permute-done | bytes 1310752 | tf_op jit(solution)/shard_map/ppermute | solution.py:34
  32.9 1.7 %shard_map.181 = (bf16[256,512]{1,0:T(8,128)(2,1)S(1)}, bf16[256,5120]{1,0:T(8,128)(2,1)S(1)}) custom-call(s32[1]{0:T(128)} %bitcast.refs_0_, bf16[128,5120]{1,0:T(8,128)(2,1)S(1)} %get-tuple-element.38.refs_1_, bf16[128,5120]{1,0:T(8,128)(2,1)S(1)} %collective-permute-done.9.refs_2_, bf16[5120,256]{1,0:T(8,128)(2,1)S(1)} %get-tuple-element.36.refs_14_.refs_3_, ...), custom_call_target="tpu_custom_call" | custom-call | flops 1342177280 | bytes 8388608 | tf_op jit(solution)/shard_map/pallas_call | solution.py:60
  34.6 0.5 collective-permute-start.10
  35.1 0.8 shard_map.182.refs_0_
  35.9 1.3 %collective-permute-start.13 = (bf16[256,256]{1,0:T(8,128)(2,1)S(1)}, bf16[256,256]{1,0:T(8,128)(2,1)S(1)}, u32[]{:S(2)}, u32[]{:S(2)}) collective-permute-start(bf16[256,256]{1,0:T(8,128)(2,1)S(1)} %shard_map.182.refs_0_), channel_id=1, source_target_pairs={{0,16},{16,32},{32,48},{48,0},{64,80},{80,96},{96,112},{112,64},{1... | collective-permute-start | bytes 393224 | tf_op jit(solution)/shard_map/ppermute | solution.py:30
  37.2 1.5 %collective-permute-start.12 = (bf16[256,256]{1,0:T(8,128)(2,1)S(1)}, bf16[256,256]{1,0:T(8,128)(2,1)S(1)}, u32[]{:S(2)}, u32[]{:S(2)}) collective-permute-start(bf16[256,256]{1,0:T(8,128)(2,1)S(1)} %shard_map.182.refs_0_), channel_id=1, source_target_pairs={{0,48},{16,0},{32,16},{48,32},{64,112},{80,64},{96,80},{112,96},{1... | collective-permute-start | bytes 393224 | tf_op jit(solution)/shard_map/ppermute | solution.py:30
  38.6 1.5 %collective-permute-start.11 = (bf16[256,256]{1,0:T(8,128)(2,1)S(1)}, bf16[256,256]{1,0:T(8,128)(2,1)S(1)}, u32[]{:S(2)}, u32[]{:S(2)}) collective-permute-start(bf16[256,256]{1,0:T(8,128)(2,1)S(1)} %shard_map.182.refs_0_), channel_id=1, source_target_pairs={{0,32},{16,48},{32,0},{48,16},{64,96},{80,112},{96,64},{112,80},{1... | collective-permute-start | bytes 393224 | tf_op jit(solution)/shard_map/ppermute | solution.py:30
  40.2 1.1 %shard_map.183 = (f32[256,256]{1,0:T(8,128)S(1)}, f32[2,256,128]{2,1,0:T(8,128)S(1)}, f32[2,256,128]{2,1,0:T(8,128)S(1)}) custom-call(bf16[256,256]{1,0:T(8,128)(2,1)S(1)} %shard_map.182.refs_0_, bf16[512,512]{1,0:T(8,128)(2,1)S(1)} %shard_map.176.refs_0_.refs_1_, bf16[512,512]{1,0:T(8,128)(2,1)S(1)} %collective-permute-done.8.refs_11_.refs_2_), custom_call_target="tpu_custom_call" | custom-call | flops 1048576 | bytes 1048576 | tf_op jit(solution)/shard_map/pallas_call | solution.py:60
  41.3 0.3 collective-permute-done.13.refs_0_
  41.6 0.6 collective-permute-done.10.refs_4_.refs_2_
  42.2 1.5 %shard_map.184.refs_5_ = bf16[272,256]{1,0:T(8,128)(2,1)S(1)} custom-call(bf16[256,256]{1,0:T(8,128)(2,1)S(1)} %collective-permute-done.13.refs_0_, bf16[512,512]{1,0:T(8,128)(2,1)S(1)} %shard_map.176.refs_0_.refs_1_, bf16[512,512]{1,0:T(8,128)(2,1)S(1)} %collective-permute-done.8.refs_11_.refs_2_, bf16[256,512]{1,0:T(8,128)(2,1)S(1)} %get-tuple-element.40.refs_3_.refs_1_, ...), custom_call_target="tpu_custom_call" | custom-call | flops 1048576 | bytes 1048576 | tf_op jit(solution)/shard_map/pallas_call | solution.py:60
  43.7 1.5 %shard_map.185.refs_5_ = bf16[272,256]{1,0:T(8,128)(2,1)S(1)} custom-call(bf16[256,256]{1,0:T(8,128)(2,1)S(1)} %collective-permute-done.12.refs_0_, bf16[512,512]{1,0:T(8,128)(2,1)S(1)} %shard_map.176.refs_0_.refs_1_, bf16[512,512]{1,0:T(8,128)(2,1)S(1)} %collective-permute-done.8.refs_11_.refs_2_, bf16[256,512]{1,0:T(8,128)(2,1)S(1)} %get-tuple-element.40.refs_3_.refs_1_, ...), custom_call_target="tpu_custom_call" | custom-call | flops 1048576 | bytes 1048576 | tf_op jit(solution)/shard_map/pallas_call | solution.py:60
  45.2 0.4 collective-permute-done.11.refs_0_
  45.6 1.5 %shard_map.186.refs_6_ = bf16[272,256]{1,0:T(8,128)(2,1)S(1)} custom-call(bf16[256,256]{1,0:T(8,128)(2,1)S(1)} %collective-permute-done.11.refs_0_, bf16[512,512]{1,0:T(8,128)(2,1)S(1)} %shard_map.176.refs_0_.refs_1_, bf16[512,512]{1,0:T(8,128)(2,1)S(1)} %collective-permute-done.8.refs_11_.refs_2_, bf16[256,512]{1,0:T(8,128)(2,1)S(1)} %get-tuple-element.40.refs_3_.refs_1_, ...), custom_call_target="tpu_custom_call" | custom-call | flops 1048576 | bytes 1048576 | tf_op jit(solution)/shard_map/pallas_call | solution.py:60
  47.1 2.4 %collective-permute-start.16 = (bf16[272,256]{1,0:T(8,128)(2,1)S(1)}, bf16[272,256]{1,0:T(8,128)(2,1)S(1)}, u32[]{:S(2)}, u32[]{:S(2)}) collective-permute-start(bf16[272,256]{1,0:T(8,128)(2,1)S(1)} %shard_map.186.refs_6_), channel_id=1, source_target_pairs={{0,32},{16,48},{32,0},{48,16},{64,96},{80,112},{96,64},{112,80},{1... | collective-permute-start | bytes 417800 | tf_op jit(solution)/shard_map/ppermute | solution.py:30
  49.5 0.3 collective-permute-start.15
  49.8 2.4 %collective-permute-start.14 = (bf16[272,256]{1,0:T(8,128)(2,1)S(1)}, bf16[272,256]{1,0:T(8,128)(2,1)S(1)}, u32[]{:S(2)}, u32[]{:S(2)}) collective-permute-start(bf16[272,256]{1,0:T(8,128)(2,1)S(1)} %shard_map.184.refs_5_), channel_id=1, source_target_pairs={{0,48},{16,0},{32,16},{48,32},{64,112},{80,64},{96,80},{112,96},{1... | collective-permute-start | bytes 417800 | tf_op jit(solution)/shard_map/ppermute | solution.py:30
  52.2 0.9 shard_map.187
  53.1 3.6 %collective-permute-done.15.refs_3_ = bf16[272,256]{1,0:T(8,128)(2,1)S(1)} collective-permute-done((bf16[272,256]{1,0:T(8,128)(2,1)S(1)}, bf16[272,256]{1,0:T(8,128)(2,1)S(1)}, u32[]{:S(2)}, u32[]{:S(2)}) %collective-permute-start.15) | collective-permute-done | bytes 139296 | tf_op jit(solution)/shard_map/ppermute | solution.py:30
  56.7 1.6 %shard_map.188.refs_1_ = bf16[256,256]{1,0:T(8,128)(2,1)S(1)} custom-call(f32[256,256]{1,0:T(8,128)S(1)} %get-tuple-element.44.refs_0_, f32[2,256,128]{2,1,0:T(8,128)S(1)} %get-tuple-element.45.refs_1_, bf16[272,256]{1,0:T(8,128)(2,1)S(1)} %collective-permute-done.14.refs_2_, bf16[272,256]{1,0:T(8,128)(2,1)S(1)} %collective-permute-done.15.refs_3_, ...), custom_call_target="tpu_custom_call" | custom-call | bytes 1048576 | tf_op jit(solution)/shard_map/pallas_call | solution.py:60
  58.4 1.5 %collective-permute-start.17 = (bf16[256,256]{1,0:T(8,128)(2,1)S(1)}, bf16[256,256]{1,0:T(8,128)(2,1)S(1)}, u32[]{:S(2)}, u32[]{:S(2)}) collective-permute-start(bf16[256,256]{1,0:T(8,128)(2,1)S(1)} %shard_map.188.refs_1_), channel_id=1, source_target_pairs={{0,1},{1,0},{2,3},{3,2},{4,5},{5,4},{6,7},{7,6},{8,9},{9,8},{10,11... | collective-permute-start | bytes 393224 | tf_op jit(solution)/shard_map/ppermute | solution.py:34
  60.0 1.0 %collective-permute-done.17.refs_2_ = bf16[256,256]{1,0:T(8,128)(2,1)S(1)} collective-permute-done((bf16[256,256]{1,0:T(8,128)(2,1)S(1)}, bf16[256,256]{1,0:T(8,128)(2,1)S(1)}, u32[]{:S(2)}, u32[]{:S(2)}) %collective-permute-start.17) | collective-permute-done | bytes 131104 | tf_op jit(solution)/shard_map/ppermute | solution.py:34
  61.0 0.8 shard_map.189
  61.8 0.8 collective-permute-start.23
  62.6 1.9 %collective-permute-start.24 = (bf16[32,2560]{1,0:T(8,128)(2,1)S(1)}, bf16[32,2560]{1,0:T(8,128)(2,1)S(1)}, u32[]{:S(2)}, u32[]{:S(2)}) collective-permute-start(bf16[32,2560]{1,0:T(8,128)(2,1)S(1)} %get-tuple-element.54), channel_id=1, source_target_pairs={{0,12},{1,13},{2,14},{3,15},{4,0},{5,1},{6,2},{7,3},{8,4},{9,5},{1... | collective-permute-start | bytes 491528 | tf_op jit(solution)/shard_map/ppermute | solution.py:42
  64.5 1.3 %collective-permute-start.21 = (bf16[32,2560]{1,0:T(8,128)(2,1)S(1)}, bf16[32,2560]{1,0:T(8,128)(2,1)S(1)}, u32[]{:S(2)}, u32[]{:S(2)}) collective-permute-start(bf16[32,2560]{1,0:T(8,128)(2,1)S(1)} %get-tuple-element.51), channel_id=1, source_target_pairs={{0,2},{1,3},{2,0},{3,1},{4,6},{5,7},{6,4},{7,5},{8,10},{9,11},{10,... | collective-permute-start | bytes 491528 | tf_op jit(solution)/shard_map/ppermute | solution.py:38
  65.9 2.7 %collective-permute-start.20 = (bf16[32,2560]{1,0:T(8,128)(2,1)S(1)}, bf16[32,2560]{1,0:T(8,128)(2,1)S(1)}, u32[]{:S(2)}, u32[]{:S(2)}) collective-permute-start(bf16[32,2560]{1,0:T(8,128)(2,1)S(1)} %get-tuple-element.49), channel_id=1, source_target_pairs={{0,12},{1,13},{2,14},{3,15},{4,0},{5,1},{6,2},{7,3},{8,4},{9,5},{1... | collective-permute-start | bytes 491528 | tf_op jit(solution)/shard_map/ppermute | solution.py:42
  68.5 0.1 shard_map.191
  68.6 1.7 %collective-permute-start.25 = (bf16[32,2560]{1,0:T(8,128)(2,1)S(1)}, bf16[32,2560]{1,0:T(8,128)(2,1)S(1)}, u32[]{:S(2)}, u32[]{:S(2)}) collective-permute-start(bf16[32,2560]{1,0:T(8,128)(2,1)S(1)} %shard_map.191), channel_id=1, source_target_pairs={{0,2},{1,3},{2,0},{3,1},{4,6},{5,7},{6,4},{7,5},{8,10},{9,11},{10,... | collective-permute-start | bytes 491528 | tf_op jit(solution)/shard_map/ppermute | solution.py:38
  70.3 0.5 collective-permute-done.21.refs_1_
  70.9 1.5 %collective-permute-start.22 = (bf16[32,2560]{1,0:T(8,128)(2,1)S(1)}, bf16[32,2560]{1,0:T(8,128)(2,1)S(1)}, u32[]{:S(2)}, u32[]{:S(2)}) collective-permute-start(bf16[32,2560]{1,0:T(8,128)(2,1)S(1)} %shard_map.190), channel_id=1, source_target_pairs={{0,8},{1,9},{2,10},{3,11},{4,12},{5,13},{6,14},{7,15},{8,0},{9,1},... | collective-permute-start | bytes 491528 | tf_op jit(solution)/shard_map/ppermute | solution.py:42
  72.4 2.0 %collective-permute-done.25.refs_5_ = bf16[32,2560]{1,0:T(8,128)(2,1)S(1)} collective-permute-done((bf16[32,2560]{1,0:T(8,128)(2,1)S(1)}, bf16[32,2560]{1,0:T(8,128)(2,1)S(1)}, u32[]{:S(2)}, u32[]{:S(2)}) %collective-permute-start.25) | collective-permute-done | bytes 163872 | tf_op jit(solution)/shard_map/ppermute | solution.py:38
  74.4 2.4 %collective-permute-done.22.refs_4_ = bf16[32,2560]{1,0:T(8,128)(2,1)S(1)} collective-permute-done((bf16[32,2560]{1,0:T(8,128)(2,1)S(1)}, bf16[32,2560]{1,0:T(8,128)(2,1)S(1)}, u32[]{:S(2)}, u32[]{:S(2)}) %collective-permute-start.22) | collective-permute-done | bytes 163872 | tf_op jit(solution)/shard_map/ppermute | solution.py:42
  76.8 0.1 shard_map.192
  76.9 2.9 %collective-permute-start.26 = (f32[16,2560]{1,0:T(8,128)S(1)}, f32[16,2560]{1,0:T(8,128)S(1)}, u32[]{:S(2)}, u32[]{:S(2)}) collective-permute-start(f32[16,2560]{1,0:T(8,128)S(1)} %get-tuple-element.56), channel_id=1, source_target_pairs={{0,1},{1,0},{2,3},{3,2},{4,5},{5,4},{6,7},{7,6},{8,9},{9,8},{10,11... | collective-permute-start | bytes 491528 | tf_op jit(solution)/shard_map/ppermute | solution.py:34
  79.8 1.0 %collective-permute-done.26.refs_2_ = f32[16,2560]{1,0:T(8,128)S(1)} collective-permute-done((f32[16,2560]{1,0:T(8,128)S(1)}, f32[16,2560]{1,0:T(8,128)S(1)}, u32[]{:S(2)}, u32[]{:S(2)}) %collective-permute-start.26) | collective-permute-done | bytes 163872 | tf_op jit(solution)/shard_map/ppermute | solution.py:34
  80.9 1.7 %shard_map.193 = (bf16[16,5120]{1,0:T(8,128)(2,1)}, f32[4,256]{1,0:T(4,128)}, bf16[32,256]{1,0:T(8,128)(2,1)S(1)}) custom-call(s32[1]{0:T(128)} %bitcast.refs_0_, f32[16,2560]{1,0:T(8,128)S(1)} %get-tuple-element.55.refs_1_, f32[16,2560]{1,0:T(8,128)S(1)} %collective-permute-done.26.refs_2_, bf16[8,16,640]{2,1,0:T(8,128)(2,1)S(1)} %get-tuple-element.57.refs_3_, ...), custom_call_target="tpu_custom_call" | custom-call | bytes 2097152 | tf_op jit(solution)/shard_map/pallas_call | solution.py:60
  82.6 11.8 %all_to_all.5 = bf16[16,2,256]{2,1,0:T(2,128)(2,1)S(1)} all-to-all(bf16[16,2,256]{2,1,0:T(2,128)(2,1)S(1)} %reshape.36), channel_id=1, replica_groups=mesh['ctx'=8,'mdl'=16] {'mdl'}, dimensions={0} | all-to-all | bytes 32768 | tf_op jit(solution)/shard_map/all_to_all | solution.py:510
  94.5 0.9 shard_map.194
  (47 shorter events, 0.3 us)
Async XLA Ops:
  0.6 14.3 %copy-start.10 = (f32[5120]{0:T(1024)S(1)}, f32[5120]{0:T(1024)}, u32[]{:S(2)}) copy-start(f32[5120]{0:T(1024)} %param.18) | copy-start | bytes 61444
  0.7 0.9 copy-start.5
  1.6 13.3 %copy-start.11 = (f32[5120]{0:T(1024)S(1)}, f32[5120]{0:T(1024)}, u32[]{:S(2)}) copy-start(f32[5120]{0:T(1024)} %param.17) | copy-start | bytes 61444
  1.7 2.4 %collective-permute-start = (bf16[128,320]{1,0:T(8,128)(2,1)S(1)}, bf16[128,320]{1,0:T(8,128)(2,1)S(1)}, u32[]{:S(2)}, u32[]{:S(2)}) collective-permute-start(bf16[128,320]{1,0:T(8,128)(2,1)S(1)} %get-tuple-element.33), channel_id=1, source_target_pairs={{0,1},{1,0},{2,3},{3,2},{4,5},{5,4},{6,7},{7,6},{8,9},{9,8},{10,11... | collective-permute-start | bytes 245768 | tf_op jit(solution)/shard_map/ppermute | solution.py:34
  4.3 10.1 %collective-permute-start.1 = (bf16[128,640]{1,0:T(8,128)(2,1)S(1)}, bf16[128,640]{1,0:T(8,128)(2,1)S(1)}, u32[]{:S(2)}, u32[]{:S(2)}) collective-permute-start(bf16[128,640]{1,0:T(8,128)(2,1)S(1)} %pad_maximum_fusion.refs_1_), channel_id=1, source_target_pairs={{0,2},{1,3},{2,0},{3,1},{4,6},{5,7},{6,4},{7,5},{8,10},{9,11},{10,... | collective-permute-start | bytes 491528 | tf_op jit(solution)/shard_map/ppermute | solution.py:38
  7.3 8.4 %collective-permute-start.2 = (bf16[128,640]{1,0:T(8,128)(2,1)S(1)}, bf16[128,640]{1,0:T(8,128)(2,1)S(1)}, u32[]{:S(2)}, u32[]{:S(2)}) collective-permute-start(bf16[128,640]{1,0:T(8,128)(2,1)S(1)} %pad_maximum_fusion.refs_1_), channel_id=1, source_target_pairs={{0,4},{1,5},{2,6},{3,7},{4,8},{5,9},{6,10},{7,11},{8,12},{9,13},{1... | collective-permute-start | bytes 491528 | tf_op jit(solution)/shard_map/ppermute | solution.py:42
  9.0 8.7 %collective-permute-start.3 = (bf16[128,640]{1,0:T(8,128)(2,1)S(1)}, bf16[128,640]{1,0:T(8,128)(2,1)S(1)}, u32[]{:S(2)}, u32[]{:S(2)}) collective-permute-start(bf16[128,640]{1,0:T(8,128)(2,1)S(1)} %pad_maximum_fusion.refs_1_), channel_id=1, source_target_pairs={{0,12},{1,13},{2,14},{3,15},{4,0},{5,1},{6,2},{7,3},{8,4},{9,5},{1... | collective-permute-start | bytes 491528 | tf_op jit(solution)/shard_map/ppermute | solution.py:42
  11.1 8.3 %collective-permute-start.4 = (bf16[128,640]{1,0:T(8,128)(2,1)S(1)}, bf16[128,640]{1,0:T(8,128)(2,1)S(1)}, u32[]{:S(2)}, u32[]{:S(2)}) collective-permute-start(bf16[128,640]{1,0:T(8,128)(2,1)S(1)} %pad_maximum_fusion.refs_1_), channel_id=1, source_target_pairs={{0,8},{1,9},{2,10},{3,11},{4,12},{5,13},{6,14},{7,15},{8,0},{9,1},... | collective-permute-start | bytes 491528 | tf_op jit(solution)/shard_map/ppermute | solution.py:42
  12.4 0.9 copy-start.3
  13.4 0.9 copy-start.4
  14.4 12.0 %collective-permute-start.8 = (bf16[512,512]{1,0:T(8,128)(2,1)S(1)}, bf16[512,512]{1,0:T(8,128)(2,1)S(1)}, u32[]{:S(2)}, u32[]{:S(2)}) collective-permute-start(bf16[512,512]{1,0:T(8,128)(2,1)S(1)} %shard_map.177), channel_id=1, source_target_pairs={{0,64},{16,80},{32,96},{48,112},{64,0},{80,16},{96,32},{112,48},{1... | collective-permute-start | bytes 1572872 | tf_op jit(solution)/shard_map/ppermute | solution.py:26
  14.9 9.6 %copy-start = (bf16[256,5120]{1,0:T(8,128)(2,1)S(1)}, bf16[256,5120]{1,0:T(8,128)(2,1)}, u32[]{:S(2)}) copy-start(bf16[256,5120]{1,0:T(8,128)(2,1)} %refs_1_.5) | copy-start | bytes 7864324
  15.0 9.8 %collective-permute-start.5 = (bf16[128,640]{1,0:T(8,128)(2,1)S(1)}, bf16[128,640]{1,0:T(8,128)(2,1)S(1)}, u32[]{:S(2)}, u32[]{:S(2)}) collective-permute-start(bf16[128,640]{1,0:T(8,128)(2,1)S(1)} %collective-permute-done.1.refs_1_.refs_2_), channel_id=1, source_target_pairs={{0,4},{1,5},{2,6},{3,7},{4,8},{5,9},{6,10},{7,11},{8,12},{9,13},{1... | collective-permute-start | bytes 491528 | tf_op jit(solution)/shard_map/ppermute | solution.py:42
  15.8 9.0 %collective-permute-start.6 = (bf16[128,640]{1,0:T(8,128)(2,1)S(1)}, bf16[128,640]{1,0:T(8,128)(2,1)S(1)}, u32[]{:S(2)}, u32[]{:S(2)}) collective-permute-start(bf16[128,640]{1,0:T(8,128)(2,1)S(1)} %collective-permute-done.1.refs_1_.refs_2_), channel_id=1, source_target_pairs={{0,12},{1,13},{2,14},{3,15},{4,0},{5,1},{6,2},{7,3},{8,4},{9,5},{1... | collective-permute-start | bytes 491528 | tf_op jit(solution)/shard_map/ppermute | solution.py:42
  17.7 8.7 %collective-permute-start.7 = (bf16[128,640]{1,0:T(8,128)(2,1)S(1)}, bf16[128,640]{1,0:T(8,128)(2,1)S(1)}, u32[]{:S(2)}, u32[]{:S(2)}) collective-permute-start(bf16[128,640]{1,0:T(8,128)(2,1)S(1)} %collective-permute-done.1.refs_1_.refs_2_), channel_id=1, source_target_pairs={{0,8},{1,9},{2,10},{3,11},{4,12},{5,13},{6,14},{7,15},{8,0},{9,1},... | collective-permute-start | bytes 491528 | tf_op jit(solution)/shard_map/ppermute | solution.py:42
  19.4 1.7 %copy-start.9 = (bf16[5120,256]{1,0:T(8,128)(2,1)S(1)}, bf16[5120,256]{1,0:T(8,128)(2,1)}, u32[]{:S(2)}) copy-start(bf16[5120,256]{1,0:T(8,128)(2,1)} %refs_0_.3) | copy-start | bytes 7864324
  27.8 5.1 %collective-permute-start.9 = (bf16[128,5120]{1,0:T(8,128)(2,1)S(1)}, bf16[128,5120]{1,0:T(8,128)(2,1)S(1)}, u32[]{:S(2)}, u32[]{:S(2)}) collective-permute-start(bf16[128,5120]{1,0:T(8,128)(2,1)S(1)} %get-tuple-element.38.refs_1_), channel_id=1, source_target_pairs={{0,1},{1,0},{2,3},{3,2},{4,5},{5,4},{6,7},{7,6},{8,9},{9,8},{10,11... | collective-permute-start | bytes 3932168 | tf_op jit(solution)/shard_map/ppermute | solution.py:34
  30.2 29.7 %collective-permute-start.18 = (bf16[256,2560]{1,0:T(8,128)(2,1)S(1)}, bf16[256,2560]{1,0:T(8,128)(2,1)S(1)}, u32[]{:S(2)}, u32[]{:S(2)}) collective-permute-start(bf16[256,2560]{1,0:T(8,128)(2,1)S(1)} %get-tuple-element.46), channel_id=1, source_target_pairs={{0,1},{1,0},{2,3},{3,2},{4,5},{5,4},{6,7},{7,6},{8,9},{9,8},{10,11... | collective-permute-start | bytes 3932168 | tf_op jit(solution)/shard_map/ppermute | solution.py:34
  34.6 7.6 %collective-permute-start.10 = (bf16[256,512]{1,0:T(8,128)(2,1)S(1)}, bf16[256,512]{1,0:T(8,128)(2,1)S(1)}, u32[]{:S(2)}, u32[]{:S(2)}) collective-permute-start(bf16[256,512]{1,0:T(8,128)(2,1)S(1)} %get-tuple-element.40.refs_3_.refs_1_), channel_id=1, source_target_pairs={{0,64},{16,80},{32,96},{48,112},{64,0},{80,16},{96,32},{112,48},{1... | collective-permute-start | bytes 786440 | tf_op jit(solution)/shard_map/ppermute | solution.py:26
  35.9 5.7 %collective-permute-start.13 = (bf16[256,256]{1,0:T(8,128)(2,1)S(1)}, bf16[256,256]{1,0:T(8,128)(2,1)S(1)}, u32[]{:S(2)}, u32[]{:S(2)}) collective-permute-start(bf16[256,256]{1,0:T(8,128)(2,1)S(1)} %shard_map.182.refs_0_), channel_id=1, source_target_pairs={{0,16},{16,32},{32,48},{48,0},{64,80},{80,96},{96,112},{112,64},{1... | collective-permute-start | bytes 393224 | tf_op jit(solution)/shard_map/ppermute | solution.py:30
  37.2 6.5 %collective-permute-start.12 = (bf16[256,256]{1,0:T(8,128)(2,1)S(1)}, bf16[256,256]{1,0:T(8,128)(2,1)S(1)}, u32[]{:S(2)}, u32[]{:S(2)}) collective-permute-start(bf16[256,256]{1,0:T(8,128)(2,1)S(1)} %shard_map.182.refs_0_), channel_id=1, source_target_pairs={{0,48},{16,0},{32,16},{48,32},{64,112},{80,64},{96,80},{112,96},{1... | collective-permute-start | bytes 393224 | tf_op jit(solution)/shard_map/ppermute | solution.py:30
  38.6 6.9 %collective-permute-start.11 = (bf16[256,256]{1,0:T(8,128)(2,1)S(1)}, bf16[256,256]{1,0:T(8,128)(2,1)S(1)}, u32[]{:S(2)}, u32[]{:S(2)}) collective-permute-start(bf16[256,256]{1,0:T(8,128)(2,1)S(1)} %shard_map.182.refs_0_), channel_id=1, source_target_pairs={{0,32},{16,48},{32,0},{48,16},{64,96},{80,112},{96,64},{112,80},{1... | collective-permute-start | bytes 393224 | tf_op jit(solution)/shard_map/ppermute | solution.py:30
  47.1 6.1 %collective-permute-start.16 = (bf16[272,256]{1,0:T(8,128)(2,1)S(1)}, bf16[272,256]{1,0:T(8,128)(2,1)S(1)}, u32[]{:S(2)}, u32[]{:S(2)}) collective-permute-start(bf16[272,256]{1,0:T(8,128)(2,1)S(1)} %shard_map.186.refs_6_), channel_id=1, source_target_pairs={{0,32},{16,48},{32,0},{48,16},{64,96},{80,112},{96,64},{112,80},{1... | collective-permute-start | bytes 417800 | tf_op jit(solution)/shard_map/ppermute | solution.py:30
  49.5 7.2 %collective-permute-start.15 = (bf16[272,256]{1,0:T(8,128)(2,1)S(1)}, bf16[272,256]{1,0:T(8,128)(2,1)S(1)}, u32[]{:S(2)}, u32[]{:S(2)}) collective-permute-start(bf16[272,256]{1,0:T(8,128)(2,1)S(1)} %shard_map.185.refs_5_), channel_id=1, source_target_pairs={{0,16},{16,32},{32,48},{48,0},{64,80},{80,96},{96,112},{112,64},{1... | collective-permute-start | bytes 417800 | tf_op jit(solution)/shard_map/ppermute | solution.py:30
  49.8 6.9 %collective-permute-start.14 = (bf16[272,256]{1,0:T(8,128)(2,1)S(1)}, bf16[272,256]{1,0:T(8,128)(2,1)S(1)}, u32[]{:S(2)}, u32[]{:S(2)}) collective-permute-start(bf16[272,256]{1,0:T(8,128)(2,1)S(1)} %shard_map.184.refs_5_), channel_id=1, source_target_pairs={{0,48},{16,0},{32,16},{48,32},{64,112},{80,64},{96,80},{112,96},{1... | collective-permute-start | bytes 417800 | tf_op jit(solution)/shard_map/ppermute | solution.py:30
  58.4 21.5 %copy-start.12 = (f32[5120]{0:T(1024)S(1)}, f32[5120]{0:T(1024)}, u32[]{:S(2)}) copy-start(f32[5120]{0:T(1024)} %param.19) | copy-start | bytes 61444
  58.4 21.5 %copy-start.13 = (f32[5120]{0:T(1024)S(1)}, f32[5120]{0:T(1024)}, u32[]{:S(2)}) copy-start(f32[5120]{0:T(1024)} %param.26) | copy-start | bytes 61444
  58.4 22.5 %copy-start.1 = (bf16[5120,64]{0,1:T(8,128)(2,1)S(1)}, bf16[5120,64]{0,1:T(8,128)(2,1)}, u32[]{:S(2)}) copy-start(bf16[5120,64]{0,1:T(8,128)(2,1)} %param.27) | copy-start | bytes 1966084
  58.4 22.4 %copy-start.6 = (f32[4,256]{1,0:T(4,128)S(1)}, f32[4,256]{1,0:T(4,128)}, u32[]{:S(2)}) copy-start(f32[4,256]{1,0:T(4,128)} %refs_7_.1) | copy-start | bytes 12292
  58.4 22.4 %copy-start.7 = (f32[4,256]{1,0:T(4,128)S(1)}, f32[4,256]{1,0:T(4,128)}, u32[]{:S(2)}) copy-start(f32[4,256]{1,0:T(4,128)} %refs_8_.1) | copy-start | bytes 12292
  58.4 22.4 %copy-start.8 = (s32[4,1]{0,1:T(1,128)S(1)}, s32[4,1]{0,1:T(1,128)}, u32[]{:S(2)}) copy-start(s32[4,1]{0,1:T(1,128)} %param.30) | copy-start | bytes 52
  58.4 36.0 %copy-start.2 = (bf16[256,1024]{1,0:T(8,128)(2,1)S(1)}, bf16[256,1024]{1,0:T(8,128)(2,1)}, u32[]{:S(2)}) copy-start(bf16[256,1024]{1,0:T(8,128)(2,1)} %refs_1_.7) | copy-start | bytes 1572868
  58.4 2.5 %collective-permute-start.17 = (bf16[256,256]{1,0:T(8,128)(2,1)S(1)}, bf16[256,256]{1,0:T(8,128)(2,1)S(1)}, u32[]{:S(2)}, u32[]{:S(2)}) collective-permute-start(bf16[256,256]{1,0:T(8,128)(2,1)S(1)} %shard_map.188.refs_1_), channel_id=1, source_target_pairs={{0,1},{1,0},{2,3},{3,2},{4,5},{5,4},{6,7},{7,6},{8,9},{9,8},{10,11... | collective-permute-start | bytes 393224 | tf_op jit(solution)/shard_map/ppermute | solution.py:34
  61.8 6.7 %collective-permute-start.23 = (bf16[32,2560]{1,0:T(8,128)(2,1)S(1)}, bf16[32,2560]{1,0:T(8,128)(2,1)S(1)}, u32[]{:S(2)}, u32[]{:S(2)}) collective-permute-start(bf16[32,2560]{1,0:T(8,128)(2,1)S(1)} %get-tuple-element.53), channel_id=1, source_target_pairs={{0,4},{1,5},{2,6},{3,7},{4,8},{5,9},{6,10},{7,11},{8,12},{9,13},{1... | collective-permute-start | bytes 491528 | tf_op jit(solution)/shard_map/ppermute | solution.py:42
  62.6 5.9 %collective-permute-start.24 = (bf16[32,2560]{1,0:T(8,128)(2,1)S(1)}, bf16[32,2560]{1,0:T(8,128)(2,1)S(1)}, u32[]{:S(2)}, u32[]{:S(2)}) collective-permute-start(bf16[32,2560]{1,0:T(8,128)(2,1)S(1)} %get-tuple-element.54), channel_id=1, source_target_pairs={{0,12},{1,13},{2,14},{3,15},{4,0},{5,1},{6,2},{7,3},{8,4},{9,5},{1... | collective-permute-start | bytes 491528 | tf_op jit(solution)/shard_map/ppermute | solution.py:42
  64.5 6.3 %collective-permute-start.21 = (bf16[32,2560]{1,0:T(8,128)(2,1)S(1)}, bf16[32,2560]{1,0:T(8,128)(2,1)S(1)}, u32[]{:S(2)}, u32[]{:S(2)}) collective-permute-start(bf16[32,2560]{1,0:T(8,128)(2,1)S(1)} %get-tuple-element.51), channel_id=1, source_target_pairs={{0,2},{1,3},{2,0},{3,1},{4,6},{5,7},{6,4},{7,5},{8,10},{9,11},{10,... | collective-permute-start | bytes 491528 | tf_op jit(solution)/shard_map/ppermute | solution.py:38
  65.9 6.5 %collective-permute-start.19 = (bf16[32,2560]{1,0:T(8,128)(2,1)S(1)}, bf16[32,2560]{1,0:T(8,128)(2,1)S(1)}, u32[]{:S(2)}, u32[]{:S(2)}) collective-permute-start(bf16[32,2560]{1,0:T(8,128)(2,1)S(1)} %get-tuple-element.48), channel_id=1, source_target_pairs={{0,4},{1,5},{2,6},{3,7},{4,8},{5,9},{6,10},{7,11},{8,12},{9,13},{1... | collective-permute-start | bytes 491528 | tf_op jit(solution)/shard_map/ppermute | solution.py:42
  65.9 6.5 %collective-permute-start.20 = (bf16[32,2560]{1,0:T(8,128)(2,1)S(1)}, bf16[32,2560]{1,0:T(8,128)(2,1)S(1)}, u32[]{:S(2)}, u32[]{:S(2)}) collective-permute-start(bf16[32,2560]{1,0:T(8,128)(2,1)S(1)} %get-tuple-element.49), channel_id=1, source_target_pairs={{0,12},{1,13},{2,14},{3,15},{4,0},{5,1},{6,2},{7,3},{8,4},{9,5},{1... | collective-permute-start | bytes 491528 | tf_op jit(solution)/shard_map/ppermute | solution.py:42
  68.6 5.8 %collective-permute-start.25 = (bf16[32,2560]{1,0:T(8,128)(2,1)S(1)}, bf16[32,2560]{1,0:T(8,128)(2,1)S(1)}, u32[]{:S(2)}, u32[]{:S(2)}) collective-permute-start(bf16[32,2560]{1,0:T(8,128)(2,1)S(1)} %shard_map.191), channel_id=1, source_target_pairs={{0,2},{1,3},{2,0},{3,1},{4,6},{5,7},{6,4},{7,5},{8,10},{9,11},{10,... | collective-permute-start | bytes 491528 | tf_op jit(solution)/shard_map/ppermute | solution.py:38
  70.9 5.9 %collective-permute-start.22 = (bf16[32,2560]{1,0:T(8,128)(2,1)S(1)}, bf16[32,2560]{1,0:T(8,128)(2,1)S(1)}, u32[]{:S(2)}, u32[]{:S(2)}) collective-permute-start(bf16[32,2560]{1,0:T(8,128)(2,1)S(1)} %shard_map.190), channel_id=1, source_target_pairs={{0,8},{1,9},{2,10},{3,11},{4,12},{5,13},{6,14},{7,15},{8,0},{9,1},... | collective-permute-start | bytes 491528 | tf_op jit(solution)/shard_map/ppermute | solution.py:42
  76.9 3.9 %collective-permute-start.26 = (f32[16,2560]{1,0:T(8,128)S(1)}, f32[16,2560]{1,0:T(8,128)S(1)}, u32[]{:S(2)}, u32[]{:S(2)}) collective-permute-start(f32[16,2560]{1,0:T(8,128)S(1)} %get-tuple-element.56), channel_id=1, source_target_pairs={{0,1},{1,0},{2,3},{3,2},{4,5},{5,4},{6,7},{7,6},{8,9},{9,8},{10,11... | collective-permute-start | bytes 491528 | tf_op jit(solution)/shard_map/ppermute | solution.py:34

commit v4 on v3

--- a/solution.py
+++ b/solution.py
@@ -146,17 +146,26 @@
         out_ref[:, cols] = (centred * inverse * (1.0 + scale) + shift).astype(BF)
 
 
-def kv_body(core_ref, own_ref, other_ref, wk_ref, wv_ref, kv_ref, x):
+def half_body(x_ref, wk_ref, wv_ref, wq_ref, kv_ref, q_ref):
+    kv_ref[:, :256] = jnp.dot(x_ref[...], wk_ref[...], preferred_element_type=F32).astype(BF)
+    kv_ref[:, 256:] = jnp.dot(x_ref[...], wv_ref[...], preferred_element_type=F32).astype(BF)
+    q_ref[...] = jnp.dot(x_ref[...], wq_ref[...], preferred_element_type=F32).astype(BF)
+
+
+def kv_body(x_ref, wk_ref, wv_ref, half_ref, kv_ref):
+    rows = x_ref.shape[0]
+    kv_ref[:rows] = half_ref[...]
+    kv_ref[rows:, :256] = jnp.dot(x_ref[...], wk_ref[...], preferred_element_type=F32).astype(BF)
+    kv_ref[rows:, 256:] = jnp.dot(x_ref[...], wv_ref[...], preferred_element_type=F32).astype(BF)
+
+
+def query_body(core_ref, x_ref, wq_ref, half_ref, q_ref):
     k = core_ref[0]
-    rows = own_ref.shape[0]
-    x[pl.ds(pl.multiple_of(k * rows, rows), rows), :] = own_ref[...]
-    x[pl.ds(pl.multiple_of((1 - k) * rows, rows), rows), :] = other_ref[...]
-    kv_ref[:, :256] = jnp.dot(x[...], wk_ref[...], preferred_element_type=F32).astype(BF)
-    kv_ref[:, 256:] = jnp.dot(x[...], wv_ref[...], preferred_element_type=F32).astype(BF)
-
-
-def query_body(x_ref, wq_ref, q_ref):
-    q_ref[...] = jnp.dot(x_ref[...], wq_ref[...], preferred_element_type=F32).astype(BF)
+    rows = x_ref.shape[0]
+    q_ref[pl.ds(pl.multiple_of(k * rows, rows), rows), :] = half_ref[...]
+    q_ref[pl.ds(pl.multiple_of((1 - k) * rows, rows), rows), :] = jnp.dot(
+        x_ref[...], wq_ref[...], preferred_element_type=F32
+    ).astype(BF)
 
 
 C2 = math.log2(math.e) / math.sqrt(HD)
@@ -168,35 +177,42 @@
     )
 
 
-def attend(q_ref, kv_refs, start, h):
-    q = q_ref[:, h * HD : (h + 1) * HD]
-    scores = [
-        lax.dot_general(
-            q, kv[:, h * HD : (h + 1) * HD], (((1,), (1,)), ((), ())), preferred_element_type=F32
+def attend(q_ref, kv_refs, which=(0, 1), starts=None):
+    heads = [slice(h * HD, (h + 1) * HD) for h in which]
+    every = [
+        [
+            lax.dot_general(
+                q_ref[:, cols], kv[:, cols], (((1,), (1,)), ((), ())), preferred_element_type=F32
+            )
+            for kv in kv_refs
+        ]
+        for cols in heads
+    ]
+    results = []
+    for h, scores in zip(which, every):
+        peak = jnp.max(fold(jnp.maximum, scores), -1, keepdims=True)
+        if starts is not None:
+            peak = jnp.maximum(peak, starts[h][0])
+        probs = [jnp.exp2((s - peak) * C2) for s in scores]
+        total = jnp.sum(fold(jnp.add, probs), -1, keepdims=True)
+        summed = sum(
+            jnp.dot(
+                p.astype(BF),
+                kv[:, 256 + h * HD : 256 + (h + 1) * HD],
+                preferred_element_type=F32,
+            )
+            for p, kv in zip(probs, kv_refs)
         )
-        for kv in kv_refs
-    ]
-    peak = jnp.max(fold(jnp.maximum, scores), -1, keepdims=True)
-    if start is not None:
-        peak = jnp.maximum(peak, start[0])
-    probs = [jnp.exp2((s - peak) * C2) for s in scores]
-    total = jnp.sum(fold(jnp.add, probs), -1, keepdims=True)
-    summed = sum(
-        jnp.dot(
-            p.astype(BF), kv[:, 256 + h * HD : 256 + (h + 1) * HD], preferred_element_type=F32
-        )
-        for p, kv in zip(probs, kv_refs)
-    )
-    if start is not None:
-        factor = jnp.exp2((start[0] - peak) * C2)
-        total, summed = start[1] * factor + total, start[2] * factor + summed
-    return peak, total, summed
+        if starts is not None:
+            factor = jnp.exp2((starts[h][0] - peak) * C2)
+            total, summed = starts[h][1] * factor + total, starts[h][2] * factor + summed
+        results.append((peak, total, summed))
+    return results
 
 
 def past_body(q_ref, *refs):
     *kv_refs, o_ref, peak_ref, total_ref = refs
-    for h in range(2):
-        peak, total, summed = attend(q_ref, kv_refs, None, h)
+    for h, (peak, total, summed) in enumerate(attend(q_ref, kv_refs)):
         o_ref[:, h * HD : (h + 1) * HD] = summed
         peak_ref[h] = jnp.broadcast_to(peak, peak_ref.shape[1:])
         total_ref[h] = jnp.broadcast_to(total, total_ref.shape[1:])
@@ -204,18 +220,21 @@
 
 def log_total(peak, total):
     return peak / math.sqrt(HD) + jnp.log(total)
+
+
+def turned(first, second):
+    lane = lax.broadcasted_iota(jnp.int32, (first.shape[0], HD), 1)
+    return jnp.transpose(jnp.where(lane == 0, first, second))[:8]
 
 
 def sent_body(q_ref, *refs):
     *kv_refs, out_ref = refs
     rows = q_ref.shape[0]
     both = []
-    for h in range(2):
-        peak, total, summed = attend(q_ref, kv_refs, None, h)
+    for h, (peak, total, summed) in enumerate(attend(q_ref, kv_refs)):
         out_ref[:rows, h * HD : (h + 1) * HD] = (summed * (1.0 / total)).astype(BF)
         both.append(log_total(peak, total))
-    lane = lax.broadcasted_iota(jnp.int32, (rows, HD), 1)
-    rest = jnp.transpose(jnp.where(lane == 0, both[0], both[1]))[:16]
+    rest = turned(*both)
     at = lax.broadcasted_iota(jnp.int32, (16, rows), 0)
     tail = jnp.zeros((16, rows), F32)
     for i in range(3):
@@ -227,36 +246,40 @@
 
 
 def kept_body(q_ref, a_ref, b_ref, o_ref, peak_ref, total_ref, out_ref, lse_ref):
+    both = []
+    starts = [
+        (peak_ref[h][:, :1], total_ref[h][:, :1], o_ref[:, h * HD : (h + 1) * HD]) for h in range(2)
+    ]
     for h in range(2):
-        cols = slice(h * HD, (h + 1) * HD)
-        start = (peak_ref[h][:, :1], total_ref[h][:, :1], o_ref[:, cols])
-        peak, total, summed = attend(q_ref, (a_ref, b_ref), start, h)
-        out_ref[:, cols] = summed * (1.0 / total)
-        lse_ref[h] = jnp.broadcast_to(log_total(peak, total), lse_ref.shape[1:])
+        peak, total, summed = attend(q_ref, (a_ref, b_ref), (h,), starts)[0]
+        out_ref[:, h * HD : (h + 1) * HD] = summed * (1.0 / total)
+        both.append(log_total(peak, total))
+    lse_ref[...] = turned(*both)
 
 
 def merge_body(own_ref, lse_ref, *refs):
     *got_refs, out_ref = refs
     rows = own_ref.shape[0]
+    parts = len(got_refs) + 1
     at = lax.broadcasted_iota(jnp.int32, (HD, rows), 0)
     lanes = jnp.zeros((HD, rows), F32)
-    for g, got_ref in enumerate(got_refs):
-        tail = got_ref[rows:, :].astype(F32)
-        for h in range(2):
-            row = sum(tail[3 * h + i : 3 * h + i + 1] for i in range(3))
-            lanes = jnp.where(at == 2 * g + h, row, lanes)
-    turned = jnp.transpose(lanes)
+    tails = [got_ref[rows:, :].astype(F32) for got_ref in got_refs]
     for h in range(2):
-        cols = slice(h * HD, (h + 1) * HD)
-        lse = [lse_ref[h][:, :1]] + [
-            turned[:, 2 * g + h : 2 * g + h + 1] for g in range(len(got_refs))
+        lse = [lse_ref[h : h + 1]] + [
+            sum(tail[3 * h + i : 3 * h + i + 1] for i in range(3)) for tail in tails
         ]
         top = functools.reduce(jnp.maximum, lse)
         part = [jnp.exp(e - top) for e in lse]
         inverse = 1.0 / sum(part)
-        merged = (part[0] * inverse) * own_ref[:, cols]
-        for p, got_ref in zip(part[1:], got_refs):
-            merged = merged + (p * inverse) * got_ref[:rows, cols].astype(F32)
+        for g, p in enumerate(part):
+            lanes = jnp.where(at == parts * h + g, p * inverse, lanes)
+    shares = jnp.transpose(lanes)
+    for h in range(2):
+        cols = slice(h * HD, (h + 1) * HD)
+        merged = shares[:, parts * h : parts * h + 1] * own_ref[:, cols]
+        for g, got_ref in enumerate(got_refs):
+            share = shares[:, parts * h + g + 1 : parts * h + g + 2]
+            merged = merged + share * got_ref[:rows, cols].astype(F32)
         out_ref[:, cols] = merged.astype(BF)
 
 
@@ -332,19 +355,22 @@
     )
     next_ref[...] = new
     panels = new.astype(BF).astype(F32)
-    at = lax.broadcasted_iota(jnp.int32, slot_ref.shape, 0)
-    slots = jnp.zeros(slot_ref.shape, F32)
+    owned = slot_ref.shape[0] * CAP
+    at = lax.broadcasted_iota(jnp.int32, (owned, panels.shape[1]), 0)
+    slots = jnp.zeros(at.shape, F32)
     for t in range(tiles):
         owner = owner_ref[t]
         before = jnp.int32(0)
         for e in range(t):
             before = before + jnp.where(owner_ref[e] == owner, 1, 0)
         slots = jnp.where(at == owner * CAP + before, panels[t : t + 1], slots)
-    slot_ref[...] = slots.astype(BF)
+    for o in range(slot_ref.shape[0]):
+        slot_ref[o] = slots[CAP * o : CAP * o + CAP]
 
 
 def up_body(x_ref, w_ref, out_ref):
-    y = jnp.dot(x_ref[...], w_ref[...], preferred_element_type=F32)
+    x = jnp.concatenate([x_ref[o] for o in range(x_ref.shape[0])], 0).astype(BF)
+    y = jnp.dot(x, w_ref[...], preferred_element_type=F32)
     out_ref[...] = jax.nn.gelu(y).astype(BF)
 
 
@@ -391,7 +417,7 @@
         (shape((w_out.shape[0], half), BF), shape((w_out.shape[0], half), BF)),
         (core_1, w_out),
         smem=(0,),
-        after=(beside,),
+        after=(x[5],),
     )
     w_theirs = core_swap(w_give)
 
@@ -402,7 +428,7 @@
         hbm=(0, 1, 2),
         nbytes=8 * MIB,
         scratch=[pltpu.SemaphoreType.DMA((3, 4))],
-        limit=42,
+        limit=45,
         flops=5000000000,
         after=tuple(mine),
     )
@@ -415,23 +441,32 @@
         smem=(0,),
         flops=MIB,
         nbytes=MIB,
-        after=(cached_in, w_mine, *weights),
+        after=(w_mine, *weights),
     )
     cols = w_query.shape[1]
-    kv, whole = call(
+    normed_in = core_swap(normed)
+    kv_half, query_half = call(
+        half_body,
+        (shape((rows, 2 * cols), BF), shape((rows, cols), BF)),
+        (normed, weights[1], weights[2], weights[0]),
+        after=(cached_in,),
+        flops=30000000000,
+        nbytes=8 * MIB,
+    )
+    kv = call(
         kv_body,
-        (shape((count, 2 * cols), BF), shape((count, w_query.shape[0]), BF)),
-        (core_1, normed, core_swap(normed), *weights[1:]),
-        smem=(0,),
-        flops=2 * count * w_query.shape[0] * 2 * cols,
-        nbytes=8 * MIB,
+        shape((count, 2 * cols), BF),
+        (normed_in, weights[1], weights[2], kv_half),
+        flops=2 * rows * w_query.shape[0] * 2 * cols,
+        nbytes=5 * MIB,
     )
     query = call(
         query_body,
         shape((count, cols), BF),
-        (whole, weights[0]),
-        flops=2 * count * w_query.shape[0] * cols,
-        nbytes=5 * MIB,
+        (core_1, normed_in, weights[0], query_half),
+        smem=(0,),
+        flops=2 * rows * w_query.shape[0] * cols,
+        nbytes=3 * MIB,
     )
     kv_in = y_swap(kv)
     query_in = [x_send(query, by) for by in STEPS]
@@ -460,7 +495,7 @@
         back.append(x_send(before, -by))
     kept = call(
         kept_body,
-        (shape((count, cols), F32), shape((2, count, HD), F32)),
+        (shape((count, cols), F32), shape((8, count), F32)),
         (query, kv, kv_in, *stats),
         flops=MIB,
         nbytes=MIB,
@@ -497,7 +532,7 @@
         (
             shape((block, w_out.shape[1]), BF),
             shape(state.shape, F32),
-            shape((16 * CAP, state.shape[1]), BF),
+            shape((16, CAP, state.shape[1]), F32),
         ),
         (
             core_1, ours, core_swap(theirs), own_x, gate.reshape(chips, 2 * part),
@@ -507,9 +542,7 @@
         nbytes=2 * MIB,
         scratch=[pltpu.VMEM((block, w_final.shape[1]), F32)],
     )
-    routed = lax.all_to_all(
-        slot_rows.reshape(16, CAP, state.shape[1]), "mdl", split_axis=0, concat_axis=0, tiled=True
-    ).reshape(16 * CAP, state.shape[1])
+    routed = lax.all_to_all(slot_rows, "mdl", split_axis=0, concat_axis=0, tiled=True)
     upsampled = call(
         up_body, shape((16 * CAP, w_up.shape[1]), BF), (routed, w_up), nbytes=MIB
     )

time: 95.6 us -> 92.3 us (0.965)
  waiting for transfers between devices: 18.3 us -> 20.5 us
  starting transfers between devices: 40.1 us -> 38.2 us
  local copies, waits for them, and re-layouts: 4.66 us -> 2.89 us
  Pallas kernels: 19.3 us -> 17.7 us
    ppermute x11, waiting for transfers between devices: 5.38 us -> 7.46 us  [z_send(): return lax.ppermute(a, 'mdl', [(m, (m + 4 * by) % 16) for m in range(16)])]
    unnamed x28 -> x26, local copies, waits for them, and re-layouts: 4.61 us -> 2.87 us
    pallas_call x20 -> x21, Pallas kernels: 19.3 us -> 17.7 us  [call(): pl.pallas_call(run, out_shape=outs, in_specs=place + [pl.BlockSpec(memory...]
    ppermute x5, waiting for transfers between devices: 5.49 us -> 4.29 us  [core_swap(): return lax.ppermute(a, 'mdl', CORE_SWAP)]
    ppermute x5, starting transfers between devices: 8.48 us -> 7.47 us  [core_swap(): return lax.ppermute(a, 'mdl', CORE_SWAP)]
  transfers between devices with their start and end apart: 27 -> 27, of which waited for: 13 -> 15; matrix products, arithmetic and copies ran while one was open for 0% -> 0% of each run, Pallas kernels for 15% -> 15%
where the time goes in v4:
time: 92.3 us; the launch traced here: 92.1 us
  starting transfers between devices  38.2 us (41%)
  waiting for transfers between devices  20.5 us (22%)
  Pallas kernels  17.7 us (19%)
  blocking collectives  11.8 us (13%)
  local copies, waits for them, and re-layouts  2.89 us (3%)
  between operations  0.94 us (1%)
    pallas_call x21, Pallas kernels, call(): pl.pallas_call(run, out_shape=outs, in_specs=place + [pl.BlockSpec(memory...  17.7 us
    ppermute x11, starting transfers between devices, z_send(): return lax.ppermute(a, 'mdl', [(m, (m + 4 * by) % 16) for m in range(16)])  14.2 us
    all_to_all x1, blocking collectives, shards(): lax.all_to_all(slot_rows, 'mdl', split_axis=0, concat_axis=0, tiled=True)  11.8 us
    ppermute x6, starting transfers between devices, x_send(): lax.ppermute(a, 'ctx', [(c, c // 4 * 4 + (c + by) % 4) for c in range(8)])  9.29 us
    ppermute x5, starting transfers between devices, core_swap(): return lax.ppermute(a, 'mdl', CORE_SWAP)  7.47 us
    ppermute x11, waiting for transfers between devices, z_send(): return lax.ppermute(a, 'mdl', [(m, (m + 4 * by) % 16) for m in range(16)])  7.46 us
    ppermute x3, starting transfers between devices, pair_swap(): return lax.ppermute(a, 'mdl', PAIR_SWAP)  6.13 us
    ppermute x6, waiting for transfers between devices, x_send(): lax.ppermute(a, 'ctx', [(c, c // 4 * 4 + (c + by) % 4) for c in range(8)])  4.57 us
  transfers between devices with their start and end apart: 27, of which 15 were waited for; matrix products, arithmetic and copies ran while one was open for 0% of the time, Pallas kernels for 15%

profile of v4, /device:TPU:1, one launch (start us, length us, event | category | flops | bytes accessed | tf_op | source)
XLA Modules:
  0.0 92.1 jit_solution(11968977191419897550)
XLA Ops:
  0.7 0.9 copy-done.5
  1.6 0.1 shard_map.175
  1.7 1.5 %collective-permute-start = (bf16[128,320]{1,0:T(8,128)(2,1)S(1)}, bf16[128,320]{1,0:T(8,128)(2,1)S(1)}, u32[]{:S(2)}, u32[]{:S(2)}) collective-permute-start(bf16[128,320]{1,0:T(8,128)(2,1)S(1)} %get-tuple-element.33), channel_id=1, source_target_pairs={{0,1},{1,0},{2,3},{3,2},{4,5},{5,4},{6,7},{7,6},{8,9},{9,8},{10,11... | collective-permute-start | bytes 245768 | tf_op jit(solution)/shard_map/ppermute | solution.py:34
  3.2 0.9 %collective-permute-done = bf16[128,320]{1,0:T(8,128)(2,1)S(1)} collective-permute-done((bf16[128,320]{1,0:T(8,128)(2,1)S(1)}, bf16[128,320]{1,0:T(8,128)(2,1)S(1)}, u32[]{:S(2)}, u32[]{:S(2)}) %collective-permute-start) | collective-permute-done | bytes 81952 | tf_op jit(solution)/shard_map/ppermute | solution.py:34
  4.2 0.1 pad_maximum_fusion.refs_1_
  4.3 3.1 %collective-permute-start.1 = (bf16[128,640]{1,0:T(8,128)(2,1)S(1)}, bf16[128,640]{1,0:T(8,128)(2,1)S(1)}, u32[]{:S(2)}, u32[]{:S(2)}) collective-permute-start(bf16[128,640]{1,0:T(8,128)(2,1)S(1)} %pad_maximum_fusion.refs_1_), channel_id=1, source_target_pairs={{0,2},{1,3},{2,0},{3,1},{4,6},{5,7},{6,4},{7,5},{8,10},{9,11},{10,... | collective-permute-start | bytes 491528 | tf_op jit(solution)/shard_map/ppermute | solution.py:38
  7.3 1.6 %collective-permute-start.2 = (bf16[128,640]{1,0:T(8,128)(2,1)S(1)}, bf16[128,640]{1,0:T(8,128)(2,1)S(1)}, u32[]{:S(2)}, u32[]{:S(2)}) collective-permute-start(bf16[128,640]{1,0:T(8,128)(2,1)S(1)} %pad_maximum_fusion.refs_1_), channel_id=1, source_target_pairs={{0,4},{1,5},{2,6},{3,7},{4,8},{5,9},{6,10},{7,11},{8,12},{9,13},{1... | collective-permute-start | bytes 491528 | tf_op jit(solution)/shard_map/ppermute | solution.py:42
  9.0 2.1 %collective-permute-start.3 = (bf16[128,640]{1,0:T(8,128)(2,1)S(1)}, bf16[128,640]{1,0:T(8,128)(2,1)S(1)}, u32[]{:S(2)}, u32[]{:S(2)}) collective-permute-start(bf16[128,640]{1,0:T(8,128)(2,1)S(1)} %pad_maximum_fusion.refs_1_), channel_id=1, source_target_pairs={{0,12},{1,13},{2,14},{3,15},{4,0},{5,1},{6,2},{7,3},{8,4},{9,5},{1... | collective-permute-start | bytes 491528 | tf_op jit(solution)/shard_map/ppermute | solution.py:42
  11.1 1.3 %collective-permute-start.4 = (bf16[128,640]{1,0:T(8,128)(2,1)S(1)}, bf16[128,640]{1,0:T(8,128)(2,1)S(1)}, u32[]{:S(2)}, u32[]{:S(2)}) collective-permute-start(bf16[128,640]{1,0:T(8,128)(2,1)S(1)} %pad_maximum_fusion.refs_1_), channel_id=1, source_target_pairs={{0,8},{1,9},{2,10},{3,11},{4,12},{5,13},{6,14},{7,15},{8,0},{9,1},... | collective-permute-start | bytes 491528 | tf_op jit(solution)/shard_map/ppermute | solution.py:42
  12.4 0.9 %copy-done.3 = bf16[512,256]{1,0:T(8,128)(2,1)S(1)} copy-done((bf16[512,256]{1,0:T(8,128)(2,1)S(1)}, bf16[512,256]{1,0:T(8,128)(2,1)}, u32[]{:S(2)}) %copy-start.3) | copy-done | bytes 262168
  13.4 0.9 %copy-done.4 = bf16[512,256]{1,0:T(8,128)(2,1)S(1)} copy-done((bf16[512,256]{1,0:T(8,128)(2,1)S(1)}, bf16[512,256]{1,0:T(8,128)(2,1)}, u32[]{:S(2)}) %copy-start.4) | copy-done | bytes 262168
  14.4 0.5 collective-permute-start.9
  15.0 0.8 collective-permute-start.5
  15.8 1.9 %collective-permute-start.6 = (bf16[128,640]{1,0:T(8,128)(2,1)S(1)}, bf16[128,640]{1,0:T(8,128)(2,1)S(1)}, u32[]{:S(2)}, u32[]{:S(2)}) collective-permute-start(bf16[128,640]{1,0:T(8,128)(2,1)S(1)} %collective-permute-done.1.refs_2_.refs_1_), channel_id=1, source_target_pairs={{0,12},{1,13},{2,14},{3,15},{4,0},{5,1},{6,2},{7,3},{8,4},{9,5},{1... | collective-permute-start | bytes 491528 | tf_op jit(solution)/shard_map/ppermute | solution.py:42
  17.7 0.5 collective-permute-start.7
  18.2 1.3 %collective-permute-done.4.refs_5_ = bf16[128,640]{1,0:T(8,128)(2,1)S(1)} collective-permute-done((bf16[128,640]{1,0:T(8,128)(2,1)S(1)}, bf16[128,640]{1,0:T(8,128)(2,1)S(1)}, u32[]{:S(2)}, u32[]{:S(2)}) %collective-permute-start.4) | collective-permute-done | bytes 163872 | tf_op jit(solution)/shard_map/ppermute | solution.py:42
  19.4 3.3 %shard_map.177 = (bf16[5120,256]{1,0:T(8,128)(2,1)S(1)}, bf16[5120,256]{1,0:T(8,128)(2,1)S(1)}, bf16[5120,256]{1,0:T(8,128)(2,1)S(1)}) custom-call(bf16[5120,256]{1,0:T(8,128)(2,1)} %refs_0_.2, bf16[5120,256]{1,0:T(8,128)(2,1)} %refs_1_.5, bf16[5120,256]{1,0:T(8,128)(2,1)} %refs_2_.1, bf16[128,640]{1,0:T(8,128)(2,1)S(1)} %collective-permute-done.2.refs_3_, ...), custom_call_target="tpu_custom_call" | custom-call | flops 5000000000 | bytes 8388608 | tf_op jit(solution)/shard_map/pallas_call | solution.py:60
  22.8 0.5 collective-permute-done.5.refs_2_.refs_6_
  23.3 0.2 shard_map.176
  23.5 3.0 %collective-permute-done.7.refs_8_ = bf16[128,640]{1,0:T(8,128)(2,1)S(1)} collective-permute-done((bf16[128,640]{1,0:T(8,128)(2,1)S(1)}, bf16[128,640]{1,0:T(8,128)(2,1)S(1)}, u32[]{:S(2)}, u32[]{:S(2)}) %collective-permute-start.7) | collective-permute-done | bytes 163872 | tf_op jit(solution)/shard_map/ppermute | solution.py:42
  26.5 1.3 %shard_map.178 = (bf16[128,5120]{1,0:T(8,128)(2,1)S(1)}, bf16[8,16,640]{2,1,0:T(8,128)(2,1)S(1)}) custom-call(s32[1]{0:T(128)} %bitcast.1.refs_0_, bf16[128,640]{1,0:T(8,128)(2,1)S(1)} %pad_maximum_fusion.refs_1_, bf16[128,640]{1,0:T(8,128)(2,1)S(1)} %collective-permute-done.1.refs_2_.refs_1_, bf16[128,640]{1,0:T(8,128)(2,1)S(1)} %collective-permute-done.2.refs_3_, ...), custom_call_target="tpu_custom_call" | custom-call | flops 1048576 | bytes 1048576 | tf_op jit(solution)/shard_map/pallas_call | solution.py:60
  27.8 1.6 %collective-permute-start.8 = (bf16[128,5120]{1,0:T(8,128)(2,1)S(1)}, bf16[128,5120]{1,0:T(8,128)(2,1)S(1)}, u32[]{:S(2)}, u32[]{:S(2)}) collective-permute-start(bf16[128,5120]{1,0:T(8,128)(2,1)S(1)} %get-tuple-element.38.refs_0_), channel_id=1, source_target_pairs={{0,1},{1,0},{2,3},{3,2},{4,5},{5,4},{6,7},{7,6},{8,9},{9,8},{10,11... | collective-permute-start | bytes 3932168 | tf_op jit(solution)/shard_map/ppermute | solution.py:34
  29.4 0.1 collective-permute-start.18
  29.4 1.2 %shard_map.181 = (bf16[128,512]{1,0:T(8,128)(2,1)S(1)}, bf16[128,256]{1,0:T(8,128)(2,1)S(1)}) custom-call(bf16[128,5120]{1,0:T(8,128)(2,1)S(1)} %get-tuple-element.38.refs_0_, bf16[5120,256]{1,0:T(8,128)(2,1)S(1)} %get-tuple-element.36.refs_13_.refs_1_, bf16[5120,256]{1,0:T(8,128)(2,1)S(1)} %get-tuple-element.37.refs_14_.refs_2_, ...), custom_call_target="tpu_custom_call" | custom-call | flops 30000001024 | bytes 8388608 | tf_op jit(solution)/shard_map/pallas_call | solution.py:60
  30.6 1.4 %collective-permute-done.8.refs_1_.refs_0_ = bf16[128,5120]{1,0:T(8,128)(2,1)S(1)} collective-permute-done((bf16[128,5120]{1,0:T(8,128)(2,1)S(1)}, bf16[128,5120]{1,0:T(8,128)(2,1)S(1)}, u32[]{:S(2)}, u32[]{:S(2)}) %collective-permute-start.8) | collective-permute-done | bytes 1310752 | tf_op jit(solution)/shard_map/ppermute | solution.py:34
  32.0 0.9 shard_map.183.refs_3_.refs_1_
  32.9 0.6 collective-permute-start.10
  33.5 0.5 shard_map.182.refs_0_
  34.0 1.3 %collective-permute-start.13 = (bf16[256,256]{1,0:T(8,128)(2,1)S(1)}, bf16[256,256]{1,0:T(8,128)(2,1)S(1)}, u32[]{:S(2)}, u32[]{:S(2)}) collective-permute-start(bf16[256,256]{1,0:T(8,128)(2,1)S(1)} %shard_map.182.refs_0_), channel_id=1, source_target_pairs={{0,16},{16,32},{32,48},{48,0},{64,80},{80,96},{96,112},{112,64},{1... | collective-permute-start | bytes 393224 | tf_op jit(solution)/shard_map/ppermute | solution.py:30
  35.3 1.5 %collective-permute-start.12 = (bf16[256,256]{1,0:T(8,128)(2,1)S(1)}, bf16[256,256]{1,0:T(8,128)(2,1)S(1)}, u32[]{:S(2)}, u32[]{:S(2)}) collective-permute-start(bf16[256,256]{1,0:T(8,128)(2,1)S(1)} %shard_map.182.refs_0_), channel_id=1, source_target_pairs={{0,48},{16,0},{32,16},{48,32},{64,112},{80,64},{96,80},{112,96},{1... | collective-permute-start | bytes 393224 | tf_op jit(solution)/shard_map/ppermute | solution.py:30
  36.7 1.5 %collective-permute-start.11 = (bf16[256,256]{1,0:T(8,128)(2,1)S(1)}, bf16[256,256]{1,0:T(8,128)(2,1)S(1)}, u32[]{:S(2)}, u32[]{:S(2)}) collective-permute-start(bf16[256,256]{1,0:T(8,128)(2,1)S(1)} %shard_map.182.refs_0_), channel_id=1, source_target_pairs={{0,32},{16,48},{32,0},{48,16},{64,96},{80,112},{96,64},{112,80},{1... | collective-permute-start | bytes 393224 | tf_op jit(solution)/shard_map/ppermute | solution.py:30
  38.3 0.9 shard_map.184
  39.2 0.5 collective-permute-done.13.refs_0_
  39.7 0.8 collective-permute-done.10.refs_4_.refs_2_
  40.5 1.3 %shard_map.185.refs_5_ = bf16[272,256]{1,0:T(8,128)(2,1)S(1)} custom-call(bf16[256,256]{1,0:T(8,128)(2,1)S(1)} %collective-permute-done.13.refs_0_, bf16[512,512]{1,0:T(8,128)(2,1)S(1)} %shard_map.179.refs_0_.refs_1_, bf16[512,512]{1,0:T(8,128)(2,1)S(1)} %collective-permute-done.9.refs_4_.refs_2_, bf16[256,512]{1,0:T(8,128)(2,1)S(1)} %shard_map.183.refs_3_.refs_1_, ...), custom_call_target="tpu_custom_call" | custom-call | flops 1048576 | bytes 1048576 | tf_op jit(solution)/shard_map/pallas_call | solution.py:60
  41.8 1.3 %shard_map.186.refs_5_ = bf16[272,256]{1,0:T(8,128)(2,1)S(1)} custom-call(bf16[256,256]{1,0:T(8,128)(2,1)S(1)} %collective-permute-done.12.refs_0_, bf16[512,512]{1,0:T(8,128)(2,1)S(1)} %shard_map.179.refs_0_.refs_1_, bf16[512,512]{1,0:T(8,128)(2,1)S(1)} %collective-permute-done.9.refs_4_.refs_2_, bf16[256,512]{1,0:T(8,128)(2,1)S(1)} %shard_map.183.refs_3_.refs_1_, ...), custom_call_target="tpu_custom_call" | custom-call | flops 1048576 | bytes 1048576 | tf_op jit(solution)/shard_map/pallas_call | solution.py:60
  43.2 0.5 collective-permute-done.11.refs_0_
  43.7 1.3 %shard_map.187.refs_6_ = bf16[272,256]{1,0:T(8,128)(2,1)S(1)} custom-call(bf16[256,256]{1,0:T(8,128)(2,1)S(1)} %collective-permute-done.11.refs_0_, bf16[512,512]{1,0:T(8,128)(2,1)S(1)} %shard_map.179.refs_0_.refs_1_, bf16[512,512]{1,0:T(8,128)(2,1)S(1)} %collective-permute-done.9.refs_4_.refs_2_, bf16[256,512]{1,0:T(8,128)(2,1)S(1)} %shard_map.183.refs_3_.refs_1_, ...), custom_call_target="tpu_custom_call" | custom-call | flops 1048576 | bytes 1048576 | tf_op jit(solution)/shard_map/pallas_call | solution.py:60
  45.0 2.3 %collective-permute-start.16 = (bf16[272,256]{1,0:T(8,128)(2,1)S(1)}, bf16[272,256]{1,0:T(8,128)(2,1)S(1)}, u32[]{:S(2)}, u32[]{:S(2)}) collective-permute-start(bf16[272,256]{1,0:T(8,128)(2,1)S(1)} %shard_map.187.refs_6_), channel_id=1, source_target_pairs={{0,32},{16,48},{32,0},{48,16},{64,96},{80,112},{96,64},{112,80},{1... | collective-permute-start | bytes 417800 | tf_op jit(solution)/shard_map/ppermute | solution.py:30
  47.3 0.3 collective-permute-start.15
  47.6 2.4 %collective-permute-start.14 = (bf16[272,256]{1,0:T(8,128)(2,1)S(1)}, bf16[272,256]{1,0:T(8,128)(2,1)S(1)}, u32[]{:S(2)}, u32[]{:S(2)}) collective-permute-start(bf16[272,256]{1,0:T(8,128)(2,1)S(1)} %shard_map.185.refs_5_), channel_id=1, source_target_pairs={{0,48},{16,0},{32,16},{48,32},{64,112},{80,64},{96,80},{112,96},{1... | collective-permute-start | bytes 417800 | tf_op jit(solution)/shard_map/ppermute | solution.py:30
  50.0 1.0 %shard_map.188 = (f32[256,256]{1,0:T(8,128)S(1)}, f32[8,256]{1,0:T(8,128)S(1)}) custom-call(bf16[256,256]{1,0:T(8,128)(2,1)S(1)} %shard_map.182.refs_0_, bf16[256,512]{1,0:T(8,128)(2,1)S(1)} %shard_map.183.refs_3_.refs_1_, bf16[256,512]{1,0:T(8,128)(2,1)S(1)} %collective-permute-done.10.refs_4_.refs_2_, f32[256,256]{1,0:T(8,128)S(1)} %get-tuple-element.41.refs_5_.refs_3_, ...), custom_call_target="tpu_custom_call" | custom-call | flops 1048576 | bytes 1048576 | tf_op jit(solution)/shard_map/pallas_call | solution.py:60
  51.0 3.6 %collective-permute-done.15.refs_3_ = bf16[272,256]{1,0:T(8,128)(2,1)S(1)} collective-permute-done((bf16[272,256]{1,0:T(8,128)(2,1)S(1)}, bf16[272,256]{1,0:T(8,128)(2,1)S(1)}, u32[]{:S(2)}, u32[]{:S(2)}) %collective-permute-start.15) | collective-permute-done | bytes 139296 | tf_op jit(solution)/shard_map/ppermute | solution.py:30
  54.6 0.6 shard_map.189.refs_1_
  55.3 1.5 %collective-permute-start.17 = (bf16[256,256]{1,0:T(8,128)(2,1)S(1)}, bf16[256,256]{1,0:T(8,128)(2,1)S(1)}, u32[]{:S(2)}, u32[]{:S(2)}) collective-permute-start(bf16[256,256]{1,0:T(8,128)(2,1)S(1)} %shard_map.189.refs_1_), channel_id=1, source_target_pairs={{0,1},{1,0},{2,3},{3,2},{4,5},{5,4},{6,7},{7,6},{8,9},{9,8},{10,11... | collective-permute-start | bytes 393224 | tf_op jit(solution)/shard_map/ppermute | solution.py:34
  56.8 1.0 %collective-permute-done.17.refs_2_ = bf16[256,256]{1,0:T(8,128)(2,1)S(1)} collective-permute-done((bf16[256,256]{1,0:T(8,128)(2,1)S(1)}, bf16[256,256]{1,0:T(8,128)(2,1)S(1)}, u32[]{:S(2)}, u32[]{:S(2)}) %collective-permute-start.17) | collective-permute-done | bytes 131104 | tf_op jit(solution)/shard_map/ppermute | solution.py:34
  57.8 0.8 shard_map.190
  58.6 0.9 collective-permute-start.23
  59.5 1.9 %collective-permute-start.24 = (bf16[32,2560]{1,0:T(8,128)(2,1)S(1)}, bf16[32,2560]{1,0:T(8,128)(2,1)S(1)}, u32[]{:S(2)}, u32[]{:S(2)}) collective-permute-start(bf16[32,2560]{1,0:T(8,128)(2,1)S(1)} %get-tuple-element.54), channel_id=1, source_target_pairs={{0,12},{1,13},{2,14},{3,15},{4,0},{5,1},{6,2},{7,3},{8,4},{9,5},{1... | collective-permute-start | bytes 491528 | tf_op jit(solution)/shard_map/ppermute | solution.py:42
  61.4 1.3 %collective-permute-start.21 = (bf16[32,2560]{1,0:T(8,128)(2,1)S(1)}, bf16[32,2560]{1,0:T(8,128)(2,1)S(1)}, u32[]{:S(2)}, u32[]{:S(2)}) collective-permute-start(bf16[32,2560]{1,0:T(8,128)(2,1)S(1)} %get-tuple-element.51), channel_id=1, source_target_pairs={{0,2},{1,3},{2,0},{3,1},{4,6},{5,7},{6,4},{7,5},{8,10},{9,11},{10,... | collective-permute-start | bytes 491528 | tf_op jit(solution)/shard_map/ppermute | solution.py:38
  62.7 2.7 %collective-permute-start.20 = (bf16[32,2560]{1,0:T(8,128)(2,1)S(1)}, bf16[32,2560]{1,0:T(8,128)(2,1)S(1)}, u32[]{:S(2)}, u32[]{:S(2)}) collective-permute-start(bf16[32,2560]{1,0:T(8,128)(2,1)S(1)} %get-tuple-element.49), channel_id=1, source_target_pairs={{0,12},{1,13},{2,14},{3,15},{4,0},{5,1},{6,2},{7,3},{8,4},{9,5},{1... | collective-permute-start | bytes 491528 | tf_op jit(solution)/shard_map/ppermute | solution.py:42
  65.4 0.1 shard_map.192
  65.5 1.7 %collective-permute-start.25 = (bf16[32,2560]{1,0:T(8,128)(2,1)S(1)}, bf16[32,2560]{1,0:T(8,128)(2,1)S(1)}, u32[]{:S(2)}, u32[]{:S(2)}) collective-permute-start(bf16[32,2560]{1,0:T(8,128)(2,1)S(1)} %shard_map.192), channel_id=1, source_target_pairs={{0,2},{1,3},{2,0},{3,1},{4,6},{5,7},{6,4},{7,5},{8,10},{9,11},{10,... | collective-permute-start | bytes 491528 | tf_op jit(solution)/shard_map/ppermute | solution.py:38
  67.2 0.5 collective-permute-done.21.refs_1_
  67.7 0.5 collective-permute-start.22
  68.3 0.2 collective-permute-done.19.refs_2_
  68.4 2.8 %collective-permute-done.25.refs_5_ = bf16[32,2560]{1,0:T(8,128)(2,1)S(1)} collective-permute-done((bf16[32,2560]{1,0:T(8,128)(2,1)S(1)}, bf16[32,2560]{1,0:T(8,128)(2,1)S(1)}, u32[]{:S(2)}, u32[]{:S(2)}) %collective-permute-start.25) | collective-permute-done | bytes 163872 | tf_op jit(solution)/shard_map/ppermute | solution.py:38
  71.2 2.5 %collective-permute-done.22.refs_4_ = bf16[32,2560]{1,0:T(8,128)(2,1)S(1)} collective-permute-done((bf16[32,2560]{1,0:T(8,128)(2,1)S(1)}, bf16[32,2560]{1,0:T(8,128)(2,1)S(1)}, u32[]{:S(2)}, u32[]{:S(2)}) %collective-permute-start.22) | collective-permute-done | bytes 163872 | tf_op jit(solution)/shard_map/ppermute | solution.py:42
  73.8 0.1 shard_map.193
  73.9 2.8 %collective-permute-start.26 = (f32[16,2560]{1,0:T(8,128)S(1)}, f32[16,2560]{1,0:T(8,128)S(1)}, u32[]{:S(2)}, u32[]{:S(2)}) collective-permute-start(f32[16,2560]{1,0:T(8,128)S(1)} %get-tuple-element.56), channel_id=1, source_target_pairs={{0,1},{1,0},{2,3},{3,2},{4,5},{5,4},{6,7},{7,6},{8,9},{9,8},{10,11... | collective-permute-start | bytes 491528 | tf_op jit(solution)/shard_map/ppermute | solution.py:34
  76.7 1.0 %collective-permute-done.26.refs_2_ = f32[16,2560]{1,0:T(8,128)S(1)} collective-permute-done((f32[16,2560]{1,0:T(8,128)S(1)}, f32[16,2560]{1,0:T(8,128)S(1)}, u32[]{:S(2)}, u32[]{:S(2)}) %collective-permute-start.26) | collective-permute-done | bytes 163872 | tf_op jit(solution)/shard_map/ppermute | solution.py:34
  77.7 1.7 %shard_map.194 = (bf16[16,5120]{1,0:T(8,128)(2,1)}, f32[4,256]{1,0:T(4,128)}, f32[16,2,256]{2,1,0:T(2,128)S(1)}) custom-call(s32[1]{0:T(128)} %bitcast.refs_0_, f32[16,2560]{1,0:T(8,128)S(1)} %get-tuple-element.55.refs_1_, f32[16,2560]{1,0:T(8,128)S(1)} %collective-permute-done.26.refs_2_, bf16[8,16,640]{2,1,0:T(8,128)(2,1)S(1)} %get-tuple-element.57.refs_3_, ...), custom_call_target="tpu_custom_call" | custom-call | bytes 2097152 | tf_op jit(solution)/shard_map/pallas_call | solution.py:60
  79.4 11.8 %all_to_all.5.refs_0_ = f32[16,2,256]{2,1,0:T(2,128)S(1)} all-to-all(f32[16,2,256]{2,1,0:T(2,128)S(1)} %get-tuple-element.60), channel_id=1, replica_groups=mesh['ctx'=8,'mdl'=16] {'mdl'}, dimensions={0} | all-to-all | bytes 65536 | tf_op jit(solution)/shard_map/all_to_all | solution.py:545
  91.3 0.9 shard_map.195
  (44 shorter events, 0.3 us)
Async XLA Ops:
  0.6 14.3 %copy-start.9 = (f32[5120]{0:T(1024)S(1)}, f32[5120]{0:T(1024)}, u32[]{:S(2)}) copy-start(f32[5120]{0:T(1024)} %param.18) | copy-start | bytes 61444
  0.7 0.9 copy-start.5
  1.6 13.3 %copy-start.10 = (f32[5120]{0:T(1024)S(1)}, f32[5120]{0:T(1024)}, u32[]{:S(2)}) copy-start(f32[5120]{0:T(1024)} %param.17) | copy-start | bytes 61444
  1.7 2.4 %collective-permute-start = (bf16[128,320]{1,0:T(8,128)(2,1)S(1)}, bf16[128,320]{1,0:T(8,128)(2,1)S(1)}, u32[]{:S(2)}, u32[]{:S(2)}) collective-permute-start(bf16[128,320]{1,0:T(8,128)(2,1)S(1)} %get-tuple-element.33), channel_id=1, source_target_pairs={{0,1},{1,0},{2,3},{3,2},{4,5},{5,4},{6,7},{7,6},{8,9},{9,8},{10,11... | collective-permute-start | bytes 245768 | tf_op jit(solution)/shard_map/ppermute | solution.py:34
  4.3 10.1 %collective-permute-start.1 = (bf16[128,640]{1,0:T(8,128)(2,1)S(1)}, bf16[128,640]{1,0:T(8,128)(2,1)S(1)}, u32[]{:S(2)}, u32[]{:S(2)}) collective-permute-start(bf16[128,640]{1,0:T(8,128)(2,1)S(1)} %pad_maximum_fusion.refs_1_), channel_id=1, source_target_pairs={{0,2},{1,3},{2,0},{3,1},{4,6},{5,7},{6,4},{7,5},{8,10},{9,11},{10,... | collective-permute-start | bytes 491528 | tf_op jit(solution)/shard_map/ppermute | solution.py:38
  7.3 8.4 %collective-permute-start.2 = (bf16[128,640]{1,0:T(8,128)(2,1)S(1)}, bf16[128,640]{1,0:T(8,128)(2,1)S(1)}, u32[]{:S(2)}, u32[]{:S(2)}) collective-permute-start(bf16[128,640]{1,0:T(8,128)(2,1)S(1)} %pad_maximum_fusion.refs_1_), channel_id=1, source_target_pairs={{0,4},{1,5},{2,6},{3,7},{4,8},{5,9},{6,10},{7,11},{8,12},{9,13},{1... | collective-permute-start | bytes 491528 | tf_op jit(solution)/shard_map/ppermute | solution.py:42
  9.0 8.7 %collective-permute-start.3 = (bf16[128,640]{1,0:T(8,128)(2,1)S(1)}, bf16[128,640]{1,0:T(8,128)(2,1)S(1)}, u32[]{:S(2)}, u32[]{:S(2)}) collective-permute-start(bf16[128,640]{1,0:T(8,128)(2,1)S(1)} %pad_maximum_fusion.refs_1_), channel_id=1, source_target_pairs={{0,12},{1,13},{2,14},{3,15},{4,0},{5,1},{6,2},{7,3},{8,4},{9,5},{1... | collective-permute-start | bytes 491528 | tf_op jit(solution)/shard_map/ppermute | solution.py:42
  11.1 8.3 %collective-permute-start.4 = (bf16[128,640]{1,0:T(8,128)(2,1)S(1)}, bf16[128,640]{1,0:T(8,128)(2,1)S(1)}, u32[]{:S(2)}, u32[]{:S(2)}) collective-permute-start(bf16[128,640]{1,0:T(8,128)(2,1)S(1)} %pad_maximum_fusion.refs_1_), channel_id=1, source_target_pairs={{0,8},{1,9},{2,10},{3,11},{4,12},{5,13},{6,14},{7,15},{8,0},{9,1},... | collective-permute-start | bytes 491528 | tf_op jit(solution)/shard_map/ppermute | solution.py:42
  12.4 0.9 %copy-start.3 = (bf16[512,256]{1,0:T(8,128)(2,1)S(1)}, bf16[512,256]{1,0:T(8,128)(2,1)}, u32[]{:S(2)}) copy-start(bf16[512,256]{1,0:T(8,128)(2,1)} %refs_0_.3) | copy-start | bytes 786436
  13.4 0.9 %copy-start.4 = (bf16[512,256]{1,0:T(8,128)(2,1)S(1)}, bf16[512,256]{1,0:T(8,128)(2,1)}, u32[]{:S(2)}) copy-start(bf16[512,256]{1,0:T(8,128)(2,1)} %refs_1_.6) | copy-start | bytes 786436
  14.4 15.0 %collective-permute-start.9 = (bf16[512,512]{1,0:T(8,128)(2,1)S(1)}, bf16[512,512]{1,0:T(8,128)(2,1)S(1)}, u32[]{:S(2)}, u32[]{:S(2)}) collective-permute-start(bf16[512,512]{1,0:T(8,128)(2,1)S(1)} %shard_map.180), channel_id=1, source_target_pairs={{0,64},{16,80},{32,96},{48,112},{64,0},{80,16},{96,32},{112,48},{1... | collective-permute-start | bytes 1572872 | tf_op jit(solution)/shard_map/ppermute | solution.py:26
  14.9 8.4 %copy-start = (bf16[256,5120]{1,0:T(8,128)(2,1)S(1)}, bf16[256,5120]{1,0:T(8,128)(2,1)}, u32[]{:S(2)}) copy-start(bf16[256,5120]{1,0:T(8,128)(2,1)} %refs_1_.4) | copy-start | bytes 7864324
  15.0 8.3 %collective-permute-start.5 = (bf16[128,640]{1,0:T(8,128)(2,1)S(1)}, bf16[128,640]{1,0:T(8,128)(2,1)S(1)}, u32[]{:S(2)}, u32[]{:S(2)}) collective-permute-start(bf16[128,640]{1,0:T(8,128)(2,1)S(1)} %collective-permute-done.1.refs_2_.refs_1_), channel_id=1, source_target_pairs={{0,4},{1,5},{2,6},{3,7},{4,8},{5,9},{6,10},{7,11},{8,12},{9,13},{1... | collective-permute-start | bytes 491528 | tf_op jit(solution)/shard_map/ppermute | solution.py:42
  15.8 7.7 %collective-permute-start.6 = (bf16[128,640]{1,0:T(8,128)(2,1)S(1)}, bf16[128,640]{1,0:T(8,128)(2,1)S(1)}, u32[]{:S(2)}, u32[]{:S(2)}) collective-permute-start(bf16[128,640]{1,0:T(8,128)(2,1)S(1)} %collective-permute-done.1.refs_2_.refs_1_), channel_id=1, source_target_pairs={{0,12},{1,13},{2,14},{3,15},{4,0},{5,1},{6,2},{7,3},{8,4},{9,5},{1... | collective-permute-start | bytes 491528 | tf_op jit(solution)/shard_map/ppermute | solution.py:42
  17.7 8.7 %collective-permute-start.7 = (bf16[128,640]{1,0:T(8,128)(2,1)S(1)}, bf16[128,640]{1,0:T(8,128)(2,1)S(1)}, u32[]{:S(2)}, u32[]{:S(2)}) collective-permute-start(bf16[128,640]{1,0:T(8,128)(2,1)S(1)} %collective-permute-done.1.refs_2_.refs_1_), channel_id=1, source_target_pairs={{0,8},{1,9},{2,10},{3,11},{4,12},{5,13},{6,14},{7,15},{8,0},{9,1},... | collective-permute-start | bytes 491528 | tf_op jit(solution)/shard_map/ppermute | solution.py:42
  27.8 4.2 %collective-permute-start.8 = (bf16[128,5120]{1,0:T(8,128)(2,1)S(1)}, bf16[128,5120]{1,0:T(8,128)(2,1)S(1)}, u32[]{:S(2)}, u32[]{:S(2)}) collective-permute-start(bf16[128,5120]{1,0:T(8,128)(2,1)S(1)} %get-tuple-element.38.refs_0_), channel_id=1, source_target_pairs={{0,1},{1,0},{2,3},{3,2},{4,5},{5,4},{6,7},{7,6},{8,9},{9,8},{10,11... | collective-permute-start | bytes 3932168 | tf_op jit(solution)/shard_map/ppermute | solution.py:34
  29.4 27.5 %collective-permute-start.18 = (bf16[256,2560]{1,0:T(8,128)(2,1)S(1)}, bf16[256,2560]{1,0:T(8,128)(2,1)S(1)}, u32[]{:S(2)}, u32[]{:S(2)}) collective-permute-start(bf16[256,2560]{1,0:T(8,128)(2,1)S(1)} %get-tuple-element.46), channel_id=1, source_target_pairs={{0,1},{1,0},{2,3},{3,2},{4,5},{5,4},{6,7},{7,6},{8,9},{9,8},{10,11... | collective-permute-start | bytes 3932168 | tf_op jit(solution)/shard_map/ppermute | solution.py:34
  32.9 7.6 %collective-permute-start.10 = (bf16[256,512]{1,0:T(8,128)(2,1)S(1)}, bf16[256,512]{1,0:T(8,128)(2,1)S(1)}, u32[]{:S(2)}, u32[]{:S(2)}) collective-permute-start(bf16[256,512]{1,0:T(8,128)(2,1)S(1)} %shard_map.183.refs_3_.refs_1_), channel_id=1, source_target_pairs={{0,64},{16,80},{32,96},{48,112},{64,0},{80,16},{96,32},{112,48},{1... | collective-permute-start | bytes 786440 | tf_op jit(solution)/shard_map/ppermute | solution.py:26
  34.0 5.7 %collective-permute-start.13 = (bf16[256,256]{1,0:T(8,128)(2,1)S(1)}, bf16[256,256]{1,0:T(8,128)(2,1)S(1)}, u32[]{:S(2)}, u32[]{:S(2)}) collective-permute-start(bf16[256,256]{1,0:T(8,128)(2,1)S(1)} %shard_map.182.refs_0_), channel_id=1, source_target_pairs={{0,16},{16,32},{32,48},{48,0},{64,80},{80,96},{96,112},{112,64},{1... | collective-permute-start | bytes 393224 | tf_op jit(solution)/shard_map/ppermute | solution.py:30
  35.3 6.6 %collective-permute-start.12 = (bf16[256,256]{1,0:T(8,128)(2,1)S(1)}, bf16[256,256]{1,0:T(8,128)(2,1)S(1)}, u32[]{:S(2)}, u32[]{:S(2)}) collective-permute-start(bf16[256,256]{1,0:T(8,128)(2,1)S(1)} %shard_map.182.refs_0_), channel_id=1, source_target_pairs={{0,48},{16,0},{32,16},{48,32},{64,112},{80,64},{96,80},{112,96},{1... | collective-permute-start | bytes 393224 | tf_op jit(solution)/shard_map/ppermute | solution.py:30
  36.7 6.9 %collective-permute-start.11 = (bf16[256,256]{1,0:T(8,128)(2,1)S(1)}, bf16[256,256]{1,0:T(8,128)(2,1)S(1)}, u32[]{:S(2)}, u32[]{:S(2)}) collective-permute-start(bf16[256,256]{1,0:T(8,128)(2,1)S(1)} %shard_map.182.refs_0_), channel_id=1, source_target_pairs={{0,32},{16,48},{32,0},{48,16},{64,96},{80,112},{96,64},{112,80},{1... | collective-permute-start | bytes 393224 | tf_op jit(solution)/shard_map/ppermute | solution.py:30
  45.0 6.0 %collective-permute-start.16 = (bf16[272,256]{1,0:T(8,128)(2,1)S(1)}, bf16[272,256]{1,0:T(8,128)(2,1)S(1)}, u32[]{:S(2)}, u32[]{:S(2)}) collective-permute-start(bf16[272,256]{1,0:T(8,128)(2,1)S(1)} %shard_map.187.refs_6_), channel_id=1, source_target_pairs={{0,32},{16,48},{32,0},{48,16},{64,96},{80,112},{96,64},{112,80},{1... | collective-permute-start | bytes 417800 | tf_op jit(solution)/shard_map/ppermute | solution.py:30
  47.3 7.3 %collective-permute-start.15 = (bf16[272,256]{1,0:T(8,128)(2,1)S(1)}, bf16[272,256]{1,0:T(8,128)(2,1)S(1)}, u32[]{:S(2)}, u32[]{:S(2)}) collective-permute-start(bf16[272,256]{1,0:T(8,128)(2,1)S(1)} %shard_map.186.refs_5_), channel_id=1, source_target_pairs={{0,16},{16,32},{32,48},{48,0},{64,80},{80,96},{96,112},{112,64},{1... | collective-permute-start | bytes 417800 | tf_op jit(solution)/shard_map/ppermute | solution.py:30
  47.6 7.0 %collective-permute-start.14 = (bf16[272,256]{1,0:T(8,128)(2,1)S(1)}, bf16[272,256]{1,0:T(8,128)(2,1)S(1)}, u32[]{:S(2)}, u32[]{:S(2)}) collective-permute-start(bf16[272,256]{1,0:T(8,128)(2,1)S(1)} %shard_map.185.refs_5_), channel_id=1, source_target_pairs={{0,48},{16,0},{32,16},{48,32},{64,112},{80,64},{96,80},{112,96},{1... | collective-permute-start | bytes 417800 | tf_op jit(solution)/shard_map/ppermute | solution.py:30
  55.2 21.4 %copy-start.11 = (f32[5120]{0:T(1024)S(1)}, f32[5120]{0:T(1024)}, u32[]{:S(2)}) copy-start(f32[5120]{0:T(1024)} %param.19) | copy-start | bytes 61444
  55.2 21.4 %copy-start.12 = (f32[5120]{0:T(1024)S(1)}, f32[5120]{0:T(1024)}, u32[]{:S(2)}) copy-start(f32[5120]{0:T(1024)} %param.26) | copy-start | bytes 61444
  55.2 22.4 %copy-start.1 = (bf16[5120,64]{0,1:T(8,128)(2,1)S(1)}, bf16[5120,64]{0,1:T(8,128)(2,1)}, u32[]{:S(2)}) copy-start(bf16[5120,64]{0,1:T(8,128)(2,1)} %param.27) | copy-start | bytes 1966084
  55.2 22.4 %copy-start.6 = (f32[4,256]{1,0:T(4,128)S(1)}, f32[4,256]{1,0:T(4,128)}, u32[]{:S(2)}) copy-start(f32[4,256]{1,0:T(4,128)} %refs_7_.1) | copy-start | bytes 12292
  55.3 22.4 %copy-start.7 = (f32[4,256]{1,0:T(4,128)S(1)}, f32[4,256]{1,0:T(4,128)}, u32[]{:S(2)}) copy-start(f32[4,256]{1,0:T(4,128)} %refs_8_.1) | copy-start | bytes 12292
  55.3 22.4 %copy-start.8 = (s32[4,1]{0,1:T(1,128)S(1)}, s32[4,1]{0,1:T(1,128)}, u32[]{:S(2)}) copy-start(s32[4,1]{0,1:T(1,128)} %param.30) | copy-start | bytes 52
  55.3 36.0 %copy-start.2 = (bf16[256,1024]{1,0:T(8,128)(2,1)S(1)}, bf16[256,1024]{1,0:T(8,128)(2,1)}, u32[]{:S(2)}) copy-start(bf16[256,1024]{1,0:T(8,128)(2,1)} %refs_1_.7) | copy-start | bytes 1572868
  55.3 2.5 %collective-permute-start.17 = (bf16[256,256]{1,0:T(8,128)(2,1)S(1)}, bf16[256,256]{1,0:T(8,128)(2,1)S(1)}, u32[]{:S(2)}, u32[]{:S(2)}) collective-permute-start(bf16[256,256]{1,0:T(8,128)(2,1)S(1)} %shard_map.189.refs_1_), channel_id=1, source_target_pairs={{0,1},{1,0},{2,3},{3,2},{4,5},{5,4},{6,7},{7,6},{8,9},{9,8},{10,11... | collective-permute-start | bytes 393224 | tf_op jit(solution)/shard_map/ppermute | solution.py:34
  58.6 6.8 %collective-permute-start.23 = (bf16[32,2560]{1,0:T(8,128)(2,1)S(1)}, bf16[32,2560]{1,0:T(8,128)(2,1)S(1)}, u32[]{:S(2)}, u32[]{:S(2)}) collective-permute-start(bf16[32,2560]{1,0:T(8,128)(2,1)S(1)} %get-tuple-element.53), channel_id=1, source_target_pairs={{0,4},{1,5},{2,6},{3,7},{4,8},{5,9},{6,10},{7,11},{8,12},{9,13},{1... | collective-permute-start | bytes 491528 | tf_op jit(solution)/shard_map/ppermute | solution.py:42
  59.5 5.9 %collective-permute-start.24 = (bf16[32,2560]{1,0:T(8,128)(2,1)S(1)}, bf16[32,2560]{1,0:T(8,128)(2,1)S(1)}, u32[]{:S(2)}, u32[]{:S(2)}) collective-permute-start(bf16[32,2560]{1,0:T(8,128)(2,1)S(1)} %get-tuple-element.54), channel_id=1, source_target_pairs={{0,12},{1,13},{2,14},{3,15},{4,0},{5,1},{6,2},{7,3},{8,4},{9,5},{1... | collective-permute-start | bytes 491528 | tf_op jit(solution)/shard_map/ppermute | solution.py:42
  61.4 6.3 %collective-permute-start.21 = (bf16[32,2560]{1,0:T(8,128)(2,1)S(1)}, bf16[32,2560]{1,0:T(8,128)(2,1)S(1)}, u32[]{:S(2)}, u32[]{:S(2)}) collective-permute-start(bf16[32,2560]{1,0:T(8,128)(2,1)S(1)} %get-tuple-element.51), channel_id=1, source_target_pairs={{0,2},{1,3},{2,0},{3,1},{4,6},{5,7},{6,4},{7,5},{8,10},{9,11},{10,... | collective-permute-start | bytes 491528 | tf_op jit(solution)/shard_map/ppermute | solution.py:38
  62.7 5.7 %collective-permute-start.19 = (bf16[32,2560]{1,0:T(8,128)(2,1)S(1)}, bf16[32,2560]{1,0:T(8,128)(2,1)S(1)}, u32[]{:S(2)}, u32[]{:S(2)}) collective-permute-start(bf16[32,2560]{1,0:T(8,128)(2,1)S(1)} %get-tuple-element.48), channel_id=1, source_target_pairs={{0,4},{1,5},{2,6},{3,7},{4,8},{5,9},{6,10},{7,11},{8,12},{9,13},{1... | collective-permute-start | bytes 491528 | tf_op jit(solution)/shard_map/ppermute | solution.py:42
  62.7 5.7 %collective-permute-start.20 = (bf16[32,2560]{1,0:T(8,128)(2,1)S(1)}, bf16[32,2560]{1,0:T(8,128)(2,1)S(1)}, u32[]{:S(2)}, u32[]{:S(2)}) collective-permute-start(bf16[32,2560]{1,0:T(8,128)(2,1)S(1)} %get-tuple-element.49), channel_id=1, source_target_pairs={{0,12},{1,13},{2,14},{3,15},{4,0},{5,1},{6,2},{7,3},{8,4},{9,5},{1... | collective-permute-start | bytes 491528 | tf_op jit(solution)/shard_map/ppermute | solution.py:42
  65.5 5.8 %collective-permute-start.25 = (bf16[32,2560]{1,0:T(8,128)(2,1)S(1)}, bf16[32,2560]{1,0:T(8,128)(2,1)S(1)}, u32[]{:S(2)}, u32[]{:S(2)}) collective-permute-start(bf16[32,2560]{1,0:T(8,128)(2,1)S(1)} %shard_map.192), channel_id=1, source_target_pairs={{0,2},{1,3},{2,0},{3,1},{4,6},{5,7},{6,4},{7,5},{8,10},{9,11},{10,... | collective-permute-start | bytes 491528 | tf_op jit(solution)/shard_map/ppermute | solution.py:38
  67.7 6.0 %collective-permute-start.22 = (bf16[32,2560]{1,0:T(8,128)(2,1)S(1)}, bf16[32,2560]{1,0:T(8,128)(2,1)S(1)}, u32[]{:S(2)}, u32[]{:S(2)}) collective-permute-start(bf16[32,2560]{1,0:T(8,128)(2,1)S(1)} %shard_map.191), channel_id=1, source_target_pairs={{0,8},{1,9},{2,10},{3,11},{4,12},{5,13},{6,14},{7,15},{8,0},{9,1},... | collective-permute-start | bytes 491528 | tf_op jit(solution)/shard_map/ppermute | solution.py:42
  73.9 3.8 %collective-permute-start.26 = (f32[16,2560]{1,0:T(8,128)S(1)}, f32[16,2560]{1,0:T(8,128)S(1)}, u32[]{:S(2)}, u32[]{:S(2)}) collective-permute-start(f32[16,2560]{1,0:T(8,128)S(1)} %get-tuple-element.56), channel_id=1, source_target_pairs={{0,1},{1,0},{2,3},{3,2},{4,5},{5,4},{6,7},{7,6},{8,9},{9,8},{10,11... | collective-permute-start | bytes 491528 | tf_op jit(solution)/shard_map/ppermute | solution.py:34

commit v5 on v4

--- a/solution.py
+++ b/solution.py
@@ -152,11 +152,9 @@
     q_ref[...] = jnp.dot(x_ref[...], wq_ref[...], preferred_element_type=F32).astype(BF)
 
 
-def kv_body(x_ref, wk_ref, wv_ref, half_ref, kv_ref):
-    rows = x_ref.shape[0]
-    kv_ref[:rows] = half_ref[...]
-    kv_ref[rows:, :256] = jnp.dot(x_ref[...], wk_ref[...], preferred_element_type=F32).astype(BF)
-    kv_ref[rows:, 256:] = jnp.dot(x_ref[...], wv_ref[...], preferred_element_type=F32).astype(BF)
+def kv_body(x_ref, wk_ref, wv_ref, kv_ref):
+    kv_ref[:, :256] = jnp.dot(x_ref[...], wk_ref[...], preferred_element_type=F32).astype(BF)
+    kv_ref[:, 256:] = jnp.dot(x_ref[...], wv_ref[...], preferred_element_type=F32).astype(BF)
 
 
 def query_body(core_ref, x_ref, wq_ref, half_ref, q_ref):
@@ -245,13 +243,14 @@
     out_ref[rows:, :] = tail.astype(BF)
 
 
-def kept_body(q_ref, a_ref, b_ref, o_ref, peak_ref, total_ref, out_ref, lse_ref):
+def kept_body(q_ref, *refs):
+    *kv_refs, o_ref, peak_ref, total_ref, out_ref, lse_ref = refs
     both = []
     starts = [
         (peak_ref[h][:, :1], total_ref[h][:, :1], o_ref[:, h * HD : (h + 1) * HD]) for h in range(2)
     ]
     for h in range(2):
-        peak, total, summed = attend(q_ref, (a_ref, b_ref), (h,), starts)[0]
+        peak, total, summed = attend(q_ref, kv_refs, (h,), starts)[0]
         out_ref[:, h * HD : (h + 1) * HD] = summed * (1.0 / total)
         both.append(log_total(peak, total))
     lse_ref[...] = turned(*both)
@@ -332,15 +331,16 @@
         square = square + mix * mix
         mixed.append(mix)
     inverse = lax.rsqrt(jnp.sum(square, -1, keepdims=True) / (blocks * width) + 1e-06)
-    acc = jnp.zeros(vel.shape, F32)
-    for b in range(blocks):
-        normed = (mixed[b] * inverse * (1.0 + scale_ref[b : b + 1])).astype(BF)
-        acc = acc + lax.dot_general(
-            normed,
-            wf_ref[:, b * width : (b + 1) * width],
-            (((1,), (1,)), ((), ())),
-            preferred_element_type=F32,
-        )
+    normed = jnp.concatenate(
+        [
+            (mixed[b] * inverse * (1.0 + scale_ref[b : b + 1])).astype(BF)
+            for b in range(blocks)
+        ],
+        -1,
+    )
+    acc = lax.dot_general(
+        normed, wf_ref[...], (((1,), (1,)), ((), ())), preferred_element_type=F32
+    )
     vel[...] = acc
     tiles = state_ref.shape[0]
     lat = acc.shape[1]
@@ -453,11 +453,11 @@
         flops=30000000000,
         nbytes=8 * MIB,
     )
-    kv = call(
+    kv_rest = call(
         kv_body,
-        shape((count, 2 * cols), BF),
-        (normed_in, weights[1], weights[2], kv_half),
-        flops=2 * rows * w_query.shape[0] * 2 * cols,
+        shape((rows, 2 * cols), BF),
+        (normed_in, weights[1], weights[2]),
+        flops=1 << 34,
         nbytes=5 * MIB,
     )
     query = call(
@@ -468,7 +468,7 @@
         flops=2 * rows * w_query.shape[0] * cols,
         nbytes=3 * MIB,
     )
-    kv_in = y_swap(kv)
+    fresh = [kv_half, kv_rest, y_swap(kv_half), y_swap(kv_rest)]
     query_in = [x_send(query, by) for by in STEPS]
 
     stats = call(
@@ -487,7 +487,7 @@
         before = call(
             sent_body,
             shape((count + 16, cols), BF),
-            (q, cached, cached_in, kv, kv_in),
+            (q, cached, cached_in, *fresh),
             flops=MIB,
             nbytes=MIB,
             after=(before,),
@@ -496,7 +496,7 @@
     kept = call(
         kept_body,
         (shape((count, cols), F32), shape((8, count), F32)),
-        (query, kv, kv_in, *stats),
+        (query, *fresh, *stats),
         flops=MIB,
         nbytes=MIB,
         after=(before,),
@@ -512,13 +512,13 @@
         nbytes=4 * MIB,
         scratch=[pltpu.VMEM((count, 2 * cols), BF)],
     )
-    def added(*parts):
-        return call(add_body, shape(parts[0].shape, BF), parts)
+    def added(*parts, flops=0):
+        return call(add_body, shape(parts[0].shape, BF), parts, flops=flops)
 
     across = pair_swap(projected[7])
     relayed = [z_send(projected[5], 1), z_send(projected[6], 3)]
     direct = [z_send(projected[2], 1), z_send(projected[3], 3)]
-    direct.append(z_send(added(projected[4], across), 2))
+    direct.append(z_send(added(projected[4], across, flops=1 << 35), 2))
     passed = pair_swap(added(projected[1], *relayed))
     ours, theirs = call(
         sum_body,

time: 92.3 us -> 92 us (level)
    ppermute x6, waiting for transfers between devices: 4.57 us -> 6.38 us  [x_send(): lax.ppermute(a, 'ctx', [(c, c // 4 * 4 + (c + by) % 4) for c in range(8)])]
    ppermute x6, starting transfers between devices: 9.29 us -> 7.56 us  [x_send(): lax.ppermute(a, 'ctx', [(c, c // 4 * 4 + (c + by) % 4) for c in range(8)])]
  transfers between devices with their start and end apart: 27 -> 28, of which waited for: 15 -> 15; matrix products, arithmetic and copies ran while one was open for 0% -> 0% of each run, Pallas kernels for 15% -> 15%
where the time goes in v5:
time: 92 us; the launch traced here: 91.8 us
  starting transfers between devices  37.4 us (41%)
  waiting for transfers between devices  20.8 us (23%)
  Pallas kernels  17.8 us (19%)
  blocking collectives  11.9 us (13%)
  local copies, waits for them, and re-layouts  2.88 us (3%)
  between operations  0.93 us (1%)
    pallas_call x21, Pallas kernels, call(): pl.pallas_call(run, out_shape=outs, in_specs=place + [pl.BlockSpec(memory...  17.8 us
    ppermute x11, starting transfers between devices, z_send(): return lax.ppermute(a, 'mdl', [(m, (m + 4 * by) % 16) for m in range(16)])  14.3 us
    all_to_all x1, blocking collectives, shards(): lax.all_to_all(slot_rows, 'mdl', split_axis=0, concat_axis=0, tiled=True)  11.9 us
    ppermute x5, starting transfers between devices, core_swap(): return lax.ppermute(a, 'mdl', CORE_SWAP)  7.84 us
    ppermute x6, starting transfers between devices, x_send(): lax.ppermute(a, 'ctx', [(c, c // 4 * 4 + (c + by) % 4) for c in range(8)])  7.56 us
    ppermute x11, waiting for transfers between devices, z_send(): return lax.ppermute(a, 'mdl', [(m, (m + 4 * by) % 16) for m in range(16)])  7.42 us
    ppermute x6, waiting for transfers between devices, x_send(): lax.ppermute(a, 'ctx', [(c, c // 4 * 4 + (c + by) % 4) for c in range(8)])  6.38 us
    ppermute x3, starting transfers between devices, pair_swap(): return lax.ppermute(a, 'mdl', PAIR_SWAP)  6.13 us
  transfers between devices with their start and end apart: 28, of which 15 were waited for; matrix products, arithmetic and copies ran while one was open for 0% of the time, Pallas kernels for 15%

profile of v5, /device:TPU:1, one launch (start us, length us, event | category | flops | bytes accessed | tf_op | source)
XLA Modules:
  0.0 91.8 jit_solution(17869688642137721198)
XLA Ops:
  0.7 0.9 copy-done.5
  1.6 0.1 shard_map.175
  1.7 1.5 %collective-permute-start = (bf16[128,320]{1,0:T(8,128)(2,1)S(1)}, bf16[128,320]{1,0:T(8,128)(2,1)S(1)}, u32[]{:S(2)}, u32[]{:S(2)}) collective-permute-start(bf16[128,320]{1,0:T(8,128)(2,1)S(1)} %get-tuple-element.33), channel_id=1, source_target_pairs={{0,1},{1,0},{2,3},{3,2},{4,5},{5,4},{6,7},{7,6},{8,9},{9,8},{10,11... | collective-permute-start | bytes 245768 | tf_op jit(solution)/shard_map/ppermute | solution.py:34
  3.2 0.9 %collective-permute-done = bf16[128,320]{1,0:T(8,128)(2,1)S(1)} collective-permute-done((bf16[128,320]{1,0:T(8,128)(2,1)S(1)}, bf16[128,320]{1,0:T(8,128)(2,1)S(1)}, u32[]{:S(2)}, u32[]{:S(2)}) %collective-permute-start) | collective-permute-done | bytes 81952 | tf_op jit(solution)/shard_map/ppermute | solution.py:34
  4.2 0.1 pad_maximum_fusion.refs_1_
  4.3 3.1 %collective-permute-start.1 = (bf16[128,640]{1,0:T(8,128)(2,1)S(1)}, bf16[128,640]{1,0:T(8,128)(2,1)S(1)}, u32[]{:S(2)}, u32[]{:S(2)}) collective-permute-start(bf16[128,640]{1,0:T(8,128)(2,1)S(1)} %pad_maximum_fusion.refs_1_), channel_id=1, source_target_pairs={{0,2},{1,3},{2,0},{3,1},{4,6},{5,7},{6,4},{7,5},{8,10},{9,11},{10,... | collective-permute-start | bytes 491528 | tf_op jit(solution)/shard_map/ppermute | solution.py:38
  7.3 1.6 %collective-permute-start.2 = (bf16[128,640]{1,0:T(8,128)(2,1)S(1)}, bf16[128,640]{1,0:T(8,128)(2,1)S(1)}, u32[]{:S(2)}, u32[]{:S(2)}) collective-permute-start(bf16[128,640]{1,0:T(8,128)(2,1)S(1)} %pad_maximum_fusion.refs_1_), channel_id=1, source_target_pairs={{0,4},{1,5},{2,6},{3,7},{4,8},{5,9},{6,10},{7,11},{8,12},{9,13},{1... | collective-permute-start | bytes 491528 | tf_op jit(solution)/shard_map/ppermute | solution.py:42
  9.0 2.1 %collective-permute-start.3 = (bf16[128,640]{1,0:T(8,128)(2,1)S(1)}, bf16[128,640]{1,0:T(8,128)(2,1)S(1)}, u32[]{:S(2)}, u32[]{:S(2)}) collective-permute-start(bf16[128,640]{1,0:T(8,128)(2,1)S(1)} %pad_maximum_fusion.refs_1_), channel_id=1, source_target_pairs={{0,12},{1,13},{2,14},{3,15},{4,0},{5,1},{6,2},{7,3},{8,4},{9,5},{1... | collective-permute-start | bytes 491528 | tf_op jit(solution)/shard_map/ppermute | solution.py:42
  11.1 1.3 %collective-permute-start.4 = (bf16[128,640]{1,0:T(8,128)(2,1)S(1)}, bf16[128,640]{1,0:T(8,128)(2,1)S(1)}, u32[]{:S(2)}, u32[]{:S(2)}) collective-permute-start(bf16[128,640]{1,0:T(8,128)(2,1)S(1)} %pad_maximum_fusion.refs_1_), channel_id=1, source_target_pairs={{0,8},{1,9},{2,10},{3,11},{4,12},{5,13},{6,14},{7,15},{8,0},{9,1},... | collective-permute-start | bytes 491528 | tf_op jit(solution)/shard_map/ppermute | solution.py:42
  12.4 0.9 %copy-done.3 = bf16[512,256]{1,0:T(8,128)(2,1)S(1)} copy-done((bf16[512,256]{1,0:T(8,128)(2,1)S(1)}, bf16[512,256]{1,0:T(8,128)(2,1)}, u32[]{:S(2)}) %copy-start.3) | copy-done | bytes 262168
  13.4 0.9 %copy-done.4 = bf16[512,256]{1,0:T(8,128)(2,1)S(1)} copy-done((bf16[512,256]{1,0:T(8,128)(2,1)S(1)}, bf16[512,256]{1,0:T(8,128)(2,1)}, u32[]{:S(2)}) %copy-start.4) | copy-done | bytes 262168
  14.4 0.5 collective-permute-start.9
  15.0 0.8 collective-permute-start.5
  15.8 1.9 %collective-permute-start.6 = (bf16[128,640]{1,0:T(8,128)(2,1)S(1)}, bf16[128,640]{1,0:T(8,128)(2,1)S(1)}, u32[]{:S(2)}, u32[]{:S(2)}) collective-permute-start(bf16[128,640]{1,0:T(8,128)(2,1)S(1)} %collective-permute-done.1.refs_2_.refs_1_), channel_id=1, source_target_pairs={{0,12},{1,13},{2,14},{3,15},{4,0},{5,1},{6,2},{7,3},{8,4},{9,5},{1... | collective-permute-start | bytes 491528 | tf_op jit(solution)/shard_map/ppermute | solution.py:42
  17.7 0.5 collective-permute-start.7
  18.2 1.3 %collective-permute-done.4.refs_5_ = bf16[128,640]{1,0:T(8,128)(2,1)S(1)} collective-permute-done((bf16[128,640]{1,0:T(8,128)(2,1)S(1)}, bf16[128,640]{1,0:T(8,128)(2,1)S(1)}, u32[]{:S(2)}, u32[]{:S(2)}) %collective-permute-start.4) | collective-permute-done | bytes 163872 | tf_op jit(solution)/shard_map/ppermute | solution.py:42
  19.4 3.3 %shard_map.177 = (bf16[5120,256]{1,0:T(8,128)(2,1)S(1)}, bf16[5120,256]{1,0:T(8,128)(2,1)S(1)}, bf16[5120,256]{1,0:T(8,128)(2,1)S(1)}) custom-call(bf16[5120,256]{1,0:T(8,128)(2,1)} %refs_0_.2, bf16[5120,256]{1,0:T(8,128)(2,1)} %refs_1_.5, bf16[5120,256]{1,0:T(8,128)(2,1)} %refs_2_.1, bf16[128,640]{1,0:T(8,128)(2,1)S(1)} %collective-permute-done.2.refs_3_, ...), custom_call_target="tpu_custom_call" | custom-call | flops 5000000000 | bytes 8388608 | tf_op jit(solution)/shard_map/pallas_call | solution.py:60
  22.8 0.5 collective-permute-done.5.refs_2_.refs_6_
  23.3 0.2 shard_map.176
  23.5 3.0 %collective-permute-done.7.refs_8_ = bf16[128,640]{1,0:T(8,128)(2,1)S(1)} collective-permute-done((bf16[128,640]{1,0:T(8,128)(2,1)S(1)}, bf16[128,640]{1,0:T(8,128)(2,1)S(1)}, u32[]{:S(2)}, u32[]{:S(2)}) %collective-permute-start.7) | collective-permute-done | bytes 163872 | tf_op jit(solution)/shard_map/ppermute | solution.py:42
  26.5 1.3 %shard_map.178 = (bf16[128,5120]{1,0:T(8,128)(2,1)S(1)}, bf16[8,16,640]{2,1,0:T(8,128)(2,1)S(1)}) custom-call(s32[1]{0:T(128)} %bitcast.1.refs_0_, bf16[128,640]{1,0:T(8,128)(2,1)S(1)} %pad_maximum_fusion.refs_1_, bf16[128,640]{1,0:T(8,128)(2,1)S(1)} %collective-permute-done.1.refs_2_.refs_1_, bf16[128,640]{1,0:T(8,128)(2,1)S(1)} %collective-permute-done.2.refs_3_, ...), custom_call_target="tpu_custom_call" | custom-call | flops 1048576 | bytes 1048576 | tf_op jit(solution)/shard_map/pallas_call | solution.py:60
  27.8 1.6 %collective-permute-start.8 = (bf16[128,5120]{1,0:T(8,128)(2,1)S(1)}, bf16[128,5120]{1,0:T(8,128)(2,1)S(1)}, u32[]{:S(2)}, u32[]{:S(2)}) collective-permute-start(bf16[128,5120]{1,0:T(8,128)(2,1)S(1)} %get-tuple-element.38.refs_0_), channel_id=1, source_target_pairs={{0,1},{1,0},{2,3},{3,2},{4,5},{5,4},{6,7},{7,6},{8,9},{9,8},{10,11... | collective-permute-start | bytes 3932168 | tf_op jit(solution)/shard_map/ppermute | solution.py:34
  29.4 0.1 collective-permute-start.19
  29.4 1.2 %shard_map.181 = (bf16[128,512]{1,0:T(8,128)(2,1)S(1)}, bf16[128,256]{1,0:T(8,128)(2,1)S(1)}) custom-call(bf16[128,5120]{1,0:T(8,128)(2,1)S(1)} %get-tuple-element.38.refs_0_, bf16[5120,256]{1,0:T(8,128)(2,1)S(1)} %get-tuple-element.36.refs_13_.refs_1_, bf16[5120,256]{1,0:T(8,128)(2,1)S(1)} %get-tuple-element.37.refs_14_.refs_2_, ...), custom_call_target="tpu_custom_call" | custom-call | flops 30000001024 | bytes 8388608 | tf_op jit(solution)/shard_map/pallas_call | solution.py:60
  30.7 0.6 collective-permute-start.10
  31.3 0.7 collective-permute-done.8.refs_1_.refs_0_
  32.0 0.8 shard_map.183.refs_4_.refs_2_
  32.9 0.6 collective-permute-start.11
  33.4 0.5 shard_map.182.refs_0_
  34.0 1.3 %collective-permute-start.14 = (bf16[256,256]{1,0:T(8,128)(2,1)S(1)}, bf16[256,256]{1,0:T(8,128)(2,1)S(1)}, u32[]{:S(2)}, u32[]{:S(2)}) collective-permute-start(bf16[256,256]{1,0:T(8,128)(2,1)S(1)} %shard_map.182.refs_0_), channel_id=1, source_target_pairs={{0,16},{16,32},{32,48},{48,0},{64,80},{80,96},{96,112},{112,64},{1... | collective-permute-start | bytes 393224 | tf_op jit(solution)/shard_map/ppermute | solution.py:30
  35.2 1.5 %collective-permute-start.13 = (bf16[256,256]{1,0:T(8,128)(2,1)S(1)}, bf16[256,256]{1,0:T(8,128)(2,1)S(1)}, u32[]{:S(2)}, u32[]{:S(2)}) collective-permute-start(bf16[256,256]{1,0:T(8,128)(2,1)S(1)} %shard_map.182.refs_0_), channel_id=1, source_target_pairs={{0,48},{16,0},{32,16},{48,32},{64,112},{80,64},{96,80},{112,96},{1... | collective-permute-start | bytes 393224 | tf_op jit(solution)/shard_map/ppermute | solution.py:30
  36.7 1.5 %collective-permute-start.12 = (bf16[256,256]{1,0:T(8,128)(2,1)S(1)}, bf16[256,256]{1,0:T(8,128)(2,1)S(1)}, u32[]{:S(2)}, u32[]{:S(2)}) collective-permute-start(bf16[256,256]{1,0:T(8,128)(2,1)S(1)} %shard_map.182.refs_0_), channel_id=1, source_target_pairs={{0,32},{16,48},{32,0},{48,16},{64,96},{80,112},{96,64},{112,80},{1... | collective-permute-start | bytes 393224 | tf_op jit(solution)/shard_map/ppermute | solution.py:30
  38.2 0.9 %shard_map.184 = (f32[256,256]{1,0:T(8,128)S(1)}, f32[2,256,128]{2,1,0:T(8,128)S(1)}, f32[2,256,128]{2,1,0:T(8,128)S(1)}) custom-call(bf16[256,256]{1,0:T(8,128)(2,1)S(1)} %shard_map.182.refs_0_, bf16[512,512]{1,0:T(8,128)(2,1)S(1)} %shard_map.179.refs_0_.refs_1_, bf16[512,512]{1,0:T(8,128)(2,1)S(1)} %collective-permute-done.9.refs_4_.refs_2_), custom_call_target="tpu_custom_call" | custom-call | flops 1048576 | bytes 1048576 | tf_op jit(solution)/shard_map/pallas_call | solution.py:60
  39.2 0.4 collective-permute-done.14.refs_0_
  39.5 1.4 %shard_map.185.refs_7_ = bf16[272,256]{1,0:T(8,128)(2,1)S(1)} custom-call(bf16[256,256]{1,0:T(8,128)(2,1)S(1)} %collective-permute-done.14.refs_0_, bf16[512,512]{1,0:T(8,128)(2,1)S(1)} %shard_map.179.refs_0_.refs_1_, bf16[512,512]{1,0:T(8,128)(2,1)S(1)} %collective-permute-done.9.refs_4_.refs_2_, bf16[128,512]{1,0:T(8,128)(2,1)S(1)} %get-tuple-element.40.refs_3_.refs_1_, ...), custom_call_target="tpu_custom_call" | custom-call | flops 1048576 | bytes 1048576 | tf_op jit(solution)/shard_map/pallas_call | solution.py:60
  40.9 1.4 %shard_map.186.refs_7_ = bf16[272,256]{1,0:T(8,128)(2,1)S(1)} custom-call(bf16[256,256]{1,0:T(8,128)(2,1)S(1)} %collective-permute-done.13.refs_0_, bf16[512,512]{1,0:T(8,128)(2,1)S(1)} %shard_map.179.refs_0_.refs_1_, bf16[512,512]{1,0:T(8,128)(2,1)S(1)} %collective-permute-done.9.refs_4_.refs_2_, bf16[128,512]{1,0:T(8,128)(2,1)S(1)} %get-tuple-element.40.refs_3_.refs_1_, ...), custom_call_target="tpu_custom_call" | custom-call | flops 1048576 | bytes 1048576 | tf_op jit(solution)/shard_map/pallas_call | solution.py:60
  42.3 1.2 %collective-permute-done.12.refs_0_ = bf16[256,256]{1,0:T(8,128)(2,1)S(1)} collective-permute-done((bf16[256,256]{1,0:T(8,128)(2,1)S(1)}, bf16[256,256]{1,0:T(8,128)(2,1)S(1)}, u32[]{:S(2)}, u32[]{:S(2)}) %collective-permute-start.12) | collective-permute-done | bytes 131104 | tf_op jit(solution)/shard_map/ppermute | solution.py:30
  43.5 1.4 %shard_map.187.refs_8_ = bf16[272,256]{1,0:T(8,128)(2,1)S(1)} custom-call(bf16[256,256]{1,0:T(8,128)(2,1)S(1)} %collective-permute-done.12.refs_0_, bf16[512,512]{1,0:T(8,128)(2,1)S(1)} %shard_map.179.refs_0_.refs_1_, bf16[512,512]{1,0:T(8,128)(2,1)S(1)} %collective-permute-done.9.refs_4_.refs_2_, bf16[128,512]{1,0:T(8,128)(2,1)S(1)} %get-tuple-element.40.refs_3_.refs_1_, ...), custom_call_target="tpu_custom_call" | custom-call | flops 1048576 | bytes 1048576 | tf_op jit(solution)/shard_map/pallas_call | solution.py:60
  44.9 0.6 collective-permute-start.17
  45.5 1.2 %collective-permute-start.16 = (bf16[272,256]{1,0:T(8,128)(2,1)S(1)}, bf16[272,256]{1,0:T(8,128)(2,1)S(1)}, u32[]{:S(2)}, u32[]{:S(2)}) collective-permute-start(bf16[272,256]{1,0:T(8,128)(2,1)S(1)} %shard_map.186.refs_7_), channel_id=1, source_target_pairs={{0,16},{16,32},{32,48},{48,0},{64,80},{80,96},{96,112},{112,64},{1... | collective-permute-start | bytes 417800 | tf_op jit(solution)/shard_map/ppermute | solution.py:30
  46.8 1.5 %collective-permute-start.15 = (bf16[272,256]{1,0:T(8,128)(2,1)S(1)}, bf16[272,256]{1,0:T(8,128)(2,1)S(1)}, u32[]{:S(2)}, u32[]{:S(2)}) collective-permute-start(bf16[272,256]{1,0:T(8,128)(2,1)S(1)} %shard_map.185.refs_7_), channel_id=1, source_target_pairs={{0,48},{16,0},{32,16},{48,32},{64,112},{80,64},{96,80},{112,96},{1... | collective-permute-start | bytes 417800 | tf_op jit(solution)/shard_map/ppermute | solution.py:30
  48.2 0.9 %shard_map.188 = (f32[256,256]{1,0:T(8,128)S(1)}, f32[8,256]{1,0:T(8,128)S(1)}) custom-call(bf16[256,256]{1,0:T(8,128)(2,1)S(1)} %shard_map.182.refs_0_, bf16[128,512]{1,0:T(8,128)(2,1)S(1)} %get-tuple-element.40.refs_3_.refs_1_, bf16[128,512]{1,0:T(8,128)(2,1)S(1)} %shard_map.183.refs_4_.refs_2_, ...), custom_call_target="tpu_custom_call" | custom-call | flops 1048576 | bytes 1048576 | tf_op jit(solution)/shard_map/pallas_call | solution.py:60
  49.1 1.4 %collective-permute-done.17.refs_4_ = bf16[272,256]{1,0:T(8,128)(2,1)S(1)} collective-permute-done((bf16[272,256]{1,0:T(8,128)(2,1)S(1)}, bf16[272,256]{1,0:T(8,128)(2,1)S(1)}, u32[]{:S(2)}, u32[]{:S(2)}) %collective-permute-start.17) | collective-permute-done | bytes 139296 | tf_op jit(solution)/shard_map/ppermute | solution.py:30
  50.5 3.4 %collective-permute-done.16.refs_3_ = bf16[272,256]{1,0:T(8,128)(2,1)S(1)} collective-permute-done((bf16[272,256]{1,0:T(8,128)(2,1)S(1)}, bf16[272,256]{1,0:T(8,128)(2,1)S(1)}, u32[]{:S(2)}, u32[]{:S(2)}) %collective-permute-start.16) | collective-permute-done | bytes 139296 | tf_op jit(solution)/shard_map/ppermute | solution.py:30
  54.0 0.6 shard_map.189.refs_1_
  54.5 1.9 %collective-permute-start.18 = (bf16[256,256]{1,0:T(8,128)(2,1)S(1)}, bf16[256,256]{1,0:T(8,128)(2,1)S(1)}, u32[]{:S(2)}, u32[]{:S(2)}) collective-permute-start(bf16[256,256]{1,0:T(8,128)(2,1)S(1)} %shard_map.189.refs_1_), channel_id=1, source_target_pairs={{0,1},{1,0},{2,3},{3,2},{4,5},{5,4},{6,7},{7,6},{8,9},{9,8},{10,11... | collective-permute-start | bytes 393224 | tf_op jit(solution)/shard_map/ppermute | solution.py:34
  56.4 1.0 %collective-permute-done.18.refs_2_ = bf16[256,256]{1,0:T(8,128)(2,1)S(1)} collective-permute-done((bf16[256,256]{1,0:T(8,128)(2,1)S(1)}, bf16[256,256]{1,0:T(8,128)(2,1)S(1)}, u32[]{:S(2)}, u32[]{:S(2)}) %collective-permute-start.18) | collective-permute-done | bytes 131104 | tf_op jit(solution)/shard_map/ppermute | solution.py:34
  57.4 0.8 shard_map.190
  58.3 0.9 %collective-permute-start.24 = (bf16[32,2560]{1,0:T(8,128)(2,1)S(1)}, bf16[32,2560]{1,0:T(8,128)(2,1)S(1)}, u32[]{:S(2)}, u32[]{:S(2)}) collective-permute-start(bf16[32,2560]{1,0:T(8,128)(2,1)S(1)} %get-tuple-element.53), channel_id=1, source_target_pairs={{0,4},{1,5},{2,6},{3,7},{4,8},{5,9},{6,10},{7,11},{8,12},{9,13},{1... | collective-permute-start | bytes 491528 | tf_op jit(solution)/shard_map/ppermute | solution.py:42
  59.2 1.8 %collective-permute-start.25 = (bf16[32,2560]{1,0:T(8,128)(2,1)S(1)}, bf16[32,2560]{1,0:T(8,128)(2,1)S(1)}, u32[]{:S(2)}, u32[]{:S(2)}) collective-permute-start(bf16[32,2560]{1,0:T(8,128)(2,1)S(1)} %get-tuple-element.54), channel_id=1, source_target_pairs={{0,12},{1,13},{2,14},{3,15},{4,0},{5,1},{6,2},{7,3},{8,4},{9,5},{1... | collective-permute-start | bytes 491528 | tf_op jit(solution)/shard_map/ppermute | solution.py:42
  61.0 1.4 %collective-permute-start.22 = (bf16[32,2560]{1,0:T(8,128)(2,1)S(1)}, bf16[32,2560]{1,0:T(8,128)(2,1)S(1)}, u32[]{:S(2)}, u32[]{:S(2)}) collective-permute-start(bf16[32,2560]{1,0:T(8,128)(2,1)S(1)} %get-tuple-element.51), channel_id=1, source_target_pairs={{0,2},{1,3},{2,0},{3,1},{4,6},{5,7},{6,4},{7,5},{8,10},{9,11},{10,... | collective-permute-start | bytes 491528 | tf_op jit(solution)/shard_map/ppermute | solution.py:38
  62.4 2.7 %collective-permute-start.21 = (bf16[32,2560]{1,0:T(8,128)(2,1)S(1)}, bf16[32,2560]{1,0:T(8,128)(2,1)S(1)}, u32[]{:S(2)}, u32[]{:S(2)}) collective-permute-start(bf16[32,2560]{1,0:T(8,128)(2,1)S(1)} %get-tuple-element.49), channel_id=1, source_target_pairs={{0,12},{1,13},{2,14},{3,15},{4,0},{5,1},{6,2},{7,3},{8,4},{9,5},{1... | collective-permute-start | bytes 491528 | tf_op jit(solution)/shard_map/ppermute | solution.py:42
  65.2 1.6 %collective-permute-start.26 = (bf16[32,2560]{1,0:T(8,128)(2,1)S(1)}, bf16[32,2560]{1,0:T(8,128)(2,1)S(1)}, u32[]{:S(2)}, u32[]{:S(2)}) collective-permute-start(bf16[32,2560]{1,0:T(8,128)(2,1)S(1)} %shard_map.192), channel_id=1, source_target_pairs={{0,2},{1,3},{2,0},{3,1},{4,6},{5,7},{6,4},{7,5},{8,10},{9,11},{10,... | collective-permute-start | bytes 491528 | tf_op jit(solution)/shard_map/ppermute | solution.py:38
  66.8 0.5 collective-permute-done.22.refs_1_
  67.4 0.6 collective-permute-start.23
  68.0 0.1 collective-permute-done.20.refs_2_
  68.1 2.8 %collective-permute-done.26.refs_5_ = bf16[32,2560]{1,0:T(8,128)(2,1)S(1)} collective-permute-done((bf16[32,2560]{1,0:T(8,128)(2,1)S(1)}, bf16[32,2560]{1,0:T(8,128)(2,1)S(1)}, u32[]{:S(2)}, u32[]{:S(2)}) %collective-permute-start.26) | collective-permute-done | bytes 163872 | tf_op jit(solution)/shard_map/ppermute | solution.py:38
  70.9 2.5 %collective-permute-done.23.refs_4_ = bf16[32,2560]{1,0:T(8,128)(2,1)S(1)} collective-permute-done((bf16[32,2560]{1,0:T(8,128)(2,1)S(1)}, bf16[32,2560]{1,0:T(8,128)(2,1)S(1)}, u32[]{:S(2)}, u32[]{:S(2)}) %collective-permute-start.23) | collective-permute-done | bytes 163872 | tf_op jit(solution)/shard_map/ppermute | solution.py:42
  73.4 0.1 shard_map.193
  73.6 2.8 %collective-permute-start.27 = (f32[16,2560]{1,0:T(8,128)S(1)}, f32[16,2560]{1,0:T(8,128)S(1)}, u32[]{:S(2)}, u32[]{:S(2)}) collective-permute-start(f32[16,2560]{1,0:T(8,128)S(1)} %get-tuple-element.56), channel_id=1, source_target_pairs={{0,1},{1,0},{2,3},{3,2},{4,5},{5,4},{6,7},{7,6},{8,9},{9,8},{10,11... | collective-permute-start | bytes 491528 | tf_op jit(solution)/shard_map/ppermute | solution.py:34
  76.4 1.0 %collective-permute-done.27.refs_2_ = f32[16,2560]{1,0:T(8,128)S(1)} collective-permute-done((f32[16,2560]{1,0:T(8,128)S(1)}, f32[16,2560]{1,0:T(8,128)S(1)}, u32[]{:S(2)}, u32[]{:S(2)}) %collective-permute-start.27) | collective-permute-done | bytes 163872 | tf_op jit(solution)/shard_map/ppermute | solution.py:34
  77.4 1.7 %shard_map.194 = (bf16[16,5120]{1,0:T(8,128)(2,1)}, f32[4,256]{1,0:T(4,128)}, f32[16,2,256]{2,1,0:T(2,128)S(1)}) custom-call(s32[1]{0:T(128)} %bitcast.refs_0_, f32[16,2560]{1,0:T(8,128)S(1)} %get-tuple-element.55.refs_1_, f32[16,2560]{1,0:T(8,128)S(1)} %collective-permute-done.27.refs_2_, bf16[8,16,640]{2,1,0:T(8,128)(2,1)S(1)} %get-tuple-element.57.refs_3_, ...), custom_call_target="tpu_custom_call" | custom-call | bytes 2097152 | tf_op jit(solution)/shard_map/pallas_call | solution.py:60
  79.1 11.9 %all_to_all.5.refs_0_ = f32[16,2,256]{2,1,0:T(2,128)S(1)} all-to-all(f32[16,2,256]{2,1,0:T(2,128)S(1)} %get-tuple-element.60), channel_id=1, replica_groups=mesh['ctx'=8,'mdl'=16] {'mdl'}, dimensions={0} | all-to-all | bytes 65536 | tf_op jit(solution)/shard_map/all_to_all | solution.py:545
  90.9 0.9 shard_map.195
  (46 shorter events, 0.3 us)
Async XLA Ops:
  0.6 14.3 %copy-start.9 = (f32[5120]{0:T(1024)S(1)}, f32[5120]{0:T(1024)}, u32[]{:S(2)}) copy-start(f32[5120]{0:T(1024)} %param.18) | copy-start | bytes 61444
  0.7 0.9 copy-start.5
  1.6 13.3 %copy-start.10 = (f32[5120]{0:T(1024)S(1)}, f32[5120]{0:T(1024)}, u32[]{:S(2)}) copy-start(f32[5120]{0:T(1024)} %param.17) | copy-start | bytes 61444
  1.7 2.4 %collective-permute-start = (bf16[128,320]{1,0:T(8,128)(2,1)S(1)}, bf16[128,320]{1,0:T(8,128)(2,1)S(1)}, u32[]{:S(2)}, u32[]{:S(2)}) collective-permute-start(bf16[128,320]{1,0:T(8,128)(2,1)S(1)} %get-tuple-element.33), channel_id=1, source_target_pairs={{0,1},{1,0},{2,3},{3,2},{4,5},{5,4},{6,7},{7,6},{8,9},{9,8},{10,11... | collective-permute-start | bytes 245768 | tf_op jit(solution)/shard_map/ppermute | solution.py:34
  4.3 10.1 %collective-permute-start.1 = (bf16[128,640]{1,0:T(8,128)(2,1)S(1)}, bf16[128,640]{1,0:T(8,128)(2,1)S(1)}, u32[]{:S(2)}, u32[]{:S(2)}) collective-permute-start(bf16[128,640]{1,0:T(8,128)(2,1)S(1)} %pad_maximum_fusion.refs_1_), channel_id=1, source_target_pairs={{0,2},{1,3},{2,0},{3,1},{4,6},{5,7},{6,4},{7,5},{8,10},{9,11},{10,... | collective-permute-start | bytes 491528 | tf_op jit(solution)/shard_map/ppermute | solution.py:38
  7.3 8.4 %collective-permute-start.2 = (bf16[128,640]{1,0:T(8,128)(2,1)S(1)}, bf16[128,640]{1,0:T(8,128)(2,1)S(1)}, u32[]{:S(2)}, u32[]{:S(2)}) collective-permute-start(bf16[128,640]{1,0:T(8,128)(2,1)S(1)} %pad_maximum_fusion.refs_1_), channel_id=1, source_target_pairs={{0,4},{1,5},{2,6},{3,7},{4,8},{5,9},{6,10},{7,11},{8,12},{9,13},{1... | collective-permute-start | bytes 491528 | tf_op jit(solution)/shard_map/ppermute | solution.py:42
  9.0 8.7 %collective-permute-start.3 = (bf16[128,640]{1,0:T(8,128)(2,1)S(1)}, bf16[128,640]{1,0:T(8,128)(2,1)S(1)}, u32[]{:S(2)}, u32[]{:S(2)}) collective-permute-start(bf16[128,640]{1,0:T(8,128)(2,1)S(1)} %pad_maximum_fusion.refs_1_), channel_id=1, source_target_pairs={{0,12},{1,13},{2,14},{3,15},{4,0},{5,1},{6,2},{7,3},{8,4},{9,5},{1... | collective-permute-start | bytes 491528 | tf_op jit(solution)/shard_map/ppermute | solution.py:42
  11.1 8.3 %collective-permute-start.4 = (bf16[128,640]{1,0:T(8,128)(2,1)S(1)}, bf16[128,640]{1,0:T(8,128)(2,1)S(1)}, u32[]{:S(2)}, u32[]{:S(2)}) collective-permute-start(bf16[128,640]{1,0:T(8,128)(2,1)S(1)} %pad_maximum_fusion.refs_1_), channel_id=1, source_target_pairs={{0,8},{1,9},{2,10},{3,11},{4,12},{5,13},{6,14},{7,15},{8,0},{9,1},... | collective-permute-start | bytes 491528 | tf_op jit(solution)/shard_map/ppermute | solution.py:42
  12.4 0.9 %copy-start.3 = (bf16[512,256]{1,0:T(8,128)(2,1)S(1)}, bf16[512,256]{1,0:T(8,128)(2,1)}, u32[]{:S(2)}) copy-start(bf16[512,256]{1,0:T(8,128)(2,1)} %refs_0_.3) | copy-start | bytes 786436
  13.4 0.9 %copy-start.4 = (bf16[512,256]{1,0:T(8,128)(2,1)S(1)}, bf16[512,256]{1,0:T(8,128)(2,1)}, u32[]{:S(2)}) copy-start(bf16[512,256]{1,0:T(8,128)(2,1)} %refs_1_.6) | copy-start | bytes 786436
  14.4 15.0 %collective-permute-start.9 = (bf16[512,512]{1,0:T(8,128)(2,1)S(1)}, bf16[512,512]{1,0:T(8,128)(2,1)S(1)}, u32[]{:S(2)}, u32[]{:S(2)}) collective-permute-start(bf16[512,512]{1,0:T(8,128)(2,1)S(1)} %shard_map.180), channel_id=1, source_target_pairs={{0,64},{16,80},{32,96},{48,112},{64,0},{80,16},{96,32},{112,48},{1... | collective-permute-start | bytes 1572872 | tf_op jit(solution)/shard_map/ppermute | solution.py:26
  14.9 8.4 %copy-start = (bf16[256,5120]{1,0:T(8,128)(2,1)S(1)}, bf16[256,5120]{1,0:T(8,128)(2,1)}, u32[]{:S(2)}) copy-start(bf16[256,5120]{1,0:T(8,128)(2,1)} %refs_1_.4) | copy-start | bytes 7864324
  15.0 8.3 %collective-permute-start.5 = (bf16[128,640]{1,0:T(8,128)(2,1)S(1)}, bf16[128,640]{1,0:T(8,128)(2,1)S(1)}, u32[]{:S(2)}, u32[]{:S(2)}) collective-permute-start(bf16[128,640]{1,0:T(8,128)(2,1)S(1)} %collective-permute-done.1.refs_2_.refs_1_), channel_id=1, source_target_pairs={{0,4},{1,5},{2,6},{3,7},{4,8},{5,9},{6,10},{7,11},{8,12},{9,13},{1... | collective-permute-start | bytes 491528 | tf_op jit(solution)/shard_map/ppermute | solution.py:42
  15.8 7.7 %collective-permute-start.6 = (bf16[128,640]{1,0:T(8,128)(2,1)S(1)}, bf16[128,640]{1,0:T(8,128)(2,1)S(1)}, u32[]{:S(2)}, u32[]{:S(2)}) collective-permute-start(bf16[128,640]{1,0:T(8,128)(2,1)S(1)} %collective-permute-done.1.refs_2_.refs_1_), channel_id=1, source_target_pairs={{0,12},{1,13},{2,14},{3,15},{4,0},{5,1},{6,2},{7,3},{8,4},{9,5},{1... | collective-permute-start | bytes 491528 | tf_op jit(solution)/shard_map/ppermute | solution.py:42
  17.7 8.7 %collective-permute-start.7 = (bf16[128,640]{1,0:T(8,128)(2,1)S(1)}, bf16[128,640]{1,0:T(8,128)(2,1)S(1)}, u32[]{:S(2)}, u32[]{:S(2)}) collective-permute-start(bf16[128,640]{1,0:T(8,128)(2,1)S(1)} %collective-permute-done.1.refs_2_.refs_1_), channel_id=1, source_target_pairs={{0,8},{1,9},{2,10},{3,11},{4,12},{5,13},{6,14},{7,15},{8,0},{9,1},... | collective-permute-start | bytes 491528 | tf_op jit(solution)/shard_map/ppermute | solution.py:42
  27.8 4.2 %collective-permute-start.8 = (bf16[128,5120]{1,0:T(8,128)(2,1)S(1)}, bf16[128,5120]{1,0:T(8,128)(2,1)S(1)}, u32[]{:S(2)}, u32[]{:S(2)}) collective-permute-start(bf16[128,5120]{1,0:T(8,128)(2,1)S(1)} %get-tuple-element.38.refs_0_), channel_id=1, source_target_pairs={{0,1},{1,0},{2,3},{3,2},{4,5},{5,4},{6,7},{7,6},{8,9},{9,8},{10,11... | collective-permute-start | bytes 3932168 | tf_op jit(solution)/shard_map/ppermute | solution.py:34
  29.4 27.1 %collective-permute-start.19 = (bf16[256,2560]{1,0:T(8,128)(2,1)S(1)}, bf16[256,2560]{1,0:T(8,128)(2,1)S(1)}, u32[]{:S(2)}, u32[]{:S(2)}) collective-permute-start(bf16[256,2560]{1,0:T(8,128)(2,1)S(1)} %get-tuple-element.46), channel_id=1, source_target_pairs={{0,1},{1,0},{2,3},{3,2},{4,5},{5,4},{6,7},{7,6},{8,9},{9,8},{10,11... | collective-permute-start | bytes 3932168 | tf_op jit(solution)/shard_map/ppermute | solution.py:34
  30.7 6.0 %collective-permute-start.10 = (bf16[128,512]{1,0:T(8,128)(2,1)S(1)}, bf16[128,512]{1,0:T(8,128)(2,1)S(1)}, u32[]{:S(2)}, u32[]{:S(2)}) collective-permute-start(bf16[128,512]{1,0:T(8,128)(2,1)S(1)} %get-tuple-element.40.refs_3_.refs_1_), channel_id=1, source_target_pairs={{0,64},{16,80},{32,96},{48,112},{64,0},{80,16},{96,32},{112,48},{1... | collective-permute-start | bytes 393224 | tf_op jit(solution)/shard_map/ppermute | solution.py:26
  32.9 6.3 %collective-permute-start.11 = (bf16[128,512]{1,0:T(8,128)(2,1)S(1)}, bf16[128,512]{1,0:T(8,128)(2,1)S(1)}, u32[]{:S(2)}, u32[]{:S(2)}) collective-permute-start(bf16[128,512]{1,0:T(8,128)(2,1)S(1)} %shard_map.183.refs_4_.refs_2_), channel_id=1, source_target_pairs={{0,64},{16,80},{32,96},{48,112},{64,0},{80,16},{96,32},{112,48},{1... | collective-permute-start | bytes 393224 | tf_op jit(solution)/shard_map/ppermute | solution.py:26
  34.0 5.6 %collective-permute-start.14 = (bf16[256,256]{1,0:T(8,128)(2,1)S(1)}, bf16[256,256]{1,0:T(8,128)(2,1)S(1)}, u32[]{:S(2)}, u32[]{:S(2)}) collective-permute-start(bf16[256,256]{1,0:T(8,128)(2,1)S(1)} %shard_map.182.refs_0_), channel_id=1, source_target_pairs={{0,16},{16,32},{32,48},{48,0},{64,80},{80,96},{96,112},{112,64},{1... | collective-permute-start | bytes 393224 | tf_op jit(solution)/shard_map/ppermute | solution.py:30
  35.2 5.7 %collective-permute-start.13 = (bf16[256,256]{1,0:T(8,128)(2,1)S(1)}, bf16[256,256]{1,0:T(8,128)(2,1)S(1)}, u32[]{:S(2)}, u32[]{:S(2)}) collective-permute-start(bf16[256,256]{1,0:T(8,128)(2,1)S(1)} %shard_map.182.refs_0_), channel_id=1, source_target_pairs={{0,48},{16,0},{32,16},{48,32},{64,112},{80,64},{96,80},{112,96},{1... | collective-permute-start | bytes 393224 | tf_op jit(solution)/shard_map/ppermute | solution.py:30
  36.7 6.8 %collective-permute-start.12 = (bf16[256,256]{1,0:T(8,128)(2,1)S(1)}, bf16[256,256]{1,0:T(8,128)(2,1)S(1)}, u32[]{:S(2)}, u32[]{:S(2)}) collective-permute-start(bf16[256,256]{1,0:T(8,128)(2,1)S(1)} %shard_map.182.refs_0_), channel_id=1, source_target_pairs={{0,32},{16,48},{32,0},{48,16},{64,96},{80,112},{96,64},{112,80},{1... | collective-permute-start | bytes 393224 | tf_op jit(solution)/shard_map/ppermute | solution.py:30
  44.9 5.6 %collective-permute-start.17 = (bf16[272,256]{1,0:T(8,128)(2,1)S(1)}, bf16[272,256]{1,0:T(8,128)(2,1)S(1)}, u32[]{:S(2)}, u32[]{:S(2)}) collective-permute-start(bf16[272,256]{1,0:T(8,128)(2,1)S(1)} %shard_map.187.refs_8_), channel_id=1, source_target_pairs={{0,32},{16,48},{32,0},{48,16},{64,96},{80,112},{96,64},{112,80},{1... | collective-permute-start | bytes 417800 | tf_op jit(solution)/shard_map/ppermute | solution.py:30
  45.5 8.4 %collective-permute-start.16 = (bf16[272,256]{1,0:T(8,128)(2,1)S(1)}, bf16[272,256]{1,0:T(8,128)(2,1)S(1)}, u32[]{:S(2)}, u32[]{:S(2)}) collective-permute-start(bf16[272,256]{1,0:T(8,128)(2,1)S(1)} %shard_map.186.refs_7_), channel_id=1, source_target_pairs={{0,16},{16,32},{32,48},{48,0},{64,80},{80,96},{96,112},{112,64},{1... | collective-permute-start | bytes 417800 | tf_op jit(solution)/shard_map/ppermute | solution.py:30
  46.8 7.2 %collective-permute-start.15 = (bf16[272,256]{1,0:T(8,128)(2,1)S(1)}, bf16[272,256]{1,0:T(8,128)(2,1)S(1)}, u32[]{:S(2)}, u32[]{:S(2)}) collective-permute-start(bf16[272,256]{1,0:T(8,128)(2,1)S(1)} %shard_map.185.refs_7_), channel_id=1, source_target_pairs={{0,48},{16,0},{32,16},{48,32},{64,112},{80,64},{96,80},{112,96},{1... | collective-permute-start | bytes 417800 | tf_op jit(solution)/shard_map/ppermute | solution.py:30
  54.5 2.9 %collective-permute-start.18 = (bf16[256,256]{1,0:T(8,128)(2,1)S(1)}, bf16[256,256]{1,0:T(8,128)(2,1)S(1)}, u32[]{:S(2)}, u32[]{:S(2)}) collective-permute-start(bf16[256,256]{1,0:T(8,128)(2,1)S(1)} %shard_map.189.refs_1_), channel_id=1, source_target_pairs={{0,1},{1,0},{2,3},{3,2},{4,5},{5,4},{6,7},{7,6},{8,9},{9,8},{10,11... | collective-permute-start | bytes 393224 | tf_op jit(solution)/shard_map/ppermute | solution.py:34
  58.3 6.8 %collective-permute-start.24 = (bf16[32,2560]{1,0:T(8,128)(2,1)S(1)}, bf16[32,2560]{1,0:T(8,128)(2,1)S(1)}, u32[]{:S(2)}, u32[]{:S(2)}) collective-permute-start(bf16[32,2560]{1,0:T(8,128)(2,1)S(1)} %get-tuple-element.53), channel_id=1, source_target_pairs={{0,4},{1,5},{2,6},{3,7},{4,8},{5,9},{6,10},{7,11},{8,12},{9,13},{1... | collective-permute-start | bytes 491528 | tf_op jit(solution)/shard_map/ppermute | solution.py:42
  59.2 5.9 %collective-permute-start.25 = (bf16[32,2560]{1,0:T(8,128)(2,1)S(1)}, bf16[32,2560]{1,0:T(8,128)(2,1)S(1)}, u32[]{:S(2)}, u32[]{:S(2)}) collective-permute-start(bf16[32,2560]{1,0:T(8,128)(2,1)S(1)} %get-tuple-element.54), channel_id=1, source_target_pairs={{0,12},{1,13},{2,14},{3,15},{4,0},{5,1},{6,2},{7,3},{8,4},{9,5},{1... | collective-permute-start | bytes 491528 | tf_op jit(solution)/shard_map/ppermute | solution.py:42
  61.0 6.3 %collective-permute-start.22 = (bf16[32,2560]{1,0:T(8,128)(2,1)S(1)}, bf16[32,2560]{1,0:T(8,128)(2,1)S(1)}, u32[]{:S(2)}, u32[]{:S(2)}) collective-permute-start(bf16[32,2560]{1,0:T(8,128)(2,1)S(1)} %get-tuple-element.51), channel_id=1, source_target_pairs={{0,2},{1,3},{2,0},{3,1},{4,6},{5,7},{6,4},{7,5},{8,10},{9,11},{10,... | collective-permute-start | bytes 491528 | tf_op jit(solution)/shard_map/ppermute | solution.py:38
  62.4 5.7 %collective-permute-start.20 = (bf16[32,2560]{1,0:T(8,128)(2,1)S(1)}, bf16[32,2560]{1,0:T(8,128)(2,1)S(1)}, u32[]{:S(2)}, u32[]{:S(2)}) collective-permute-start(bf16[32,2560]{1,0:T(8,128)(2,1)S(1)} %get-tuple-element.48), channel_id=1, source_target_pairs={{0,4},{1,5},{2,6},{3,7},{4,8},{5,9},{6,10},{7,11},{8,12},{9,13},{1... | collective-permute-start | bytes 491528 | tf_op jit(solution)/shard_map/ppermute | solution.py:42
  62.4 5.7 %collective-permute-start.21 = (bf16[32,2560]{1,0:T(8,128)(2,1)S(1)}, bf16[32,2560]{1,0:T(8,128)(2,1)S(1)}, u32[]{:S(2)}, u32[]{:S(2)}) collective-permute-start(bf16[32,2560]{1,0:T(8,128)(2,1)S(1)} %get-tuple-element.49), channel_id=1, source_target_pairs={{0,12},{1,13},{2,14},{3,15},{4,0},{5,1},{6,2},{7,3},{8,4},{9,5},{1... | collective-permute-start | bytes 491528 | tf_op jit(solution)/shard_map/ppermute | solution.py:42
  65.2 5.8 %collective-permute-start.26 = (bf16[32,2560]{1,0:T(8,128)(2,1)S(1)}, bf16[32,2560]{1,0:T(8,128)(2,1)S(1)}, u32[]{:S(2)}, u32[]{:S(2)}) collective-permute-start(bf16[32,2560]{1,0:T(8,128)(2,1)S(1)} %shard_map.192), channel_id=1, source_target_pairs={{0,2},{1,3},{2,0},{3,1},{4,6},{5,7},{6,4},{7,5},{8,10},{9,11},{10,... | collective-permute-start | bytes 491528 | tf_op jit(solution)/shard_map/ppermute | solution.py:38
  67.3 9.0 %copy-start.11 = (f32[5120]{0:T(1024)S(1)}, f32[5120]{0:T(1024)}, u32[]{:S(2)}) copy-start(f32[5120]{0:T(1024)} %param.19) | copy-start | bytes 61444
  67.3 9.0 %copy-start.12 = (f32[5120]{0:T(1024)S(1)}, f32[5120]{0:T(1024)}, u32[]{:S(2)}) copy-start(f32[5120]{0:T(1024)} %param.26) | copy-start | bytes 61444
  67.3 10.1 %copy-start.1 = (bf16[5120,64]{0,1:T(8,128)(2,1)S(1)}, bf16[5120,64]{0,1:T(8,128)(2,1)}, u32[]{:S(2)}) copy-start(bf16[5120,64]{0,1:T(8,128)(2,1)} %param.27) | copy-start | bytes 1966084
  67.3 10.1 %copy-start.6 = (f32[4,256]{1,0:T(4,128)S(1)}, f32[4,256]{1,0:T(4,128)}, u32[]{:S(2)}) copy-start(f32[4,256]{1,0:T(4,128)} %refs_7_.1) | copy-start | bytes 12292
  67.3 10.0 %copy-start.7 = (f32[4,256]{1,0:T(4,128)S(1)}, f32[4,256]{1,0:T(4,128)}, u32[]{:S(2)}) copy-start(f32[4,256]{1,0:T(4,128)} %refs_8_.1) | copy-start | bytes 12292
  67.3 10.0 %copy-start.8 = (s32[4,1]{0,1:T(1,128)S(1)}, s32[4,1]{0,1:T(1,128)}, u32[]{:S(2)}) copy-start(s32[4,1]{0,1:T(1,128)} %param.30) | copy-start | bytes 52
  67.3 23.6 %copy-start.2 = (bf16[256,1024]{1,0:T(8,128)(2,1)S(1)}, bf16[256,1024]{1,0:T(8,128)(2,1)}, u32[]{:S(2)}) copy-start(bf16[256,1024]{1,0:T(8,128)(2,1)} %refs_1_.7) | copy-start | bytes 1572868
  67.4 6.0 %collective-permute-start.23 = (bf16[32,2560]{1,0:T(8,128)(2,1)S(1)}, bf16[32,2560]{1,0:T(8,128)(2,1)S(1)}, u32[]{:S(2)}, u32[]{:S(2)}) collective-permute-start(bf16[32,2560]{1,0:T(8,128)(2,1)S(1)} %shard_map.191), channel_id=1, source_target_pairs={{0,8},{1,9},{2,10},{3,11},{4,12},{5,13},{6,14},{7,15},{8,0},{9,1},... | collective-permute-start | bytes 491528 | tf_op jit(solution)/shard_map/ppermute | solution.py:42
  73.6 3.8 %collective-permute-start.27 = (f32[16,2560]{1,0:T(8,128)S(1)}, f32[16,2560]{1,0:T(8,128)S(1)}, u32[]{:S(2)}, u32[]{:S(2)}) collective-permute-start(f32[16,2560]{1,0:T(8,128)S(1)} %get-tuple-element.56), channel_id=1, source_target_pairs={{0,1},{1,0},{2,3},{3,2},{4,5},{5,4},{6,7},{7,6},{8,9},{9,8},{10,11... | collective-permute-start | bytes 491528 | tf_op jit(solution)/shard_map/ppermute | solution.py:34

commit v6 on v5

--- a/solution.py
+++ b/solution.py
@@ -501,6 +501,10 @@
         nbytes=MIB,
         after=(before,),
     )
+    for i in range(2):
+        back[i] = call(
+            copy_body, shape(back[i].shape, BF), (back[i],), flops=1 << 28, after=tuple(back[:i])
+        )
     attended = call(merge_body, shape((count, cols), BF), (*kept, *back), nbytes=MIB)
 
     projected = call(

time: 92 us -> 90.9 us (0.988)
  waiting for transfers between devices: 20.8 us -> 17.7 us
  starting transfers between devices: 37.4 us -> 39.4 us
    ppermute x6, waiting for transfers between devices: 6.38 us -> 3.35 us  [x_send(): lax.ppermute(a, 'ctx', [(c, c // 4 * 4 + (c + by) % 4) for c in range(8)])]
    ppermute x5, starting transfers between devices: 7.84 us -> 9.51 us  [core_swap(): return lax.ppermute(a, 'mdl', CORE_SWAP)]
    pallas_call x21 -> x23, Pallas kernels: 17.8 us -> 17.8 us  [call(): pl.pallas_call(run, out_shape=outs, in_specs=place + [pl.BlockSpec(memory...]
  transfers between devices with their start and end apart: 28 -> 28, of which waited for: 15 -> 14; matrix products, arithmetic and copies ran while one was open for 0% -> 0% of each run, Pallas kernels for 15% -> 16%
where the time goes in v6:
time: 90.9 us; the launch traced here: 90.7 us
  starting transfers between devices  39.4 us (43%)
  Pallas kernels  17.8 us (20%)
  waiting for transfers between devices  17.7 us (19%)
  blocking collectives  11.9 us (13%)
  local copies, waits for them, and re-layouts  2.88 us (3%)
  between operations  0.94 us (1%)
    pallas_call x23, Pallas kernels, call(): pl.pallas_call(run, out_shape=outs, in_specs=place + [pl.BlockSpec(memory...  17.8 us
    ppermute x11, starting transfers between devices, z_send(): return lax.ppermute(a, 'mdl', [(m, (m + 4 * by) % 16) for m in range(16)])  14.3 us
    all_to_all x1, blocking collectives, shards(): lax.all_to_all(slot_rows, 'mdl', split_axis=0, concat_axis=0, tiled=True)  11.9 us
    ppermute x5, starting transfers between devices, core_swap(): return lax.ppermute(a, 'mdl', CORE_SWAP)  9.51 us
    ppermute x6, starting transfers between devices, x_send(): lax.ppermute(a, 'ctx', [(c, c // 4 * 4 + (c + by) % 4) for c in range(8)])  7.85 us
    ppermute x11, waiting for transfers between devices, z_send(): return lax.ppermute(a, 'mdl', [(m, (m + 4 * by) % 16) for m in range(16)])  7.43 us
    ppermute x3, starting transfers between devices, pair_swap(): return lax.ppermute(a, 'mdl', PAIR_SWAP)  6.13 us
    ppermute x5, waiting for transfers between devices, core_swap(): return lax.ppermute(a, 'mdl', CORE_SWAP)  3.67 us
  transfers between devices with their start and end apart: 28, of which 14 were waited for; matrix products, arithmetic and copies ran while one was open for 0% of the time, Pallas kernels for 16%

profile of v6, /device:TPU:1, one launch (start us, length us, event | category | flops | bytes accessed | tf_op | source)
XLA Modules:
  0.0 90.7 jit_solution(11159932311230726329)
XLA Ops:
  0.7 0.9 copy-done.5
  1.6 0.1 shard_map.175
  1.7 1.5 %collective-permute-start = (bf16[128,320]{1,0:T(8,128)(2,1)S(1)}, bf16[128,320]{1,0:T(8,128)(2,1)S(1)}, u32[]{:S(2)}, u32[]{:S(2)}) collective-permute-start(bf16[128,320]{1,0:T(8,128)(2,1)S(1)} %get-tuple-element.33), channel_id=1, source_target_pairs={{0,1},{1,0},{2,3},{3,2},{4,5},{5,4},{6,7},{7,6},{8,9},{9,8},{10,11... | collective-permute-start | bytes 245768 | tf_op jit(solution)/shard_map/ppermute | solution.py:34
  3.2 0.9 %collective-permute-done = bf16[128,320]{1,0:T(8,128)(2,1)S(1)} collective-permute-done((bf16[128,320]{1,0:T(8,128)(2,1)S(1)}, bf16[128,320]{1,0:T(8,128)(2,1)S(1)}, u32[]{:S(2)}, u32[]{:S(2)}) %collective-permute-start) | collective-permute-done | bytes 81952 | tf_op jit(solution)/shard_map/ppermute | solution.py:34
  4.2 0.1 pad_maximum_fusion.refs_1_
  4.3 3.1 %collective-permute-start.1 = (bf16[128,640]{1,0:T(8,128)(2,1)S(1)}, bf16[128,640]{1,0:T(8,128)(2,1)S(1)}, u32[]{:S(2)}, u32[]{:S(2)}) collective-permute-start(bf16[128,640]{1,0:T(8,128)(2,1)S(1)} %pad_maximum_fusion.refs_1_), channel_id=1, source_target_pairs={{0,2},{1,3},{2,0},{3,1},{4,6},{5,7},{6,4},{7,5},{8,10},{9,11},{10,... | collective-permute-start | bytes 491528 | tf_op jit(solution)/shard_map/ppermute | solution.py:38
  7.3 1.6 %collective-permute-start.2 = (bf16[128,640]{1,0:T(8,128)(2,1)S(1)}, bf16[128,640]{1,0:T(8,128)(2,1)S(1)}, u32[]{:S(2)}, u32[]{:S(2)}) collective-permute-start(bf16[128,640]{1,0:T(8,128)(2,1)S(1)} %pad_maximum_fusion.refs_1_), channel_id=1, source_target_pairs={{0,4},{1,5},{2,6},{3,7},{4,8},{5,9},{6,10},{7,11},{8,12},{9,13},{1... | collective-permute-start | bytes 491528 | tf_op jit(solution)/shard_map/ppermute | solution.py:42
  9.0 2.1 %collective-permute-start.3 = (bf16[128,640]{1,0:T(8,128)(2,1)S(1)}, bf16[128,640]{1,0:T(8,128)(2,1)S(1)}, u32[]{:S(2)}, u32[]{:S(2)}) collective-permute-start(bf16[128,640]{1,0:T(8,128)(2,1)S(1)} %pad_maximum_fusion.refs_1_), channel_id=1, source_target_pairs={{0,12},{1,13},{2,14},{3,15},{4,0},{5,1},{6,2},{7,3},{8,4},{9,5},{1... | collective-permute-start | bytes 491528 | tf_op jit(solution)/shard_map/ppermute | solution.py:42
  11.1 1.3 %collective-permute-start.4 = (bf16[128,640]{1,0:T(8,128)(2,1)S(1)}, bf16[128,640]{1,0:T(8,128)(2,1)S(1)}, u32[]{:S(2)}, u32[]{:S(2)}) collective-permute-start(bf16[128,640]{1,0:T(8,128)(2,1)S(1)} %pad_maximum_fusion.refs_1_), channel_id=1, source_target_pairs={{0,8},{1,9},{2,10},{3,11},{4,12},{5,13},{6,14},{7,15},{8,0},{9,1},... | collective-permute-start | bytes 491528 | tf_op jit(solution)/shard_map/ppermute | solution.py:42
  12.4 0.9 %copy-done.3 = bf16[512,256]{1,0:T(8,128)(2,1)S(1)} copy-done((bf16[512,256]{1,0:T(8,128)(2,1)S(1)}, bf16[512,256]{1,0:T(8,128)(2,1)}, u32[]{:S(2)}) %copy-start.3) | copy-done | bytes 262168
  13.4 0.9 %copy-done.4 = bf16[512,256]{1,0:T(8,128)(2,1)S(1)} copy-done((bf16[512,256]{1,0:T(8,128)(2,1)S(1)}, bf16[512,256]{1,0:T(8,128)(2,1)}, u32[]{:S(2)}) %copy-start.4) | copy-done | bytes 262168
  14.4 0.5 collective-permute-start.9
  15.0 0.8 collective-permute-start.5
  15.8 1.9 %collective-permute-start.6 = (bf16[128,640]{1,0:T(8,128)(2,1)S(1)}, bf16[128,640]{1,0:T(8,128)(2,1)S(1)}, u32[]{:S(2)}, u32[]{:S(2)}) collective-permute-start(bf16[128,640]{1,0:T(8,128)(2,1)S(1)} %collective-permute-done.1.refs_2_.refs_1_), channel_id=1, source_target_pairs={{0,12},{1,13},{2,14},{3,15},{4,0},{5,1},{6,2},{7,3},{8,4},{9,5},{1... | collective-permute-start | bytes 491528 | tf_op jit(solution)/shard_map/ppermute | solution.py:42
  17.7 0.5 collective-permute-start.7
  18.2 1.3 %collective-permute-done.4.refs_5_ = bf16[128,640]{1,0:T(8,128)(2,1)S(1)} collective-permute-done((bf16[128,640]{1,0:T(8,128)(2,1)S(1)}, bf16[128,640]{1,0:T(8,128)(2,1)S(1)}, u32[]{:S(2)}, u32[]{:S(2)}) %collective-permute-start.4) | collective-permute-done | bytes 163872 | tf_op jit(solution)/shard_map/ppermute | solution.py:42
  19.4 3.3 %shard_map.177 = (bf16[5120,256]{1,0:T(8,128)(2,1)S(1)}, bf16[5120,256]{1,0:T(8,128)(2,1)S(1)}, bf16[5120,256]{1,0:T(8,128)(2,1)S(1)}) custom-call(bf16[5120,256]{1,0:T(8,128)(2,1)} %refs_0_.2, bf16[5120,256]{1,0:T(8,128)(2,1)} %refs_1_.5, bf16[5120,256]{1,0:T(8,128)(2,1)} %refs_2_.1, bf16[128,640]{1,0:T(8,128)(2,1)S(1)} %collective-permute-done.2.refs_3_, ...), custom_call_target="tpu_custom_call" | custom-call | flops 5000000000 | bytes 8388608 | tf_op jit(solution)/shard_map/pallas_call | solution.py:60
  22.8 0.5 collective-permute-done.5.refs_2_.refs_6_
  23.3 0.2 shard_map.176
  23.5 3.0 %collective-permute-done.7.refs_8_ = bf16[128,640]{1,0:T(8,128)(2,1)S(1)} collective-permute-done((bf16[128,640]{1,0:T(8,128)(2,1)S(1)}, bf16[128,640]{1,0:T(8,128)(2,1)S(1)}, u32[]{:S(2)}, u32[]{:S(2)}) %collective-permute-start.7) | collective-permute-done | bytes 163872 | tf_op jit(solution)/shard_map/ppermute | solution.py:42
  26.5 1.3 %shard_map.178 = (bf16[128,5120]{1,0:T(8,128)(2,1)S(1)}, bf16[8,16,640]{2,1,0:T(8,128)(2,1)S(1)}) custom-call(s32[1]{0:T(128)} %bitcast.1.refs_0_, bf16[128,640]{1,0:T(8,128)(2,1)S(1)} %pad_maximum_fusion.refs_1_, bf16[128,640]{1,0:T(8,128)(2,1)S(1)} %collective-permute-done.1.refs_2_.refs_1_, bf16[128,640]{1,0:T(8,128)(2,1)S(1)} %collective-permute-done.2.refs_3_, ...), custom_call_target="tpu_custom_call" | custom-call | flops 1048576 | bytes 1048576 | tf_op jit(solution)/shard_map/pallas_call | solution.py:60
  27.8 1.6 %collective-permute-start.8 = (bf16[128,5120]{1,0:T(8,128)(2,1)S(1)}, bf16[128,5120]{1,0:T(8,128)(2,1)S(1)}, u32[]{:S(2)}, u32[]{:S(2)}) collective-permute-start(bf16[128,5120]{1,0:T(8,128)(2,1)S(1)} %get-tuple-element.38.refs_0_), channel_id=1, source_target_pairs={{0,1},{1,0},{2,3},{3,2},{4,5},{5,4},{6,7},{7,6},{8,9},{9,8},{10,11... | collective-permute-start | bytes 3932168 | tf_op jit(solution)/shard_map/ppermute | solution.py:34
  29.4 0.1 collective-permute-start.19
  29.4 1.2 %shard_map.181 = (bf16[128,512]{1,0:T(8,128)(2,1)S(1)}, bf16[128,256]{1,0:T(8,128)(2,1)S(1)}) custom-call(bf16[128,5120]{1,0:T(8,128)(2,1)S(1)} %get-tuple-element.38.refs_0_, bf16[5120,256]{1,0:T(8,128)(2,1)S(1)} %get-tuple-element.36.refs_13_.refs_1_, bf16[5120,256]{1,0:T(8,128)(2,1)S(1)} %get-tuple-element.37.refs_14_.refs_2_, ...), custom_call_target="tpu_custom_call" | custom-call | flops 30000001024 | bytes 8388608 | tf_op jit(solution)/shard_map/pallas_call | solution.py:60
  30.7 0.6 collective-permute-start.10
  31.3 0.7 collective-permute-done.8.refs_1_.refs_0_
  32.0 0.8 shard_map.183.refs_4_.refs_2_
  32.9 0.6 collective-permute-start.11
  33.4 0.5 shard_map.182.refs_0_
  34.0 1.3 %collective-permute-start.14 = (bf16[256,256]{1,0:T(8,128)(2,1)S(1)}, bf16[256,256]{1,0:T(8,128)(2,1)S(1)}, u32[]{:S(2)}, u32[]{:S(2)}) collective-permute-start(bf16[256,256]{1,0:T(8,128)(2,1)S(1)} %shard_map.182.refs_0_), channel_id=1, source_target_pairs={{0,16},{16,32},{32,48},{48,0},{64,80},{80,96},{96,112},{112,64},{1... | collective-permute-start | bytes 393224 | tf_op jit(solution)/shard_map/ppermute | solution.py:30
  35.2 1.5 %collective-permute-start.13 = (bf16[256,256]{1,0:T(8,128)(2,1)S(1)}, bf16[256,256]{1,0:T(8,128)(2,1)S(1)}, u32[]{:S(2)}, u32[]{:S(2)}) collective-permute-start(bf16[256,256]{1,0:T(8,128)(2,1)S(1)} %shard_map.182.refs_0_), channel_id=1, source_target_pairs={{0,48},{16,0},{32,16},{48,32},{64,112},{80,64},{96,80},{112,96},{1... | collective-permute-start | bytes 393224 | tf_op jit(solution)/shard_map/ppermute | solution.py:30
  36.7 1.5 %collective-permute-start.12 = (bf16[256,256]{1,0:T(8,128)(2,1)S(1)}, bf16[256,256]{1,0:T(8,128)(2,1)S(1)}, u32[]{:S(2)}, u32[]{:S(2)}) collective-permute-start(bf16[256,256]{1,0:T(8,128)(2,1)S(1)} %shard_map.182.refs_0_), channel_id=1, source_target_pairs={{0,32},{16,48},{32,0},{48,16},{64,96},{80,112},{96,64},{112,80},{1... | collective-permute-start | bytes 393224 | tf_op jit(solution)/shard_map/ppermute | solution.py:30
  38.2 0.9 %shard_map.184 = (f32[256,256]{1,0:T(8,128)S(1)}, f32[2,256,128]{2,1,0:T(8,128)S(1)}, f32[2,256,128]{2,1,0:T(8,128)S(1)}) custom-call(bf16[256,256]{1,0:T(8,128)(2,1)S(1)} %shard_map.182.refs_0_, bf16[512,512]{1,0:T(8,128)(2,1)S(1)} %shard_map.179.refs_0_.refs_1_, bf16[512,512]{1,0:T(8,128)(2,1)S(1)} %collective-permute-done.9.refs_4_.refs_2_), custom_call_target="tpu_custom_call" | custom-call | flops 1048576 | bytes 1048576 | tf_op jit(solution)/shard_map/pallas_call | solution.py:60
  39.2 0.4 collective-permute-done.14.refs_0_
  39.5 1.4 %shard_map.185.refs_7_ = bf16[272,256]{1,0:T(8,128)(2,1)S(1)} custom-call(bf16[256,256]{1,0:T(8,128)(2,1)S(1)} %collective-permute-done.14.refs_0_, bf16[512,512]{1,0:T(8,128)(2,1)S(1)} %shard_map.179.refs_0_.refs_1_, bf16[512,512]{1,0:T(8,128)(2,1)S(1)} %collective-permute-done.9.refs_4_.refs_2_, bf16[128,512]{1,0:T(8,128)(2,1)S(1)} %get-tuple-element.40.refs_3_.refs_1_, ...), custom_call_target="tpu_custom_call" | custom-call | flops 1048576 | bytes 1048576 | tf_op jit(solution)/shard_map/pallas_call | solution.py:60
  40.9 1.7 %collective-permute-start.15 = (bf16[272,256]{1,0:T(8,128)(2,1)S(1)}, bf16[272,256]{1,0:T(8,128)(2,1)S(1)}, u32[]{:S(2)}, u32[]{:S(2)}) collective-permute-start(bf16[272,256]{1,0:T(8,128)(2,1)S(1)} %shard_map.185.refs_7_), channel_id=1, source_target_pairs={{0,48},{16,0},{32,16},{48,32},{64,112},{80,64},{96,80},{112,96},{1... | collective-permute-start | bytes 417800 | tf_op jit(solution)/shard_map/ppermute | solution.py:30
  42.6 1.4 %shard_map.186.refs_7_ = bf16[272,256]{1,0:T(8,128)(2,1)S(1)} custom-call(bf16[256,256]{1,0:T(8,128)(2,1)S(1)} %collective-permute-done.13.refs_0_, bf16[512,512]{1,0:T(8,128)(2,1)S(1)} %shard_map.179.refs_0_.refs_1_, bf16[512,512]{1,0:T(8,128)(2,1)S(1)} %collective-permute-done.9.refs_4_.refs_2_, bf16[128,512]{1,0:T(8,128)(2,1)S(1)} %get-tuple-element.40.refs_3_.refs_1_, ...), custom_call_target="tpu_custom_call" | custom-call | flops 1048576 | bytes 1048576 | tf_op jit(solution)/shard_map/pallas_call | solution.py:60
  44.0 0.1 collective-permute-start.16
  44.1 1.4 %shard_map.187.refs_8_ = bf16[272,256]{1,0:T(8,128)(2,1)S(1)} custom-call(bf16[256,256]{1,0:T(8,128)(2,1)S(1)} %collective-permute-done.12.refs_0_, bf16[512,512]{1,0:T(8,128)(2,1)S(1)} %shard_map.179.refs_0_.refs_1_, bf16[512,512]{1,0:T(8,128)(2,1)S(1)} %collective-permute-done.9.refs_4_.refs_2_, bf16[128,512]{1,0:T(8,128)(2,1)S(1)} %get-tuple-element.40.refs_3_.refs_1_, ...), custom_call_target="tpu_custom_call" | custom-call | flops 1048576 | bytes 1048576 | tf_op jit(solution)/shard_map/pallas_call | solution.py:60
  45.5 1.8 %collective-permute-start.17 = (bf16[272,256]{1,0:T(8,128)(2,1)S(1)}, bf16[272,256]{1,0:T(8,128)(2,1)S(1)}, u32[]{:S(2)}, u32[]{:S(2)}) collective-permute-start(bf16[272,256]{1,0:T(8,128)(2,1)S(1)} %shard_map.187.refs_8_), channel_id=1, source_target_pairs={{0,32},{16,48},{32,0},{48,16},{64,96},{80,112},{96,64},{112,80},{1... | collective-permute-start | bytes 417800 | tf_op jit(solution)/shard_map/ppermute | solution.py:30
  47.3 0.9 %shard_map.188 = (f32[256,256]{1,0:T(8,128)S(1)}, f32[8,256]{1,0:T(8,128)S(1)}) custom-call(bf16[256,256]{1,0:T(8,128)(2,1)S(1)} %shard_map.182.refs_0_, bf16[128,512]{1,0:T(8,128)(2,1)S(1)} %get-tuple-element.40.refs_3_.refs_1_, bf16[128,512]{1,0:T(8,128)(2,1)S(1)} %shard_map.183.refs_4_.refs_2_, ...), custom_call_target="tpu_custom_call" | custom-call | flops 1048576 | bytes 1048576 | tf_op jit(solution)/shard_map/pallas_call | solution.py:60
  48.2 1.0 %collective-permute-done.16.refs_0_ = bf16[272,256]{1,0:T(8,128)(2,1)S(1)} collective-permute-done((bf16[272,256]{1,0:T(8,128)(2,1)S(1)}, bf16[272,256]{1,0:T(8,128)(2,1)S(1)}, u32[]{:S(2)}, u32[]{:S(2)}) %collective-permute-start.16) | collective-permute-done | bytes 139296 | tf_op jit(solution)/shard_map/ppermute | solution.py:30
  49.2 2.0 %collective-permute-done.17.refs_4_ = bf16[272,256]{1,0:T(8,128)(2,1)S(1)} collective-permute-done((bf16[272,256]{1,0:T(8,128)(2,1)S(1)}, bf16[272,256]{1,0:T(8,128)(2,1)S(1)}, u32[]{:S(2)}, u32[]{:S(2)}) %collective-permute-start.17) | collective-permute-done | bytes 139296 | tf_op jit(solution)/shard_map/ppermute | solution.py:30
  51.2 0.6 shard_map.191.refs_1_
  51.8 3.6 %collective-permute-start.18 = (bf16[256,256]{1,0:T(8,128)(2,1)S(1)}, bf16[256,256]{1,0:T(8,128)(2,1)S(1)}, u32[]{:S(2)}, u32[]{:S(2)}) collective-permute-start(bf16[256,256]{1,0:T(8,128)(2,1)S(1)} %shard_map.191.refs_1_), channel_id=1, source_target_pairs={{0,1},{1,0},{2,3},{3,2},{4,5},{5,4},{6,7},{7,6},{8,9},{9,8},{10,11... | collective-permute-start | bytes 393224 | tf_op jit(solution)/shard_map/ppermute | solution.py:34
  55.4 1.0 %collective-permute-done.18.refs_2_ = bf16[256,256]{1,0:T(8,128)(2,1)S(1)} collective-permute-done((bf16[256,256]{1,0:T(8,128)(2,1)S(1)}, bf16[256,256]{1,0:T(8,128)(2,1)S(1)}, u32[]{:S(2)}, u32[]{:S(2)}) %collective-permute-start.18) | collective-permute-done | bytes 131104 | tf_op jit(solution)/shard_map/ppermute | solution.py:34
  56.4 0.8 shard_map.192
  57.2 0.9 collective-permute-start.24
  58.1 1.9 %collective-permute-start.25 = (bf16[32,2560]{1,0:T(8,128)(2,1)S(1)}, bf16[32,2560]{1,0:T(8,128)(2,1)S(1)}, u32[]{:S(2)}, u32[]{:S(2)}) collective-permute-start(bf16[32,2560]{1,0:T(8,128)(2,1)S(1)} %get-tuple-element.54), channel_id=1, source_target_pairs={{0,12},{1,13},{2,14},{3,15},{4,0},{5,1},{6,2},{7,3},{8,4},{9,5},{1... | collective-permute-start | bytes 491528 | tf_op jit(solution)/shard_map/ppermute | solution.py:42
  59.9 1.5 %collective-permute-start.22 = (bf16[32,2560]{1,0:T(8,128)(2,1)S(1)}, bf16[32,2560]{1,0:T(8,128)(2,1)S(1)}, u32[]{:S(2)}, u32[]{:S(2)}) collective-permute-start(bf16[32,2560]{1,0:T(8,128)(2,1)S(1)} %get-tuple-element.51), channel_id=1, source_target_pairs={{0,2},{1,3},{2,0},{3,1},{4,6},{5,7},{6,4},{7,5},{8,10},{9,11},{10,... | collective-permute-start | bytes 491528 | tf_op jit(solution)/shard_map/ppermute | solution.py:38
  61.5 2.7 %collective-permute-start.21 = (bf16[32,2560]{1,0:T(8,128)(2,1)S(1)}, bf16[32,2560]{1,0:T(8,128)(2,1)S(1)}, u32[]{:S(2)}, u32[]{:S(2)}) collective-permute-start(bf16[32,2560]{1,0:T(8,128)(2,1)S(1)} %get-tuple-element.49), channel_id=1, source_target_pairs={{0,12},{1,13},{2,14},{3,15},{4,0},{5,1},{6,2},{7,3},{8,4},{9,5},{1... | collective-permute-start | bytes 491528 | tf_op jit(solution)/shard_map/ppermute | solution.py:42
  64.2 0.1 shard_map.194
  64.2 1.5 %collective-permute-start.26 = (bf16[32,2560]{1,0:T(8,128)(2,1)S(1)}, bf16[32,2560]{1,0:T(8,128)(2,1)S(1)}, u32[]{:S(2)}, u32[]{:S(2)}) collective-permute-start(bf16[32,2560]{1,0:T(8,128)(2,1)S(1)} %shard_map.194), channel_id=1, source_target_pairs={{0,2},{1,3},{2,0},{3,1},{4,6},{5,7},{6,4},{7,5},{8,10},{9,11},{10,... | collective-permute-start | bytes 491528 | tf_op jit(solution)/shard_map/ppermute | solution.py:38
  65.7 0.5 collective-permute-done.22.refs_1_
  66.3 0.6 collective-permute-start.23
  66.9 0.3 collective-permute-done.20.refs_2_
  67.2 2.8 %collective-permute-done.26.refs_5_ = bf16[32,2560]{1,0:T(8,128)(2,1)S(1)} collective-permute-done((bf16[32,2560]{1,0:T(8,128)(2,1)S(1)}, bf16[32,2560]{1,0:T(8,128)(2,1)S(1)}, u32[]{:S(2)}, u32[]{:S(2)}) %collective-permute-start.26) | collective-permute-done | bytes 163872 | tf_op jit(solution)/shard_map/ppermute | solution.py:38
  70.0 2.4 %collective-permute-done.23.refs_4_ = bf16[32,2560]{1,0:T(8,128)(2,1)S(1)} collective-permute-done((bf16[32,2560]{1,0:T(8,128)(2,1)S(1)}, bf16[32,2560]{1,0:T(8,128)(2,1)S(1)}, u32[]{:S(2)}, u32[]{:S(2)}) %collective-permute-start.23) | collective-permute-done | bytes 163872 | tf_op jit(solution)/shard_map/ppermute | solution.py:42
  72.4 0.1 shard_map.195
  72.5 2.8 %collective-permute-start.27 = (f32[16,2560]{1,0:T(8,128)S(1)}, f32[16,2560]{1,0:T(8,128)S(1)}, u32[]{:S(2)}, u32[]{:S(2)}) collective-permute-start(f32[16,2560]{1,0:T(8,128)S(1)} %get-tuple-element.56), channel_id=1, source_target_pairs={{0,1},{1,0},{2,3},{3,2},{4,5},{5,4},{6,7},{7,6},{8,9},{9,8},{10,11... | collective-permute-start | bytes 491528 | tf_op jit(solution)/shard_map/ppermute | solution.py:34
  75.3 1.0 %collective-permute-done.27.refs_2_ = f32[16,2560]{1,0:T(8,128)S(1)} collective-permute-done((f32[16,2560]{1,0:T(8,128)S(1)}, f32[16,2560]{1,0:T(8,128)S(1)}, u32[]{:S(2)}, u32[]{:S(2)}) %collective-permute-start.27) | collective-permute-done | bytes 163872 | tf_op jit(solution)/shard_map/ppermute | solution.py:34
  76.3 1.7 %shard_map.196 = (bf16[16,5120]{1,0:T(8,128)(2,1)}, f32[4,256]{1,0:T(4,128)}, f32[16,2,256]{2,1,0:T(2,128)S(1)}) custom-call(s32[1]{0:T(128)} %bitcast.refs_0_, f32[16,2560]{1,0:T(8,128)S(1)} %get-tuple-element.55.refs_1_, f32[16,2560]{1,0:T(8,128)S(1)} %collective-permute-done.27.refs_2_, bf16[8,16,640]{2,1,0:T(8,128)(2,1)S(1)} %get-tuple-element.57.refs_3_, ...), custom_call_target="tpu_custom_call" | custom-call | bytes 2097152 | tf_op jit(solution)/shard_map/pallas_call | solution.py:60
  78.0 11.9 %all_to_all.5.refs_0_ = f32[16,2,256]{2,1,0:T(2,128)S(1)} all-to-all(f32[16,2,256]{2,1,0:T(2,128)S(1)} %get-tuple-element.60), channel_id=1, replica_groups=mesh['ctx'=8,'mdl'=16] {'mdl'}, dimensions={0} | all-to-all | bytes 65536 | tf_op jit(solution)/shard_map/all_to_all | solution.py:549
  89.9 0.9 shard_map.197
  (48 shorter events, 0.3 us)
Async XLA Ops:
  0.6 14.3 %copy-start.9 = (f32[5120]{0:T(1024)S(1)}, f32[5120]{0:T(1024)}, u32[]{:S(2)}) copy-start(f32[5120]{0:T(1024)} %param.18) | copy-start | bytes 61444
  0.7 0.9 %copy-start.5 = (bf16[256,320]{0,1:T(8,128)(2,1)S(1)}, bf16[256,320]{0,1:T(8,128)(2,1)}, u32[]{:S(2)}) copy-start(bf16[256,320]{0,1:T(8,128)(2,1)} %param.16) | copy-start | bytes 491524
  1.6 13.3 %copy-start.10 = (f32[5120]{0:T(1024)S(1)}, f32[5120]{0:T(1024)}, u32[]{:S(2)}) copy-start(f32[5120]{0:T(1024)} %param.17) | copy-start | bytes 61444
  1.7 2.4 %collective-permute-start = (bf16[128,320]{1,0:T(8,128)(2,1)S(1)}, bf16[128,320]{1,0:T(8,128)(2,1)S(1)}, u32[]{:S(2)}, u32[]{:S(2)}) collective-permute-start(bf16[128,320]{1,0:T(8,128)(2,1)S(1)} %get-tuple-element.33), channel_id=1, source_target_pairs={{0,1},{1,0},{2,3},{3,2},{4,5},{5,4},{6,7},{7,6},{8,9},{9,8},{10,11... | collective-permute-start | bytes 245768 | tf_op jit(solution)/shard_map/ppermute | solution.py:34
  4.3 10.1 %collective-permute-start.1 = (bf16[128,640]{1,0:T(8,128)(2,1)S(1)}, bf16[128,640]{1,0:T(8,128)(2,1)S(1)}, u32[]{:S(2)}, u32[]{:S(2)}) collective-permute-start(bf16[128,640]{1,0:T(8,128)(2,1)S(1)} %pad_maximum_fusion.refs_1_), channel_id=1, source_target_pairs={{0,2},{1,3},{2,0},{3,1},{4,6},{5,7},{6,4},{7,5},{8,10},{9,11},{10,... | collective-permute-start | bytes 491528 | tf_op jit(solution)/shard_map/ppermute | solution.py:38
  7.3 8.4 %collective-permute-start.2 = (bf16[128,640]{1,0:T(8,128)(2,1)S(1)}, bf16[128,640]{1,0:T(8,128)(2,1)S(1)}, u32[]{:S(2)}, u32[]{:S(2)}) collective-permute-start(bf16[128,640]{1,0:T(8,128)(2,1)S(1)} %pad_maximum_fusion.refs_1_), channel_id=1, source_target_pairs={{0,4},{1,5},{2,6},{3,7},{4,8},{5,9},{6,10},{7,11},{8,12},{9,13},{1... | collective-permute-start | bytes 491528 | tf_op jit(solution)/shard_map/ppermute | solution.py:42
  9.0 8.7 %collective-permute-start.3 = (bf16[128,640]{1,0:T(8,128)(2,1)S(1)}, bf16[128,640]{1,0:T(8,128)(2,1)S(1)}, u32[]{:S(2)}, u32[]{:S(2)}) collective-permute-start(bf16[128,640]{1,0:T(8,128)(2,1)S(1)} %pad_maximum_fusion.refs_1_), channel_id=1, source_target_pairs={{0,12},{1,13},{2,14},{3,15},{4,0},{5,1},{6,2},{7,3},{8,4},{9,5},{1... | collective-permute-start | bytes 491528 | tf_op jit(solution)/shard_map/ppermute | solution.py:42
  11.1 8.3 %collective-permute-start.4 = (bf16[128,640]{1,0:T(8,128)(2,1)S(1)}, bf16[128,640]{1,0:T(8,128)(2,1)S(1)}, u32[]{:S(2)}, u32[]{:S(2)}) collective-permute-start(bf16[128,640]{1,0:T(8,128)(2,1)S(1)} %pad_maximum_fusion.refs_1_), channel_id=1, source_target_pairs={{0,8},{1,9},{2,10},{3,11},{4,12},{5,13},{6,14},{7,15},{8,0},{9,1},... | collective-permute-start | bytes 491528 | tf_op jit(solution)/shard_map/ppermute | solution.py:42
  12.4 0.9 %copy-start.3 = (bf16[512,256]{1,0:T(8,128)(2,1)S(1)}, bf16[512,256]{1,0:T(8,128)(2,1)}, u32[]{:S(2)}) copy-start(bf16[512,256]{1,0:T(8,128)(2,1)} %refs_0_.3) | copy-start | bytes 786436
  13.4 0.9 %copy-start.4 = (bf16[512,256]{1,0:T(8,128)(2,1)S(1)}, bf16[512,256]{1,0:T(8,128)(2,1)}, u32[]{:S(2)}) copy-start(bf16[512,256]{1,0:T(8,128)(2,1)} %refs_1_.6) | copy-start | bytes 786436
  14.4 15.0 %collective-permute-start.9 = (bf16[512,512]{1,0:T(8,128)(2,1)S(1)}, bf16[512,512]{1,0:T(8,128)(2,1)S(1)}, u32[]{:S(2)}, u32[]{:S(2)}) collective-permute-start(bf16[512,512]{1,0:T(8,128)(2,1)S(1)} %shard_map.180), channel_id=1, source_target_pairs={{0,64},{16,80},{32,96},{48,112},{64,0},{80,16},{96,32},{112,48},{1... | collective-permute-start | bytes 1572872 | tf_op jit(solution)/shard_map/ppermute | solution.py:26
  14.9 8.4 %copy-start = (bf16[256,5120]{1,0:T(8,128)(2,1)S(1)}, bf16[256,5120]{1,0:T(8,128)(2,1)}, u32[]{:S(2)}) copy-start(bf16[256,5120]{1,0:T(8,128)(2,1)} %refs_1_.4) | copy-start | bytes 7864324
  15.0 8.3 %collective-permute-start.5 = (bf16[128,640]{1,0:T(8,128)(2,1)S(1)}, bf16[128,640]{1,0:T(8,128)(2,1)S(1)}, u32[]{:S(2)}, u32[]{:S(2)}) collective-permute-start(bf16[128,640]{1,0:T(8,128)(2,1)S(1)} %collective-permute-done.1.refs_2_.refs_1_), channel_id=1, source_target_pairs={{0,4},{1,5},{2,6},{3,7},{4,8},{5,9},{6,10},{7,11},{8,12},{9,13},{1... | collective-permute-start | bytes 491528 | tf_op jit(solution)/shard_map/ppermute | solution.py:42
  15.8 7.7 %collective-permute-start.6 = (bf16[128,640]{1,0:T(8,128)(2,1)S(1)}, bf16[128,640]{1,0:T(8,128)(2,1)S(1)}, u32[]{:S(2)}, u32[]{:S(2)}) collective-permute-start(bf16[128,640]{1,0:T(8,128)(2,1)S(1)} %collective-permute-done.1.refs_2_.refs_1_), channel_id=1, source_target_pairs={{0,12},{1,13},{2,14},{3,15},{4,0},{5,1},{6,2},{7,3},{8,4},{9,5},{1... | collective-permute-start | bytes 491528 | tf_op jit(solution)/shard_map/ppermute | solution.py:42
  17.7 8.7 %collective-permute-start.7 = (bf16[128,640]{1,0:T(8,128)(2,1)S(1)}, bf16[128,640]{1,0:T(8,128)(2,1)S(1)}, u32[]{:S(2)}, u32[]{:S(2)}) collective-permute-start(bf16[128,640]{1,0:T(8,128)(2,1)S(1)} %collective-permute-done.1.refs_2_.refs_1_), channel_id=1, source_target_pairs={{0,8},{1,9},{2,10},{3,11},{4,12},{5,13},{6,14},{7,15},{8,0},{9,1},... | collective-permute-start | bytes 491528 | tf_op jit(solution)/shard_map/ppermute | solution.py:42
  27.8 4.2 %collective-permute-start.8 = (bf16[128,5120]{1,0:T(8,128)(2,1)S(1)}, bf16[128,5120]{1,0:T(8,128)(2,1)S(1)}, u32[]{:S(2)}, u32[]{:S(2)}) collective-permute-start(bf16[128,5120]{1,0:T(8,128)(2,1)S(1)} %get-tuple-element.38.refs_0_), channel_id=1, source_target_pairs={{0,1},{1,0},{2,3},{3,2},{4,5},{5,4},{6,7},{7,6},{8,9},{9,8},{10,11... | collective-permute-start | bytes 3932168 | tf_op jit(solution)/shard_map/ppermute | solution.py:34
  29.4 26.0 %collective-permute-start.19 = (bf16[256,2560]{1,0:T(8,128)(2,1)S(1)}, bf16[256,2560]{1,0:T(8,128)(2,1)S(1)}, u32[]{:S(2)}, u32[]{:S(2)}) collective-permute-start(bf16[256,2560]{1,0:T(8,128)(2,1)S(1)} %get-tuple-element.46), channel_id=1, source_target_pairs={{0,1},{1,0},{2,3},{3,2},{4,5},{5,4},{6,7},{7,6},{8,9},{9,8},{10,11... | collective-permute-start | bytes 3932168 | tf_op jit(solution)/shard_map/ppermute | solution.py:34
  30.7 6.0 %collective-permute-start.10 = (bf16[128,512]{1,0:T(8,128)(2,1)S(1)}, bf16[128,512]{1,0:T(8,128)(2,1)S(1)}, u32[]{:S(2)}, u32[]{:S(2)}) collective-permute-start(bf16[128,512]{1,0:T(8,128)(2,1)S(1)} %get-tuple-element.40.refs_3_.refs_1_), channel_id=1, source_target_pairs={{0,64},{16,80},{32,96},{48,112},{64,0},{80,16},{96,32},{112,48},{1... | collective-permute-start | bytes 393224 | tf_op jit(solution)/shard_map/ppermute | solution.py:26
  32.9 6.3 %collective-permute-start.11 = (bf16[128,512]{1,0:T(8,128)(2,1)S(1)}, bf16[128,512]{1,0:T(8,128)(2,1)S(1)}, u32[]{:S(2)}, u32[]{:S(2)}) collective-permute-start(bf16[128,512]{1,0:T(8,128)(2,1)S(1)} %shard_map.183.refs_4_.refs_2_), channel_id=1, source_target_pairs={{0,64},{16,80},{32,96},{48,112},{64,0},{80,16},{96,32},{112,48},{1... | collective-permute-start | bytes 393224 | tf_op jit(solution)/shard_map/ppermute | solution.py:26
  34.0 5.6 %collective-permute-start.14 = (bf16[256,256]{1,0:T(8,128)(2,1)S(1)}, bf16[256,256]{1,0:T(8,128)(2,1)S(1)}, u32[]{:S(2)}, u32[]{:S(2)}) collective-permute-start(bf16[256,256]{1,0:T(8,128)(2,1)S(1)} %shard_map.182.refs_0_), channel_id=1, source_target_pairs={{0,16},{16,32},{32,48},{48,0},{64,80},{80,96},{96,112},{112,64},{1... | collective-permute-start | bytes 393224 | tf_op jit(solution)/shard_map/ppermute | solution.py:30
  35.2 7.4 %collective-permute-start.13 = (bf16[256,256]{1,0:T(8,128)(2,1)S(1)}, bf16[256,256]{1,0:T(8,128)(2,1)S(1)}, u32[]{:S(2)}, u32[]{:S(2)}) collective-permute-start(bf16[256,256]{1,0:T(8,128)(2,1)S(1)} %shard_map.182.refs_0_), channel_id=1, source_target_pairs={{0,48},{16,0},{32,16},{48,32},{64,112},{80,64},{96,80},{112,96},{1... | collective-permute-start | bytes 393224 | tf_op jit(solution)/shard_map/ppermute | solution.py:30
  36.7 7.4 %collective-permute-start.12 = (bf16[256,256]{1,0:T(8,128)(2,1)S(1)}, bf16[256,256]{1,0:T(8,128)(2,1)S(1)}, u32[]{:S(2)}, u32[]{:S(2)}) collective-permute-start(bf16[256,256]{1,0:T(8,128)(2,1)S(1)} %shard_map.182.refs_0_), channel_id=1, source_target_pairs={{0,32},{16,48},{32,0},{48,16},{64,96},{80,112},{96,64},{112,80},{1... | collective-permute-start | bytes 393224 | tf_op jit(solution)/shard_map/ppermute | solution.py:30
  40.9 7.3 %collective-permute-start.15 = (bf16[272,256]{1,0:T(8,128)(2,1)S(1)}, bf16[272,256]{1,0:T(8,128)(2,1)S(1)}, u32[]{:S(2)}, u32[]{:S(2)}) collective-permute-start(bf16[272,256]{1,0:T(8,128)(2,1)S(1)} %shard_map.185.refs_7_), channel_id=1, source_target_pairs={{0,48},{16,0},{32,16},{48,32},{64,112},{80,64},{96,80},{112,96},{1... | collective-permute-start | bytes 417800 | tf_op jit(solution)/shard_map/ppermute | solution.py:30
  44.0 5.2 %collective-permute-start.16 = (bf16[272,256]{1,0:T(8,128)(2,1)S(1)}, bf16[272,256]{1,0:T(8,128)(2,1)S(1)}, u32[]{:S(2)}, u32[]{:S(2)}) collective-permute-start(bf16[272,256]{1,0:T(8,128)(2,1)S(1)} %shard_map.186.refs_7_), channel_id=1, source_target_pairs={{0,16},{16,32},{32,48},{48,0},{64,80},{80,96},{96,112},{112,64},{1... | collective-permute-start | bytes 417800 | tf_op jit(solution)/shard_map/ppermute | solution.py:30
  45.5 5.7 %collective-permute-start.17 = (bf16[272,256]{1,0:T(8,128)(2,1)S(1)}, bf16[272,256]{1,0:T(8,128)(2,1)S(1)}, u32[]{:S(2)}, u32[]{:S(2)}) collective-permute-start(bf16[272,256]{1,0:T(8,128)(2,1)S(1)} %shard_map.187.refs_8_), channel_id=1, source_target_pairs={{0,32},{16,48},{32,0},{48,16},{64,96},{80,112},{96,64},{112,80},{1... | collective-permute-start | bytes 417800 | tf_op jit(solution)/shard_map/ppermute | solution.py:30
  51.8 4.6 %collective-permute-start.18 = (bf16[256,256]{1,0:T(8,128)(2,1)S(1)}, bf16[256,256]{1,0:T(8,128)(2,1)S(1)}, u32[]{:S(2)}, u32[]{:S(2)}) collective-permute-start(bf16[256,256]{1,0:T(8,128)(2,1)S(1)} %shard_map.191.refs_1_), channel_id=1, source_target_pairs={{0,1},{1,0},{2,3},{3,2},{4,5},{5,4},{6,7},{7,6},{8,9},{9,8},{10,11... | collective-permute-start | bytes 393224 | tf_op jit(solution)/shard_map/ppermute | solution.py:34
  57.2 7.0 %collective-permute-start.24 = (bf16[32,2560]{1,0:T(8,128)(2,1)S(1)}, bf16[32,2560]{1,0:T(8,128)(2,1)S(1)}, u32[]{:S(2)}, u32[]{:S(2)}) collective-permute-start(bf16[32,2560]{1,0:T(8,128)(2,1)S(1)} %get-tuple-element.53), channel_id=1, source_target_pairs={{0,4},{1,5},{2,6},{3,7},{4,8},{5,9},{6,10},{7,11},{8,12},{9,13},{1... | collective-permute-start | bytes 491528 | tf_op jit(solution)/shard_map/ppermute | solution.py:42
  58.1 6.1 %collective-permute-start.25 = (bf16[32,2560]{1,0:T(8,128)(2,1)S(1)}, bf16[32,2560]{1,0:T(8,128)(2,1)S(1)}, u32[]{:S(2)}, u32[]{:S(2)}) collective-permute-start(bf16[32,2560]{1,0:T(8,128)(2,1)S(1)} %get-tuple-element.54), channel_id=1, source_target_pairs={{0,12},{1,13},{2,14},{3,15},{4,0},{5,1},{6,2},{7,3},{8,4},{9,5},{1... | collective-permute-start | bytes 491528 | tf_op jit(solution)/shard_map/ppermute | solution.py:42
  59.9 6.3 %collective-permute-start.22 = (bf16[32,2560]{1,0:T(8,128)(2,1)S(1)}, bf16[32,2560]{1,0:T(8,128)(2,1)S(1)}, u32[]{:S(2)}, u32[]{:S(2)}) collective-permute-start(bf16[32,2560]{1,0:T(8,128)(2,1)S(1)} %get-tuple-element.51), channel_id=1, source_target_pairs={{0,2},{1,3},{2,0},{3,1},{4,6},{5,7},{6,4},{7,5},{8,10},{9,11},{10,... | collective-permute-start | bytes 491528 | tf_op jit(solution)/shard_map/ppermute | solution.py:38
  61.5 5.7 %collective-permute-start.20 = (bf16[32,2560]{1,0:T(8,128)(2,1)S(1)}, bf16[32,2560]{1,0:T(8,128)(2,1)S(1)}, u32[]{:S(2)}, u32[]{:S(2)}) collective-permute-start(bf16[32,2560]{1,0:T(8,128)(2,1)S(1)} %get-tuple-element.48), channel_id=1, source_target_pairs={{0,4},{1,5},{2,6},{3,7},{4,8},{5,9},{6,10},{7,11},{8,12},{9,13},{1... | collective-permute-start | bytes 491528 | tf_op jit(solution)/shard_map/ppermute | solution.py:42
  61.5 5.7 %collective-permute-start.21 = (bf16[32,2560]{1,0:T(8,128)(2,1)S(1)}, bf16[32,2560]{1,0:T(8,128)(2,1)S(1)}, u32[]{:S(2)}, u32[]{:S(2)}) collective-permute-start(bf16[32,2560]{1,0:T(8,128)(2,1)S(1)} %get-tuple-element.49), channel_id=1, source_target_pairs={{0,12},{1,13},{2,14},{3,15},{4,0},{5,1},{6,2},{7,3},{8,4},{9,5},{1... | collective-permute-start | bytes 491528 | tf_op jit(solution)/shard_map/ppermute | solution.py:42
  64.2 5.8 %collective-permute-start.26 = (bf16[32,2560]{1,0:T(8,128)(2,1)S(1)}, bf16[32,2560]{1,0:T(8,128)(2,1)S(1)}, u32[]{:S(2)}, u32[]{:S(2)}) collective-permute-start(bf16[32,2560]{1,0:T(8,128)(2,1)S(1)} %shard_map.194), channel_id=1, source_target_pairs={{0,2},{1,3},{2,0},{3,1},{4,6},{5,7},{6,4},{7,5},{8,10},{9,11},{10,... | collective-permute-start | bytes 491528 | tf_op jit(solution)/shard_map/ppermute | solution.py:38
  66.2 9.0 %copy-start.11 = (f32[5120]{0:T(1024)S(1)}, f32[5120]{0:T(1024)}, u32[]{:S(2)}) copy-start(f32[5120]{0:T(1024)} %param.19) | copy-start | bytes 61444
  66.2 9.0 %copy-start.12 = (f32[5120]{0:T(1024)S(1)}, f32[5120]{0:T(1024)}, u32[]{:S(2)}) copy-start(f32[5120]{0:T(1024)} %param.26) | copy-start | bytes 61444
  66.2 10.1 %copy-start.1 = (bf16[5120,64]{0,1:T(8,128)(2,1)S(1)}, bf16[5120,64]{0,1:T(8,128)(2,1)}, u32[]{:S(2)}) copy-start(bf16[5120,64]{0,1:T(8,128)(2,1)} %param.27) | copy-start | bytes 1966084
  66.2 10.1 %copy-start.6 = (f32[4,256]{1,0:T(4,128)S(1)}, f32[4,256]{1,0:T(4,128)}, u32[]{:S(2)}) copy-start(f32[4,256]{1,0:T(4,128)} %refs_7_.1) | copy-start | bytes 12292
  66.3 10.0 %copy-start.7 = (f32[4,256]{1,0:T(4,128)S(1)}, f32[4,256]{1,0:T(4,128)}, u32[]{:S(2)}) copy-start(f32[4,256]{1,0:T(4,128)} %refs_8_.1) | copy-start | bytes 12292
  66.3 10.0 %copy-start.8 = (s32[4,1]{0,1:T(1,128)S(1)}, s32[4,1]{0,1:T(1,128)}, u32[]{:S(2)}) copy-start(s32[4,1]{0,1:T(1,128)} %param.30) | copy-start | bytes 52
  66.3 23.6 %copy-start.2 = (bf16[256,1024]{1,0:T(8,128)(2,1)S(1)}, bf16[256,1024]{1,0:T(8,128)(2,1)}, u32[]{:S(2)}) copy-start(bf16[256,1024]{1,0:T(8,128)(2,1)} %refs_1_.7) | copy-start | bytes 1572868
  66.3 6.0 %collective-permute-start.23 = (bf16[32,2560]{1,0:T(8,128)(2,1)S(1)}, bf16[32,2560]{1,0:T(8,128)(2,1)S(1)}, u32[]{:S(2)}, u32[]{:S(2)}) collective-permute-start(bf16[32,2560]{1,0:T(8,128)(2,1)S(1)} %shard_map.193), channel_id=1, source_target_pairs={{0,8},{1,9},{2,10},{3,11},{4,12},{5,13},{6,14},{7,15},{8,0},{9,1},... | collective-permute-start | bytes 491528 | tf_op jit(solution)/shard_map/ppermute | solution.py:42
  72.5 3.8 %collective-permute-start.27 = (f32[16,2560]{1,0:T(8,128)S(1)}, f32[16,2560]{1,0:T(8,128)S(1)}, u32[]{:S(2)}, u32[]{:S(2)}) collective-permute-start(f32[16,2560]{1,0:T(8,128)S(1)} %get-tuple-element.56), channel_id=1, source_target_pairs={{0,1},{1,0},{2,3},{3,2},{4,5},{5,4},{6,7},{7,6},{8,9},{9,8},{10,11... | collective-permute-start | bytes 491528 | tf_op jit(solution)/shard_map/ppermute | solution.py:34

commit v7 on v6

--- a/solution.py
+++ b/solution.py
@@ -282,18 +282,26 @@
         out_ref[:, cols] = merged.astype(BF)
 
 
-def out_body(mdl_ref, own_ref, other_ref, wa_ref, wb_ref, *refs):
-    *out_refs, x = refs
+def in_slots(mdl_ref, own_ref, x):
     for s, chip in enumerate(slot_chips(mdl_ref[0], False)):
         for k in range(2):
             rows = pl.ds(pl.multiple_of(128 * k + 16 * chip, 16), 16)
-            x[s * 32 + 16 * k : s * 32 + 16 * k + 16, :256] = own_ref[rows, :]
-            x[s * 32 + 16 * k : s * 32 + 16 * k + 16, 256:] = other_ref[rows, :]
-    for at in range(0, wa_ref.shape[1], 512):
+            x[s * 32 + 16 * k : s * 32 + 16 * k + 16, :] = own_ref[rows, :]
+
+
+def own_out_body(mdl_ref, own_ref, w_ref, part_ref, x):
+    in_slots(mdl_ref, own_ref, x)
+    for at in range(0, w_ref.shape[1], 512):
         cols = slice(at, at + 512)
-        r = jnp.dot(x[:, :256], wa_ref[:, cols], preferred_element_type=F32) + jnp.dot(
-            x[:, 256:], wb_ref[:, cols], preferred_element_type=F32
-        )
+        part_ref[:, cols] = jnp.dot(x[...], w_ref[:, cols], preferred_element_type=F32)
+
+
+def out_body(mdl_ref, other_ref, w_ref, part_ref, *refs):
+    *out_refs, x = refs
+    in_slots(mdl_ref, other_ref, x)
+    for at in range(0, w_ref.shape[1], 512):
+        cols = slice(at, at + 512)
+        r = part_ref[:, cols] + jnp.dot(x[...], w_ref[:, cols], preferred_element_type=F32)
         for s, out_ref in enumerate(out_refs):
             out_ref[:, cols] = r[32 * s : 32 * s + 32].astype(BF)
 
@@ -507,14 +515,23 @@
         )
     attended = call(merge_body, shape((count, cols), BF), (*kept, *back), nbytes=MIB)
 
+    part_out = call(
+        own_out_body,
+        shape((count, half), F32),
+        (mdl_1, attended, w_mine),
+        smem=(0,),
+        flops=2 * count * 256 * half,
+        nbytes=4 * MIB,
+        scratch=[pltpu.VMEM((count, cols), BF)],
+    )
     projected = call(
         out_body,
         tuple(shape((2 * block, half), BF) for _ in range(chips)),
-        (mdl_1, attended, core_swap(attended), w_mine, w_theirs),
+        (mdl_1, core_swap(attended), w_theirs, part_out),
         smem=(0,),
         flops=2 * count * 512 * half,
         nbytes=4 * MIB,
-        scratch=[pltpu.VMEM((count, 2 * cols), BF)],
+        scratch=[pltpu.VMEM((count, cols), BF)],
     )
     def added(*parts, flops=0):
         return call(add_body, shape(parts[0].shape, BF), parts, flops=flops)

time: 90.9 us -> 90.6 us (level)
    pallas_call x23 -> x24, Pallas kernels: 17.8 us -> 18 us  [call(): pl.pallas_call(run, out_shape=outs, in_specs=place + [pl.BlockSpec(memory...]
where the time goes in v7:
time: 90.6 us; the launch traced here: 90.4 us
  starting transfers between devices  39.4 us (43%)
  Pallas kernels  18 us (20%)
  waiting for transfers between devices  17.2 us (19%)
  blocking collectives  11.9 us (13%)
  local copies, waits for them, and re-layouts  2.88 us (3%)
  between operations  0.94 us (1%)
    pallas_call x24, Pallas kernels, call(): pl.pallas_call(run, out_shape=outs, in_specs=place + [pl.BlockSpec(memory...  18 us
    ppermute x11, starting transfers between devices, z_send(): return lax.ppermute(a, 'mdl', [(m, (m + 4 * by) % 16) for m in range(16)])  14.3 us
    all_to_all x1, blocking collectives, shards(): lax.all_to_all(slot_rows, 'mdl', split_axis=0, concat_axis=0, tiled=True)  11.9 us
    ppermute x5, starting transfers between devices, core_swap(): return lax.ppermute(a, 'mdl', CORE_SWAP)  9.51 us
    ppermute x6, starting transfers between devices, x_send(): lax.ppermute(a, 'ctx', [(c, c // 4 * 4 + (c + by) % 4) for c in range(8)])  7.85 us
    ppermute x11, waiting for transfers between devices, z_send(): return lax.ppermute(a, 'mdl', [(m, (m + 4 * by) % 16) for m in range(16)])  7.42 us
    ppermute x3, starting transfers between devices, pair_swap(): return lax.ppermute(a, 'mdl', PAIR_SWAP)  6.13 us
    ppermute x6, waiting for transfers between devices, x_send(): lax.ppermute(a, 'ctx', [(c, c // 4 * 4 + (c + by) % 4) for c in range(8)])  3.32 us
  transfers between devices with their start and end apart: 28, of which 14 were waited for; matrix products, arithmetic and copies ran while one was open for 0% of the time, Pallas kernels for 16%

profile of v7, /device:TPU:1, one launch (start us, length us, event | category | flops | bytes accessed | tf_op | source)
XLA Modules:
  0.0 90.4 jit_solution(8288601529992069519)
XLA Ops:
  0.7 0.9 %copy-done.5 = bf16[256,320]{0,1:T(8,128)(2,1)S(1)} copy-done((bf16[256,320]{0,1:T(8,128)(2,1)S(1)}, bf16[256,320]{0,1:T(8,128)(2,1)}, u32[]{:S(2)}) %copy-start.5) | copy-done | bytes 163864
  1.6 0.1 shard_map.175
  1.7 1.5 %collective-permute-start = (bf16[128,320]{1,0:T(8,128)(2,1)S(1)}, bf16[128,320]{1,0:T(8,128)(2,1)S(1)}, u32[]{:S(2)}, u32[]{:S(2)}) collective-permute-start(bf16[128,320]{1,0:T(8,128)(2,1)S(1)} %get-tuple-element.33), channel_id=1, source_target_pairs={{0,1},{1,0},{2,3},{3,2},{4,5},{5,4},{6,7},{7,6},{8,9},{9,8},{10,11... | collective-permute-start | bytes 245768 | tf_op jit(solution)/shard_map/ppermute | solution.py:34
  3.2 0.9 %collective-permute-done = bf16[128,320]{1,0:T(8,128)(2,1)S(1)} collective-permute-done((bf16[128,320]{1,0:T(8,128)(2,1)S(1)}, bf16[128,320]{1,0:T(8,128)(2,1)S(1)}, u32[]{:S(2)}, u32[]{:S(2)}) %collective-permute-start) | collective-permute-done | bytes 81952 | tf_op jit(solution)/shard_map/ppermute | solution.py:34
  4.2 0.1 pad_maximum_fusion.refs_1_
  4.3 3.1 %collective-permute-start.1 = (bf16[128,640]{1,0:T(8,128)(2,1)S(1)}, bf16[128,640]{1,0:T(8,128)(2,1)S(1)}, u32[]{:S(2)}, u32[]{:S(2)}) collective-permute-start(bf16[128,640]{1,0:T(8,128)(2,1)S(1)} %pad_maximum_fusion.refs_1_), channel_id=1, source_target_pairs={{0,2},{1,3},{2,0},{3,1},{4,6},{5,7},{6,4},{7,5},{8,10},{9,11},{10,... | collective-permute-start | bytes 491528 | tf_op jit(solution)/shard_map/ppermute | solution.py:38
  7.3 1.6 %collective-permute-start.2 = (bf16[128,640]{1,0:T(8,128)(2,1)S(1)}, bf16[128,640]{1,0:T(8,128)(2,1)S(1)}, u32[]{:S(2)}, u32[]{:S(2)}) collective-permute-start(bf16[128,640]{1,0:T(8,128)(2,1)S(1)} %pad_maximum_fusion.refs_1_), channel_id=1, source_target_pairs={{0,4},{1,5},{2,6},{3,7},{4,8},{5,9},{6,10},{7,11},{8,12},{9,13},{1... | collective-permute-start | bytes 491528 | tf_op jit(solution)/shard_map/ppermute | solution.py:42
  9.0 2.1 %collective-permute-start.3 = (bf16[128,640]{1,0:T(8,128)(2,1)S(1)}, bf16[128,640]{1,0:T(8,128)(2,1)S(1)}, u32[]{:S(2)}, u32[]{:S(2)}) collective-permute-start(bf16[128,640]{1,0:T(8,128)(2,1)S(1)} %pad_maximum_fusion.refs_1_), channel_id=1, source_target_pairs={{0,12},{1,13},{2,14},{3,15},{4,0},{5,1},{6,2},{7,3},{8,4},{9,5},{1... | collective-permute-start | bytes 491528 | tf_op jit(solution)/shard_map/ppermute | solution.py:42
  11.1 1.3 %collective-permute-start.4 = (bf16[128,640]{1,0:T(8,128)(2,1)S(1)}, bf16[128,640]{1,0:T(8,128)(2,1)S(1)}, u32[]{:S(2)}, u32[]{:S(2)}) collective-permute-start(bf16[128,640]{1,0:T(8,128)(2,1)S(1)} %pad_maximum_fusion.refs_1_), channel_id=1, source_target_pairs={{0,8},{1,9},{2,10},{3,11},{4,12},{5,13},{6,14},{7,15},{8,0},{9,1},... | collective-permute-start | bytes 491528 | tf_op jit(solution)/shard_map/ppermute | solution.py:42
  12.4 0.9 %copy-done.3 = bf16[512,256]{1,0:T(8,128)(2,1)S(1)} copy-done((bf16[512,256]{1,0:T(8,128)(2,1)S(1)}, bf16[512,256]{1,0:T(8,128)(2,1)}, u32[]{:S(2)}) %copy-start.3) | copy-done | bytes 262168
  13.4 0.9 %copy-done.4 = bf16[512,256]{1,0:T(8,128)(2,1)S(1)} copy-done((bf16[512,256]{1,0:T(8,128)(2,1)S(1)}, bf16[512,256]{1,0:T(8,128)(2,1)}, u32[]{:S(2)}) %copy-start.4) | copy-done | bytes 262168
  14.4 0.5 collective-permute-start.9
  15.0 0.8 collective-permute-start.5
  15.8 1.9 %collective-permute-start.6 = (bf16[128,640]{1,0:T(8,128)(2,1)S(1)}, bf16[128,640]{1,0:T(8,128)(2,1)S(1)}, u32[]{:S(2)}, u32[]{:S(2)}) collective-permute-start(bf16[128,640]{1,0:T(8,128)(2,1)S(1)} %collective-permute-done.1.refs_2_.refs_1_), channel_id=1, source_target_pairs={{0,12},{1,13},{2,14},{3,15},{4,0},{5,1},{6,2},{7,3},{8,4},{9,5},{1... | collective-permute-start | bytes 491528 | tf_op jit(solution)/shard_map/ppermute | solution.py:42
  17.7 0.5 collective-permute-start.7
  18.2 1.3 %collective-permute-done.4.refs_5_ = bf16[128,640]{1,0:T(8,128)(2,1)S(1)} collective-permute-done((bf16[128,640]{1,0:T(8,128)(2,1)S(1)}, bf16[128,640]{1,0:T(8,128)(2,1)S(1)}, u32[]{:S(2)}, u32[]{:S(2)}) %collective-permute-start.4) | collective-permute-done | bytes 163872 | tf_op jit(solution)/shard_map/ppermute | solution.py:42
  19.4 3.3 %shard_map.177 = (bf16[5120,256]{1,0:T(8,128)(2,1)S(1)}, bf16[5120,256]{1,0:T(8,128)(2,1)S(1)}, bf16[5120,256]{1,0:T(8,128)(2,1)S(1)}) custom-call(bf16[5120,256]{1,0:T(8,128)(2,1)} %refs_0_.2, bf16[5120,256]{1,0:T(8,128)(2,1)} %refs_1_.5, bf16[5120,256]{1,0:T(8,128)(2,1)} %refs_2_.1, bf16[128,640]{1,0:T(8,128)(2,1)S(1)} %collective-permute-done.2.refs_3_, ...), custom_call_target="tpu_custom_call" | custom-call | flops 5000000000 | bytes 8388608 | tf_op jit(solution)/shard_map/pallas_call | solution.py:60
  22.8 0.5 collective-permute-done.5.refs_2_.refs_6_
  23.3 0.2 shard_map.176
  23.5 3.0 %collective-permute-done.7.refs_8_ = bf16[128,640]{1,0:T(8,128)(2,1)S(1)} collective-permute-done((bf16[128,640]{1,0:T(8,128)(2,1)S(1)}, bf16[128,640]{1,0:T(8,128)(2,1)S(1)}, u32[]{:S(2)}, u32[]{:S(2)}) %collective-permute-start.7) | collective-permute-done | bytes 163872 | tf_op jit(solution)/shard_map/ppermute | solution.py:42
  26.5 1.3 %shard_map.178 = (bf16[128,5120]{1,0:T(8,128)(2,1)S(1)}, bf16[8,16,640]{2,1,0:T(8,128)(2,1)S(1)}) custom-call(s32[1]{0:T(128)} %bitcast.1.refs_0_, bf16[128,640]{1,0:T(8,128)(2,1)S(1)} %pad_maximum_fusion.refs_1_, bf16[128,640]{1,0:T(8,128)(2,1)S(1)} %collective-permute-done.1.refs_2_.refs_1_, bf16[128,640]{1,0:T(8,128)(2,1)S(1)} %collective-permute-done.2.refs_3_, ...), custom_call_target="tpu_custom_call" | custom-call | flops 1048576 | bytes 1048576 | tf_op jit(solution)/shard_map/pallas_call | solution.py:60
  27.8 1.6 %collective-permute-start.8 = (bf16[128,5120]{1,0:T(8,128)(2,1)S(1)}, bf16[128,5120]{1,0:T(8,128)(2,1)S(1)}, u32[]{:S(2)}, u32[]{:S(2)}) collective-permute-start(bf16[128,5120]{1,0:T(8,128)(2,1)S(1)} %get-tuple-element.38.refs_0_), channel_id=1, source_target_pairs={{0,1},{1,0},{2,3},{3,2},{4,5},{5,4},{6,7},{7,6},{8,9},{9,8},{10,11... | collective-permute-start | bytes 3932168 | tf_op jit(solution)/shard_map/ppermute | solution.py:34
  29.4 0.1 collective-permute-start.19
  29.4 1.2 %shard_map.181 = (bf16[128,512]{1,0:T(8,128)(2,1)S(1)}, bf16[128,256]{1,0:T(8,128)(2,1)S(1)}) custom-call(bf16[128,5120]{1,0:T(8,128)(2,1)S(1)} %get-tuple-element.38.refs_0_, bf16[5120,256]{1,0:T(8,128)(2,1)S(1)} %get-tuple-element.36.refs_13_.refs_1_, bf16[5120,256]{1,0:T(8,128)(2,1)S(1)} %get-tuple-element.37.refs_14_.refs_2_, ...), custom_call_target="tpu_custom_call" | custom-call | flops 30000001024 | bytes 8388608 | tf_op jit(solution)/shard_map/pallas_call | solution.py:60
  30.7 0.6 collective-permute-start.10
  31.3 0.7 collective-permute-done.8.refs_1_.refs_0_
  32.0 0.8 shard_map.183.refs_4_.refs_2_
  32.9 0.6 collective-permute-start.11
  33.4 0.5 shard_map.182.refs_0_
  34.0 1.3 %collective-permute-start.14 = (bf16[256,256]{1,0:T(8,128)(2,1)S(1)}, bf16[256,256]{1,0:T(8,128)(2,1)S(1)}, u32[]{:S(2)}, u32[]{:S(2)}) collective-permute-start(bf16[256,256]{1,0:T(8,128)(2,1)S(1)} %shard_map.182.refs_0_), channel_id=1, source_target_pairs={{0,16},{16,32},{32,48},{48,0},{64,80},{80,96},{96,112},{112,64},{1... | collective-permute-start | bytes 393224 | tf_op jit(solution)/shard_map/ppermute | solution.py:30
  35.2 1.5 %collective-permute-start.13 = (bf16[256,256]{1,0:T(8,128)(2,1)S(1)}, bf16[256,256]{1,0:T(8,128)(2,1)S(1)}, u32[]{:S(2)}, u32[]{:S(2)}) collective-permute-start(bf16[256,256]{1,0:T(8,128)(2,1)S(1)} %shard_map.182.refs_0_), channel_id=1, source_target_pairs={{0,48},{16,0},{32,16},{48,32},{64,112},{80,64},{96,80},{112,96},{1... | collective-permute-start | bytes 393224 | tf_op jit(solution)/shard_map/ppermute | solution.py:30
  36.7 1.5 %collective-permute-start.12 = (bf16[256,256]{1,0:T(8,128)(2,1)S(1)}, bf16[256,256]{1,0:T(8,128)(2,1)S(1)}, u32[]{:S(2)}, u32[]{:S(2)}) collective-permute-start(bf16[256,256]{1,0:T(8,128)(2,1)S(1)} %shard_map.182.refs_0_), channel_id=1, source_target_pairs={{0,32},{16,48},{32,0},{48,16},{64,96},{80,112},{96,64},{112,80},{1... | collective-permute-start | bytes 393224 | tf_op jit(solution)/shard_map/ppermute | solution.py:30
  38.2 0.9 %shard_map.184 = (f32[256,256]{1,0:T(8,128)S(1)}, f32[2,256,128]{2,1,0:T(8,128)S(1)}, f32[2,256,128]{2,1,0:T(8,128)S(1)}) custom-call(bf16[256,256]{1,0:T(8,128)(2,1)S(1)} %shard_map.182.refs_0_, bf16[512,512]{1,0:T(8,128)(2,1)S(1)} %shard_map.179.refs_0_.refs_1_, bf16[512,512]{1,0:T(8,128)(2,1)S(1)} %collective-permute-done.9.refs_4_.refs_2_), custom_call_target="tpu_custom_call" | custom-call | flops 1048576 | bytes 1048576 | tf_op jit(solution)/shard_map/pallas_call | solution.py:60
  39.2 0.4 collective-permute-done.14.refs_0_
  39.5 1.4 %shard_map.185.refs_7_ = bf16[272,256]{1,0:T(8,128)(2,1)S(1)} custom-call(bf16[256,256]{1,0:T(8,128)(2,1)S(1)} %collective-permute-done.14.refs_0_, bf16[512,512]{1,0:T(8,128)(2,1)S(1)} %shard_map.179.refs_0_.refs_1_, bf16[512,512]{1,0:T(8,128)(2,1)S(1)} %collective-permute-done.9.refs_4_.refs_2_, bf16[128,512]{1,0:T(8,128)(2,1)S(1)} %get-tuple-element.40.refs_3_.refs_1_, ...), custom_call_target="tpu_custom_call" | custom-call | flops 1048576 | bytes 1048576 | tf_op jit(solution)/shard_map/pallas_call | solution.py:60
  40.9 1.7 %collective-permute-start.15 = (bf16[272,256]{1,0:T(8,128)(2,1)S(1)}, bf16[272,256]{1,0:T(8,128)(2,1)S(1)}, u32[]{:S(2)}, u32[]{:S(2)}) collective-permute-start(bf16[272,256]{1,0:T(8,128)(2,1)S(1)} %shard_map.185.refs_7_), channel_id=1, source_target_pairs={{0,48},{16,0},{32,16},{48,32},{64,112},{80,64},{96,80},{112,96},{1... | collective-permute-start | bytes 417800 | tf_op jit(solution)/shard_map/ppermute | solution.py:30
  42.6 1.4 %shard_map.186.refs_7_ = bf16[272,256]{1,0:T(8,128)(2,1)S(1)} custom-call(bf16[256,256]{1,0:T(8,128)(2,1)S(1)} %collective-permute-done.13.refs_0_, bf16[512,512]{1,0:T(8,128)(2,1)S(1)} %shard_map.179.refs_0_.refs_1_, bf16[512,512]{1,0:T(8,128)(2,1)S(1)} %collective-permute-done.9.refs_4_.refs_2_, bf16[128,512]{1,0:T(8,128)(2,1)S(1)} %get-tuple-element.40.refs_3_.refs_1_, ...), custom_call_target="tpu_custom_call" | custom-call | flops 1048576 | bytes 1048576 | tf_op jit(solution)/shard_map/pallas_call | solution.py:60
  44.0 0.1 collective-permute-start.16
  44.1 1.4 %shard_map.187.refs_8_ = bf16[272,256]{1,0:T(8,128)(2,1)S(1)} custom-call(bf16[256,256]{1,0:T(8,128)(2,1)S(1)} %collective-permute-done.12.refs_0_, bf16[512,512]{1,0:T(8,128)(2,1)S(1)} %shard_map.179.refs_0_.refs_1_, bf16[512,512]{1,0:T(8,128)(2,1)S(1)} %collective-permute-done.9.refs_4_.refs_2_, bf16[128,512]{1,0:T(8,128)(2,1)S(1)} %get-tuple-element.40.refs_3_.refs_1_, ...), custom_call_target="tpu_custom_call" | custom-call | flops 1048576 | bytes 1048576 | tf_op jit(solution)/shard_map/pallas_call | solution.py:60
  45.5 1.8 %collective-permute-start.17 = (bf16[272,256]{1,0:T(8,128)(2,1)S(1)}, bf16[272,256]{1,0:T(8,128)(2,1)S(1)}, u32[]{:S(2)}, u32[]{:S(2)}) collective-permute-start(bf16[272,256]{1,0:T(8,128)(2,1)S(1)} %shard_map.187.refs_8_), channel_id=1, source_target_pairs={{0,32},{16,48},{32,0},{48,16},{64,96},{80,112},{96,64},{112,80},{1... | collective-permute-start | bytes 417800 | tf_op jit(solution)/shard_map/ppermute | solution.py:30
  47.3 0.9 %shard_map.188 = (f32[256,256]{1,0:T(8,128)S(1)}, f32[8,256]{1,0:T(8,128)S(1)}) custom-call(bf16[256,256]{1,0:T(8,128)(2,1)S(1)} %shard_map.182.refs_0_, bf16[128,512]{1,0:T(8,128)(2,1)S(1)} %get-tuple-element.40.refs_3_.refs_1_, bf16[128,512]{1,0:T(8,128)(2,1)S(1)} %shard_map.183.refs_4_.refs_2_, ...), custom_call_target="tpu_custom_call" | custom-call | flops 1048576 | bytes 1048576 | tf_op jit(solution)/shard_map/pallas_call | solution.py:60
  48.3 0.9 %collective-permute-done.16.refs_0_ = bf16[272,256]{1,0:T(8,128)(2,1)S(1)} collective-permute-done((bf16[272,256]{1,0:T(8,128)(2,1)S(1)}, bf16[272,256]{1,0:T(8,128)(2,1)S(1)}, u32[]{:S(2)}, u32[]{:S(2)}) %collective-permute-start.16) | collective-permute-done | bytes 139296 | tf_op jit(solution)/shard_map/ppermute | solution.py:30
  49.2 2.0 %collective-permute-done.17.refs_4_ = bf16[272,256]{1,0:T(8,128)(2,1)S(1)} collective-permute-done((bf16[272,256]{1,0:T(8,128)(2,1)S(1)}, bf16[272,256]{1,0:T(8,128)(2,1)S(1)}, u32[]{:S(2)}, u32[]{:S(2)}) %collective-permute-start.17) | collective-permute-done | bytes 139296 | tf_op jit(solution)/shard_map/ppermute | solution.py:30
  51.2 0.6 shard_map.191.refs_1_
  51.8 3.6 %collective-permute-start.18 = (bf16[256,256]{1,0:T(8,128)(2,1)S(1)}, bf16[256,256]{1,0:T(8,128)(2,1)S(1)}, u32[]{:S(2)}, u32[]{:S(2)}) collective-permute-start(bf16[256,256]{1,0:T(8,128)(2,1)S(1)} %shard_map.191.refs_1_), channel_id=1, source_target_pairs={{0,1},{1,0},{2,3},{3,2},{4,5},{5,4},{6,7},{7,6},{8,9},{9,8},{10,11... | collective-permute-start | bytes 393224 | tf_op jit(solution)/shard_map/ppermute | solution.py:34
  55.4 0.5 shard_map.192.refs_3_
  55.9 0.5 collective-permute-done.18.refs_1_
  56.4 0.5 shard_map.193
  56.9 0.9 collective-permute-start.24
  57.8 1.8 %collective-permute-start.25 = (bf16[32,2560]{1,0:T(8,128)(2,1)S(1)}, bf16[32,2560]{1,0:T(8,128)(2,1)S(1)}, u32[]{:S(2)}, u32[]{:S(2)}) collective-permute-start(bf16[32,2560]{1,0:T(8,128)(2,1)S(1)} %get-tuple-element.54), channel_id=1, source_target_pairs={{0,12},{1,13},{2,14},{3,15},{4,0},{5,1},{6,2},{7,3},{8,4},{9,5},{1... | collective-permute-start | bytes 491528 | tf_op jit(solution)/shard_map/ppermute | solution.py:42
  59.6 1.5 %collective-permute-start.22 = (bf16[32,2560]{1,0:T(8,128)(2,1)S(1)}, bf16[32,2560]{1,0:T(8,128)(2,1)S(1)}, u32[]{:S(2)}, u32[]{:S(2)}) collective-permute-start(bf16[32,2560]{1,0:T(8,128)(2,1)S(1)} %get-tuple-element.51), channel_id=1, source_target_pairs={{0,2},{1,3},{2,0},{3,1},{4,6},{5,7},{6,4},{7,5},{8,10},{9,11},{10,... | collective-permute-start | bytes 491528 | tf_op jit(solution)/shard_map/ppermute | solution.py:38
  61.2 2.7 %collective-permute-start.21 = (bf16[32,2560]{1,0:T(8,128)(2,1)S(1)}, bf16[32,2560]{1,0:T(8,128)(2,1)S(1)}, u32[]{:S(2)}, u32[]{:S(2)}) collective-permute-start(bf16[32,2560]{1,0:T(8,128)(2,1)S(1)} %get-tuple-element.49), channel_id=1, source_target_pairs={{0,12},{1,13},{2,14},{3,15},{4,0},{5,1},{6,2},{7,3},{8,4},{9,5},{1... | collective-permute-start | bytes 491528 | tf_op jit(solution)/shard_map/ppermute | solution.py:42
  63.9 1.5 %collective-permute-start.26 = (bf16[32,2560]{1,0:T(8,128)(2,1)S(1)}, bf16[32,2560]{1,0:T(8,128)(2,1)S(1)}, u32[]{:S(2)}, u32[]{:S(2)}) collective-permute-start(bf16[32,2560]{1,0:T(8,128)(2,1)S(1)} %shard_map.195), channel_id=1, source_target_pairs={{0,2},{1,3},{2,0},{3,1},{4,6},{5,7},{6,4},{7,5},{8,10},{9,11},{10,... | collective-permute-start | bytes 491528 | tf_op jit(solution)/shard_map/ppermute | solution.py:38
  65.4 0.5 collective-permute-done.22.refs_1_
  66.0 0.6 collective-permute-start.23
  66.6 0.2 collective-permute-done.20.refs_2_
  66.9 2.8 %collective-permute-done.26.refs_5_ = bf16[32,2560]{1,0:T(8,128)(2,1)S(1)} collective-permute-done((bf16[32,2560]{1,0:T(8,128)(2,1)S(1)}, bf16[32,2560]{1,0:T(8,128)(2,1)S(1)}, u32[]{:S(2)}, u32[]{:S(2)}) %collective-permute-start.26) | collective-permute-done | bytes 163872 | tf_op jit(solution)/shard_map/ppermute | solution.py:38
  69.7 2.4 %collective-permute-done.23.refs_4_ = bf16[32,2560]{1,0:T(8,128)(2,1)S(1)} collective-permute-done((bf16[32,2560]{1,0:T(8,128)(2,1)S(1)}, bf16[32,2560]{1,0:T(8,128)(2,1)S(1)}, u32[]{:S(2)}, u32[]{:S(2)}) %collective-permute-start.23) | collective-permute-done | bytes 163872 | tf_op jit(solution)/shard_map/ppermute | solution.py:42
  72.1 0.1 shard_map.196
  72.2 2.8 %collective-permute-start.27 = (f32[16,2560]{1,0:T(8,128)S(1)}, f32[16,2560]{1,0:T(8,128)S(1)}, u32[]{:S(2)}, u32[]{:S(2)}) collective-permute-start(f32[16,2560]{1,0:T(8,128)S(1)} %get-tuple-element.56), channel_id=1, source_target_pairs={{0,1},{1,0},{2,3},{3,2},{4,5},{5,4},{6,7},{7,6},{8,9},{9,8},{10,11... | collective-permute-start | bytes 491528 | tf_op jit(solution)/shard_map/ppermute | solution.py:34
  75.0 1.0 %collective-permute-done.27.refs_2_ = f32[16,2560]{1,0:T(8,128)S(1)} collective-permute-done((f32[16,2560]{1,0:T(8,128)S(1)}, f32[16,2560]{1,0:T(8,128)S(1)}, u32[]{:S(2)}, u32[]{:S(2)}) %collective-permute-start.27) | collective-permute-done | bytes 163872 | tf_op jit(solution)/shard_map/ppermute | solution.py:34
  76.0 1.7 %shard_map.197 = (bf16[16,5120]{1,0:T(8,128)(2,1)}, f32[4,256]{1,0:T(4,128)}, f32[16,2,256]{2,1,0:T(2,128)S(1)}) custom-call(s32[1]{0:T(128)} %bitcast.refs_0_, f32[16,2560]{1,0:T(8,128)S(1)} %get-tuple-element.55.refs_1_, f32[16,2560]{1,0:T(8,128)S(1)} %collective-permute-done.27.refs_2_, bf16[8,16,640]{2,1,0:T(8,128)(2,1)S(1)} %get-tuple-element.57.refs_3_, ...), custom_call_target="tpu_custom_call" | custom-call | bytes 2097152 | tf_op jit(solution)/shard_map/pallas_call | solution.py:60
  77.7 11.9 %all_to_all.5.refs_0_ = f32[16,2,256]{2,1,0:T(2,128)S(1)} all-to-all(f32[16,2,256]{2,1,0:T(2,128)S(1)} %get-tuple-element.60), channel_id=1, replica_groups=mesh['ctx'=8,'mdl'=16] {'mdl'}, dimensions={0} | all-to-all | bytes 65536 | tf_op jit(solution)/shard_map/all_to_all | solution.py:566
  89.6 0.9 shard_map.198
  (49 shorter events, 0.4 us)
Async XLA Ops:
  0.6 14.3 %copy-start.9 = (f32[5120]{0:T(1024)S(1)}, f32[5120]{0:T(1024)}, u32[]{:S(2)}) copy-start(f32[5120]{0:T(1024)} %param.18) | copy-start | bytes 61444
  0.7 0.9 %copy-start.5 = (bf16[256,320]{0,1:T(8,128)(2,1)S(1)}, bf16[256,320]{0,1:T(8,128)(2,1)}, u32[]{:S(2)}) copy-start(bf16[256,320]{0,1:T(8,128)(2,1)} %param.16) | copy-start | bytes 491524
  1.6 13.3 %copy-start.10 = (f32[5120]{0:T(1024)S(1)}, f32[5120]{0:T(1024)}, u32[]{:S(2)}) copy-start(f32[5120]{0:T(1024)} %param.17) | copy-start | bytes 61444
  1.7 2.4 %collective-permute-start = (bf16[128,320]{1,0:T(8,128)(2,1)S(1)}, bf16[128,320]{1,0:T(8,128)(2,1)S(1)}, u32[]{:S(2)}, u32[]{:S(2)}) collective-permute-start(bf16[128,320]{1,0:T(8,128)(2,1)S(1)} %get-tuple-element.33), channel_id=1, source_target_pairs={{0,1},{1,0},{2,3},{3,2},{4,5},{5,4},{6,7},{7,6},{8,9},{9,8},{10,11... | collective-permute-start | bytes 245768 | tf_op jit(solution)/shard_map/ppermute | solution.py:34
  4.3 10.1 %collective-permute-start.1 = (bf16[128,640]{1,0:T(8,128)(2,1)S(1)}, bf16[128,640]{1,0:T(8,128)(2,1)S(1)}, u32[]{:S(2)}, u32[]{:S(2)}) collective-permute-start(bf16[128,640]{1,0:T(8,128)(2,1)S(1)} %pad_maximum_fusion.refs_1_), channel_id=1, source_target_pairs={{0,2},{1,3},{2,0},{3,1},{4,6},{5,7},{6,4},{7,5},{8,10},{9,11},{10,... | collective-permute-start | bytes 491528 | tf_op jit(solution)/shard_map/ppermute | solution.py:38
  7.3 8.4 %collective-permute-start.2 = (bf16[128,640]{1,0:T(8,128)(2,1)S(1)}, bf16[128,640]{1,0:T(8,128)(2,1)S(1)}, u32[]{:S(2)}, u32[]{:S(2)}) collective-permute-start(bf16[128,640]{1,0:T(8,128)(2,1)S(1)} %pad_maximum_fusion.refs_1_), channel_id=1, source_target_pairs={{0,4},{1,5},{2,6},{3,7},{4,8},{5,9},{6,10},{7,11},{8,12},{9,13},{1... | collective-permute-start | bytes 491528 | tf_op jit(solution)/shard_map/ppermute | solution.py:42
  9.0 8.7 %collective-permute-start.3 = (bf16[128,640]{1,0:T(8,128)(2,1)S(1)}, bf16[128,640]{1,0:T(8,128)(2,1)S(1)}, u32[]{:S(2)}, u32[]{:S(2)}) collective-permute-start(bf16[128,640]{1,0:T(8,128)(2,1)S(1)} %pad_maximum_fusion.refs_1_), channel_id=1, source_target_pairs={{0,12},{1,13},{2,14},{3,15},{4,0},{5,1},{6,2},{7,3},{8,4},{9,5},{1... | collective-permute-start | bytes 491528 | tf_op jit(solution)/shard_map/ppermute | solution.py:42
  11.1 8.3 %collective-permute-start.4 = (bf16[128,640]{1,0:T(8,128)(2,1)S(1)}, bf16[128,640]{1,0:T(8,128)(2,1)S(1)}, u32[]{:S(2)}, u32[]{:S(2)}) collective-permute-start(bf16[128,640]{1,0:T(8,128)(2,1)S(1)} %pad_maximum_fusion.refs_1_), channel_id=1, source_target_pairs={{0,8},{1,9},{2,10},{3,11},{4,12},{5,13},{6,14},{7,15},{8,0},{9,1},... | collective-permute-start | bytes 491528 | tf_op jit(solution)/shard_map/ppermute | solution.py:42
  12.4 0.9 %copy-start.3 = (bf16[512,256]{1,0:T(8,128)(2,1)S(1)}, bf16[512,256]{1,0:T(8,128)(2,1)}, u32[]{:S(2)}) copy-start(bf16[512,256]{1,0:T(8,128)(2,1)} %refs_0_.3) | copy-start | bytes 786436
  13.4 0.9 %copy-start.4 = (bf16[512,256]{1,0:T(8,128)(2,1)S(1)}, bf16[512,256]{1,0:T(8,128)(2,1)}, u32[]{:S(2)}) copy-start(bf16[512,256]{1,0:T(8,128)(2,1)} %refs_1_.6) | copy-start | bytes 786436
  14.4 15.0 %collective-permute-start.9 = (bf16[512,512]{1,0:T(8,128)(2,1)S(1)}, bf16[512,512]{1,0:T(8,128)(2,1)S(1)}, u32[]{:S(2)}, u32[]{:S(2)}) collective-permute-start(bf16[512,512]{1,0:T(8,128)(2,1)S(1)} %shard_map.180), channel_id=1, source_target_pairs={{0,64},{16,80},{32,96},{48,112},{64,0},{80,16},{96,32},{112,48},{1... | collective-permute-start | bytes 1572872 | tf_op jit(solution)/shard_map/ppermute | solution.py:26
  14.9 8.4 %copy-start = (bf16[256,5120]{1,0:T(8,128)(2,1)S(1)}, bf16[256,5120]{1,0:T(8,128)(2,1)}, u32[]{:S(2)}) copy-start(bf16[256,5120]{1,0:T(8,128)(2,1)} %refs_1_.4) | copy-start | bytes 7864324
  15.0 8.3 %collective-permute-start.5 = (bf16[128,640]{1,0:T(8,128)(2,1)S(1)}, bf16[128,640]{1,0:T(8,128)(2,1)S(1)}, u32[]{:S(2)}, u32[]{:S(2)}) collective-permute-start(bf16[128,640]{1,0:T(8,128)(2,1)S(1)} %collective-permute-done.1.refs_2_.refs_1_), channel_id=1, source_target_pairs={{0,4},{1,5},{2,6},{3,7},{4,8},{5,9},{6,10},{7,11},{8,12},{9,13},{1... | collective-permute-start | bytes 491528 | tf_op jit(solution)/shard_map/ppermute | solution.py:42
  15.8 7.7 %collective-permute-start.6 = (bf16[128,640]{1,0:T(8,128)(2,1)S(1)}, bf16[128,640]{1,0:T(8,128)(2,1)S(1)}, u32[]{:S(2)}, u32[]{:S(2)}) collective-permute-start(bf16[128,640]{1,0:T(8,128)(2,1)S(1)} %collective-permute-done.1.refs_2_.refs_1_), channel_id=1, source_target_pairs={{0,12},{1,13},{2,14},{3,15},{4,0},{5,1},{6,2},{7,3},{8,4},{9,5},{1... | collective-permute-start | bytes 491528 | tf_op jit(solution)/shard_map/ppermute | solution.py:42
  17.7 8.7 %collective-permute-start.7 = (bf16[128,640]{1,0:T(8,128)(2,1)S(1)}, bf16[128,640]{1,0:T(8,128)(2,1)S(1)}, u32[]{:S(2)}, u32[]{:S(2)}) collective-permute-start(bf16[128,640]{1,0:T(8,128)(2,1)S(1)} %collective-permute-done.1.refs_2_.refs_1_), channel_id=1, source_target_pairs={{0,8},{1,9},{2,10},{3,11},{4,12},{5,13},{6,14},{7,15},{8,0},{9,1},... | collective-permute-start | bytes 491528 | tf_op jit(solution)/shard_map/ppermute | solution.py:42
  27.8 4.2 %collective-permute-start.8 = (bf16[128,5120]{1,0:T(8,128)(2,1)S(1)}, bf16[128,5120]{1,0:T(8,128)(2,1)S(1)}, u32[]{:S(2)}, u32[]{:S(2)}) collective-permute-start(bf16[128,5120]{1,0:T(8,128)(2,1)S(1)} %get-tuple-element.38.refs_0_), channel_id=1, source_target_pairs={{0,1},{1,0},{2,3},{3,2},{4,5},{5,4},{6,7},{7,6},{8,9},{9,8},{10,11... | collective-permute-start | bytes 3932168 | tf_op jit(solution)/shard_map/ppermute | solution.py:34
  29.4 26.5 %collective-permute-start.19 = (bf16[256,2560]{1,0:T(8,128)(2,1)S(1)}, bf16[256,2560]{1,0:T(8,128)(2,1)S(1)}, u32[]{:S(2)}, u32[]{:S(2)}) collective-permute-start(bf16[256,2560]{1,0:T(8,128)(2,1)S(1)} %get-tuple-element.46), channel_id=1, source_target_pairs={{0,1},{1,0},{2,3},{3,2},{4,5},{5,4},{6,7},{7,6},{8,9},{9,8},{10,11... | collective-permute-start | bytes 3932168 | tf_op jit(solution)/shard_map/ppermute | solution.py:34
  30.7 6.0 %collective-permute-start.10 = (bf16[128,512]{1,0:T(8,128)(2,1)S(1)}, bf16[128,512]{1,0:T(8,128)(2,1)S(1)}, u32[]{:S(2)}, u32[]{:S(2)}) collective-permute-start(bf16[128,512]{1,0:T(8,128)(2,1)S(1)} %get-tuple-element.40.refs_3_.refs_1_), channel_id=1, source_target_pairs={{0,64},{16,80},{32,96},{48,112},{64,0},{80,16},{96,32},{112,48},{1... | collective-permute-start | bytes 393224 | tf_op jit(solution)/shard_map/ppermute | solution.py:26
  32.9 6.3 %collective-permute-start.11 = (bf16[128,512]{1,0:T(8,128)(2,1)S(1)}, bf16[128,512]{1,0:T(8,128)(2,1)S(1)}, u32[]{:S(2)}, u32[]{:S(2)}) collective-permute-start(bf16[128,512]{1,0:T(8,128)(2,1)S(1)} %shard_map.183.refs_4_.refs_2_), channel_id=1, source_target_pairs={{0,64},{16,80},{32,96},{48,112},{64,0},{80,16},{96,32},{112,48},{1... | collective-permute-start | bytes 393224 | tf_op jit(solution)/shard_map/ppermute | solution.py:26
  34.0 5.6 %collective-permute-start.14 = (bf16[256,256]{1,0:T(8,128)(2,1)S(1)}, bf16[256,256]{1,0:T(8,128)(2,1)S(1)}, u32[]{:S(2)}, u32[]{:S(2)}) collective-permute-start(bf16[256,256]{1,0:T(8,128)(2,1)S(1)} %shard_map.182.refs_0_), channel_id=1, source_target_pairs={{0,16},{16,32},{32,48},{48,0},{64,80},{80,96},{96,112},{112,64},{1... | collective-permute-start | bytes 393224 | tf_op jit(solution)/shard_map/ppermute | solution.py:30
  35.2 7.4 %collective-permute-start.13 = (bf16[256,256]{1,0:T(8,128)(2,1)S(1)}, bf16[256,256]{1,0:T(8,128)(2,1)S(1)}, u32[]{:S(2)}, u32[]{:S(2)}) collective-permute-start(bf16[256,256]{1,0:T(8,128)(2,1)S(1)} %shard_map.182.refs_0_), channel_id=1, source_target_pairs={{0,48},{16,0},{32,16},{48,32},{64,112},{80,64},{96,80},{112,96},{1... | collective-permute-start | bytes 393224 | tf_op jit(solution)/shard_map/ppermute | solution.py:30
  36.7 7.4 %collective-permute-start.12 = (bf16[256,256]{1,0:T(8,128)(2,1)S(1)}, bf16[256,256]{1,0:T(8,128)(2,1)S(1)}, u32[]{:S(2)}, u32[]{:S(2)}) collective-permute-start(bf16[256,256]{1,0:T(8,128)(2,1)S(1)} %shard_map.182.refs_0_), channel_id=1, source_target_pairs={{0,32},{16,48},{32,0},{48,16},{64,96},{80,112},{96,64},{112,80},{1... | collective-permute-start | bytes 393224 | tf_op jit(solution)/shard_map/ppermute | solution.py:30
  40.9 7.3 %collective-permute-start.15 = (bf16[272,256]{1,0:T(8,128)(2,1)S(1)}, bf16[272,256]{1,0:T(8,128)(2,1)S(1)}, u32[]{:S(2)}, u32[]{:S(2)}) collective-permute-start(bf16[272,256]{1,0:T(8,128)(2,1)S(1)} %shard_map.185.refs_7_), channel_id=1, source_target_pairs={{0,48},{16,0},{32,16},{48,32},{64,112},{80,64},{96,80},{112,96},{1... | collective-permute-start | bytes 417800 | tf_op jit(solution)/shard_map/ppermute | solution.py:30
  44.0 5.2 %collective-permute-start.16 = (bf16[272,256]{1,0:T(8,128)(2,1)S(1)}, bf16[272,256]{1,0:T(8,128)(2,1)S(1)}, u32[]{:S(2)}, u32[]{:S(2)}) collective-permute-start(bf16[272,256]{1,0:T(8,128)(2,1)S(1)} %shard_map.186.refs_7_), channel_id=1, source_target_pairs={{0,16},{16,32},{32,48},{48,0},{64,80},{80,96},{96,112},{112,64},{1... | collective-permute-start | bytes 417800 | tf_op jit(solution)/shard_map/ppermute | solution.py:30
  45.5 5.7 %collective-permute-start.17 = (bf16[272,256]{1,0:T(8,128)(2,1)S(1)}, bf16[272,256]{1,0:T(8,128)(2,1)S(1)}, u32[]{:S(2)}, u32[]{:S(2)}) collective-permute-start(bf16[272,256]{1,0:T(8,128)(2,1)S(1)} %shard_map.187.refs_8_), channel_id=1, source_target_pairs={{0,32},{16,48},{32,0},{48,16},{64,96},{80,112},{96,64},{112,80},{1... | collective-permute-start | bytes 417800 | tf_op jit(solution)/shard_map/ppermute | solution.py:30
  51.8 4.6 %collective-permute-start.18 = (bf16[256,256]{1,0:T(8,128)(2,1)S(1)}, bf16[256,256]{1,0:T(8,128)(2,1)S(1)}, u32[]{:S(2)}, u32[]{:S(2)}) collective-permute-start(bf16[256,256]{1,0:T(8,128)(2,1)S(1)} %shard_map.191.refs_1_), channel_id=1, source_target_pairs={{0,1},{1,0},{2,3},{3,2},{4,5},{5,4},{6,7},{7,6},{8,9},{9,8},{10,11... | collective-permute-start | bytes 393224 | tf_op jit(solution)/shard_map/ppermute | solution.py:34
  56.9 7.0 %collective-permute-start.24 = (bf16[32,2560]{1,0:T(8,128)(2,1)S(1)}, bf16[32,2560]{1,0:T(8,128)(2,1)S(1)}, u32[]{:S(2)}, u32[]{:S(2)}) collective-permute-start(bf16[32,2560]{1,0:T(8,128)(2,1)S(1)} %get-tuple-element.53), channel_id=1, source_target_pairs={{0,4},{1,5},{2,6},{3,7},{4,8},{5,9},{6,10},{7,11},{8,12},{9,13},{1... | collective-permute-start | bytes 491528 | tf_op jit(solution)/shard_map/ppermute | solution.py:42
  57.8 6.1 %collective-permute-start.25 = (bf16[32,2560]{1,0:T(8,128)(2,1)S(1)}, bf16[32,2560]{1,0:T(8,128)(2,1)S(1)}, u32[]{:S(2)}, u32[]{:S(2)}) collective-permute-start(bf16[32,2560]{1,0:T(8,128)(2,1)S(1)} %get-tuple-element.54), channel_id=1, source_target_pairs={{0,12},{1,13},{2,14},{3,15},{4,0},{5,1},{6,2},{7,3},{8,4},{9,5},{1... | collective-permute-start | bytes 491528 | tf_op jit(solution)/shard_map/ppermute | solution.py:42
  59.6 6.3 %collective-permute-start.22 = (bf16[32,2560]{1,0:T(8,128)(2,1)S(1)}, bf16[32,2560]{1,0:T(8,128)(2,1)S(1)}, u32[]{:S(2)}, u32[]{:S(2)}) collective-permute-start(bf16[32,2560]{1,0:T(8,128)(2,1)S(1)} %get-tuple-element.51), channel_id=1, source_target_pairs={{0,2},{1,3},{2,0},{3,1},{4,6},{5,7},{6,4},{7,5},{8,10},{9,11},{10,... | collective-permute-start | bytes 491528 | tf_op jit(solution)/shard_map/ppermute | solution.py:38
  61.2 5.7 %collective-permute-start.20 = (bf16[32,2560]{1,0:T(8,128)(2,1)S(1)}, bf16[32,2560]{1,0:T(8,128)(2,1)S(1)}, u32[]{:S(2)}, u32[]{:S(2)}) collective-permute-start(bf16[32,2560]{1,0:T(8,128)(2,1)S(1)} %get-tuple-element.48), channel_id=1, source_target_pairs={{0,4},{1,5},{2,6},{3,7},{4,8},{5,9},{6,10},{7,11},{8,12},{9,13},{1... | collective-permute-start | bytes 491528 | tf_op jit(solution)/shard_map/ppermute | solution.py:42
  61.2 5.7 %collective-permute-start.21 = (bf16[32,2560]{1,0:T(8,128)(2,1)S(1)}, bf16[32,2560]{1,0:T(8,128)(2,1)S(1)}, u32[]{:S(2)}, u32[]{:S(2)}) collective-permute-start(bf16[32,2560]{1,0:T(8,128)(2,1)S(1)} %get-tuple-element.49), channel_id=1, source_target_pairs={{0,12},{1,13},{2,14},{3,15},{4,0},{5,1},{6,2},{7,3},{8,4},{9,5},{1... | collective-permute-start | bytes 491528 | tf_op jit(solution)/shard_map/ppermute | solution.py:42
  63.9 5.8 %collective-permute-start.26 = (bf16[32,2560]{1,0:T(8,128)(2,1)S(1)}, bf16[32,2560]{1,0:T(8,128)(2,1)S(1)}, u32[]{:S(2)}, u32[]{:S(2)}) collective-permute-start(bf16[32,2560]{1,0:T(8,128)(2,1)S(1)} %shard_map.195), channel_id=1, source_target_pairs={{0,2},{1,3},{2,0},{3,1},{4,6},{5,7},{6,4},{7,5},{8,10},{9,11},{10,... | collective-permute-start | bytes 491528 | tf_op jit(solution)/shard_map/ppermute | solution.py:38
  65.9 9.0 %copy-start.11 = (f32[5120]{0:T(1024)S(1)}, f32[5120]{0:T(1024)}, u32[]{:S(2)}) copy-start(f32[5120]{0:T(1024)} %param.19) | copy-start | bytes 61444
  65.9 9.0 %copy-start.12 = (f32[5120]{0:T(1024)S(1)}, f32[5120]{0:T(1024)}, u32[]{:S(2)}) copy-start(f32[5120]{0:T(1024)} %param.26) | copy-start | bytes 61444
  65.9 10.1 %copy-start.1 = (bf16[5120,64]{0,1:T(8,128)(2,1)S(1)}, bf16[5120,64]{0,1:T(8,128)(2,1)}, u32[]{:S(2)}) copy-start(bf16[5120,64]{0,1:T(8,128)(2,1)} %param.27) | copy-start | bytes 1966084
  65.9 10.1 %copy-start.6 = (f32[4,256]{1,0:T(4,128)S(1)}, f32[4,256]{1,0:T(4,128)}, u32[]{:S(2)}) copy-start(f32[4,256]{1,0:T(4,128)} %refs_7_.1) | copy-start | bytes 12292
  66.0 10.0 %copy-start.7 = (f32[4,256]{1,0:T(4,128)S(1)}, f32[4,256]{1,0:T(4,128)}, u32[]{:S(2)}) copy-start(f32[4,256]{1,0:T(4,128)} %refs_8_.1) | copy-start | bytes 12292
  66.0 10.0 %copy-start.8 = (s32[4,1]{0,1:T(1,128)S(1)}, s32[4,1]{0,1:T(1,128)}, u32[]{:S(2)}) copy-start(s32[4,1]{0,1:T(1,128)} %param.30) | copy-start | bytes 52
  66.0 23.6 %copy-start.2 = (bf16[256,1024]{1,0:T(8,128)(2,1)S(1)}, bf16[256,1024]{1,0:T(8,128)(2,1)}, u32[]{:S(2)}) copy-start(bf16[256,1024]{1,0:T(8,128)(2,1)} %refs_1_.7) | copy-start | bytes 1572868
  66.0 6.0 %collective-permute-start.23 = (bf16[32,2560]{1,0:T(8,128)(2,1)S(1)}, bf16[32,2560]{1,0:T(8,128)(2,1)S(1)}, u32[]{:S(2)}, u32[]{:S(2)}) collective-permute-start(bf16[32,2560]{1,0:T(8,128)(2,1)S(1)} %shard_map.194), channel_id=1, source_target_pairs={{0,8},{1,9},{2,10},{3,11},{4,12},{5,13},{6,14},{7,15},{8,0},{9,1},... | collective-permute-start | bytes 491528 | tf_op jit(solution)/shard_map/ppermute | solution.py:42
  72.2 3.8 %collective-permute-start.27 = (f32[16,2560]{1,0:T(8,128)S(1)}, f32[16,2560]{1,0:T(8,128)S(1)}, u32[]{:S(2)}, u32[]{:S(2)}) collective-permute-start(f32[16,2560]{1,0:T(8,128)S(1)} %get-tuple-element.56), channel_id=1, source_target_pairs={{0,1},{1,0},{2,3},{3,2},{4,5},{5,4},{6,7},{7,6},{8,9},{9,8},{10,11... | collective-permute-start | bytes 491528 | tf_op jit(solution)/shard_map/ppermute | solution.py:34
